TPU v7x, 32 devices: a whole 2x2x4 slice. The times are simulated.
32 devices in a mesh: dp: 8 (over z, y), shard: 4 (over x, core).
Axes of the slice: x: 2, y: 2, z: 4, core: 2. Of those that a mesh axis runs over, the one named last changes fastest.
Arguments:
- tokens: bfloat16 [8192, 2304], P(('dp', 'shard')), may hold values from -6 to 6
- cotangent: bfloat16 [8192, 2304], P(('dp', 'shard')), may hold values from -6 to 6
- arrival: int32 [32, 256], P(('dp', 'shard')), may hold values from 0 to 255, each once within a row
- lengths: int32 [32, 4], P(('dp', 'shard')), may hold values from 1 to 128, 256 in all within a row
- adapter_set: int32 [32, 4], P(('dp', 'shard')), may hold values from 0 to 7
- gain_one: bfloat16 [2304], replicated, may hold values from 0.099609375 to 1.8984375
- gain_two: bfloat16 [2304], replicated, may hold values from 0.099609375 to 1.8984375
- w_query: bfloat16 [2304, 2304], P('dp'), may hold values from -0.125 to 0.125
- w_key: bfloat16 [2304, 2304], P('dp'), may hold values from -0.125 to 0.125
- w_value: bfloat16 [2304, 2304], P('dp'), may hold values from -0.125 to 0.125
- w_out: bfloat16 [2304, 2304], P('dp'), may hold values from -2 to 2
- w_gate: bfloat16 [2304, 5760], P('dp'), may hold values from -0.125 to 0.125
- w_up: bfloat16 [2304, 5760], P('dp'), may hold values from -0.125 to 0.125
- w_down: bfloat16 [5760, 2304], P('dp'), may hold values from -0.5 to 0.5
- adapters: bfloat16 [5455872], replicated, may hold values from -0.5 to 0.5
- first_moment_running: float32 [5455872], P(('dp', 'shard')), may hold values from -6 to 6
- second_moment_running: float32 [5455872], P(('dp', 'shard')), may hold values from 0.01 to 1
Outputs:
- token_layer_output: bfloat16 [8192, 2304], P(('dp', 'shard'))
- token_input_gradient: bfloat16 [8192, 2304], P(('dp', 'shard'))
- adapter_gradients: float32 [5455872], P(('dp', 'shard'))
- fresh_first_moment: float32 [5455872], P(('dp', 'shard'))
- fresh_second_moment: float32 [5455872], P(('dp', 'shard'))
- updated_adapter_weights: bfloat16 [5455872], replicated
Inputs may be any that keep to these rules, and one draw needn't show every extreme that they name: `arrival`: each device's row lists every number of 0 to 255 once. Each device's 4 lengths sum to 256; the longest of each device is exactly 128.
All inputs are finite; a program needn't handle non-finite values.
Results may differ from a plain program's by a relative error of at most 0.018.
Values may be sent and summed in bfloat16 or wider, within the bound.
No kernel may reach another device: no remote copies, remote signals or barrier semaphores. Data moves between devices by JAX's collectives and lax.ppermute only.
A program may use at most 320 MiB of HBM per device.

v0:
```python
import math

import jax
import jax.numpy as jnp
from jax import lax
from jax.sharding import PartitionSpec as P

MODEL_WIDTH = 2304
ATTENTION_HEADS = 36
HEAD_SIZE = 64
FEEDFORWARD_UNITS = 5760
ADAPTER_RANK = 16
OPT_STEP = 10
SEQ_DEV = 4
TOK_DEV = 256
ADAPTER_COLUMNS = 128


norm_eps = 1e-05
residual_branch_scale = 1.4 / math.sqrt(40.0)
adapter_scale = 2.0
rope_base = 10000.0
first_decay_rate = 0.9
second_decay_rate = 0.999
adaptive_epsilon = 1e-08
weight_shrink_rate = 0.01
learning_rate = 0.01


def matrix_product(left_side, right_side):
    return jnp.dot(left_side, right_side, preferred_element_type=jnp.float32)


def matrix_product_backward(left_side, right_side):
    return lax.dot_general(
        left_side, right_side, (((1,), (1,)), ((), ())), preferred_element_type=jnp.float32
    )


def outer_product_sum(left_side, right_side):
    return lax.dot_general(
        left_side, right_side, (((0,), (0,)), ((), ())), preferred_element_type=jnp.float32
    )


def project_to_rank(values):
    return values.astype(jnp.bfloat16)


def block_tables(sequence_lengths, sequence_adapter_index):
    row_ids = jnp.arange(TOK_DEV, dtype=jnp.int32)
    seq_ends = jnp.cumsum(sequence_lengths, dtype=jnp.int32)
    seq_starts = seq_ends - sequence_lengths
    segment = jnp.sum(
        (row_ids[:, None] >= seq_ends[None, :]).astype(jnp.int32), axis=1, dtype=jnp.int32
    )
    member = (segment[:, None] == jnp.arange(SEQ_DEV, dtype=jnp.int32)[None, :]).astype(jnp.int32)
    position = row_ids - jnp.sum(member * seq_starts[None, :], axis=1, dtype=jnp.int32)
    token_adapter_index = jnp.sum(member * sequence_adapter_index[None, :], axis=1, dtype=jnp.int32)
    adapter_choice_index = (
        jnp.arange(ADAPTER_COLUMNS, dtype=jnp.int32)[None, :] // ADAPTER_RANK
        == token_adapter_index[:, None]
    ).astype(jnp.float32)
    allowed = (segment[:, None] == segment[None, :]) & (row_ids[None, :] <= row_ids[:, None])
    half_dim = HEAD_SIZE // 2
    inv_freq = jnp.power(rope_base, -2.0 * jnp.arange(half_dim, dtype=jnp.float32) / HEAD_SIZE)
    angles = position.astype(jnp.float32)[:, None] * inv_freq[None, :]
    return (adapter_choice_index, allowed, jnp.cos(angles)[:, None, :], jnp.sin(angles)[:, None, :])


def rotary_embedding(values, cosine_table, sine_table):
    shaped = values.reshape(values.shape[0], ATTENTION_HEADS, HEAD_SIZE)
    first_half = shaped[..., : HEAD_SIZE // 2]
    second_half = shaped[..., HEAD_SIZE // 2 :]
    turned = jnp.concatenate(
        [
            first_half * cosine_table - second_half * sine_table,
            second_half * cosine_table + first_half * sine_table,
        ],
        axis=-1,
    )
    return turned.reshape(values.shape[0], MODEL_WIDTH)


def rotary_back(gradient_value, cosine_table, sine_table):
    first_half = gradient_value[..., : HEAD_SIZE // 2]
    second_half = gradient_value[..., HEAD_SIZE // 2 :]
    turned = jnp.concatenate(
        [
            first_half * cosine_table + second_half * sine_table,
            second_half * cosine_table - first_half * sine_table,
        ],
        axis=-1,
    )
    return turned.reshape(gradient_value.shape[0], MODEL_WIDTH)


def restore_structure(flattened_vector):
    first_boundary = 6 * MODEL_WIDTH * ADAPTER_COLUMNS
    second_boundary = first_boundary + FEEDFORWARD_UNITS * ADAPTER_COLUMNS
    third_boundary = second_boundary + 5 * ADAPTER_COLUMNS * MODEL_WIDTH
    return (
        flattened_vector[:first_boundary].reshape(6, MODEL_WIDTH, ADAPTER_COLUMNS),
        flattened_vector[first_boundary:second_boundary].reshape(
            FEEDFORWARD_UNITS, ADAPTER_COLUMNS
        ),
        flattened_vector[second_boundary:third_boundary].reshape(5, ADAPTER_COLUMNS, MODEL_WIDTH),
        flattened_vector[third_boundary:].reshape(2, ADAPTER_COLUMNS, FEEDFORWARD_UNITS),
    )


def rms_scale(values):
    return lax.rsqrt(jnp.mean(values * values, axis=-1, keepdims=True) + norm_eps)


def norm_back(values, scale, gain, gradient_value):
    weighted = gradient_value * gain
    return scale * weighted - values * scale**3 * jnp.mean(
        values * weighted, axis=-1, keepdims=True
    )


def apply_adapter_delta(input_rows, adapter_down_pair, adapter_up_pair, adapter_choice_index):
    reduced_total = project_to_rank(
        matrix_product(input_rows, adapter_down_pair) * adapter_choice_index
    )
    return (reduced_total, adapter_scale * matrix_product(reduced_total, adapter_up_pair))


def adapter_backward_pass(
    gradient_value,
    input_rows,
    reduced_total,
    adapter_down_pair,
    adapter_up_pair,
    adapter_choice_index,
):
    reduced_gradient_sum = project_to_rank(
        adapter_scale
        * matrix_product_backward(gradient_value, adapter_up_pair)
        * adapter_choice_index
    )
    up_weight_gradient = adapter_scale * outer_product_sum(reduced_total, gradient_value)
    down_weight_gradient = outer_product_sum(input_rows, reduced_gradient_sum)
    return (
        down_weight_gradient,
        up_weight_gradient,
        matrix_product_backward(reduced_gradient_sum, adapter_down_pair),
    )


def fold_rows(input_rows, pieces):
    return tuple((matrix_product(input_rows, shard_rows) for shard_rows in pieces))


def fold_cols(gradients, pieces):
    product = matrix_product_backward(gradients[0], pieces[0])
    for gradient_value, shard_rows in zip(gradients[1:], pieces[1:]):
        product = product + matrix_product_backward(gradient_value, shard_rows)
    return product


def attention_scores(query_rows, key_rows, allowed):
    scores = jnp.einsum(
        "qhd,khd->hqk", query_rows, key_rows, preferred_element_type=jnp.float32
    ) * HEAD_SIZE ** (-0.5)
    return jnp.where(allowed[None], scores, -jnp.inf)


def attention_forward(query_rows, key_rows, value_matrix_rows, allowed):
    scores = attention_scores(query_rows, key_rows, allowed)
    row_top = jnp.max(scores, axis=-1, keepdims=True)
    expanded = jnp.exp(scores - row_top)
    row_total = jnp.sum(expanded, axis=-1, keepdims=True)
    probs_low = project_to_rank(expanded / row_total)
    attention_result = jnp.einsum(
        "hqk,khd->qhd", probs_low, value_matrix_rows, preferred_element_type=jnp.float32
    )
    return (attention_result, row_top, row_total)


def attention_back(
    query_rows, key_rows, value_matrix_rows, allowed, row_top, row_total, grad_attended
):
    probs_full = jnp.exp(attention_scores(query_rows, key_rows, allowed) - row_top) / row_total
    grad_probs = jnp.einsum(
        "qhd,khd->hqk", grad_attended, value_matrix_rows, preferred_element_type=jnp.float32
    )
    row_delta = jnp.sum(probs_full * grad_probs, axis=-1, keepdims=True)
    grad_scores = project_to_rank(probs_full * (grad_probs - row_delta))
    grad_queries = HEAD_SIZE ** (-0.5) * jnp.einsum(
        "hqk,khd->qhd", grad_scores, key_rows, preferred_element_type=jnp.float32
    )
    grad_keys = HEAD_SIZE ** (-0.5) * jnp.einsum(
        "hqk,qhd->khd", grad_scores, query_rows, preferred_element_type=jnp.float32
    )
    grad_values = jnp.einsum(
        "hqk,qhd->khd",
        project_to_rank(probs_full),
        grad_attended,
        preferred_element_type=jnp.float32,
    )
    return (grad_queries, grad_keys, grad_values)


def shards(
    tokens,
    cotangent,
    arrival,
    lengths,
    adapter_set,
    gain_one,
    gain_two,
    w_query,
    w_key,
    w_value,
    w_out,
    w_gate,
    w_up,
    w_down,
    adapters,
    first_moment_running,
    second_moment_running,
):
    arrived_x, arrived_cot = (
        lax.all_to_all(tokens, "dp", split_axis=0, concat_axis=0, tiled=True),
        lax.all_to_all(cotangent, "dp", split_axis=0, concat_axis=0, tiled=True),
    )
    token_order = arrival[0]
    count_of_rows = token_order.shape[0]
    input_row_matrix = arrived_x[token_order].astype(jnp.float32)
    cot_rows = arrived_cot[token_order].astype(jnp.float32)
    adapter_choice_index, allowed, cosine_table, sine_table = block_tables(
        lengths[0], adapter_set[0]
    )
    lower_model_factor, lower_hidden_factor, upper_model_factor, upper_hidden_factor = (
        restore_structure(adapters)
    )
    gain_first = gain_one.astype(jnp.float32)
    gain_second = gain_two.astype(jnp.float32)
    scale_one = rms_scale(input_row_matrix)
    first_normalized = project_to_rank(input_row_matrix * scale_one * gain_first)
    frozen_query_weight, frozen_key_weight, frozen_value_weight = fold_rows(
        first_normalized,
        (
            lax.all_gather(w_query, "dp", axis=0, tiled=True),
            lax.all_gather(w_key, "dp", axis=0, tiled=True),
            lax.all_gather(w_value, "dp", axis=0, tiled=True),
        ),
    )
    summed_query_gradient, adapter_query_pair = apply_adapter_delta(
        first_normalized, lower_model_factor[0], upper_model_factor[0], adapter_choice_index
    )
    summed_key_gradient, adapter_key_pair = apply_adapter_delta(
        first_normalized, lower_model_factor[1], upper_model_factor[1], adapter_choice_index
    )
    summed_value_gradient, adapter_value_pair = apply_adapter_delta(
        first_normalized, lower_model_factor[2], upper_model_factor[2], adapter_choice_index
    )
    value_matrix_rows = project_to_rank(frozen_value_weight + adapter_value_pair).reshape(
        count_of_rows, ATTENTION_HEADS, HEAD_SIZE
    )
    query_rows = project_to_rank(
        rotary_embedding(frozen_query_weight + adapter_query_pair, cosine_table, sine_table)
    ).reshape(count_of_rows, ATTENTION_HEADS, HEAD_SIZE)
    key_rows = project_to_rank(
        rotary_embedding(frozen_key_weight + adapter_key_pair, cosine_table, sine_table)
    ).reshape(count_of_rows, ATTENTION_HEADS, HEAD_SIZE)
    attention_result, row_top, row_total = attention_forward(
        query_rows, key_rows, value_matrix_rows, allowed
    )
    attention_result = project_to_rank(attention_result.reshape(count_of_rows, MODEL_WIDTH))
    (frozen_output_weight,) = fold_rows(
        attention_result, (lax.all_gather(w_out, "dp", axis=0, tiled=True),)
    )
    summed_output_gradient, adapter_output_pair = apply_adapter_delta(
        attention_result, lower_model_factor[3], upper_model_factor[3], adapter_choice_index
    )
    middle_residual = input_row_matrix + residual_branch_scale * (
        frozen_output_weight + adapter_output_pair
    )
    scale_two = rms_scale(middle_residual)
    second_normalized = project_to_rank(middle_residual * scale_two * gain_second)
    frozen_gate_weight, frozen_up_weight = fold_rows(
        second_normalized,
        (
            lax.all_gather(w_gate, "dp", axis=0, tiled=True),
            lax.all_gather(w_up, "dp", axis=0, tiled=True),
        ),
    )
    summed_gate_gradient, adapter_gate_pair = apply_adapter_delta(
        second_normalized, lower_model_factor[4], upper_hidden_factor[0], adapter_choice_index
    )
    summed_up_gradient, adapter_upper_factor = apply_adapter_delta(
        second_normalized, lower_model_factor[5], upper_hidden_factor[1], adapter_choice_index
    )
    gate_linear_output = frozen_gate_weight + adapter_gate_pair
    up_linear_output = frozen_up_weight + adapter_upper_factor
    gate_sigmoid = jax.nn.sigmoid(gate_linear_output)
    gate_act = gate_linear_output * gate_sigmoid
    hidden_activation = project_to_rank(gate_act * up_linear_output)
    (frozen_down_weight,) = fold_rows(
        hidden_activation, (lax.all_gather(w_down, "dp", axis=0, tiled=True),)
    )
    summed_down_gradient, adapter_lower_factor = apply_adapter_delta(
        hidden_activation, lower_hidden_factor, upper_model_factor[4], adapter_choice_index
    )
    block_output_rows = middle_residual + residual_branch_scale * (
        frozen_down_weight + adapter_lower_factor
    )
    grad_down_lin = project_to_rank(residual_branch_scale * cot_rows)
    grad_hidden = fold_cols((grad_down_lin,), (lax.all_gather(w_down, "dp", axis=0, tiled=True),))
    down_grad_down, up_grad_down, through_down = adapter_backward_pass(
        grad_down_lin,
        hidden_activation,
        summed_down_gradient,
        lower_hidden_factor,
        upper_model_factor[4],
        adapter_choice_index,
    )
    grad_hidden = grad_hidden + through_down
    grad_gate = project_to_rank(
        grad_hidden
        * up_linear_output
        * (gate_sigmoid + gate_linear_output * gate_sigmoid * (1.0 - gate_sigmoid))
    )
    up_weight_gradient = project_to_rank(grad_hidden * gate_act)
    down_grad_gate, up_grad_gate, through_gate = adapter_backward_pass(
        grad_gate,
        second_normalized,
        summed_gate_gradient,
        lower_model_factor[4],
        upper_hidden_factor[0],
        adapter_choice_index,
    )
    down_grad_up, up_grad_up, through_up = adapter_backward_pass(
        up_weight_gradient,
        second_normalized,
        summed_up_gradient,
        lower_model_factor[5],
        upper_hidden_factor[1],
        adapter_choice_index,
    )
    grad_normed_two = fold_cols(
        (grad_gate, up_weight_gradient),
        (
            lax.all_gather(w_gate, "dp", axis=0, tiled=True),
            lax.all_gather(w_up, "dp", axis=0, tiled=True),
        ),
    )
    grad_middle = cot_rows + norm_back(
        middle_residual, scale_two, gain_second, grad_normed_two + through_gate + through_up
    )
    grad_out_lin = project_to_rank(residual_branch_scale * grad_middle)
    grad_attended = fold_cols((grad_out_lin,), (lax.all_gather(w_out, "dp", axis=0, tiled=True),))
    down_grad_out, up_grad_out, through_out = adapter_backward_pass(
        grad_out_lin,
        attention_result,
        summed_output_gradient,
        lower_model_factor[3],
        upper_model_factor[3],
        adapter_choice_index,
    )
    grad_attended = project_to_rank(grad_attended + through_out).reshape(
        count_of_rows, ATTENTION_HEADS, HEAD_SIZE
    )
    grad_queries, grad_keys, grad_values = attention_back(
        query_rows, key_rows, value_matrix_rows, allowed, row_top, row_total, grad_attended
    )
    grad_query = project_to_rank(rotary_back(grad_queries, cosine_table, sine_table))
    grad_key = project_to_rank(rotary_back(grad_keys, cosine_table, sine_table))
    grad_value = project_to_rank(grad_values.reshape(count_of_rows, MODEL_WIDTH))
    down_grad_query, up_grad_query, through_query = adapter_backward_pass(
        grad_query,
        first_normalized,
        summed_query_gradient,
        lower_model_factor[0],
        upper_model_factor[0],
        adapter_choice_index,
    )
    down_grad_key, up_grad_key, through_key = adapter_backward_pass(
        grad_key,
        first_normalized,
        summed_key_gradient,
        lower_model_factor[1],
        upper_model_factor[1],
        adapter_choice_index,
    )
    down_grad_value, up_grad_value, through_value = adapter_backward_pass(
        grad_value,
        first_normalized,
        summed_value_gradient,
        lower_model_factor[2],
        upper_model_factor[2],
        adapter_choice_index,
    )
    grad_normed_one = fold_cols(
        (grad_query, grad_key, grad_value),
        (
            lax.all_gather(w_query, "dp", axis=0, tiled=True),
            lax.all_gather(w_key, "dp", axis=0, tiled=True),
            lax.all_gather(w_value, "dp", axis=0, tiled=True),
        ),
    )
    grad_rows = grad_middle + norm_back(
        input_row_matrix,
        scale_one,
        gain_first,
        grad_normed_one + through_query + through_key + through_value,
    )
    adapter_gradients = jnp.concatenate(
        [
            jnp.stack(
                [
                    down_grad_query,
                    down_grad_key,
                    down_grad_value,
                    down_grad_out,
                    down_grad_gate,
                    down_grad_up,
                ]
            ).reshape(-1),
            down_grad_down.reshape(-1),
            jnp.stack(
                [up_grad_query, up_grad_key, up_grad_value, up_grad_out, up_grad_down]
            ).reshape(-1),
            jnp.stack([up_grad_gate, up_grad_up]).reshape(-1),
        ]
    )
    gradient_portion = lax.psum_scatter(
        adapter_gradients, ("dp", "shard"), scatter_dimension=0, tiled=True
    )
    inverse = (
        jnp.zeros_like(token_order).at[token_order].set(jnp.arange(count_of_rows, dtype=jnp.int32))
    )
    back_out, back_grad = (
        lax.all_to_all(
            project_to_rank(block_output_rows)[inverse],
            "dp",
            split_axis=0,
            concat_axis=0,
            tiled=True,
        ),
        lax.all_to_all(
            project_to_rank(grad_rows)[inverse], "dp", split_axis=0, concat_axis=0, tiled=True
        ),
    )
    share_len = first_moment_running.shape[0]
    offset = lax.axis_index(("dp", "shard")) * share_len
    own_params = lax.dynamic_slice_in_dim(adapters, offset, share_len).astype(jnp.float32)
    fresh_first_moment = (
        first_decay_rate * first_moment_running + (1.0 - first_decay_rate) * gradient_portion
    )
    fresh_second_moment = (
        second_decay_rate * second_moment_running
        + (1.0 - second_decay_rate) * gradient_portion * gradient_portion
    )
    unbiased_first = fresh_first_moment / (1.0 - first_decay_rate**OPT_STEP)
    unbiased_second = fresh_second_moment / (1.0 - second_decay_rate**OPT_STEP)
    optimizer_update = (
        unbiased_first / (jnp.sqrt(unbiased_second) + adaptive_epsilon)
        + weight_shrink_rate * own_params
    )
    fresh_params = project_to_rank(own_params - learning_rate * optimizer_update)
    updated_adapter_weights = lax.all_gather(fresh_params, ("dp", "shard"), axis=0, tiled=True)
    return (
        back_out,
        back_grad,
        gradient_portion,
        fresh_first_moment,
        fresh_second_moment,
        updated_adapter_weights,
    )


def solution(mesh):
    return jax.shard_map(
        shards,
        mesh=mesh,
        in_specs=(
            P(("dp", "shard"), None),
            P(("dp", "shard"), None),
            P(("dp", "shard"), None),
            P(("dp", "shard"), None),
            P(("dp", "shard"), None),
            P(),
            P(),
            P("dp", None),
            P("dp", None),
            P("dp", None),
            P("dp", None),
            P("dp", None),
            P("dp", None),
            P("dp", None),
            P(),
            P(("dp", "shard")),
            P(("dp", "shard")),
        ),
        out_specs=(
            P(("dp", "shard"), None),
            P(("dp", "shard"), None),
            P(("dp", "shard")),
            P(("dp", "shard")),
            P(("dp", "shard")),
            P(),
        ),
        check_vma=False,
    )
```

profile of v0, /device:TPU:0, one launch (start us, length us, event | category | flops | bytes accessed | tf_op | source)
XLA Modules:
  0.0 3123.1 jit_solution(10283514594536927025)
XLA Ops:
  11.9 7.3 all-to-all-start
  19.2 4.0 fusion.154
  23.2 51.3 %all-to-all-done = bf16[8,32,2304]{2,1,0:T(8,128)(2,1)S(1)} async-done(((bf16[8,32,2304]{2,1,0:T(8,128)(2,1)}), bf16[8,32,2304]{2,1,0:T(8,128)(2,1)S(1)}, u32[]{:S(2)}, u32[]{:S(2)}) %all-to-all-start) | async-done | bytes 1179680 | tf_op jit(solution)/shard_map/all_to_all | solution.py:226
  74.5 7.2 all-to-all-start.2
  95.1 4.0 squeeze.8
  99.2 4.1 squeeze.7
  109.5 6.3 all-to-all-done.2
  126.6 77.8 %all-gather.12.cloned.1.call-done = bf16[2304,2304]{1,0:T(8,128)(2,1)} async-done(((bf16[288,2304]{1,0:T(8,128)(2,1)}), bf16[2304,2304]{1,0:T(8,128)(2,1)}) %all-gather.12.cloned.1.call-update) | async-done | bytes 10616848 | tf_op jit(solution)/shard_map/all_gather | solution.py:246
  204.4 6.2 fusion.147
  214.8 142.4 %all-gather.14.cloned.1.call-done = bf16[2304,2304]{1,0:T(8,128)(2,1)} async-done(((bf16[288,2304]{1,0:T(8,128)(2,1)}), bf16[2304,2304]{1,0:T(8,128)(2,1)}) %all-gather.14.cloned.1.call-update) | async-done | bytes 10616848 | tf_op jit(solution)/shard_map/all_gather | solution.py:247
  357.2 6.1 fusion.144
  368.6 141.5 %all-gather.10.cloned.1.call-done = bf16[2304,2304]{1,0:T(8,128)(2,1)} async-done(((bf16[288,2304]{1,0:T(8,128)(2,1)}), bf16[2304,2304]{1,0:T(8,128)(2,1)}) %all-gather.10.cloned.1.call-update) | async-done | bytes 10616848 | tf_op jit(solution)/shard_map/all_gather | solution.py:248
  510.1 6.1 fusion.150
  520.2 4.1 subtract_convert_fusion.3
  524.3 9.1 fusion.155
  533.4 4.7 fusion.52
  540.7 122.0 %all-gather.16.cloned.1.call-done = bf16[2304,2304]{1,0:T(8,128)(2,1)} async-done(((bf16[288,2304]{1,0:T(8,128)(2,1)}), bf16[2304,2304]{1,0:T(8,128)(2,1)}) %all-gather.16.cloned.1.call-update) | async-done | bytes 10616848 | tf_op jit(solution)/shard_map/all_gather | solution.py:274
  662.8 6.5 fusion.156
  675.7 492.9 %all-gather.20.cloned.1.call-done = bf16[2304,5760]{1,0:T(8,128)(2,1)} async-done(((bf16[288,5760]{1,0:T(8,128)(2,1)}), bf16[2304,5760]{1,0:T(8,128)(2,1)}) %all-gather.20.cloned.1.call-update) | async-done | bytes 26542096 | tf_op jit(solution)/shard_map/all_gather | solution.py:288
  1168.6 13.1 fusion.158
  1185.2 491.1 %all-gather.18.cloned.1.call-done = bf16[2304,5760]{1,0:T(8,128)(2,1)} async-done(((bf16[288,5760]{1,0:T(8,128)(2,1)}), bf16[2304,5760]{1,0:T(8,128)(2,1)}) %all-gather.18.cloned.1.call-update) | async-done | bytes 26542096 | tf_op jit(solution)/shard_map/all_gather | solution.py:287
  1676.2 13.1 fusion.157
  1692.8 491.2 %all-gather.22.cloned.1.call-done = bf16[5760,2304]{1,0:T(8,128)(2,1)} async-done(((bf16[720,2304]{1,0:T(8,128)(2,1)}), bf16[5760,2304]{1,0:T(8,128)(2,1)}) %all-gather.22.cloned.1.call-update) | async-done | bytes 26542096 | tf_op jit(solution)/shard_map/all_gather | solution.py:303
  2184.0 14.7 fusion.91
  2198.7 9.6 multiply_convert_fusion.1
  2212.5 14.8 fusion.160
  2227.3 15.2 convolution_add_fusion.7
  2255.1 10.2 multiply_reduce_fusion
  2265.3 10.4 multiply_convert_fusion
  2281.4 5.3 fusion.55
  2318.0 6.8 reshape.405
  2324.8 5.6 pad_maximum_fusion.1
  2330.4 6.8 reshape.406
  2337.2 20.3 pad_maximum_fusion
  2357.6 351.3 %all-reduce.3.cloned.1.call-done = f32[5455872]{0:T(1024)} async-done(((f32[5455872]{0:T(1024)}), f32[5455872]{0:T(1024)}) %all-reduce.3.cloned.1.call-update) | async-done | bytes 21823504
  2709.0 3.6 fusion.97
  2712.5 4.6 reshape.449
  2719.3 6.7 fusion.161
  2726.1 8.7 convolution_add_fusion.9
  2734.8 4.8 convolution_add_fusion.8
  2748.1 4.2 all-to-all-start.3
  2752.4 13.1 fusion.159
  2768.6 37.2 %all-to-all-done.3 = bf16[8,32,2304]{2,1,0:T(8,128)(2,1)} async-done(((bf16[8,32,2304]{2,1,0:T(8,128)(2,1)}), bf16[8,32,2304]{2,1,0:T(8,128)(2,1)}, u32[]{:S(2)}, u32[]{:S(2)}) %all-to-all-start.3) | async-done | bytes 1179680 | tf_op jit(solution)/shard_map/all_to_all | solution.py:444
  2805.8 3.8 all-to-all-start.1
  2809.6 61.0 %all-to-all-done.1 = bf16[8,32,2304]{2,1,0:T(8,128)(2,1)S(1)} async-done(((bf16[8,32,2304]{2,1,0:T(8,128)(2,1)}), bf16[8,32,2304]{2,1,0:T(8,128)(2,1)S(1)}, u32[]{:S(2)}, u32[]{:S(2)}) %all-to-all-start.1) | async-done | bytes 1179680 | tf_op jit(solution)/shard_map/all_to_all | solution.py:437
  2870.6 29.1 all-gather.24.cloned.1.call-done
  2899.8 193.5 %reduce = bf16[32,170496]{1,0:T(8,128)(2,1)} reduce(bf16[32,1,170496]{2,1,0:T(2,128)(2,1)} %all-gather.24.cloned.1.call-done, bf16[]{:T(256)} %constant.111), dimensions={1}, to_apply=%all-gather.reduce_sub_computation | reduce | bytes 21823490 | tf_op jit(solution)/shard_map/all_gather | solution.py:465
  3093.2 19.6 reshape.450
  (303 shorter events, 134.4 us)
Async XLA Ops:
  7.2 197.2 %all-gather.12.cloned.1.call-start = ((), (), s32[]{:S(2)}) async-start(), calls=%async_computation.5 | async-start | bytes 11943936 | tf_op jit(solution)/shard_map/all_gather | solution.py:246
  7.9 349.3 %all-gather.14.cloned.1.call-start = ((), (), s32[]{:S(2)}) async-start(), calls=%async_computation.6 | async-start | bytes 11943936 | tf_op jit(solution)/shard_map/all_gather | solution.py:247
  8.6 501.4 %all-gather.10.cloned.1.call-start = ((), (), s32[]{:S(2)}) async-start(), calls=%async_computation.4 | async-start | bytes 11943936 | tf_op jit(solution)/shard_map/all_gather | solution.py:248
  9.4 653.4 %all-gather.16.cloned.1.call-start = ((), (), s32[]{:S(2)}) async-start(), calls=%async_computation.7 | async-start | bytes 11943936 | tf_op jit(solution)/shard_map/all_gather | solution.py:274
  10.0 1158.6 %all-gather.20.cloned.1.call-start = ((), (), s32[]{:S(2)}) async-start(), calls=%async_computation.9 | async-start | bytes 29859840 | tf_op jit(solution)/shard_map/all_gather | solution.py:288
  10.5 1665.7 %all-gather.18.cloned.1.call-start = ((), (), s32[]{:S(2)}) async-start(), calls=%async_computation.8 | async-start | bytes 29859840 | tf_op jit(solution)/shard_map/all_gather | solution.py:287
  11.1 2172.9 %all-gather.22.cloned.1.call-start = ((), (), s32[]{:S(2)}) async-start(), calls=%async_computation.10 | async-start | bytes 29859840 | tf_op jit(solution)/shard_map/all_gather | solution.py:303
  11.9 62.6 %all-to-all-start = ((bf16[8,32,2304]{2,1,0:T(8,128)(2,1)}), bf16[8,32,2304]{2,1,0:T(8,128)(2,1)S(1)}, u32[]{:S(2)}, u32[]{:S(2)}) async-start(bf16[8,32,2304]{2,1,0:T(8,128)(2,1)} %bitcast), calls=%async_computation | async-start | bytes 2359296 | tf_op jit(solution)/shard_map/all_to_all | solution.py:226
  74.5 41.3 %all-to-all-start.2 = ((bf16[8,32,2304]{2,1,0:T(8,128)(2,1)}), bf16[8,32,2304]{2,1,0:T(8,128)(2,1)S(1)}, u32[]{:S(2)}, u32[]{:S(2)}) async-start(bf16[8,32,2304]{2,1,0:T(8,128)(2,1)} %bitcast.24), calls=%async_computation.2 | async-start | bytes 2359296 | tf_op jit(solution)/shard_map/all_to_all | solution.py:227
  81.7 2627.2 %all-reduce.3.cloned.1.call-start = ((), (), s32[]{:S(2)}) async-start(), calls=%async_computation.12 | async-start | bytes 43646976
  99.2 6.4 copy-start.89
  99.2 7.1 copy-start.90
  109.5 559.8 %copy-start.4 = (bf16[256,2304]{1,0:T(8,128)(2,1)}, bf16[256,2304]{1,0:T(8,128)(2,1)S(1)}, u32[]{:S(2)}) copy-start(bf16[256,2304]{1,0:T(8,128)(2,1)S(1)} %gather_fusion) | copy-start | bytes 3538948
  118.3 86.1 %copy-start.84 = (f32[256]{0:T(256)}, f32[256]{0:T(256)S(1)}, u32[]{:S(2)}) copy-start(f32[256]{0:T(256)S(1)} %get-tuple-element.37) | copy-start | bytes 3076
  122.1 88.5 %copy-start.62 = (bf16[256,128]{1,0:T(8,128)(2,1)}, bf16[256,128]{1,0:T(8,128)(2,1)S(1)}, u32[]{:S(2)}) copy-start(bf16[256,128]{1,0:T(8,128)(2,1)S(1)} %fusion.74) | copy-start | bytes 196612
  126.6 84.0 %copy-start.30 = (bf16[128,2304]{1,0:T(8,128)(2,1)S(1)}, bf16[128,2304]{1,0:T(8,128)(2,1)}, u32[]{:S(2)}) copy-start(bf16[128,2304]{1,0:T(8,128)(2,1)} %slice.235) | copy-start | bytes 1769476
  357.2 6.1 copy-start.26
  357.2 6.1 copy-start.58
  510.1 6.1 copy-start.28
  510.1 6.1 copy-start.56
  524.3 9.1 copy-start.41
  538.1 124.7 %copy-start.23 = (bf16[36,64,256]{2,1,0:T(8,128)(2,1)}, bf16[36,64,256]{2,1,0:T(8,128)(2,1)S(1)}, u32[]{:S(2)}) copy-start(bf16[36,64,256]{2,1,0:T(8,128)(2,1)S(1)} %fusion.52) | copy-start | bytes 3538948
  662.8 6.5 copy-start.32
  662.8 6.5 copy-start.50
  670.9 1005.3 %copy-start.18 = (bf16[256,2304]{1,0:T(8,128)(2,1)}, bf16[256,2304]{1,0:T(8,128)(2,1)S(1)}, u32[]{:S(2)}) copy-start(bf16[256,2304]{1,0:T(8,128)(2,1)S(1)} %multiply_convert_fusion.5) | copy-start | bytes 3538948
  1168.6 13.1 copy-start.7
  1168.6 13.2 copy-start.52
  1676.2 13.1 copy-start.9
  1676.2 13.1 copy-start.54
  1689.4 494.7 %copy-start.16 = (bf16[256,2304]{1,0:T(8,128)(2,1)S(1)}, bf16[256,2304]{1,0:T(8,128)(2,1)}, u32[]{:S(2)}) copy-start(bf16[256,2304]{1,0:T(8,128)(2,1)} %copy-done.15) | copy-start | bytes 3538948
  2198.7 9.7 copy-start.10
  2198.7 9.7 copy-start.77
  2265.3 10.4 copy-start.38
  2265.3 10.4 copy-start.39
  2286.7 26.8 copy-start.34
  2287.8 24.1 copy-start.20
  2289.2 11.6 copy-start.64
  2298.1 18.4 copy-start.60
  2357.6 542.2 %all-gather.24.cloned.1.call-start = ((), (), s32[]{:S(2)}) async-start(), calls=%async_computation.11 | async-start | bytes 22505472 | tf_op jit(solution)/shard_map/all_gather | solution.py:465
  2719.3 6.8 copy-start.21
  2719.3 15.5 slice-start.3
  2719.3 15.5 slice-start.4
  2726.1 8.7 copy-start.35
  2726.1 8.7 slice-start.5
  2748.1 57.7 %all-to-all-start.3 = ((bf16[8,32,2304]{2,1,0:T(8,128)(2,1)}), bf16[8,32,2304]{2,1,0:T(8,128)(2,1)}, u32[]{:S(2)}, u32[]{:S(2)}) async-start(bf16[8,32,2304]{2,1,0:T(8,128)(2,1)} %bitcast.240), calls=%async_computation.3 | async-start | bytes 2359296 | tf_op jit(solution)/shard_map/all_to_all | solution.py:444
  2752.4 13.2 copy-start.40
  2752.4 13.2 copy-start.61
  2805.8 64.8 %all-to-all-start.1 = ((bf16[8,32,2304]{2,1,0:T(8,128)(2,1)}), bf16[8,32,2304]{2,1,0:T(8,128)(2,1)S(1)}, u32[]{:S(2)}, u32[]{:S(2)}) async-start(bf16[8,32,2304]{2,1,0:T(8,128)(2,1)} %bitcast.22), calls=%async_computation.1 | async-start | bytes 2359296 | tf_op jit(solution)/shard_map/all_to_all | solution.py:437
  (63 other events, 175.5 us)
Sparse Core Ops, SparseCore 0:
  10.2 194.1 all-gather.11
  206.5 150.6 all-gather.13
  359.4 150.6 all-gather.9
  512.1 150.6 all-gather.15
  664.1 504.4 all-gather.19
  1170.0 506.1 all-gather.17
  1677.8 506.1 all-gather.21
  2357.7 351.2 all-reduce.2
  2717.3 182.4 all-gather.23
where the time goes:
time: 3130 us; the launch traced here: 3120 us
  waiting for transfers between devices  2500 us (80%)
  matrix products  248 us (8%)
  other arithmetic  246 us (8%)
  local copies, waits for them, and re-layouts  91 us (3%)
    all_gather x1, waiting for transfers between devices, shards(): lax.all_gather(w_up, 'dp', axis=0, tiled=True)  493 us
    all_gather x1, waiting for transfers between devices, shards(): lax.all_gather(w_down, 'dp', axis=0, tiled=True)  491 us
    all_gather x1, waiting for transfers between devices, shards(): lax.all_gather(w_gate, 'dp', axis=0, tiled=True)  491 us
    unnamed x10, waiting for transfers between devices  356 us
    all_gather x1, other arithmetic, shards(): lax.all_gather(fresh_params, ('dp', 'shard'), axis=0, tiled=True)  193 us
    all_gather x1, waiting for transfers between devices, shards(): lax.all_gather(w_key, 'dp', axis=0, tiled=True)  142 us
    all_gather x1, waiting for transfers between devices, shards(): lax.all_gather(w_value, 'dp', axis=0, tiled=True)  141 us
    all_gather x1, waiting for transfers between devices, shards(): lax.all_gather(w_out, 'dp', axis=0, tiled=True)  122 us
  transfers between devices with their start and end apart: 13, of which 13 were waited for; matrix products, arithmetic and copies ran while one was open for 6% of the time, Pallas kernels for 0%

commit v1 on v0

v1 whole, which is shorter than its diff:
```python
import functools
import math

import jax
import jax.numpy as jnp
from jax import lax
from jax.sharding import PartitionSpec as P

MODEL_WIDTH = 2304
ATTENTION_HEADS = 36
HEAD_SIZE = 64
FEEDFORWARD_UNITS = 5760
ADAPTER_RANK = 16
OPT_STEP = 10
SEQ_DEV = 4
TOK_DEV = 256
ADAPTER_COLUMNS = 128


norm_eps = 1e-05
residual_branch_scale = 1.4 / math.sqrt(40.0)
adapter_scale = 2.0
rope_base = 10000.0
first_decay_rate = 0.9
second_decay_rate = 0.999
adaptive_epsilon = 1e-08
weight_shrink_rate = 0.01
learning_rate = 0.01


def matrix_product(left_side, right_side):
    return jnp.dot(left_side, right_side, preferred_element_type=jnp.float32)


def matrix_product_backward(left_side, right_side):
    return lax.dot_general(
        left_side, right_side, (((1,), (1,)), ((), ())), preferred_element_type=jnp.float32
    )


def outer_product_sum(left_side, right_side):
    return lax.dot_general(
        left_side, right_side, (((0,), (0,)), ((), ())), preferred_element_type=jnp.float32
    )


def project_to_rank(values):
    return values.astype(jnp.bfloat16)


def block_tables(sequence_lengths, sequence_adapter_index):
    row_ids = jnp.arange(TOK_DEV, dtype=jnp.int32)
    seq_ends = jnp.cumsum(sequence_lengths, dtype=jnp.int32)
    seq_starts = seq_ends - sequence_lengths
    segment = jnp.sum(
        (row_ids[:, None] >= seq_ends[None, :]).astype(jnp.int32), axis=1, dtype=jnp.int32
    )
    member = (segment[:, None] == jnp.arange(SEQ_DEV, dtype=jnp.int32)[None, :]).astype(jnp.int32)
    position = row_ids - jnp.sum(member * seq_starts[None, :], axis=1, dtype=jnp.int32)
    token_adapter_index = jnp.sum(member * sequence_adapter_index[None, :], axis=1, dtype=jnp.int32)
    adapter_choice_index = (
        jnp.arange(ADAPTER_COLUMNS, dtype=jnp.int32)[None, :] // ADAPTER_RANK
        == token_adapter_index[:, None]
    ).astype(jnp.float32)
    allowed = (segment[:, None] == segment[None, :]) & (row_ids[None, :] <= row_ids[:, None])
    half_dim = HEAD_SIZE // 2
    inv_freq = jnp.power(rope_base, -2.0 * jnp.arange(half_dim, dtype=jnp.float32) / HEAD_SIZE)
    angles = position.astype(jnp.float32)[:, None] * inv_freq[None, :]
    return (adapter_choice_index, allowed, jnp.cos(angles)[:, None, :], jnp.sin(angles)[:, None, :])


def rotary_embedding(values, cosine_table, sine_table):
    shaped = values.reshape(values.shape[0], ATTENTION_HEADS, HEAD_SIZE)
    first_half = shaped[..., : HEAD_SIZE // 2]
    second_half = shaped[..., HEAD_SIZE // 2 :]
    turned = jnp.concatenate(
        [
            first_half * cosine_table - second_half * sine_table,
            second_half * cosine_table + first_half * sine_table,
        ],
        axis=-1,
    )
    return turned.reshape(values.shape[0], MODEL_WIDTH)


def rotary_back(gradient_value, cosine_table, sine_table):
    first_half = gradient_value[..., : HEAD_SIZE // 2]
    second_half = gradient_value[..., HEAD_SIZE // 2 :]
    turned = jnp.concatenate(
        [
            first_half * cosine_table + second_half * sine_table,
            second_half * cosine_table - first_half * sine_table,
        ],
        axis=-1,
    )
    return turned.reshape(gradient_value.shape[0], MODEL_WIDTH)


def restore_structure(flattened_vector):
    first_boundary = 6 * MODEL_WIDTH * ADAPTER_COLUMNS
    second_boundary = first_boundary + FEEDFORWARD_UNITS * ADAPTER_COLUMNS
    third_boundary = second_boundary + 5 * ADAPTER_COLUMNS * MODEL_WIDTH
    return (
        flattened_vector[:first_boundary].reshape(6, MODEL_WIDTH, ADAPTER_COLUMNS),
        flattened_vector[first_boundary:second_boundary].reshape(
            FEEDFORWARD_UNITS, ADAPTER_COLUMNS
        ),
        flattened_vector[second_boundary:third_boundary].reshape(5, ADAPTER_COLUMNS, MODEL_WIDTH),
        flattened_vector[third_boundary:].reshape(2, ADAPTER_COLUMNS, FEEDFORWARD_UNITS),
    )


def rms_scale(values):
    return lax.rsqrt(jnp.mean(values * values, axis=-1, keepdims=True) + norm_eps)


def norm_back(values, scale, gain, gradient_value):
    weighted = gradient_value * gain
    return scale * weighted - values * scale**3 * jnp.mean(
        values * weighted, axis=-1, keepdims=True
    )


def apply_adapter_delta(input_rows, adapter_down_pair, adapter_up_pair, adapter_choice_index):
    reduced_total = project_to_rank(
        matrix_product(input_rows, adapter_down_pair) * adapter_choice_index
    )
    return (reduced_total, adapter_scale * matrix_product(reduced_total, adapter_up_pair))


def adapter_backward_pass(
    gradient_value,
    input_rows,
    reduced_total,
    adapter_down_pair,
    adapter_up_pair,
    adapter_choice_index,
):
    reduced_gradient_sum = project_to_rank(
        adapter_scale
        * matrix_product_backward(gradient_value, adapter_up_pair)
        * adapter_choice_index
    )
    up_weight_gradient = adapter_scale * outer_product_sum(reduced_total, gradient_value)
    down_weight_gradient = outer_product_sum(input_rows, reduced_gradient_sum)
    return (
        down_weight_gradient,
        up_weight_gradient,
        matrix_product_backward(reduced_gradient_sum, adapter_down_pair),
    )


def attention_scores(query_rows, key_rows, allowed):
    scores = jnp.einsum(
        "qhd,khd->hqk", query_rows, key_rows, preferred_element_type=jnp.float32
    ) * HEAD_SIZE ** (-0.5)
    return jnp.where(allowed[None], scores, -jnp.inf)


def attention_forward(query_rows, key_rows, value_matrix_rows, allowed):
    scores = attention_scores(query_rows, key_rows, allowed)
    row_top = jnp.max(scores, axis=-1, keepdims=True)
    expanded = jnp.exp(scores - row_top)
    row_total = jnp.sum(expanded, axis=-1, keepdims=True)
    probs_low = project_to_rank(expanded / row_total)
    attention_result = jnp.einsum(
        "hqk,khd->qhd", probs_low, value_matrix_rows, preferred_element_type=jnp.float32
    )
    return (attention_result, row_top, row_total)


def attention_back(
    query_rows, key_rows, value_matrix_rows, allowed, row_top, row_total, grad_attended
):
    probs_full = jnp.exp(attention_scores(query_rows, key_rows, allowed) - row_top) / row_total
    grad_probs = jnp.einsum(
        "qhd,khd->hqk", grad_attended, value_matrix_rows, preferred_element_type=jnp.float32
    )
    row_delta = jnp.sum(probs_full * grad_probs, axis=-1, keepdims=True)
    grad_scores = project_to_rank(probs_full * (grad_probs - row_delta))
    grad_queries = HEAD_SIZE ** (-0.5) * jnp.einsum(
        "hqk,khd->qhd", grad_scores, key_rows, preferred_element_type=jnp.float32
    )
    grad_keys = HEAD_SIZE ** (-0.5) * jnp.einsum(
        "hqk,qhd->khd", grad_scores, query_rows, preferred_element_type=jnp.float32
    )
    grad_values = jnp.einsum(
        "hqk,qhd->khd",
        project_to_rank(probs_full),
        grad_attended,
        preferred_element_type=jnp.float32,
    )
    return (grad_queries, grad_keys, grad_values)


GROUP = 4
AXES = ("dp", "shard")


class Place:
    def __init__(self, dp, shard):
        self.line, self.shard = dp // 2, shard
        i, s = lax.axis_index("dp"), lax.axis_index("shard")
        self.z, self.y, self.x, self.c = i // 2, i % 2, s // 2, s % 2
        self.q = self.y * 2 + self.c
        self.spots = [
            (z, y, x, c)
            for z in range(self.line)
            for y in range(2)
            for x in range(shard // 2)
            for c in range(2)
        ]

    def number(self, z, y, x, c):
        return (z * 2 + y) * self.shard + x * 2 + c

    def move(self, value, target):
        pairs = []
        for spot in self.spots:
            to = target(*spot)
            if to is not None:
                pairs.append((self.number(*spot), self.number(*to)))
        return lax.ppermute(value, AXES, pairs)

    def by_y(self, value):
        return self.move(value, lambda z, y, x, c: (z, 1 - y, x, c))

    def by_x(self, value):
        return self.move(value, lambda z, y, x, c: (z, y, 1 - x, c))

    def by_c(self, value):
        return self.move(value, lambda z, y, x, c: (z, y, x, 1 - c))

    def step_z(self, value, step):
        return self.move(
            value, lambda z, y, x, c: (z + step, y, x, c) if 0 <= z + step < self.line else None
        )

    def ring_z(self, value, step):
        return self.move(value, lambda z, y, x, c: ((z + step) % self.line, y, x, c))

    def along_z(self, block):
        ups, downs = [block], [block]
        for _ in range(self.line - 1):
            ups.append(self.step_z(ups[-1], 1))
            downs.append(self.step_z(downs[-1], -1))
        return jnp.stack(
            [
                jnp.where(self.z >= k, ups[k], downs[self.line - k])
                for k in range(1, self.line)
            ]
        )

    def gather_group(self, rows):
        pair = jnp.concatenate([rows, self.by_y(rows)], axis=0)
        return jnp.concatenate([pair, self.by_c(pair)], axis=0)

    def sum_group(self, partial):
        rows = partial.shape[0] // GROUP
        partial = partial.reshape(GROUP, rows, -1)
        got = self.by_c(partial[2:].astype(jnp.bfloat16))
        pair = partial[:2] + got.astype(jnp.float32)
        got = self.by_y(pair[1].astype(jnp.bfloat16))
        return pair[0] + got.astype(jnp.float32)


def put(buffer, block, *where):
    block = block.reshape((1,) * len(where) + block.shape)
    return lax.dynamic_update_slice(
        buffer, block, tuple(where) + (0,) * (buffer.ndim - len(where))
    )


def gather_quarter(place, own, other):
    got = place.by_y(other)
    same = place.y == place.x
    carry, rest = jnp.where(same, own, got), jnp.where(same, got, own)
    lines = place.along_z(carry)
    mates = place.by_x(lines)
    full = jnp.zeros((place.line, 2) + own.shape, own.dtype)
    full = put(full, carry, place.z, place.x)
    full = put(full, rest, place.z, 1 - place.x)
    for k in range(1, place.line):
        plane = (place.z - k) % place.line
        full = put(full, lines[k - 1], plane, place.x)
        full = put(full, mates[k - 1], plane, 1 - place.x)
    return full.reshape((-1,) + own.shape[1:])


def gather_attention(place, blocks, y_first):
    s = place.x * 2 + place.c
    native = jnp.stack(blocks)
    carry = lax.dynamic_index_in_dim(native, s, 0, keepdims=False)
    lines = place.along_z(carry)
    if y_first:
        y_near, y_lines = place.by_y(carry), place.by_y(lines)
        x_lines, xy_near, xy_lines = place.by_x(lines), place.by_x(y_near), place.by_x(y_lines)
    else:
        x_lines = place.by_x(lines)
        x_near = lax.dynamic_index_in_dim(native, s ^ 2, 0, keepdims=False)
        y_near, y_lines = place.by_y(carry), place.by_y(lines)
        xy_near, xy_lines = place.by_y(x_near), place.by_y(x_lines)
    full = jnp.zeros((GROUP, place.line, 2) + carry.shape, carry.dtype)
    for t in range(GROUP):
        full = put(full, blocks[t], t, place.z, place.y)
    parts = (
        (lines, place.y, s, True),
        (y_near, 1 - place.y, s, False),
        (y_lines, 1 - place.y, s, True),
        (x_lines, place.y, s ^ 2, True),
        (xy_near, 1 - place.y, s ^ 2, False),
        (xy_lines, 1 - place.y, s ^ 2, True),
    )
    for value, y, which, many in parts:
        for held, weight in ((value, which), (place.by_c(value), which ^ 1)):
            if many:
                for k in range(1, place.line):
                    full = put(full, held[k - 1], weight, (place.z - k) % place.line, y)
            else:
                full = put(full, held, weight, place.z, y)
    return [full[t].reshape((-1,) + carry.shape[1:]) for t in range(GROUP)]


def hidden_columns(place, values, blocks, padded):
    each = FEEDFORWARD_UNITS // blocks
    own = each // GROUP

    def take(quarter):
        def cut(value):
            pieces = []
            for i in range(blocks):
                start = each * i + own * quarter
                piece = value[:, start : start + own]
                pieces.append(jnp.pad(piece, ((0, 0), (0, padded - own))))
            return pieces

        return lambda *given: jnp.concatenate([p for v in given for p in cut(v)], axis=1)

    branches = [take(k) for k in range(GROUP)]
    return lax.switch(place.q, branches, *values), lambda: lax.switch(
        place.q ^ 2, branches, *values
    )


def spread_columns(place, value, blocks, padded):
    each = FEEDFORWARD_UNITS // blocks
    own = each // GROUP

    def lay(quarter):
        def build(given):
            pieces = []
            for i in range(blocks):
                piece = given[:, padded * i : padded * i + own]
                pieces.append(
                    jnp.pad(piece, ((0, 0), (own * quarter, each - own * (quarter + 1))))
                )
            return jnp.concatenate(pieces, axis=1)

        return build

    return lax.switch(place.q, [lay(k) for k in range(GROUP)], value)


def hidden_rows(place, value, quarter, blocks, padded):
    own = value.shape[0] // (blocks * GROUP)
    split = value.reshape(blocks, GROUP, own, -1)
    got = lax.dynamic_index_in_dim(split, quarter, 1, keepdims=False)
    return jnp.pad(got, ((0, 0), (0, padded - own), (0, 0))).reshape(blocks * padded, -1)


def reduce_to_owner(place, flat):
    owners = place.line * 2 * place.shard
    share = flat.shape[0] // owners
    half = -(-share // 8) * 8
    start = 2 * share - half
    pairs = flat.reshape(place.line, 2, place.shard // 2, 2 * share, ADAPTER_COLUMNS)
    keep = lax.dynamic_slice_in_dim(pairs, place.c * start, half, 3)
    send = lax.dynamic_slice_in_dim(pairs, (1 - place.c) * start, half, 3)
    total = keep + place.by_c(send.astype(jnp.bfloat16)).astype(jnp.float32)
    for axis, mine, move in ((1, place.y, place.by_y), (1, place.x, place.by_x)):
        keep = lax.dynamic_index_in_dim(total, mine, axis, keepdims=False)
        send = lax.dynamic_index_in_dim(total, 1 - mine, axis, keepdims=False)
        total = keep + move(send.astype(jnp.bfloat16)).astype(jnp.float32)
    low = total.astype(jnp.bfloat16)
    result = lax.dynamic_index_in_dim(total, place.z, 0, keepdims=False)
    for k in range(1, place.line):
        send = lax.dynamic_index_in_dim(low, (place.z + k) % place.line, 0, keepdims=False)
        result = result + place.ring_z(send, k).astype(jnp.float32)
    return lax.dynamic_slice_in_dim(result, place.c * (half - share), share, 0)


def gather_owners(place, own):
    share = own.shape[0]
    half = -(-share // 8) * 8
    start = 2 * share - half
    mate = place.by_c(own)
    first, second = jnp.where(place.c == 0, own, mate), jnp.where(place.c == 0, mate, own)
    pair = jnp.concatenate([first, second], axis=0)
    carry = lax.dynamic_slice_in_dim(pair, place.c * start, half, 0)
    lines = jnp.stack([carry] + [place.ring_z(carry, k) for k in range(1, place.line)])
    mates = place.by_x(lines)
    y_lines, y_mates = place.by_y(lines), place.by_y(mates)
    full = jnp.zeros(
        (place.line, 2, place.shard // 2, 2 * share, ADAPTER_COLUMNS), own.dtype
    )
    for value, y, x in (
        (lines, place.y, place.x),
        (mates, place.y, 1 - place.x),
        (y_lines, 1 - place.y, place.x),
        (y_mates, 1 - place.y, 1 - place.x),
    ):
        for held, c in ((value, place.c), (place.by_c(value), 1 - place.c)):
            for k in range(place.line):
                block = held[k].reshape(1, 1, 1, half, ADAPTER_COLUMNS)
                where = ((place.z - k) % place.line, y, x, c * start, 0)
                full = lax.dynamic_update_slice(full, block, where)
    return full.reshape(-1)


def low(values):
    return values.astype(jnp.bfloat16)


def shards(
    dp,
    shard,
    tokens,
    cotangent,
    arrival,
    lengths,
    adapter_set,
    gain_one,
    gain_two,
    w_query,
    w_key,
    w_value,
    w_out,
    w_gate,
    w_up,
    w_down,
    adapters,
    first_moment_running,
    second_moment_running,
):
    place = Place(dp, shard)
    token_order = arrival[0]
    count = token_order.shape[0]
    padded = -(-(FEEDFORWARD_UNITS // (dp * GROUP)) // 8) * 8
    arrived_x = lax.all_to_all(tokens, "dp", split_axis=0, concat_axis=0, tiled=True)
    arrived_cot = lax.all_to_all(cotangent, "dp", split_axis=0, concat_axis=0, tiled=True)

    half = MODEL_WIDTH // 2
    attention_weights = (w_query, w_key, w_value, w_out)
    left = gather_attention(place, [w[:, :half] for w in attention_weights], True)
    right = gather_attention(place, [w[:, half:] for w in attention_weights], False)
    own, other = hidden_columns(place, (w_gate, w_up), dp, padded)
    gate_up = gather_quarter(place, own, other())
    down = gather_quarter(
        place,
        hidden_rows(place, w_down, place.q, 1, padded),
        hidden_rows(place, w_down, place.q ^ 2, 1, padded),
    )
    hidden = dp * padded

    A_model, A_hidden, B_model, B_hidden = restore_structure(adapters)
    table = jnp.concatenate([lengths, adapter_set], axis=1)
    tables = place.gather_group(table)
    choice, allowed, cosine_table, sine_table = block_tables(lengths[0], adapter_set[0])
    choices = jnp.concatenate(
        [block_tables(tables[k, :SEQ_DEV], tables[k, SEQ_DEV:])[0] for k in range(GROUP)], axis=0
    )
    gain_first = gain_one.astype(jnp.float32)
    gain_second = gain_two.astype(jnp.float32)

    x = arrived_x[token_order].astype(jnp.float32)
    g = arrived_cot[token_order].astype(jnp.float32)
    scale_one = rms_scale(x)
    n1 = low(x * scale_one * gain_first)

    def project(values, which):
        return jnp.concatenate(
            [matrix_product(values, left[which]), matrix_product(values, right[which])], axis=1
        )

    def project_back(values, which):
        return matrix_product_backward(values[:, :half], left[which]) + matrix_product_backward(
            values[:, half:], right[which]
        )

    z_query, delta_query = apply_adapter_delta(n1, A_model[0], B_model[0], choice)
    z_key, delta_key = apply_adapter_delta(n1, A_model[1], B_model[1], choice)
    z_value, delta_value = apply_adapter_delta(n1, A_model[2], B_model[2], choice)
    heads = (count, ATTENTION_HEADS, HEAD_SIZE)
    queries = low(
        rotary_embedding(project(n1, 0) + delta_query, cosine_table, sine_table)
    ).reshape(heads)
    keys = low(rotary_embedding(project(n1, 1) + delta_key, cosine_table, sine_table)).reshape(
        heads
    )
    values = low(project(n1, 2) + delta_value).reshape(heads)
    o, row_top, row_total = attention_forward(queries, keys, values, allowed)
    o = low(o.reshape(count, MODEL_WIDTH))
    z_out, delta_out = apply_adapter_delta(o, A_model[3], B_model[3], choice)
    m = x + residual_branch_scale * (project(o, 3) + delta_out)
    scale_two = rms_scale(m)
    n2 = low(m * scale_two * gain_second)

    n2_all = place.gather_group(n2)
    e_down = low(residual_branch_scale * g)
    dz_down = low(adapter_scale * matrix_product_backward(e_down, B_model[4]) * choice)
    sent = place.gather_group(jnp.concatenate([e_down, dz_down], axis=1))
    e_down_all, dz_down_all = sent[:, :MODEL_WIDTH], sent[:, MODEL_WIDTH:]
    B_gate_up, _ = hidden_columns(place, (B_hidden[0], B_hidden[1]), dp, padded)
    A_down = hidden_rows(place, A_hidden, place.q, dp, padded)
    z_gate = low(matrix_product(n2_all, A_model[4]) * choices)
    z_up = low(matrix_product(n2_all, A_model[5]) * choices)
    both = matrix_product(n2_all, gate_up)
    gt = both[:, :hidden] + adapter_scale * matrix_product(z_gate, B_gate_up[:, :hidden])
    up = both[:, hidden:] + adapter_scale * matrix_product(z_up, B_gate_up[:, hidden:])
    sg = jax.nn.sigmoid(gt)
    act = gt * sg
    h = low(act * up)
    y_sum = place.sum_group(
        jnp.concatenate([matrix_product(h, down), matrix_product(h, A_down)], axis=1)
    )
    z_down = low(y_sum[:, MODEL_WIDTH:] * choice)
    y = m + residual_branch_scale * (
        y_sum[:, :MODEL_WIDTH] + adapter_scale * matrix_product(z_down, B_model[4])
    )
    dh = matrix_product_backward(e_down_all, down) + matrix_product_backward(dz_down_all, A_down)
    e_gate = low(dh * up * (sg + gt * sg * (1.0 - sg)))
    e_up = low(dh * act)
    e_both = jnp.concatenate([e_gate, e_up], axis=1)
    back_sum = place.sum_group(
        jnp.concatenate(
            [
                matrix_product_backward(e_both, gate_up),
                matrix_product_backward(e_gate, B_gate_up[:, :hidden]),
                matrix_product_backward(e_up, B_gate_up[:, hidden:]),
            ],
            axis=1,
        )
    )
    split = MODEL_WIDTH + ADAPTER_COLUMNS
    dz_gate = low(adapter_scale * back_sum[:, MODEL_WIDTH:split] * choice)
    dz_up = low(adapter_scale * back_sum[:, split:] * choice)
    dn2 = (
        back_sum[:, :MODEL_WIDTH]
        + matrix_product_backward(dz_gate, A_model[4])
        + matrix_product_backward(dz_up, A_model[5])
    )
    dA_gate, dA_up = outer_product_sum(n2, dz_gate), outer_product_sum(n2, dz_up)
    dB_gate = adapter_scale * outer_product_sum(z_gate, e_gate)
    dB_up = adapter_scale * outer_product_sum(z_up, e_up)
    dA_down = outer_product_sum(h, dz_down_all)
    dB_down = adapter_scale * outer_product_sum(z_down, e_down)

    dm = g + norm_back(m, scale_two, gain_second, dn2)
    e_out = low(residual_branch_scale * dm)
    dA_out, dB_out, through_out = adapter_backward_pass(
        e_out, o, z_out, A_model[3], B_model[3], choice
    )
    e_o = low(project_back(e_out, 3) + through_out).reshape(heads)
    dq, dk, dv = attention_back(queries, keys, values, allowed, row_top, row_total, e_o)
    e_query = low(rotary_back(dq, cosine_table, sine_table))
    e_key = low(rotary_back(dk, cosine_table, sine_table))
    e_value = low(dv.reshape(count, MODEL_WIDTH))
    dA_query, dB_query, through_query = adapter_backward_pass(
        e_query, n1, z_query, A_model[0], B_model[0], choice
    )
    dA_key, dB_key, through_key = adapter_backward_pass(
        e_key, n1, z_key, A_model[1], B_model[1], choice
    )
    dA_value, dB_value, through_value = adapter_backward_pass(
        e_value, n1, z_value, A_model[2], B_model[2], choice
    )
    dn1 = (
        project_back(e_query, 0)
        + project_back(e_key, 1)
        + project_back(e_value, 2)
        + through_query
        + through_key
        + through_value
    )
    dx = dm + norm_back(x, scale_one, gain_first, dn1)

    own_hidden = FEEDFORWARD_UNITS // (dp * GROUP)
    dA_hidden = lax.dynamic_update_slice(
        jnp.zeros((dp, GROUP, own_hidden, ADAPTER_COLUMNS), jnp.float32),
        dA_down.reshape(dp, 1, padded, ADAPTER_COLUMNS)[:, :, :own_hidden],
        (0, place.q, 0, 0),
    )
    flat = jnp.concatenate(
        [
            piece.reshape(-1, ADAPTER_COLUMNS)
            for piece in (
                dA_query,
                dA_key,
                dA_value,
                dA_out,
                dA_gate,
                dA_up,
                dA_hidden,
                dB_query,
                dB_key,
                dB_value,
                dB_out,
                dB_down,
                spread_columns(place, dB_gate, dp, padded),
                spread_columns(place, dB_up, dp, padded),
            )
        ]
    )
    gradient = reduce_to_owner(place, flat)
    share = gradient.shape[0]
    offset = lax.axis_index(AXES) * share
    own_params = lax.dynamic_slice_in_dim(
        adapters.reshape(-1, ADAPTER_COLUMNS), offset, share
    ).astype(jnp.float32)
    first = first_moment_running.reshape(share, ADAPTER_COLUMNS)
    second = second_moment_running.reshape(share, ADAPTER_COLUMNS)
    fresh_first = first_decay_rate * first + (1.0 - first_decay_rate) * gradient
    fresh_second = second_decay_rate * second + (1.0 - second_decay_rate) * gradient * gradient
    unbiased_first = fresh_first / (1.0 - first_decay_rate**OPT_STEP)
    unbiased_second = fresh_second / (1.0 - second_decay_rate**OPT_STEP)
    update = (
        unbiased_first / (jnp.sqrt(unbiased_second) + adaptive_epsilon)
        + weight_shrink_rate * own_params
    )
    updated = gather_owners(place, low(own_params - learning_rate * update))

    inverse = (
        jnp.zeros_like(token_order).at[token_order].set(jnp.arange(count, dtype=jnp.int32))
    )
    back_out = lax.all_to_all(low(y)[inverse], "dp", split_axis=0, concat_axis=0, tiled=True)
    back_grad = lax.all_to_all(low(dx)[inverse], "dp", split_axis=0, concat_axis=0, tiled=True)
    return (
        back_out,
        back_grad,
        gradient.reshape(-1),
        fresh_first.reshape(-1),
        fresh_second.reshape(-1),
        updated,
    )


def solution(mesh):
    rows = P(AXES, None)
    weight = P("dp", None)
    return jax.shard_map(
        functools.partial(shards, mesh.shape["dp"], mesh.shape["shard"]),
        mesh=mesh,
        in_specs=(rows,) * 5 + (P(), P()) + (weight,) * 7 + (P(), P(AXES), P(AXES)),
        out_specs=(rows, rows, P(AXES), P(AXES), P(AXES), P()),
        check_vma=False,
    )
```

time: 3130 us -> 1500 us (0.48)
  waiting for transfers between devices: 2500 us -> 591 us
  local copies, waits for them, and re-layouts: 91 us -> 341 us
  starting transfers between devices: 23 us -> 166 us
  other arithmetic: 246 us -> 145 us
    all_gather x8 -> x0, waiting for transfers between devices: 1990 us -> none  [the longest x1 493 us: shards(): lax.all_gather(w_up, 'dp', axis=0, tiled=True)]
    ppermute x0 -> x77, waiting for transfers between devices: none -> 578 us  [move(): return lax.ppermute(value, AXES, pairs)]
    unnamed x10 -> x0, waiting for transfers between devices: 356 us -> none
    all_gather x1 -> x0, other arithmetic: 193 us -> none  [shards(): lax.all_gather(fresh_params, ('dp', 'shard'), axis=0, tiled=True)]
    ppermute x0 -> x77, starting transfers between devices: none -> 143 us  [move(): return lax.ppermute(value, AXES, pairs)]
    all_to_all x2, waiting for transfers between devices: 98.2 us -> 0.01 us  [the longest x1 0.01 us: shards(): lax.all_to_all(low(y)[inverse], 'dp', split_axis=0, concat_axis=0, tiled=...]
    dynamic_update_slice x0 -> x93, local copies, waits for them, and re-layouts: none -> 76.8 us  [the longest x61 75.1 us: put(): lax.dynamic_update_slice(buffer, block, tuple(where) + (0,) * (buffer.ndi...]
    all_to_all x1, waiting for transfers between devices: 51.3 us -> 0.01 us  [shards(): lax.all_to_all(tokens, 'dp', split_axis=0, concat_axis=0, tiled=True)]
  transfers between devices with their start and end apart: 13 -> 81, of which waited for: 13 -> 41; matrix products, arithmetic and copies ran while one was open for 6% -> 30% of each run, Pallas kernels for 0% -> 0%
where the time goes in v1:
time: 1500 us; the launch traced here: 1480 us
  waiting for transfers between devices  591 us (39%)
  local copies, waits for them, and re-layouts  341 us (23%)
  matrix products  233 us (16%)
  starting transfers between devices  166 us (11%)
  other arithmetic  145 us (10%)
    ppermute x77, waiting for transfers between devices, move(): return lax.ppermute(value, AXES, pairs)  578 us
    ppermute x77, starting transfers between devices, move(): return lax.ppermute(value, AXES, pairs)  143 us
    dot_general x24, matrix products, matrix_product_backward(): lax.dot_general(left_side, right_side, (((1,), (1,)), ((), ())), preferre...  90.7 us
    dot_general x24, matrix products, matrix_product(): return jnp.dot(left_side, right_side, preferred_element_type=jnp.float32)  80.7 us
    dynamic_update_slice x61, local copies, waits for them, and re-layouts, put(): lax.dynamic_update_slice(buffer, block, tuple(where) + (0,) * (buffer.ndi...  75.1 us
    unnamed x389, local copies, waits for them, and re-layouts  39.7 us
  transfers between devices with their start and end apart: 81, of which 41 were waited for; matrix products, arithmetic and copies ran while one was open for 30% of the time, Pallas kernels for 0%

profile of v1, /device:TPU:0, one launch (start us, length us, event | category | flops | bytes accessed | tf_op | source)
XLA Modules:
  0.0 1481.5 jit_solution(2943896636624573597)
XLA Ops:
  41.3 7.4 broadcast.842.clone.1
  49.6 7.7 broadcast.842.clone
  68.6 15.2 %conditional.6 = (bf16[288,2944]{1,0:T(8,128)(2,1)S(1)}) conditional(s32[]{:T(128)} %clamp.10, (bf16[288,5760]{1,0:T(8,128)(2,1)}, bf16[288,5760]{1,0:T(8,128)(2,1)}) %tuple.92, (bf16[288,5760]{1,0:T(8,128)(2,1)}, bf16[288,5760]{1,0:T(8,128)(2,1)}) %tuple.92, (bf16[288,5760]{1,0:T(8,128)(2,1)}, ...), branch_computations={%region_12.13_spmd, %region_13.14_spmd, %region_14.15_spmd, %regio... | conditional | flops 105984 | bytes 10063912 | solution.py:340
  85.0 14.7 conditional.5
  107.8 17.6 %conditional.7 = (bf16[128,1472]{1,0:T(8,128)(2,1)}, bf16[128,1472]{1,0:T(8,128)(2,1)S(1)}) conditional(s32[]{:T(128)} %clamp.4, (bf16[128,5760]{1,0:T(8,128)(2,1)}, bf16[128,5760]{1,0:T(8,128)(2,1)}) %tuple.93, (bf16[128,5760]{1,0:T(8,128)(2,1)}, bf16[128,5760]{1,0:T(8,128)(2,1)}) %tuple.93, ...), branch_computations={%region_25.26_spmd, %region_26.27_spmd, %region_27.28_spmd, %regio... | conditional | flops 47104 | bytes 4472880 | solution.py:340
  152.7 11.3 collective-permute-start.36
  188.9 8.0 collective-permute-done.19
  214.6 20.6 %collective-permute-done.3 = bf16[288,1152]{1,0:T(8,128)(2,1)} collective-permute-done((bf16[288,1152]{1,0:T(8,128)(2,1)}, bf16[288,1152]{1,0:T(8,128)(2,1)}, u32[]{:S(2)}, u32[]{:S(2)}) %collective-permute-start.3) | collective-permute-done | bytes 663584 | tf_op jit(solution)/shard_map/ppermute | solution.py:223
  259.1 12.8 collective-permute-done.5
  306.3 13.2 all-to-all-done.2
  333.7 20.2 %collective-permute-done.56 = bf16[256,2432]{1,0:T(8,128)(2,1)S(1)} collective-permute-done((bf16[256,2432]{1,0:T(8,128)(2,1)S(1)}, bf16[256,2432]{1,0:T(8,128)(2,1)S(1)}, u32[]{:S(2)}, u32[]{:S(2)}) %collective-permute-start.56) | collective-permute-done | bytes 1245216 | tf_op jit(solution)/shard_map/ppermute | solution.py:223
  353.9 9.2 collective-permute-start.52
  363.5 10.0 collective-permute-done.52
  384.2 29.4 %collective-permute-done.9 = bf16[3,288,1152]{2,1,0:T(8,128)(2,1)} collective-permute-done((bf16[3,288,1152]{2,1,0:T(8,128)(2,1)}, bf16[3,288,1152]{2,1,0:T(8,128)(2,1)}, u32[]{:S(2)}, u32[]{:S(2)}) %collective-permute-start.9) | collective-permute-done | bytes 1990688 | tf_op jit(solution)/shard_map/ppermute | solution.py:223
  432.2 16.5 %collective-permute-done.37 = bf16[288,2944]{1,0:T(8,128)(2,1)S(1)} collective-permute-done((bf16[288,2944]{1,0:T(8,128)(2,1)S(1)}, bf16[288,2944]{1,0:T(8,128)(2,1)S(1)}, u32[]{:S(2)}, u32[]{:S(2)}) %collective-permute-start.37) | collective-permute-done | bytes 1695776 | tf_op jit(solution)/shard_map/ppermute | solution.py:223
  448.7 8.4 collective-permute-start.41
  463.9 9.7 collective-permute-done.39
  482.4 49.1 %collective-permute-done.13 = bf16[288,1152]{1,0:T(8,128)(2,1)} collective-permute-done((bf16[288,1152]{1,0:T(8,128)(2,1)}, bf16[288,1152]{1,0:T(8,128)(2,1)}, u32[]{:S(2)}, u32[]{:S(2)}) %collective-permute-start.13) | collective-permute-done | bytes 663584 | tf_op jit(solution)/shard_map/ppermute | solution.py:223
  535.7 8.7 pad_maximum_fusion.3
  548.2 26.0 %collective-permute-done.11 = bf16[3,288,1152]{2,1,0:T(8,128)(2,1)} collective-permute-done((bf16[3,288,1152]{2,1,0:T(8,128)(2,1)}, bf16[3,288,1152]{2,1,0:T(8,128)(2,1)}, u32[]{:S(2)}, u32[]{:S(2)}) %collective-permute-start.11) | collective-permute-done | bytes 1990688 | tf_op jit(solution)/shard_map/ppermute | solution.py:223
  587.8 28.9 %collective-permute-done.28 = bf16[3,288,1152]{2,1,0:T(8,128)(2,1)S(1)} collective-permute-done((bf16[3,288,1152]{2,1,0:T(8,128)(2,1)S(1)}, bf16[3,288,1152]{2,1,0:T(8,128)(2,1)S(1)}, u32[]{:S(2)}, u32[]{:S(2)}) %collective-permute-start.28) | collective-permute-done | bytes 1990688 | tf_op jit(solution)/shard_map/ppermute | solution.py:223
  624.9 21.1 %collective-permute-done.15 = bf16[3,288,1152]{2,1,0:T(8,128)(2,1)S(1)} collective-permute-done((bf16[3,288,1152]{2,1,0:T(8,128)(2,1)}, bf16[3,288,1152]{2,1,0:T(8,128)(2,1)S(1)}, u32[]{:S(2)}, u32[]{:S(2)}) %collective-permute-start.15) | collective-permute-done | bytes 1990688 | tf_op jit(solution)/shard_map/ppermute | solution.py:223
  650.1 8.5 collective-permute-start.42
  687.0 14.2 fusion.295
  706.2 14.2 fusion.296
  751.6 9.1 fusion.299
  780.9 13.7 collective-permute-done.34
  808.2 73.0 %collective-permute-done.43 = bf16[3,288,2944]{2,1,0:T(8,128)(2,1)S(1)} collective-permute-done((bf16[3,288,2944]{2,1,0:T(8,128)(2,1)S(1)}, bf16[3,288,2944]{2,1,0:T(8,128)(2,1)S(1)}, u32[]{:S(2)}, u32[]{:S(2)}) %collective-permute-start.43) | collective-permute-done | bytes 5087264 | tf_op jit(solution)/shard_map/ppermute | solution.py:223
  886.7 19.5 %fusion.241 = f32[1024,2944]{1,0:T(8,128)} fusion(bf16[2304,2944]{1,0:T(8,128)(2,1)S(1)} %bitcast.727, bf16[512,2304]{1,0:T(8,128)(2,1)S(1)} %copy-done.169, bf16[256,2304]{1,0:T(8,128)(2,1)S(1)} %copy-done.112, bf16[256,2304]{1,0:T(8,128)(2,1)S(1)} %multiply_convert_fusion.5), kind=kOutput, calls=%fused_computation.567 | convolution fusion | flops 13905690624 | bytes 30343168 | tf_op jit(solution)/shard_map/dot_general | solution.py:32
  906.2 7.1 slice_add_fusion.1
  919.1 19.1 %multiply_convert_fusion.2 = (bf16[1024,1472]{1,0:T(8,128)(2,1)}, bf16[1024,1472]{1,0:T(8,128)(2,1)S(1)}, bf16[1024,1472]{1,0:T(8,128)(2,1)}) fusion(f32[1024,1472]{1,0:T(8,128)} %slice_add_fusion, f32[1024,1472]{1,0:T(8,128)} %slice_add_fusion.1, f32[1024,1472]{1,0:T(8,128)} %fusion.304, bf16[1472,2304]{1,0:T(8,128)(2,1)} %bitcast.737, ...), kind=kOutput, calls=%fused_computation.35 | convolution fusion | flops 6968377344 | bytes 39419904 | tf_op jit(solution)/shard_map/dot_general | solution.py:36
  938.3 9.5 fusion.302
  955.0 19.7 %fusion.2 = f32[1024,2304]{1,0:T(8,128)} fusion(bf16[2304,2944]{1,0:T(8,128)(2,1)} %bitcast.728, bf16[1024,1472]{1,0:T(8,128)(2,1)S(1)} %copy-done.24, bf16[1024,1472]{1,0:T(8,128)(2,1)S(1)} %copy-done.23), kind=kOutput, calls=%fused_computation.38 | convolution fusion | flops 13903593472 | bytes 29032448 | tf_op jit(solution)/shard_map/dot_general | solution.py:36
  990.4 18.1 %conditional.9 = (f32[5760,128]{1,0:T(8,128)}) conditional(s32[]{:T(128)} %clamp.4, f32[128,1472]{0,1:T(8,128)} %fusion.309, f32[128,1472]{0,1:T(8,128)} %fusion.309, f32[128,1472]{0,1:T(8,128)} %fusion.309, f32[128,1472]{0,1:T(8,128)} %fusion.309), branch_computations={%region_37.38_spmd, %region_38.39_spmd, %region_39.40_spmd, %regio... | conditional | flops 280576 | bytes 20067920 | solution.py:361
  1012.7 19.1 %conditional.8 = (f32[5760,128]{1,0:T(8,128)}) conditional(s32[]{:T(128)} %clamp.4, f32[128,1472]{0,1:T(8,128)} %fusion.308, f32[128,1472]{0,1:T(8,128)} %fusion.308, f32[128,1472]{0,1:T(8,128)} %fusion.308, f32[128,1472]{0,1:T(8,128)} %fusion.308), branch_computations={%region_33.34_spmd, %region_34.35_spmd, %region_35.36_spmd, %regio... | conditional | flops 280576 | bytes 20067920 | solution.py:361
  1047.7 23.0 %collective-permute-done.55 = bf16[256,2432]{1,0:T(8,128)(2,1)} collective-permute-done((bf16[256,2432]{1,0:T(8,128)(2,1)}, bf16[256,2432]{1,0:T(8,128)(2,1)}, u32[]{:S(2)}, u32[]{:S(2)}) %collective-permute-start.55) | collective-permute-done | bytes 1245216 | tf_op jit(solution)/shard_map/ppermute | solution.py:223
  1076.0 22.5 %collective-permute-done.59 = bf16[256,2560]{1,0:T(8,128)(2,1)} collective-permute-done((bf16[256,2560]{1,0:T(8,128)(2,1)}, bf16[256,2560]{1,0:T(8,128)(2,1)}, u32[]{:S(2)}, u32[]{:S(2)}) %collective-permute-start.59) | collective-permute-done | bytes 1310752 | tf_op jit(solution)/shard_map/ppermute | solution.py:223
  1116.6 10.2 multiply_reduce_fusion
  1126.8 10.4 multiply_convert_fusion
  1192.8 7.2 dynamic-slice_convert_fusion
  1206.6 7.6 all-to-all-start.1
  1225.7 10.7 convert_add_fusion
  1258.2 42.8 %collective-permute-done.61 = bf16[4,2,1336,128]{3,2,1,0:T(8,128)(2,1)S(1)} collective-permute-done((bf16[4,2,1336,128]{3,2,1,0:T(8,128)(2,1)S(1)}, bf16[4,2,1336,128]{3,2,1,0:T(8,128)(2,1)S(1)}, u32[]{:S(2)}, u32[]{:S(2)}) %collective-permute-start.61) | collective-permute-done | bytes 2736160 | tf_op jit(solution)/shard_map/ppermute | solution.py:223
  1316.1 18.6 %collective-permute-done.62 = bf16[4,1336,128]{2,1,0:T(8,128)(2,1)} collective-permute-done((bf16[4,1336,128]{2,1,0:T(8,128)(2,1)}, bf16[4,1336,128]{2,1,0:T(8,128)(2,1)}, u32[]{:S(2)}, u32[]{:S(2)}) %collective-permute-start.62) | collective-permute-done | bytes 1368096 | tf_op jit(solution)/shard_map/ppermute | solution.py:223
  1352.9 14.6 collective-permute-done.64
  1393.8 14.1 collective-permute-done.68
  1411.6 29.0 %collective-permute-done.71 = bf16[4,1336,128]{2,1,0:T(8,128)(2,1)S(1)} collective-permute-done((bf16[4,1336,128]{2,1,0:T(8,128)(2,1)S(1)}, bf16[4,1336,128]{2,1,0:T(8,128)(2,1)S(1)}, u32[]{:S(2)}, u32[]{:S(2)}) %collective-permute-start.71) | collective-permute-done | bytes 1368096 | tf_op jit(solution)/shard_map/ppermute | solution.py:223
  1446.1 26.9 %collective-permute-done.75 = bf16[4,1336,128]{2,1,0:T(8,128)(2,1)S(1)} collective-permute-done((bf16[4,1336,128]{2,1,0:T(8,128)(2,1)S(1)}, bf16[4,1336,128]{2,1,0:T(8,128)(2,1)S(1)}, u32[]{:S(2)}, u32[]{:S(2)}) %collective-permute-start.75) | collective-permute-done | bytes 1368096 | tf_op jit(solution)/shard_map/ppermute | solution.py:223
  (915 shorter events, 712.1 us)
Async XLA Ops:
  6.2 146.5 %collective-permute-start.1 = (bf16[288,1152]{1,0:T(8,128)(2,1)}, bf16[288,1152]{1,0:T(8,128)(2,1)}, u32[]{:S(2)}, u32[]{:S(2)}) collective-permute-start(bf16[288,1152]{1,0:T(8,128)(2,1)} %fusion.90), channel_id=1, source_target_pairs={{8,0},{9,1},{10,2},{11,3},{12,4},{13,5},{14,6},{15,7},{16,8},{17,9... | collective-permute-start | bytes 1990664 | tf_op jit(solution)/shard_map/ppermute | solution.py:223
  7.5 156.5 %collective-permute-start = (bf16[288,1152]{1,0:T(8,128)(2,1)}, bf16[288,1152]{1,0:T(8,128)(2,1)}, u32[]{:S(2)}, u32[]{:S(2)}) collective-permute-start(bf16[288,1152]{1,0:T(8,128)(2,1)} %fusion.90), channel_id=1, source_target_pairs={{0,8},{1,9},{2,10},{3,11},{4,12},{5,13},{6,14},{7,15},{8,16},{9,17... | collective-permute-start | bytes 1990664 | tf_op jit(solution)/shard_map/ppermute | solution.py:223
  13.9 276.6 %all-to-all-start = ((bf16[8,32,2304]{2,1,0:T(8,128)(2,1)}), bf16[8,32,2304]{2,1,0:T(8,128)(2,1)S(1)}, u32[]{:S(2)}, u32[]{:S(2)}) async-start(bf16[8,32,2304]{2,1,0:T(8,128)(2,1)} %bitcast.756), calls=%async_computation | async-start | bytes 2359296 | tf_op jit(solution)/shard_map/all_to_all | solution.py:449
  22.3 143.1 %collective-permute-start.18 = (bf16[288,1152]{1,0:T(8,128)(2,1)}, bf16[288,1152]{1,0:T(8,128)(2,1)}, u32[]{:S(2)}, u32[]{:S(2)}) collective-permute-start(bf16[288,1152]{1,0:T(8,128)(2,1)} %get-tuple-element.538), channel_id=1, source_target_pairs={{8,0},{9,1},{10,2},{11,3},{12,4},{13,5},{14,6},{15,7},{16,8},{17,9... | collective-permute-start | bytes 1990664 | tf_op jit(solution)/shard_map/ppermute | solution.py:223
  24.2 115.7 %collective-permute-start.44 = (s32[1,8]{1,0:T(1,128)}, s32[1,8]{1,0:T(1,128)S(1)}, u32[]{:S(2)}, u32[]{:S(2)}) collective-permute-start(s32[1,8]{1,0:T(1,128)} %pad_add_fusion.2), channel_id=1, source_target_pairs={{0,4},{1,5},{2,6},{3,7},{4,0},{5,1},{6,2},{7,3},{8,12},{9,13},{10,... | collective-permute-start | bytes 104 | tf_op jit(solution)/shard_map/ppermute | solution.py:223
  33.1 138.1 %collective-permute-start.46 = (bf16[184,2304]{1,0:T(8,128)(2,1)}, bf16[184,2304]{1,0:T(8,128)(2,1)}, u32[]{:S(2)}, u32[]{:S(2)}) collective-permute-start(bf16[184,2304]{1,0:T(8,128)(2,1)} %pad_bitcast_fusion), channel_id=1, source_target_pairs={{0,4},{1,5},{2,6},{3,7},{4,0},{5,1},{6,2},{7,3},{8,12},{9,13},{10,... | collective-permute-start | bytes 2543624 | tf_op jit(solution)/shard_map/ppermute | solution.py:223
  152.7 49.5 %collective-permute-start.36 = (bf16[288,2944]{1,0:T(8,128)(2,1)}, bf16[288,2944]{1,0:T(8,128)(2,1)}, u32[]{:S(2)}, u32[]{:S(2)}) collective-permute-start(bf16[288,2944]{1,0:T(8,128)(2,1)} %copy-done.108), channel_id=1, source_target_pairs={{0,4},{1,5},{2,6},{3,7},{4,0},{5,1},{6,2},{7,3},{8,12},{9,13},{10,... | collective-permute-start | bytes 5087240 | tf_op jit(solution)/shard_map/ppermute | solution.py:223
  184.1 145.4 %collective-permute-start.7 = (bf16[288,1152]{1,0:T(8,128)(2,1)}, bf16[288,1152]{1,0:T(8,128)(2,1)}, u32[]{:S(2)}, u32[]{:S(2)}) collective-permute-start(bf16[288,1152]{1,0:T(8,128)(2,1)} %fusion.90), channel_id=1, source_target_pairs={{0,4},{1,5},{2,6},{3,7},{4,0},{5,1},{6,2},{7,3},{8,12},{9,13},{10,... | collective-permute-start | bytes 1990664 | tf_op jit(solution)/shard_map/ppermute | solution.py:223
  185.6 145.1 %collective-permute-start.24 = (bf16[288,1152]{1,0:T(8,128)(2,1)}, bf16[288,1152]{1,0:T(8,128)(2,1)}, u32[]{:S(2)}, u32[]{:S(2)}) collective-permute-start(bf16[288,1152]{1,0:T(8,128)(2,1)} %get-tuple-element.538), channel_id=1, source_target_pairs={{0,4},{1,5},{2,6},{3,7},{4,0},{5,1},{6,2},{7,3},{8,12},{9,13},{10,... | collective-permute-start | bytes 1990664 | tf_op jit(solution)/shard_map/ppermute | solution.py:223
  196.9 58.6 %collective-permute-start.48 = (bf16[184,2304]{1,0:T(8,128)(2,1)}, bf16[184,2304]{1,0:T(8,128)(2,1)}, u32[]{:S(2)}, u32[]{:S(2)}) collective-permute-start(bf16[184,2304]{1,0:T(8,128)(2,1)} %get-tuple-element.166), channel_id=1, source_target_pairs={{8,0},{9,1},{10,2},{11,3},{12,4},{13,5},{14,6},{15,7},{16,8},{17,9... | collective-permute-start | bytes 2543624 | tf_op jit(solution)/shard_map/ppermute | solution.py:223
  198.2 36.9 %collective-permute-start.3 = (bf16[288,1152]{1,0:T(8,128)(2,1)}, bf16[288,1152]{1,0:T(8,128)(2,1)}, u32[]{:S(2)}, u32[]{:S(2)}) collective-permute-start(bf16[288,1152]{1,0:T(8,128)(2,1)} %collective-permute-done.2), channel_id=1, source_target_pairs={{8,0},{9,1},{10,2},{11,3},{12,4},{13,5},{14,6},{15,7},{16,8},{17,9... | collective-permute-start | bytes 1990664 | tf_op jit(solution)/shard_map/ppermute | solution.py:223
  202.2 45.4 %collective-permute-start.20 = (bf16[288,1152]{1,0:T(8,128)(2,1)}, bf16[288,1152]{1,0:T(8,128)(2,1)}, u32[]{:S(2)}, u32[]{:S(2)}) collective-permute-start(bf16[288,1152]{1,0:T(8,128)(2,1)} %collective-permute-done.19), channel_id=1, source_target_pairs={{8,0},{9,1},{10,2},{11,3},{12,4},{13,5},{14,6},{15,7},{16,8},{17,9... | collective-permute-start | bytes 1990664 | tf_op jit(solution)/shard_map/ppermute | solution.py:223
  257.9 72.8 %collective-permute-start.49 = (bf16[184,2304]{1,0:T(8,128)(2,1)}, bf16[184,2304]{1,0:T(8,128)(2,1)}, u32[]{:S(2)}, u32[]{:S(2)}) collective-permute-start(bf16[184,2304]{1,0:T(8,128)(2,1)} %collective-permute-done.48), channel_id=1, source_target_pairs={{8,0},{9,1},{10,2},{11,3},{12,4},{13,5},{14,6},{15,7},{16,8},{17,9... | collective-permute-start | bytes 2543624 | tf_op jit(solution)/shard_map/ppermute | solution.py:223
  272.0 59.2 %collective-permute-start.51 = (bf16[184,2304]{1,0:T(8,128)(2,1)}, bf16[184,2304]{1,0:T(8,128)(2,1)}, u32[]{:S(2)}, u32[]{:S(2)}) collective-permute-start(bf16[184,2304]{1,0:T(8,128)(2,1)} %collective-permute-done.47), channel_id=1, source_target_pairs={{0,8},{1,9},{2,10},{3,11},{4,12},{5,13},{6,14},{7,15},{8,16},{9,17... | collective-permute-start | bytes 2543624 | tf_op jit(solution)/shard_map/ppermute | solution.py:223
  329.5 133.8 %collective-permute-start.30 = (bf16[288,1152]{1,0:T(8,128)(2,1)S(1)}, bf16[288,1152]{1,0:T(8,128)(2,1)S(1)}, u32[]{:S(2)}, u32[]{:S(2)}) collective-permute-start(bf16[288,1152]{1,0:T(8,128)(2,1)S(1)} %copy-done.116), channel_id=1, source_target_pairs={{0,4},{1,5},{2,6},{3,7},{4,0},{5,1},{6,2},{7,3},{8,12},{9,13},{10,... | collective-permute-start | bytes 1990664 | tf_op jit(solution)/shard_map/ppermute | solution.py:223
  330.6 52.6 %collective-permute-start.8 = (bf16[288,1152]{1,0:T(8,128)(2,1)}, bf16[288,1152]{1,0:T(8,128)(2,1)S(1)}, u32[]{:S(2)}, u32[]{:S(2)}) collective-permute-start(bf16[288,1152]{1,0:T(8,128)(2,1)} %collective-permute-done.7), channel_id=1, source_target_pairs={{0,1},{1,0},{2,3},{3,2},{4,5},{5,4},{6,7},{7,6},{8,9},{9,8},{10,11... | collective-permute-start | bytes 1990664 | tf_op jit(solution)/shard_map/ppermute | solution.py:223
  330.6 100.2 %collective-permute-start.25 = (bf16[288,1152]{1,0:T(8,128)(2,1)}, bf16[288,1152]{1,0:T(8,128)(2,1)S(1)}, u32[]{:S(2)}, u32[]{:S(2)}) collective-permute-start(bf16[288,1152]{1,0:T(8,128)(2,1)} %collective-permute-done.24), channel_id=1, source_target_pairs={{0,1},{1,0},{2,3},{3,2},{4,5},{5,4},{6,7},{7,6},{8,9},{9,8},{10,11... | collective-permute-start | bytes 1990664 | tf_op jit(solution)/shard_map/ppermute | solution.py:223
  373.5 57.4 %collective-permute-start.38 = (bf16[288,2944]{1,0:T(8,128)(2,1)S(1)}, bf16[288,2944]{1,0:T(8,128)(2,1)S(1)}, u32[]{:S(2)}, u32[]{:S(2)}) collective-permute-start(bf16[288,2944]{1,0:T(8,128)(2,1)S(1)} %copy-done.107), channel_id=1, source_target_pairs={{8,0},{9,1},{10,2},{11,3},{12,4},{13,5},{14,6},{15,7},{16,8},{17,9... | collective-permute-start | bytes 5087240 | tf_op jit(solution)/shard_map/ppermute | solution.py:223
  377.5 36.1 %collective-permute-start.9 = (bf16[3,288,1152]{2,1,0:T(8,128)(2,1)}, bf16[3,288,1152]{2,1,0:T(8,128)(2,1)}, u32[]{:S(2)}, u32[]{:S(2)}) collective-permute-start(bf16[3,288,1152]{2,1,0:T(8,128)(2,1)} %pad_maximum_fusion.9), channel_id=1, source_target_pairs={{0,4},{1,5},{2,6},{3,7},{4,0},{5,1},{6,2},{7,3},{8,12},{9,13},{10,... | collective-permute-start | bytes 5971976 | tf_op jit(solution)/shard_map/ppermute | solution.py:223
  383.2 41.9 %collective-permute-start.23 = (bf16[3,288,1152]{2,1,0:T(8,128)(2,1)S(1)}, bf16[3,288,1152]{2,1,0:T(8,128)(2,1)S(1)}, u32[]{:S(2)}, u32[]{:S(2)}) collective-permute-start(bf16[3,288,1152]{2,1,0:T(8,128)(2,1)S(1)} %copy-done.104), channel_id=1, source_target_pairs={{0,1},{1,0},{2,3},{3,2},{4,5},{5,4},{6,7},{7,6},{8,9},{9,8},{10,11... | collective-permute-start | bytes 5971976 | tf_op jit(solution)/shard_map/ppermute | solution.py:223
  413.6 35.1 %collective-permute-start.37 = (bf16[288,2944]{1,0:T(8,128)(2,1)S(1)}, bf16[288,2944]{1,0:T(8,128)(2,1)S(1)}, u32[]{:S(2)}, u32[]{:S(2)}) collective-permute-start(bf16[288,2944]{1,0:T(8,128)(2,1)S(1)} %copy-done.107), channel_id=1, source_target_pairs={{0,8},{1,9},{2,10},{3,11},{4,12},{5,13},{6,14},{7,15},{8,16},{9,17... | collective-permute-start | bytes 5087240 | tf_op jit(solution)/shard_map/ppermute | solution.py:223
  425.1 33.9 %collective-permute-start.26 = (bf16[3,288,1152]{2,1,0:T(8,128)(2,1)S(1)}, bf16[3,288,1152]{2,1,0:T(8,128)(2,1)S(1)}, u32[]{:S(2)}, u32[]{:S(2)}) collective-permute-start(bf16[3,288,1152]{2,1,0:T(8,128)(2,1)S(1)} %copy-done.104), channel_id=1, source_target_pairs={{0,4},{1,5},{2,6},{3,7},{4,0},{5,1},{6,2},{7,3},{8,12},{9,13},{10,... | collective-permute-start | bytes 5971976 | tf_op jit(solution)/shard_map/ppermute | solution.py:223
  430.9 100.6 %collective-permute-start.57 = (bf16[512,2432]{1,0:T(8,128)(2,1)S(1)}, bf16[512,2432]{1,0:T(8,128)(2,1)S(1)}, u32[]{:S(2)}, u32[]{:S(2)}) collective-permute-start(bf16[512,2432]{1,0:T(8,128)(2,1)S(1)} %pad_maximum_fusion.7), channel_id=1, source_target_pairs={{0,1},{1,0},{2,3},{3,2},{4,5},{5,4},{6,7},{7,6},{8,9},{9,8},{10,11... | collective-permute-start | bytes 7471112 | tf_op jit(solution)/shard_map/ppermute | solution.py:223
  430.9 42.7 %collective-permute-start.39 = (bf16[288,2944]{1,0:T(8,128)(2,1)S(1)}, bf16[288,2944]{1,0:T(8,128)(2,1)S(1)}, u32[]{:S(2)}, u32[]{:S(2)}) collective-permute-start(bf16[288,2944]{1,0:T(8,128)(2,1)S(1)} %collective-permute-done.38), channel_id=1, source_target_pairs={{8,0},{9,1},{10,2},{11,3},{12,4},{13,5},{14,6},{15,7},{16,8},{17,9... | collective-permute-start | bytes 5087240 | tf_op jit(solution)/shard_map/ppermute | solution.py:223
  459.0 85.4 %collective-permute-start.53 = (bf16[3,184,2304]{2,1,0:T(8,128)(2,1)S(1)}, bf16[3,184,2304]{2,1,0:T(8,128)(2,1)}, u32[]{:S(2)}, u32[]{:S(2)}) collective-permute-start(bf16[3,184,2304]{2,1,0:T(8,128)(2,1)S(1)} %pad_maximum_fusion.6), channel_id=1, source_target_pairs={{0,2},{1,3},{2,0},{3,1},{4,6},{5,7},{6,4},{7,5},{8,10},{9,11},{10,... | collective-permute-start | bytes 7630856 | tf_op jit(solution)/shard_map/ppermute | solution.py:223
  463.3 68.2 %collective-permute-start.13 = (bf16[288,1152]{1,0:T(8,128)(2,1)}, bf16[288,1152]{1,0:T(8,128)(2,1)}, u32[]{:S(2)}, u32[]{:S(2)}) collective-permute-start(bf16[288,1152]{1,0:T(8,128)(2,1)} %collective-permute-done.7), channel_id=1, source_target_pairs={{0,2},{1,3},{2,0},{3,1},{4,6},{5,7},{6,4},{7,5},{8,10},{9,11},{10,... | collective-permute-start | bytes 1990664 | tf_op jit(solution)/shard_map/ppermute | solution.py:223
  473.6 100.6 %collective-permute-start.11 = (bf16[3,288,1152]{2,1,0:T(8,128)(2,1)}, bf16[3,288,1152]{2,1,0:T(8,128)(2,1)}, u32[]{:S(2)}, u32[]{:S(2)}) collective-permute-start(bf16[3,288,1152]{2,1,0:T(8,128)(2,1)} %pad_maximum_fusion.9), channel_id=1, source_target_pairs={{0,2},{1,3},{2,0},{3,1},{4,6},{5,7},{6,4},{7,5},{8,10},{9,11},{10,... | collective-permute-start | bytes 5971976 | tf_op jit(solution)/shard_map/ppermute | solution.py:223
  480.8 95.0 %collective-permute-start.10 = (bf16[3,288,1152]{2,1,0:T(8,128)(2,1)}, bf16[3,288,1152]{2,1,0:T(8,128)(2,1)}, u32[]{:S(2)}, u32[]{:S(2)}) collective-permute-start(bf16[3,288,1152]{2,1,0:T(8,128)(2,1)} %collective-permute-done.9), channel_id=1, source_target_pairs={{0,1},{1,0},{2,3},{3,2},{4,5},{5,4},{6,7},{7,6},{8,9},{9,8},{10,11... | collective-permute-start | bytes 5971976 | tf_op jit(solution)/shard_map/ppermute | solution.py:223
  531.5 136.7 %collective-permute-start.31 = (bf16[288,1152]{1,0:T(8,128)(2,1)S(1)}, bf16[288,1152]{1,0:T(8,128)(2,1)}, u32[]{:S(2)}, u32[]{:S(2)}) collective-permute-start(bf16[288,1152]{1,0:T(8,128)(2,1)S(1)} %collective-permute-done.30), channel_id=1, source_target_pairs={{0,1},{1,0},{2,3},{3,2},{4,5},{5,4},{6,7},{7,6},{8,9},{9,8},{10,11... | collective-permute-start | bytes 1990664 | tf_op jit(solution)/shard_map/ppermute | solution.py:223
  531.5 90.5 %collective-permute-start.14 = (bf16[288,1152]{1,0:T(8,128)(2,1)}, bf16[288,1152]{1,0:T(8,128)(2,1)}, u32[]{:S(2)}, u32[]{:S(2)}) collective-permute-start(bf16[288,1152]{1,0:T(8,128)(2,1)} %collective-permute-done.13), channel_id=1, source_target_pairs={{0,1},{1,0},{2,3},{3,2},{4,5},{5,4},{6,7},{7,6},{8,9},{9,8},{10,11... | collective-permute-start | bytes 1990664 | tf_op jit(solution)/shard_map/ppermute | solution.py:223
  544.5 72.2 %collective-permute-start.28 = (bf16[3,288,1152]{2,1,0:T(8,128)(2,1)S(1)}, bf16[3,288,1152]{2,1,0:T(8,128)(2,1)S(1)}, u32[]{:S(2)}, u32[]{:S(2)}) collective-permute-start(bf16[3,288,1152]{2,1,0:T(8,128)(2,1)S(1)} %copy-done.104), channel_id=1, source_target_pairs={{0,2},{1,3},{2,0},{3,1},{4,6},{5,7},{6,4},{7,5},{8,10},{9,11},{10,... | collective-permute-start | bytes 5971976 | tf_op jit(solution)/shard_map/ppermute | solution.py:223
  574.2 71.9 %collective-permute-start.15 = (bf16[3,288,1152]{2,1,0:T(8,128)(2,1)}, bf16[3,288,1152]{2,1,0:T(8,128)(2,1)S(1)}, u32[]{:S(2)}, u32[]{:S(2)}) collective-permute-start(bf16[3,288,1152]{2,1,0:T(8,128)(2,1)} %collective-permute-done.9), channel_id=1, source_target_pairs={{0,2},{1,3},{2,0},{3,1},{4,6},{5,7},{6,4},{7,5},{8,10},{9,11},{10,... | collective-permute-start | bytes 5971976 | tf_op jit(solution)/shard_map/ppermute | solution.py:223
  575.7 41.0 %collective-permute-start.12 = (bf16[3,288,1152]{2,1,0:T(8,128)(2,1)}, bf16[3,288,1152]{2,1,0:T(8,128)(2,1)S(1)}, u32[]{:S(2)}, u32[]{:S(2)}) collective-permute-start(bf16[3,288,1152]{2,1,0:T(8,128)(2,1)} %collective-permute-done.11), channel_id=1, source_target_pairs={{0,1},{1,0},{2,3},{3,2},{4,5},{5,4},{6,7},{7,6},{8,9},{9,8},{10,11... | collective-permute-start | bytes 5971976 | tf_op jit(solution)/shard_map/ppermute | solution.py:223
  616.7 33.4 %collective-permute-start.27 = (bf16[3,288,1152]{2,1,0:T(8,128)(2,1)S(1)}, bf16[3,288,1152]{2,1,0:T(8,128)(2,1)S(1)}, u32[]{:S(2)}, u32[]{:S(2)}) collective-permute-start(bf16[3,288,1152]{2,1,0:T(8,128)(2,1)S(1)} %copy-done.106), channel_id=1, source_target_pairs={{0,1},{1,0},{2,3},{3,2},{4,5},{5,4},{6,7},{7,6},{8,9},{9,8},{10,11... | collective-permute-start | bytes 5971976 | tf_op jit(solution)/shard_map/ppermute | solution.py:223
  616.7 47.3 %collective-permute-start.29 = (bf16[3,288,1152]{2,1,0:T(8,128)(2,1)S(1)}, bf16[3,288,1152]{2,1,0:T(8,128)(2,1)S(1)}, u32[]{:S(2)}, u32[]{:S(2)}) collective-permute-start(bf16[3,288,1152]{2,1,0:T(8,128)(2,1)S(1)} %collective-permute-done.28), channel_id=1, source_target_pairs={{0,1},{1,0},{2,3},{3,2},{4,5},{5,4},{6,7},{7,6},{8,9},{9,8},{10,11... | collective-permute-start | bytes 5971976 | tf_op jit(solution)/shard_map/ppermute | solution.py:223
  622.0 45.2 %collective-permute-start.32 = (bf16[3,288,1152]{2,1,0:T(8,128)(2,1)S(1)}, bf16[3,288,1152]{2,1,0:T(8,128)(2,1)S(1)}, u32[]{:S(2)}, u32[]{:S(2)}) collective-permute-start(bf16[3,288,1152]{2,1,0:T(8,128)(2,1)S(1)} %collective-permute-done.28), channel_id=1, source_target_pairs={{0,4},{1,5},{2,6},{3,7},{4,0},{5,1},{6,2},{7,3},{8,12},{9,13},{10,... | collective-permute-start | bytes 5971976 | tf_op jit(solution)/shard_map/ppermute | solution.py:223
  646.1 32.5 %collective-permute-start.40 = (bf16[288,2944]{1,0:T(8,128)(2,1)S(1)}, bf16[288,2944]{1,0:T(8,128)(2,1)S(1)}, u32[]{:S(2)}, u32[]{:S(2)}) collective-permute-start(bf16[288,2944]{1,0:T(8,128)(2,1)S(1)} %collective-permute-done.39), channel_id=1, source_target_pairs={{8,0},{9,1},{10,2},{11,3},{12,4},{13,5},{14,6},{15,7},{16,8},{17,9... | collective-permute-start | bytes 5087240 | tf_op jit(solution)/shard_map/ppermute | solution.py:223
  667.3 36.2 %collective-permute-start.33 = (bf16[3,288,1152]{2,1,0:T(8,128)(2,1)S(1)}, bf16[3,288,1152]{2,1,0:T(8,128)(2,1)S(1)}, u32[]{:S(2)}, u32[]{:S(2)}) collective-permute-start(bf16[3,288,1152]{2,1,0:T(8,128)(2,1)S(1)} %collective-permute-done.32), channel_id=1, source_target_pairs={{0,1},{1,0},{2,3},{3,2},{4,5},{5,4},{6,7},{7,6},{8,9},{9,8},{10,11... | collective-permute-start | bytes 5971976 | tf_op jit(solution)/shard_map/ppermute | solution.py:223
  776.9 104.2 %collective-permute-start.43 = (bf16[3,288,2944]{2,1,0:T(8,128)(2,1)S(1)}, bf16[3,288,2944]{2,1,0:T(8,128)(2,1)S(1)}, u32[]{:S(2)}, u32[]{:S(2)}) collective-permute-start(bf16[3,288,2944]{2,1,0:T(8,128)(2,1)S(1)} %pad_maximum_fusion.1), channel_id=1, source_target_pairs={{0,2},{1,3},{2,0},{3,1},{4,6},{5,7},{6,4},{7,5},{8,10},{9,11},{10,... | collective-permute-start | bytes 15261704 | tf_op jit(solution)/shard_map/ppermute | solution.py:223
  953.5 82.7 %collective-permute-start.54 = (bf16[2,256,2432]{2,1,0:T(8,128)(2,1)}, bf16[2,256,2432]{2,1,0:T(8,128)(2,1)}, u32[]{:S(2)}, u32[]{:S(2)}) collective-permute-start(bf16[2,256,2432]{2,1,0:T(8,128)(2,1)} %bitcast.150), channel_id=1, source_target_pairs={{0,1},{1,0},{2,3},{3,2},{4,5},{5,4},{6,7},{7,6},{8,9},{9,8},{10,11... | collective-permute-start | bytes 7471112 | tf_op jit(solution)/shard_map/ppermute | solution.py:223
  1044.4 54.2 %collective-permute-start.59 = (bf16[256,2560]{1,0:T(8,128)(2,1)}, bf16[256,2560]{1,0:T(8,128)(2,1)}, u32[]{:S(2)}, u32[]{:S(2)}) collective-permute-start(bf16[256,2560]{1,0:T(8,128)(2,1)} %fusion.58), channel_id=1, source_target_pairs={{0,4},{1,5},{2,6},{3,7},{4,0},{5,1},{6,2},{7,3},{8,12},{9,13},{10,... | collective-permute-start | bytes 3932168 | tf_op jit(solution)/shard_map/ppermute | solution.py:223
  1206.6 103.7 %all-to-all-start.1 = ((bf16[8,32,2304]{2,1,0:T(8,128)(2,1)}), bf16[8,32,2304]{2,1,0:T(8,128)(2,1)S(1)}, u32[]{:S(2)}, u32[]{:S(2)}) async-start(bf16[8,32,2304]{2,1,0:T(8,128)(2,1)} %bitcast.153), calls=%async_computation.1 | async-start | bytes 2359296 | tf_op jit(solution)/shard_map/all_to_all | solution.py:635
  1239.5 61.5 %collective-permute-start.61 = (bf16[4,2,1336,128]{3,2,1,0:T(8,128)(2,1)S(1)}, bf16[4,2,1336,128]{3,2,1,0:T(8,128)(2,1)S(1)}, u32[]{:S(2)}, u32[]{:S(2)}) collective-permute-start(bf16[4,2,1336,128]{3,2,1,0:T(8,128)(2,1)S(1)} %fusion.27), channel_id=1, source_target_pairs={{0,4},{1,5},{2,6},{3,7},{4,0},{5,1},{6,2},{7,3},{8,12},{9,13},{10,... | collective-permute-start | bytes 8208392 | tf_op jit(solution)/shard_map/ppermute | solution.py:223
  1310.2 60.7 %all-to-all-start.3 = ((bf16[8,32,2304]{2,1,0:T(8,128)(2,1)}), bf16[8,32,2304]{2,1,0:T(8,128)(2,1)S(1)}, u32[]{:S(2)}, u32[]{:S(2)}) async-start(bf16[8,32,2304]{2,1,0:T(8,128)(2,1)} %bitcast.169), calls=%async_computation.3 | async-start | bytes 2359296 | tf_op jit(solution)/shard_map/all_to_all | solution.py:636
  1408.1 34.2 %collective-permute-start.70 = (bf16[4,1336,128]{2,1,0:T(8,128)(2,1)S(1)}, bf16[4,1336,128]{2,1,0:T(8,128)(2,1)S(1)}, u32[]{:S(2)}, u32[]{:S(2)}) collective-permute-start(bf16[4,1336,128]{2,1,0:T(8,128)(2,1)S(1)} %pad_maximum_fusion.11), channel_id=1, source_target_pairs={{0,1},{1,0},{2,3},{3,2},{4,5},{5,4},{6,7},{7,6},{8,9},{9,8},{10,11... | collective-permute-start | bytes 4104200 | tf_op jit(solution)/shard_map/ppermute | solution.py:223
  1408.2 32.4 %collective-permute-start.71 = (bf16[4,1336,128]{2,1,0:T(8,128)(2,1)S(1)}, bf16[4,1336,128]{2,1,0:T(8,128)(2,1)S(1)}, u32[]{:S(2)}, u32[]{:S(2)}) collective-permute-start(bf16[4,1336,128]{2,1,0:T(8,128)(2,1)S(1)} %pad_maximum_fusion.11), channel_id=1, source_target_pairs={{0,2},{1,3},{2,0},{3,1},{4,6},{5,7},{6,4},{7,5},{8,10},{9,11},{10,... | collective-permute-start | bytes 4104200 | tf_op jit(solution)/shard_map/ppermute | solution.py:223
  1409.7 33.0 %collective-permute-start.73 = (bf16[4,1336,128]{2,1,0:T(8,128)(2,1)S(1)}, bf16[4,1336,128]{2,1,0:T(8,128)(2,1)S(1)}, u32[]{:S(2)}, u32[]{:S(2)}) collective-permute-start(bf16[4,1336,128]{2,1,0:T(8,128)(2,1)S(1)} %pad_maximum_fusion.11), channel_id=1, source_target_pairs={{0,4},{1,5},{2,6},{3,7},{4,0},{5,1},{6,2},{7,3},{8,12},{9,13},{10,... | collective-permute-start | bytes 4104200 | tf_op jit(solution)/shard_map/ppermute | solution.py:223
  1440.6 32.4 %collective-permute-start.75 = (bf16[4,1336,128]{2,1,0:T(8,128)(2,1)S(1)}, bf16[4,1336,128]{2,1,0:T(8,128)(2,1)S(1)}, u32[]{:S(2)}, u32[]{:S(2)}) collective-permute-start(bf16[4,1336,128]{2,1,0:T(8,128)(2,1)S(1)} %collective-permute-done.71), channel_id=1, source_target_pairs={{0,4},{1,5},{2,6},{3,7},{4,0},{5,1},{6,2},{7,3},{8,12},{9,13},{10,... | collective-permute-start | bytes 4104200 | tf_op jit(solution)/shard_map/ppermute | solution.py:223
  (227 other events, 6871.5 us)

commit v2 on v1

v2 whole, which is shorter than its diff:
```python
import functools
import math

import jax
import jax.numpy as jnp
from jax import lax
from jax.experimental import pallas as pl
from jax.experimental.pallas import tpu as pltpu
from jax.sharding import PartitionSpec as P

MODEL_WIDTH = 2304
ATTENTION_HEADS = 36
HEAD_SIZE = 64
FEEDFORWARD_UNITS = 5760
ADAPTER_RANK = 16
OPT_STEP = 10
SEQ_DEV = 4
TOK_DEV = 256
ADAPTER_COLUMNS = 128


norm_eps = 1e-05
residual_branch_scale = 1.4 / math.sqrt(40.0)
adapter_scale = 2.0
rope_base = 10000.0
first_decay_rate = 0.9
second_decay_rate = 0.999
adaptive_epsilon = 1e-08
weight_shrink_rate = 0.01
learning_rate = 0.01


def matrix_product(left_side, right_side):
    return jnp.dot(left_side, right_side, preferred_element_type=jnp.float32)


def matrix_product_backward(left_side, right_side):
    return lax.dot_general(
        left_side, right_side, (((1,), (1,)), ((), ())), preferred_element_type=jnp.float32
    )


def outer_product_sum(left_side, right_side):
    return lax.dot_general(
        left_side, right_side, (((0,), (0,)), ((), ())), preferred_element_type=jnp.float32
    )


def low(values):
    return values.astype(jnp.bfloat16)


def block_tables(sequence_lengths, sequence_adapter_index):
    row_ids = jnp.arange(TOK_DEV, dtype=jnp.int32)
    seq_ends = jnp.cumsum(sequence_lengths, dtype=jnp.int32)
    seq_starts = seq_ends - sequence_lengths
    segment = jnp.sum(
        (row_ids[:, None] >= seq_ends[None, :]).astype(jnp.int32), axis=1, dtype=jnp.int32
    )
    member = (segment[:, None] == jnp.arange(SEQ_DEV, dtype=jnp.int32)[None, :]).astype(jnp.int32)
    position = row_ids - jnp.sum(member * seq_starts[None, :], axis=1, dtype=jnp.int32)
    token_adapter_index = jnp.sum(member * sequence_adapter_index[None, :], axis=1, dtype=jnp.int32)
    adapter_choice_index = (
        jnp.arange(ADAPTER_COLUMNS, dtype=jnp.int32)[None, :] // ADAPTER_RANK
        == token_adapter_index[:, None]
    ).astype(jnp.float32)
    allowed = (segment[:, None] == segment[None, :]) & (row_ids[None, :] <= row_ids[:, None])
    half_dim = HEAD_SIZE // 2
    inv_freq = jnp.power(rope_base, -2.0 * jnp.arange(half_dim, dtype=jnp.float32) / HEAD_SIZE)
    angles = position.astype(jnp.float32)[:, None] * inv_freq[None, :]
    cosine, sine = jnp.cos(angles), jnp.sin(angles)
    return (
        adapter_choice_index,
        allowed,
        jnp.concatenate([cosine] * 4, axis=1),
        jnp.concatenate([-sine, sine] * 2, axis=1),
    )


def restore_structure(flattened_vector):
    first_boundary = 6 * MODEL_WIDTH * ADAPTER_COLUMNS
    second_boundary = first_boundary + FEEDFORWARD_UNITS * ADAPTER_COLUMNS
    third_boundary = second_boundary + 5 * ADAPTER_COLUMNS * MODEL_WIDTH
    return (
        flattened_vector[:first_boundary].reshape(6, MODEL_WIDTH, ADAPTER_COLUMNS),
        flattened_vector[first_boundary:second_boundary].reshape(
            FEEDFORWARD_UNITS, ADAPTER_COLUMNS
        ),
        flattened_vector[second_boundary:third_boundary].reshape(5, ADAPTER_COLUMNS, MODEL_WIDTH),
        flattened_vector[third_boundary:].reshape(2, ADAPTER_COLUMNS, FEEDFORWARD_UNITS),
    )


def rms_scale(values):
    return lax.rsqrt(jnp.mean(values * values, axis=-1, keepdims=True) + norm_eps)


def norm_back(values, scale, gain, gradient_value):
    weighted = gradient_value * gain
    return scale * weighted - values * scale**3 * jnp.mean(
        values * weighted, axis=-1, keepdims=True
    )


def apply_adapter_delta(input_rows, adapter_down_pair, adapter_up_pair, adapter_choice_index):
    reduced_total = low(
        matrix_product(input_rows, adapter_down_pair) * adapter_choice_index
    )
    return (reduced_total, adapter_scale * matrix_product(reduced_total, adapter_up_pair))


def swap_halves(values):
    lane = lax.broadcasted_iota(jnp.int32, values.shape, 1)
    half, width = HEAD_SIZE // 2, values.shape[1]
    return jnp.where(
        lane % HEAD_SIZE < half, pltpu.roll(values, width - half, 1), pltpu.roll(values, half, 1)
    )


def head_scores(query, key, bias):
    scores = matrix_product_backward(query, key) * HEAD_SIZE ** (-0.5) + bias
    expanded = jnp.exp(scores - jnp.max(scores, axis=-1, keepdims=True))
    return expanded / jnp.sum(expanded, axis=-1, keepdims=True)


def attention_kernel(lin, z, up, cosine, sine, bias, qkv, attended):
    full = [lin[t] + adapter_scale * matrix_product(z[t], up[t]) for t in range(3)]
    query, key = (
        low(v * cosine[...] + swap_halves(v) * sine[...]) for v in full[:2]
    )
    value = low(full[2])
    qkv[0], qkv[1], qkv[2] = query, key, value
    first = lax.broadcasted_iota(jnp.int32, query.shape, 1) < HEAD_SIZE
    results = []
    for mine in (first, ~first):
        probs = head_scores(jnp.where(mine, query, jnp.zeros_like(query)), key, bias[...])
        results.append(matrix_product(low(probs), value))
    attended[...] = low(jnp.where(first, results[0], results[1]))


def attention_back_kernel(qkv, lin, dz, down, cosine, sine, bias, grads):
    query, key, value = qkv[0], qkv[1], qkv[2]
    grad = low(lin[...] + matrix_product_backward(dz[...], down[...]))
    first = lax.broadcasted_iota(jnp.int32, query.shape, 1) < HEAD_SIZE
    nothing = jnp.zeros_like(query)
    results = []
    for mine in (first, ~first):
        probs = head_scores(jnp.where(mine, query, nothing), key, bias[...])
        grad_probs = matrix_product_backward(jnp.where(mine, grad, nothing), value)
        row_delta = jnp.sum(probs * grad_probs, axis=-1, keepdims=True)
        grad_scores = low(probs * (grad_probs - row_delta))
        results.append(
            (
                matrix_product(grad_scores, key),
                outer_product_sum(grad_scores, query),
                outer_product_sum(low(probs), grad),
            )
        )
    scale = HEAD_SIZE ** (-0.5)
    grad_query, grad_key, grad_value = (
        jnp.where(first, one, two) for one, two in zip(*results)
    )
    for t, v in enumerate((grad_query * scale, grad_key * scale)):
        grads[t] = low(v * cosine[...] - swap_halves(v) * sine[...])
    grads[2] = low(grad_value)


def attention_call(kernel, operands, outs):
    pairs = 2 * HEAD_SIZE

    def spec(shape, axis):
        block = tuple(pairs if k == axis else n for k, n in enumerate(shape))
        return pl.BlockSpec(block, lambda i: tuple(i if k == axis else 0 for k in range(len(shape))))

    count = operands[-1][0].shape[0]
    return pl.pallas_call(
        kernel,
        grid=(ATTENTION_HEADS // 2,),
        out_shape=[jax.ShapeDtypeStruct(shape, jnp.bfloat16) for shape, _ in outs],
        in_specs=[spec(v.shape, axis) for v, axis in operands],
        out_specs=[spec(shape, axis) for shape, axis in outs],
        compiler_params=pltpu.CompilerParams(vmem_limit_bytes=48 << 20),
        cost_estimate=pl.CostEstimate(
            flops=8 * count * count * MODEL_WIDTH,
            bytes_accessed=24 * count * MODEL_WIDTH,
            transcendentals=count * count * ATTENTION_HEADS,
        ),
    )(*[v for v, _ in operands])


GROUP = 4
AXES = ("dp", "shard")


def together(*values):
    return lax.optimization_barrier(values)


class Place:
    def __init__(self, dp, shard):
        self.line, self.shard = dp // 2, shard
        i, s = lax.axis_index("dp"), lax.axis_index("shard")
        self.z, self.y, self.x, self.c = i // 2, i % 2, s // 2, s % 2
        self.q = self.y * 2 + self.c
        self.spots = [
            (z, y, x, c)
            for z in range(self.line)
            for y in range(2)
            for x in range(shard // 2)
            for c in range(2)
        ]

    def number(self, z, y, x, c):
        return (z * 2 + y) * self.shard + x * 2 + c

    def move(self, value, target):
        pairs = []
        for spot in self.spots:
            to = target(*spot)
            if to is not None:
                pairs.append((self.number(*spot), self.number(*to)))
        return lax.ppermute(value, AXES, pairs)

    def by_y(self, value):
        return self.move(value, lambda z, y, x, c: (z, 1 - y, x, c))

    def by_x(self, value):
        return self.move(value, lambda z, y, x, c: (z, y, 1 - x, c))

    def by_c(self, value):
        return self.move(value, lambda z, y, x, c: (z, y, x, 1 - c))

    def ring_z(self, value, step):
        return self.move(value, lambda z, y, x, c: ((z + step) % self.line, y, x, c))

    def all_z(self, block):
        groups = [[z * 2 + y for z in range(self.line)] for y in range(2)]
        return lax.all_gather(block, "dp", axis=0, axis_index_groups=groups)

    def other_z(self, blocks):
        return jnp.stack(
            [
                lax.dynamic_index_in_dim(blocks, (self.z + k) % self.line, 0, keepdims=False)
                for k in range(1, self.line)
            ]
        )

    def gather_group(self, rows):
        pair = jnp.concatenate([rows, self.by_y(rows)], axis=0)
        return jnp.concatenate([pair, self.by_c(pair)], axis=0)

    def sum_group(self, partial):
        rows = partial.shape[0] // GROUP
        partial = partial.reshape(GROUP, rows, -1)
        got = self.by_c(partial[2:].astype(jnp.bfloat16))
        pair = partial[:2] + got.astype(jnp.float32)
        got = self.by_y(pair[1].astype(jnp.bfloat16))
        return pair[0] + got.astype(jnp.float32)


def put(buffer, block, *where):
    block = block.reshape((1,) * len(where) + block.shape)
    return lax.dynamic_update_slice(
        buffer, block, tuple(where) + (0,) * (buffer.ndim - len(where))
    )


def put_quarter(place, planes, rest, mates):
    full = jnp.zeros((place.line, 2) + rest.shape, rest.dtype)
    full = lax.dynamic_update_slice(full, planes[:, None], (0, place.x) + (0,) * rest.ndim)
    full = put(full, rest, place.z, 1 - place.x)
    for k in range(1, place.line):
        full = put(full, mates[k - 1], (place.z + k) % place.line, 1 - place.x)
    return full.reshape((-1,) + rest.shape[1:])


class AttentionWeights:
    def __init__(self, place, weights, same, across, near):
        self.place, self.native = place, weights
        self.same, self.across, self.near = same, across, near
        self.s = place.x * 2 + place.c
        self.rows, self.half = weights[0].shape[0], weights[0].shape[1] // 2

    def full(self, t):
        place = self.place
        halves = []
        for h in range(2):
            cols = slice(h * self.half, (h + 1) * self.half)
            buffer = jnp.zeros((place.line, 2, self.rows, self.half), self.native[t].dtype)
            buffer = put(buffer, self.native[t][:, cols], place.z, place.y)
            for r in range(4):
                near = self.near[r][:, cols]
                with_r = put(buffer, near, place.z, 1 - place.y)
                for k in range(1, place.line):
                    plane = (place.z + k) % place.line
                    with_r = put(with_r, self.same[h][r][k - 1], plane, place.y)
                    with_r = put(with_r, self.across[h][r][k - 1], plane, 1 - place.y)
                buffer = jnp.where(self.s ^ r == t, with_r, buffer)
            halves.append(buffer.reshape(-1, self.half))
        return jnp.concatenate(halves, axis=1)

    def times(self, values, first, count):
        if self.rows % 16:
            return jnp.stack([matrix_product(values, self.full(first + j)) for j in range(count)])
        return self.call(values, first, count, False)

    def times_transposed(self, values, first, count):
        if self.rows % 16:
            return sum(
                matrix_product_backward(values[j], self.full(first + j)) for j in range(count)
            )
        return self.call(values, first, count, True)

    def call(self, values, first, count, back):
        place, rows, half = self.place, self.rows, self.half
        where = jnp.stack([place.z, place.y, self.s]).astype(jnp.int32)
        width, depth = 2 * half, rows * 2 * place.line
        tokens = values.shape[-2]
        shape = (tokens, depth) if back else (count, tokens, width)
        held = pl.BlockSpec(memory_space=pltpu.VMEM)
        given = pl.BlockSpec(memory_space=pl.ANY)
        pieces = (
            list(self.native[first : first + count])
            + [v for h in range(2) for v in self.same[h]]
            + [v for h in range(2) for v in self.across[h]]
            + list(self.near)
        )
        return pl.pallas_call(
            functools.partial(weights_kernel, place.line, first, count, back),
            out_shape=jax.ShapeDtypeStruct(shape, jnp.float32),
            in_specs=[pl.BlockSpec(memory_space=pltpu.SMEM), held] + [given] * len(pieces),
            out_specs=held,
            scratch_shapes=[
                pltpu.VMEM((2, count, depth, half), jnp.bfloat16),
                pltpu.SemaphoreType.DMA((2, count)),
            ],
            compiler_params=pltpu.CompilerParams(vmem_limit_bytes=56 << 20),
            cost_estimate=pl.CostEstimate(
                flops=2 * tokens * depth * width * count,
                bytes_accessed=2 * depth * width * count + 4 * math.prod(shape),
                transcendentals=0,
            ),
        )(where, values, *pieces)


def weights_kernel(line, first, count, back, where, values, *refs):
    native = refs[:count]
    same = (refs[count : count + 4], refs[count + 4 : count + 8])
    across = (refs[count + 8 : count + 12], refs[count + 12 : count + 16])
    near = refs[count + 16 : count + 20]
    out, held, sems = refs[count + 20 :]
    z, y, s = where[0], where[1], where[2]
    rows, width = native[0].shape
    half = width // 2

    def place(h, j, plane, side):
        start = pl.multiple_of(rows * (2 * plane + side), 16)
        return held.at[h, j, pl.ds(start, rows)]

    for h in range(2):
        cols = pl.ds(h * half, half)
        for j in range(count):
            pltpu.make_async_copy(
                native[j].at[:, cols], place(h, j, z, y), sems.at[h, j]
            ).start()
        for r in range(4):
            j = (s ^ r) - first

            @pl.when((j >= 0) & (j < count))
            def _():
                pltpu.make_async_copy(
                    near[r].at[:, cols], place(h, j, z, 1 - y), sems.at[h, j]
                ).start()
                for k in range(1, line):
                    plane = lax.rem(z + k, line)
                    pltpu.make_async_copy(
                        same[h][r].at[k - 1], place(h, j, plane, y), sems.at[h, j]
                    ).start()
                    pltpu.make_async_copy(
                        across[h][r].at[k - 1], place(h, j, plane, 1 - y), sems.at[h, j]
                    ).start()

    if back:
        out[...] = jnp.zeros_like(out)

    def step(i, carry):
        h, j = i // count, lax.rem(i, count)
        cols = pl.ds(pl.multiple_of(h * half, 128), half)
        pltpu.make_async_copy(held.at[h, j], held.at[h, j], sems.at[h, j]).wait()
        if back:
            out[...] += matrix_product_backward(values[j, :, cols], held[h, j])
        else:
            out[j, :, cols] = matrix_product(values[...], held[h, j])
        return carry

    lax.fori_loop(0, 2 * count, step, 0)


def columns_kernel(own, padded, quarter, value, *outs):
    each, window = GROUP * own, 2 * padded
    rows, width = value.shape
    step = pl.program_id(0)
    lane = lax.broadcasted_iota(jnp.int32, (rows, window), 1)
    for out, k in zip(outs, (quarter[0], quarter[0] ^ 2)):
        turned = []
        for n in range(2):
            start = each * (2 * step + n) + own * k
            base = jnp.minimum(start // 128, (width - window) // 128) * 128
            piece = value[:, pl.ds(pl.multiple_of(base, 128), window)].astype(jnp.float32)
            turned.append(pltpu.roll(piece, lax.rem(window + n * padded - (start - base), window), 1))
        kept = jnp.where(lane < own, turned[0], 0.0)
        kept = jnp.where((lane >= padded) & (lane < padded + own), turned[1], kept)
        out[...] = low(kept)


def hidden_columns(place, value, blocks, padded):
    rows, width = value.shape
    own = width // (blocks * GROUP)
    if padded % 64 or 2 * padded > width:

        def take(k):
            def cut(given):
                pieces = []
                for i in range(blocks):
                    start = own * (GROUP * i + k)
                    piece = given[:, start : start + own]
                    pieces.append(jnp.pad(piece, ((0, 0), (0, padded - own))))
                return jnp.concatenate(pieces, axis=1)

            return cut

        branches = [take(k) for k in range(GROUP)]
        return [lax.switch(k, branches, value) for k in (place.q, place.q ^ 2)]
    return pl.pallas_call(
        functools.partial(columns_kernel, own, padded),
        grid=(blocks // 2,),
        out_shape=[jax.ShapeDtypeStruct((rows, blocks * padded), value.dtype)] * 2,
        in_specs=[
            pl.BlockSpec(memory_space=pltpu.SMEM),
            pl.BlockSpec((rows, width), lambda i: (0, 0)),
        ],
        out_specs=[pl.BlockSpec((rows, 2 * padded), lambda i: (0, i))] * 2,
        compiler_params=pltpu.CompilerParams(vmem_limit_bytes=32 << 20),
        cost_estimate=pl.CostEstimate(
            flops=8 * rows * width, bytes_accessed=4 * rows * width, transcendentals=0
        ),
    )(place.q.astype(jnp.int32).reshape(1), value)


def hidden_rows(place, value, quarter, blocks, padded):
    own = value.shape[0] // (blocks * GROUP)
    split = value.reshape(blocks, GROUP, own, -1)
    got = lax.dynamic_index_in_dim(split, quarter, 1, keepdims=False)
    return jnp.pad(got, ((0, 0), (0, padded - own), (0, 0))).reshape(blocks * padded, -1)


def spread_kernel(own, padded, quarter, value, out, total):
    rows, width = total.shape
    window = 2 * padded
    total[...] = jnp.zeros_like(total)
    lane = lax.broadcasted_iota(jnp.int32, (rows, window), 1)
    for i in range(width // (GROUP * own)):
        pair, n = i // 2, i % 2
        start = own * (GROUP * i + quarter[0])
        base = jnp.minimum(start // 128, (width - window) // 128) * 128
        piece = value[:, pair * window : (pair + 1) * window].astype(jnp.float32)
        inside = (lane >= n * padded) & (lane < n * padded + own)
        turned = pltpu.roll(
            jnp.where(inside, piece, 0.0),
            lax.rem(window - n * padded + (start - base), window),
            1,
        )
        total[:, pl.ds(pl.multiple_of(base, 128), window)] += turned
    out[...] = low(total[...])


def spread_columns(place, value, width, blocks, padded):
    rows = value.shape[0]
    own = width // (blocks * GROUP)
    if padded % 64 or 2 * padded > width:

        def lay(k):
            def build(given):
                pieces = []
                for i in range(blocks):
                    piece = given[:, padded * i : padded * i + own]
                    pieces.append(jnp.pad(piece, ((0, 0), (own * k, own * (GROUP - 1 - k)))))
                return jnp.concatenate(pieces, axis=1)

            return build

        return lax.switch(place.q, [lay(k) for k in range(GROUP)], value)
    return pl.pallas_call(
        functools.partial(spread_kernel, own, padded),
        out_shape=jax.ShapeDtypeStruct((rows, width), jnp.bfloat16),
        in_specs=[
            pl.BlockSpec(memory_space=pltpu.SMEM),
            pl.BlockSpec(memory_space=pltpu.VMEM),
        ],
        out_specs=pl.BlockSpec(memory_space=pltpu.VMEM),
        scratch_shapes=[pltpu.VMEM((rows, width), jnp.float32)],
        compiler_params=pltpu.CompilerParams(vmem_limit_bytes=32 << 20),
        cost_estimate=pl.CostEstimate(
            flops=8 * rows * width, bytes_accessed=4 * rows * width, transcendentals=0
        ),
    )(place.q.astype(jnp.int32).reshape(1), value)


def both(kept, got):
    return low(kept.astype(jnp.float32) + got.astype(jnp.float32))


def pick(values, index, axis):
    return lax.dynamic_index_in_dim(values, index, axis, keepdims=False)


def reduce_over_cores(place, flat):
    pairs = place.line * 2 * (place.shard // 2)
    rows = flat.shape[0] // pairs
    half = -(-rows // 16) * 8
    split = flat.reshape(place.line, 2, place.shard // 2, rows, ADAPTER_COLUMNS)
    start = rows - half
    keep = lax.dynamic_slice_in_dim(split, place.c * start, half, 3)
    send = lax.dynamic_slice_in_dim(split, (1 - place.c) * start, half, 3)
    return both(keep, place.by_c(send))


def reduce_to_owner(place, total, share):
    half = total.shape[3]
    cut = half // 16 * 8
    one, two = total[:, :, :, :cut], total[:, :, :, cut:]
    got_one = place.by_y(pick(one, 1 - place.y, 1))
    got_two = place.by_x(pick(two, 1 - place.x, 2))
    one, two = both(pick(one, place.y, 1), got_one), both(pick(two, place.x, 2), got_two)
    got_one = place.by_x(pick(one, 1 - place.x, 1))
    got_two = place.by_y(pick(two, 1 - place.y, 1))
    one, two = both(pick(one, place.x, 1), got_one), both(pick(two, place.y, 1), got_two)
    total = jnp.concatenate([one, two], axis=1)
    result = pick(total, place.z, 0).astype(jnp.float32)
    for k in range(1, place.line):
        send = pick(total, (place.z + k) % place.line, 0)
        result = result + place.ring_z(send, k).astype(jnp.float32)
    return lax.dynamic_slice_in_dim(result, place.c * (half - share), share, 0)


def gather_owners(place, own):
    share = own.shape[0]
    half = -(-share // 8) * 8
    start = 2 * share - half
    mate = place.by_c(own)
    head, tail = jnp.where(place.c == 0, own, mate), jnp.where(place.c == 0, mate, own)
    pair = jnp.concatenate([head, tail], axis=0)
    planes = place.all_z(lax.dynamic_slice_in_dim(pair, place.c * start, half, 0))
    cut = half // 16 * 8
    full = jnp.zeros(
        (place.line, 2, place.shard // 2, 2 * share, ADAPTER_COLUMNS), own.dtype
    )
    for part, x_first, at in ((planes[:, :cut], True, 0), (planes[:, cut:], False, cut)):
        x_part, y_part = place.by_x(part), place.by_y(part)
        xy_part = place.by_y(x_part) if x_first else place.by_x(y_part)
        for value, y, x in (
            (part, place.y, place.x),
            (x_part, place.y, 1 - place.x),
            (y_part, 1 - place.y, place.x),
            (xy_part, 1 - place.y, 1 - place.x),
        ):
            for held, c in ((value, place.c), (place.by_c(value), 1 - place.c)):
                where = (0, y, x, c * start + at, 0)
                full = lax.dynamic_update_slice(full, held[:, None, None], where)
    return full.reshape(-1)


def shards(
    dp,
    shard,
    tokens,
    cotangent,
    arrival,
    lengths,
    adapter_set,
    gain_one,
    gain_two,
    w_query,
    w_key,
    w_value,
    w_out,
    w_gate,
    w_up,
    w_down,
    adapters,
    first_moment_running,
    second_moment_running,
):
    place = Place(dp, shard)
    token_order = arrival[0]
    count = token_order.shape[0]
    padded = -(-(FEEDFORWARD_UNITS // (dp * GROUP)) // 16) * 16


    weights = (w_query, w_key, w_value, w_out)
    s, half = place.x * 2 + place.c, MODEL_WIDTH // 2
    stacked = jnp.stack(weights)
    mine = lax.dynamic_index_in_dim(stacked, s, 0, keepdims=False)
    first = place.all_z(mine[:, :half])
    second = place.all_z(mine[:, half:])
    near_y = place.by_y(mine)
    table = jnp.concatenate([lengths, adapter_set], axis=1)
    table_y = place.by_y(table)
    own_gate, other_gate = hidden_columns(place, w_gate, dp, padded)
    own_up, other_up = hidden_columns(place, w_up, dp, padded)
    near_y, table_y, other_gate, other_up = together(near_y, table_y, other_gate, other_up)

    near_x = place.by_x(near_y)
    got_gate, got_up = place.by_y(other_gate), place.by_y(other_up)
    near_y_c = place.by_c(near_y)
    tables = jnp.concatenate([table, table_y], axis=0)
    tables_c = place.by_c(tables)
    own_down = hidden_rows(place, w_down, place.q, 1, padded)
    other_down = hidden_rows(place, w_down, place.q ^ 2, 1, padded)
    first, got_gate, got_up, near_x, near_y_c, tables_c, tokens = together(
        first, got_gate, got_up, near_x, near_y_c, tables_c, tokens
    )

    straight = place.y == place.x
    gate_planes = place.all_z(jnp.where(straight, own_gate, got_gate))
    up_planes = place.all_z(jnp.where(straight, own_up, got_up))
    gate_rest, up_rest = (
        jnp.where(straight, got_gate, own_gate),
        jnp.where(straight, got_up, own_up),
    )
    tables = jnp.concatenate([tables, tables_c], axis=0)
    lines = place.other_z(first)
    x0, y0, lines_c = place.by_x(lines), place.by_y(lines), place.by_c(lines)
    near_x_c = place.by_c(near_x)
    arrived_x = lax.all_to_all(tokens, "dp", split_axis=0, concat_axis=0, tiled=True)
    x0, y0, lines_c, near_x_c, second, cotangent = together(
        x0, y0, lines_c, near_x_c, second, cotangent
    )

    lines2 = place.other_z(second)
    x1, y1, lines2_c = place.by_x(lines2), place.by_y(lines2), place.by_c(lines2)
    x0_c, y0_c = place.by_c(x0), place.by_c(y0)
    x1, y1, lines2_c, x0_c, y0_c, x0, other_down, arrived_x, cotangent = together(
        x1, y1, lines2_c, x0_c, y0_c, x0, other_down, arrived_x, cotangent
    )

    arrived_cot = lax.all_to_all(cotangent, "dp", split_axis=0, concat_axis=0, tiled=True)
    xy0, xy1, got_down = place.by_y(x0), place.by_x(y1), place.by_y(other_down)
    x1_c, y1_c = place.by_c(x1), place.by_c(y1)
    xy0, xy1, x1_c, y1_c, gate_planes, got_down = together(
        xy0, xy1, x1_c, y1_c, gate_planes, got_down
    )

    down_planes = place.all_z(jnp.where(straight, own_down, got_down))
    down_rest = jnp.where(straight, got_down, own_down)
    gate_mates = place.by_x(place.other_z(gate_planes))
    attention = AttentionWeights(
        place,
        weights,
        ((lines, lines_c, x0, x0_c), (lines2, lines2_c, x1, x1_c)),
        ((y0, y0_c, xy0, place.by_c(xy0)), (y1, y1_c, xy1, place.by_c(xy1))),
        (near_y, near_y_c, near_x, near_x_c),
    )
    A_model, A_hidden, B_model, B_hidden = restore_structure(adapters)
    choice, allowed, cosine_table, sine_table = block_tables(lengths[0], adapter_set[0])
    choices = jnp.concatenate(
        [block_tables(tables[k, :SEQ_DEV], tables[k, SEQ_DEV:])[0] for k in range(GROUP)], axis=0
    )
    gain_first = gain_one.astype(jnp.float32)
    gain_second = gain_two.astype(jnp.float32)

    x = arrived_x[token_order].astype(jnp.float32)
    scale_one = rms_scale(x)
    n1 = low(x * scale_one * gain_first)

    z_qkv = low(
        jnp.einsum("nd,tdr->tnr", n1, A_model[:3], preferred_element_type=jnp.float32) * choice
    )
    bias = jnp.where(allowed, 0.0, -jnp.inf)
    qkv, o = attention_call(
        attention_kernel,
        (
            (attention.times(n1, 0, 3), 2),
            (z_qkv, None),
            (B_model[:3], 2),
            (cosine_table, None),
            (sine_table, None),
            (bias, None),
        ),
        (((3, count, MODEL_WIDTH), 2), ((count, MODEL_WIDTH), 1)),
    )
    o, up_planes, arrived_cot = together(o, up_planes, arrived_cot)
    up_mates = place.by_x(place.other_z(up_planes))
    z_out, delta_out = apply_adapter_delta(o, A_model[3], B_model[3], choice)
    m = x + residual_branch_scale * (attention.times(o, 3, 1)[0] + delta_out)
    scale_two = rms_scale(m)
    n2 = low(m * scale_two * gain_second)

    g = arrived_cot[token_order].astype(jnp.float32)
    e_down = low(residual_branch_scale * g)
    dz_down = low(adapter_scale * matrix_product_backward(e_down, B_model[4]) * choice)
    sent = jnp.concatenate([e_down, dz_down], axis=1)
    sent_pair = jnp.concatenate([sent, place.by_y(sent)], axis=0)
    gate_mates, down_planes, n2 = together(gate_mates, down_planes, n2)
    down_mates = place.by_x(place.other_z(down_planes))
    n2_all = place.gather_group(n2)
    sent = jnp.concatenate([sent_pair, place.by_c(sent_pair)], axis=0)
    gate = put_quarter(place, gate_planes, gate_rest, gate_mates)
    up_part = put_quarter(place, up_planes, up_rest, up_mates)
    down = put_quarter(place, down_planes, down_rest, down_mates)
    e_down_all, dz_down_all = sent[:, :MODEL_WIDTH], sent[:, MODEL_WIDTH:]
    B_gate, _ = hidden_columns(place, B_hidden[0], dp, padded)
    B_up, _ = hidden_columns(place, B_hidden[1], dp, padded)
    A_down = hidden_rows(place, A_hidden, place.q, dp, padded)
    z_gate = low(matrix_product(n2_all, A_model[4]) * choices)
    z_up = low(matrix_product(n2_all, A_model[5]) * choices)
    gt = matrix_product(n2_all, gate) + adapter_scale * matrix_product(z_gate, B_gate)
    up = matrix_product(n2_all, up_part) + adapter_scale * matrix_product(z_up, B_up)
    sg = jax.nn.sigmoid(gt)
    act = gt * sg
    h = low(act * up)
    dh = matrix_product_backward(e_down_all, down) + matrix_product_backward(dz_down_all, A_down)
    e_gate = low(dh * up * (sg + gt * sg * (1.0 - sg)))
    e_up = low(dh * act)
    back_sum = place.sum_group(
        jnp.concatenate(
            [
                matrix_product_backward(e_gate, gate)
                + matrix_product_backward(e_up, up_part),
                matrix_product_backward(e_gate, B_gate),
                matrix_product_backward(e_up, B_up),
                matrix_product(h, A_down),
            ],
            axis=1,
        )
    )
    cuts = [MODEL_WIDTH + k * ADAPTER_COLUMNS for k in range(3)]
    dz_gate, dz_up, z_down = jnp.split(back_sum, cuts, axis=1)[1:]
    dz_gate, dz_up = low(adapter_scale * dz_gate * choice), low(adapter_scale * dz_up * choice)
    z_down = low(z_down * choice)
    dn2 = (
        back_sum[:, :MODEL_WIDTH]
        + matrix_product_backward(dz_gate, A_model[4])
        + matrix_product_backward(dz_up, A_model[5])
    )
    dA_gate, dA_up = outer_product_sum(n2, dz_gate), outer_product_sum(n2, dz_up)
    dB_gate = adapter_scale * outer_product_sum(z_gate, e_gate)
    dB_up = adapter_scale * outer_product_sum(z_up, e_up)
    dA_down = outer_product_sum(h, dz_down_all)
    dB_down = adapter_scale * outer_product_sum(z_down, e_down)

    dm = g + norm_back(m, scale_two, gain_second, dn2)
    e_out = low(residual_branch_scale * dm)
    dz_out = low(adapter_scale * matrix_product_backward(e_out, B_model[3]) * choice)
    (e_qkv,) = attention_call(
        attention_back_kernel,
        (
            (qkv, 2),
            (attention.times_transposed(e_out[None], 3, 1), 1),
            (dz_out, None),
            (A_model[3], 0),
            (cosine_table, None),
            (sine_table, None),
            (bias, None),
        ),
        (((3, count, MODEL_WIDTH), 2),),
    )
    dA_out, dB_out = outer_product_sum(o, dz_out), adapter_scale * outer_product_sum(z_out, e_out)
    dz_qkv = low(
        adapter_scale
        * jnp.einsum("tnd,trd->tnr", e_qkv, B_model[:3], preferred_element_type=jnp.float32)
        * choice
    )
    dA_qkv = jnp.einsum("nd,tnr->tdr", n1, dz_qkv, preferred_element_type=jnp.float32)
    dB_qkv = adapter_scale * jnp.einsum(
        "tnr,tnd->trd", z_qkv, e_qkv, preferred_element_type=jnp.float32
    )
    own_hidden = FEEDFORWARD_UNITS // (dp * GROUP)
    dA_hidden = lax.dynamic_update_slice(
        jnp.zeros((dp, GROUP, own_hidden, ADAPTER_COLUMNS), jnp.bfloat16),
        low(dA_down).reshape(dp, 1, padded, ADAPTER_COLUMNS)[:, :, :own_hidden],
        (0, place.q, 0, 0),
    )
    flat = jnp.concatenate(
        [
            low(piece).reshape(-1, ADAPTER_COLUMNS)
            for piece in (
                dA_qkv,
                dA_out,
                dA_gate,
                dA_up,
                dA_hidden,
                dB_qkv,
                dB_out,
                dB_down,
                spread_columns(place, low(dB_gate), FEEDFORWARD_UNITS, dp, padded),
                spread_columns(place, low(dB_up), FEEDFORWARD_UNITS, dp, padded),
            )
        ]
    )
    flat, e_qkv, dz_qkv = together(flat, e_qkv, dz_qkv)
    total = reduce_over_cores(place, flat)
    dn1 = attention.times_transposed(e_qkv, 0, 3) + jnp.einsum(
        "tnr,tdr->nd", dz_qkv, A_model[:3], preferred_element_type=jnp.float32
    )
    dx = dm + norm_back(x, scale_one, gain_first, dn1)
    total, h = together(total, h)
    y = m + residual_branch_scale * (
        place.sum_group(matrix_product(h, down))
        + adapter_scale * matrix_product(z_down, B_model[4])
    )
    share = flat.shape[0] // (dp * shard)
    gradient = reduce_to_owner(place, total, share)
    offset = lax.axis_index(AXES) * share
    own_params = lax.dynamic_slice_in_dim(
        adapters.reshape(-1, ADAPTER_COLUMNS), offset, share
    ).astype(jnp.float32)
    first = first_moment_running.reshape(share, ADAPTER_COLUMNS)
    second = second_moment_running.reshape(share, ADAPTER_COLUMNS)
    fresh_first = first_decay_rate * first + (1.0 - first_decay_rate) * gradient
    fresh_second = second_decay_rate * second + (1.0 - second_decay_rate) * gradient * gradient
    unbiased_first = fresh_first / (1.0 - first_decay_rate**OPT_STEP)
    unbiased_second = fresh_second / (1.0 - second_decay_rate**OPT_STEP)
    update = (
        unbiased_first / (jnp.sqrt(unbiased_second) + adaptive_epsilon)
        + weight_shrink_rate * own_params
    )
    updated = gather_owners(place, low(own_params - learning_rate * update))

    inverse = (
        jnp.zeros_like(token_order).at[token_order].set(jnp.arange(count, dtype=jnp.int32))
    )
    back_out = lax.all_to_all(low(y)[inverse], "dp", split_axis=0, concat_axis=0, tiled=True)
    back_grad = lax.all_to_all(low(dx)[inverse], "dp", split_axis=0, concat_axis=0, tiled=True)
    return (
        back_out,
        back_grad,
        gradient.reshape(-1),
        fresh_first.reshape(-1),
        fresh_second.reshape(-1),
        updated,
    )


def solution(mesh):
    rows = P(AXES, None)
    weight = P("dp", None)
    return jax.shard_map(
        functools.partial(shards, mesh.shape["dp"], mesh.shape["shard"]),
        mesh=mesh,
        in_specs=(rows,) * 5 + (P(), P()) + (weight,) * 7 + (P(), P(AXES), P(AXES)),
        out_specs=(rows, rows, P(AXES), P(AXES), P(AXES), P()),
        check_vma=False,
    )
```

time: 1500 us -> 957 us (0.64)
  waiting for transfers between devices: 591 us -> 364 us
  local copies, waits for them, and re-layouts: 341 us -> 191 us
  Pallas kernels: 0 us -> 107 us
  matrix products: 233 us -> 129 us
  starting transfers between devices: 166 us -> 62.7 us
  other arithmetic: 145 us -> 78.9 us
    ppermute x77 -> x57, waiting for transfers between devices: 578 us -> 350 us  [move(): return lax.ppermute(value, AXES, pairs)]
    pallas_call x0 -> x12, Pallas kernels: none -> 107 us  [the longest x4 51.9 us: call(): pl.pallas_call(functools.partial(weights_kernel, place.line, first, count...]
    ppermute x77 -> x57, starting transfers between devices: 143 us -> 42.6 us  [move(): return lax.ppermute(value, AXES, pairs)]
    dynamic_update_slice x61 -> x9, local copies, waits for them, and re-layouts: 75.1 us -> 15.1 us  [put(): lax.dynamic_update_slice(buffer, block, tuple(where) + (0,) * (buffer.ndi...]
    dot_general x24 -> x11, matrix products: 80.7 us -> 43.5 us  [matrix_product(): return jnp.dot(left_side, right_side, preferred_element_type=jnp.float32)]
    pad x58 -> x0, local copies, waits for them, and re-layouts: 35.2 us -> none  [the longest x44 25 us: cut(): pieces.append(jnp.pad(piece, ((0, 0), (0, padded - own))))]
    slice x12 -> x9, local copies, waits for them, and re-layouts: 52.5 us -> 18.3 us  [the longest x2 6.19 us: shards(): B_model[:3]]
    dot_general x24 -> x10, matrix products: 90.7 us -> 61.1 us  [matrix_product_backward(): lax.dot_general(left_side, right_side, (((1,), (1,)), ((), ())), preferre...]
  transfers between devices with their start and end apart: 81 -> 67, of which waited for: 41 -> 25; matrix products, arithmetic and copies ran while one was open for 30% -> 23% of each run, Pallas kernels for 0% -> 8%
where the time goes in v2:
time: 957 us; the launch traced here: 949 us
  waiting for transfers between devices  364 us (38%)
  local copies, waits for them, and re-layouts  191 us (20%)
  matrix products  129 us (13%)
  Pallas kernels  107 us (11%)
  other arithmetic  78.9 us (8%)
  starting transfers between devices  62.7 us (7%)
  between operations  16.3 us (2%)
    ppermute x57, waiting for transfers between devices, move(): return lax.ppermute(value, AXES, pairs)  350 us
    dot_general x10, matrix products, matrix_product_backward(): lax.dot_general(left_side, right_side, (((1,), (1,)), ((), ())), preferre...  61.1 us
    pallas_call x4, Pallas kernels, call(): pl.pallas_call(functools.partial(weights_kernel, place.line, first, count...  51.9 us
    pallas_call x2, Pallas kernels, attention_call(): pl.pallas_call(kernel, grid=(ATTENTION_HEADS // 2,), out_shape=[jax.Shape...  45 us
    dot_general x11, matrix products, matrix_product(): return jnp.dot(left_side, right_side, preferred_element_type=jnp.float32)  43.5 us
    ppermute x57, starting transfers between devices, move(): return lax.ppermute(value, AXES, pairs)  42.6 us
    unnamed x260, local copies, waits for them, and re-layouts  37 us
    dynamic_update_slice x16, local copies, waits for them, and re-layouts, gather_owners(): full = lax.dynamic_update_slice(full, held[:, None, None], where)  22 us
  transfers between devices with their start and end apart: 67, of which 25 were waited for; matrix products, arithmetic and copies ran while one was open for 23% of the time, Pallas kernels for 8%

profile of v2, /device:TPU:0, one launch (start us, length us, event | category | flops | bytes accessed | tf_op | source)
XLA Modules:
  0.0 948.7 jit_solution(11657547178631592647)
XLA Ops:
  24.6 21.0 %collective-permute-done.1 = s32[1,8]{1,0:T(1,128)S(1)} collective-permute-done((s32[1,8]{1,0:T(1,128)S(1)}, s32[1,8]{1,0:T(1,128)S(1)}, u32[]{:S(2)}, u32[]{:S(2)}) %collective-permute-start.1) | collective-permute-done | bytes 64 | tf_op jit(solution)/shard_map/ppermute | solution.py:222
  49.4 4.1 fusion.114
  54.8 15.2 %collective-permute-done.2 = bf16[288,1536]{1,0:T(8,128)(2,1)} collective-permute-done((bf16[288,1536]{1,0:T(8,128)(2,1)S(1)}, bf16[288,1536]{1,0:T(8,128)(2,1)}, u32[]{:S(2)}, u32[]{:S(2)}) %collective-permute-start.2) | collective-permute-done | bytes 884768 | tf_op jit(solution)/shard_map/ppermute | solution.py:222
  69.9 18.6 %collective-permute-done.3 = bf16[288,1536]{1,0:T(8,128)(2,1)} collective-permute-done((bf16[288,1536]{1,0:T(8,128)(2,1)S(1)}, bf16[288,1536]{1,0:T(8,128)(2,1)}, u32[]{:S(2)}, u32[]{:S(2)}) %collective-permute-start.3) | collective-permute-done | bytes 884768 | tf_op jit(solution)/shard_map/ppermute | solution.py:222
  89.6 4.6 fusion.113
  112.7 5.3 all-to-all-start
  118.3 13.8 %all-gather.15.cloned.1.call-done = bf16[1152,1152]{1,0:T(8,128)(2,1)} async-done(((bf16[288,1152]{1,0:T(8,128)(2,1)}), bf16[1152,1152]{1,0:T(8,128)(2,1)}) %all-gather.15.cloned.1.call-update) | async-done | bytes 2654224 | tf_op jit(solution)/shard_map/all_gather | solution.py:238
  132.0 8.6 collective-permute-done.7.refs_5_.refs_3_
  140.7 12.3 %collective-permute-done.8.refs_11_.refs_9_ = bf16[3,288,1152]{2,1,0:T(8,128)(2,1)} collective-permute-done((bf16[3,288,1152]{2,1,0:T(8,128)(2,1)S(1)}, bf16[3,288,1152]{2,1,0:T(8,128)(2,1)}, u32[]{:S(2)}, u32[]{:S(2)}) %collective-permute-start.8) | collective-permute-done | bytes 1990688 | tf_op jit(solution)/shard_map/ppermute | solution.py:222
  166.8 4.0 slice.261.value
  187.7 11.0 %collective-permute-done.11.refs_9_.refs_7_ = bf16[3,288,1152]{2,1,0:T(8,128)(2,1)} collective-permute-done((bf16[3,288,1152]{2,1,0:T(8,128)(2,1)}, bf16[3,288,1152]{2,1,0:T(8,128)(2,1)}, u32[]{:S(2)}, u32[]{:S(2)}) %collective-permute-start.11) | collective-permute-done | bytes 1990688 | tf_op jit(solution)/shard_map/ppermute | solution.py:222
  204.5 5.9 all-to-all-start.1
  210.7 4.0 gather_fusion
  217.8 57.9 %collective-permute-done.20 = bf16[192,2304]{1,0:T(8,128)(2,1)} collective-permute-done((bf16[192,2304]{1,0:T(8,128)(2,1)}, bf16[192,2304]{1,0:T(8,128)(2,1)}, u32[]{:S(2)}, u32[]{:S(2)}) %collective-permute-start.20) | collective-permute-done | bytes 884768 | tf_op jit(solution)/shard_map/ppermute | solution.py:222
  290.2 17.4 %shard_map.210.lin = f32[3,256,2304]{2,1,0:T(8,128)} custom-call(s32[3]{0:T(128)} %pad_add_fusion.2.where, bf16[256,2304]{1,0:T(8,128)(2,1)} %copy-done.51, bf16[288,2304]{1,0:T(8,128)(2,1)} %refs_0_.7, bf16[288,2304]{1,0:T(8,128)(2,1)} %refs_1_.3, bf16[288,2304]{1,0:T(8,128)(2,1)} %refs_2_.3, bf16[3,288,1152]{2,1,0:T(8,128)(2,1)} %copy-done.27, ...), custom_call_target="tpu_custom_call" | custom-call | flops 8153726976 | bytes 38928384 | tf_op jit(solution)/shard_map/pallas_call | solution.py:328
  307.7 18.8 %shard_map.211 = (bf16[3,256,2304]{2,1,0:T(8,128)(2,1)}, bf16[256,2304]{1,0:T(8,128)(2,1)S(1)}) custom-call(f32[3,256,2304]{2,1,0:T(8,128)} %shard_map.210.lin, bf16[3,256,128]{2,1,0:T(8,128)(2,1)S(1)} %fusion.51.z, bf16[3,128,2304]{2,1,0:T(8,128)(2,1)S(1)} %slice.236.up, f32[256,128]{1,0:T(8,128)S(1)} %get-tuple-element.177.cosine, ...), custom_call_target="tpu_custom_call" | custom-call | flops 1207959552 | bytes 14155776 | tf_op jit(solution)/shard_map/pallas_call | solution.py:176
  333.2 5.1 gather_fusion.1
  344.2 8.8 shard_map.212
  366.0 7.0 collective-permute-done.23
  374.8 22.0 %collective-permute-done.29 = bf16[3,288,1536]{2,1,0:T(8,128)(2,1)} collective-permute-done((bf16[3,288,1536]{2,1,0:T(8,128)(2,1)}, bf16[3,288,1536]{2,1,0:T(8,128)(2,1)}, u32[]{:S(2)}, u32[]{:S(2)}) %collective-permute-start.29) | collective-permute-done | bytes 2654240 | tf_op jit(solution)/shard_map/ppermute | solution.py:222
  428.7 8.0 pad_maximum_fusion.1
  438.0 31.8 %collective-permute-done.26 = bf16[3,192,2304]{2,1,0:T(8,128)(2,1)S(1)} collective-permute-done((bf16[3,192,2304]{2,1,0:T(8,128)(2,1)}, bf16[3,192,2304]{2,1,0:T(8,128)(2,1)S(1)}, u32[]{:S(2)}, u32[]{:S(2)}) %collective-permute-start.26) | collective-permute-done | bytes 2654240 | tf_op jit(solution)/shard_map/ppermute | solution.py:222
  479.8 11.6 %multiply_add_fusion.1 = f32[1024,1536]{1,0:T(8,128)} fusion(f32[1024,1536]{1,0:T(8,128)S(1)} %fusion.117, bf16[1024,2304]{1,0:T(8,128)(2,1)S(1)} %constant_dynamic-update-slice_fusion, bf16[2304,1536]{1,0:T(8,128)(2,1)} %bitcast.49), kind=kOutput, calls=%fused_computation.13 | convolution fusion | flops 7250903040 | bytes 24379392 | tf_op jit(solution)/shard_map/dot_general | solution.py:34
  492.4 9.4 multiply_add_fusion
  501.8 19.8 %multiply_convert_fusion.2 = (bf16[1024,1536]{1,0:T(8,128)(2,1)}, bf16[1024,1536]{1,0:T(8,128)(2,1)}, bf16[1024,1536]{1,0:T(8,128)(2,1)}) fusion(f32[1024,1536]{1,0:T(8,128)} %multiply_add_fusion.1, f32[1024,1536]{1,0:T(8,128)} %multiply_add_fusion, f32[1024,1536]{1,0:T(8,128)} %fusion.116, bf16[1536,2304]{1,0:T(8,128)(2,1)} %bitcast.40, ...), kind=kOutput, calls=%fused_computation.10 | convolution fusion | flops 7271350272 | bytes 40108032 | tf_op jit(solution)/shard_map/dot_general | solution.py:38
  524.7 13.3 %fusion.119 = f32[1024,2304]{1,0:T(8,128)} fusion(bf16[1024,1536]{1,0:T(8,128)(2,1)S(1)} %copy-done.42, bf16[2304,1536]{1,0:T(8,128)(2,1)} %bitcast.365), kind=kOutput, calls=%fused_computation.323 | convolution fusion | flops 7247757312 | bytes 19660800 | tf_op jit(solution)/shard_map/dot_general | solution.py:38
  540.8 14.0 %convolution_add_fusion = f32[1024,2304]{1,0:T(8,128)} fusion(f32[1024,2304]{1,0:T(8,128)} %fusion.119, bf16[1024,1536]{1,0:T(8,128)(2,1)S(1)} %copy-done.41, bf16[2304,1536]{1,0:T(8,128)(2,1)} %bitcast.49), kind=kOutput, calls=%fused_computation.7 | convolution fusion | flops 7250116608 | bytes 29097984 | tf_op jit(solution)/shard_map/dot_general | solution.py:38
  554.8 4.5 pad_maximum_fusion
  559.3 4.1 copy-done.34
  565.2 5.4 collective-permute-done.30
  591.3 15.9 %collective-permute-done.31 = bf16[256,2688]{1,0:T(8,128)(2,1)} collective-permute-done((bf16[256,2688]{1,0:T(8,128)(2,1)}, bf16[256,2688]{1,0:T(8,128)(2,1)}, u32[]{:S(2)}, u32[]{:S(2)}) %collective-permute-start.31) | collective-permute-done | bytes 1376288 | tf_op jit(solution)/shard_map/ppermute | solution.py:222
  619.7 8.8 shard_map.215.lin
  630.2 26.2 %shard_map.216.values = bf16[3,256,2304]{2,1,0:T(8,128)(2,1)} custom-call(bf16[3,256,2304]{2,1,0:T(8,128)(2,1)} %get-tuple-element.92.qkv, f32[256,2304]{1,0:T(8,128)S(1)} %copy-done, bf16[256,128]{1,0:T(8,128)(2,1)S(1)} %fusion.58.dz, bf16[2304,128]{1,0:T(8,128)(2,1)S(1)} %copy-done.11, f32[256,128]{1,0:T(8,128)S(1)} %copy-done.19, ...), custom_call_target="tpu_custom_call" | custom-call | flops 1207959552 | bytes 14155776 | tf_op jit(solution)/shard_map/pallas_call | solution.py:176
  656.5 4.0 fusion.3
  688.3 5.3 constant_dynamic-slice_fusion
  695.1 7.7 collective-permute-done.32
  702.9 5.6 add_convert_fusion
  713.7 16.9 %shard_map.219 = f32[256,2304]{1,0:T(8,128)} custom-call(s32[3]{0:T(128)} %pad_add_fusion.2.where, bf16[3,256,2304]{2,1,0:T(8,128)(2,1)} %shard_map.216.values, bf16[288,2304]{1,0:T(8,128)(2,1)} %refs_0_.7, bf16[288,2304]{1,0:T(8,128)(2,1)} %refs_1_.3, bf16[288,2304]{1,0:T(8,128)(2,1)} %refs_2_.3, bf16[3,288,1152]{2,1,0:T(8,128)(2,1)} %copy-done.27, ...), custom_call_target="tpu_custom_call" | custom-call | flops 8153726976 | bytes 34209792 | tf_op jit(solution)/shard_map/pallas_call | solution.py:328
  733.8 8.7 collective-permute-done.35
  746.9 9.5 %fusion.123 = f32[1024,2304]{1,0:T(8,128)S(1)} fusion(bf16[1024,1536]{1,0:T(8,128)(2,1)S(1)} %copy-done.39, bf16[1536,2304]{1,0:T(8,128)(2,1)} %bitcast.40), kind=kOutput, calls=%fused_computation.327 | convolution fusion | flops 7247757312 | bytes 19660800 | tf_op jit(solution)/shard_map/dot_general | solution.py:34
  771.9 4.2 all-to-all-start.3
  776.2 34.4 %collective-permute-done.40 = bf16[1336,128]{1,0:T(8,128)(2,1)} collective-permute-done((bf16[1336,128]{1,0:T(8,128)(2,1)}, bf16[1336,128]{1,0:T(8,128)(2,1)}, u32[]{:S(2)}, u32[]{:S(2)}) %collective-permute-start.40) | collective-permute-done | bytes 342048 | tf_op jit(solution)/shard_map/ppermute | solution.py:222
  813.6 4.5 convert_add_fusion.1
  825.0 26.9 %collective-permute-done.34 = bf16[256,2304]{1,0:T(8,128)(2,1)} collective-permute-done((bf16[256,2304]{1,0:T(8,128)(2,1)}, bf16[256,2304]{1,0:T(8,128)(2,1)}, u32[]{:S(2)}, u32[]{:S(2)}) %collective-permute-start.34) | collective-permute-done | bytes 1179680 | tf_op jit(solution)/shard_map/ppermute | solution.py:222
  868.8 11.6 %collective-permute-done.44 = bf16[4,664,128]{2,1,0:T(8,128)(2,1)} collective-permute-done((bf16[4,664,128]{2,1,0:T(8,128)(2,1)S(1)}, bf16[4,664,128]{2,1,0:T(8,128)(2,1)}, u32[]{:S(2)}, u32[]{:S(2)}) %collective-permute-start.44) | collective-permute-done | bytes 679968 | tf_op jit(solution)/shard_map/ppermute | solution.py:222
  882.4 5.6 broadcast_in_dim.65
  895.1 11.6 %collective-permute-done.53 = bf16[4,672,128]{2,1,0:T(8,128)(2,1)S(1)} collective-permute-done((bf16[4,672,128]{2,1,0:T(8,128)(2,1)}, bf16[4,672,128]{2,1,0:T(8,128)(2,1)S(1)}, u32[]{:S(2)}, u32[]{:S(2)}) %collective-permute-start.53) | collective-permute-done | bytes 688160 | tf_op jit(solution)/shard_map/ppermute | solution.py:222
  906.9 13.3 %collective-permute-done.48 = bf16[4,664,128]{2,1,0:T(8,128)(2,1)} collective-permute-done((bf16[4,664,128]{2,1,0:T(8,128)(2,1)}, bf16[4,664,128]{2,1,0:T(8,128)(2,1)}, u32[]{:S(2)}, u32[]{:S(2)}) %collective-permute-start.48) | collective-permute-done | bytes 679968 | tf_op jit(solution)/shard_map/ppermute | solution.py:222
  (559 shorter events, 324.5 us)
Async XLA Ops:
  7.2 81.4 %all-gather.13.cloned.1.call-start = ((), (), s32[]{:S(2)}) async-start(), calls=%async_computation.4 | async-start | bytes 3317760 | tf_op jit(solution)/shard_map/all_gather | solution.py:238
  13.1 118.9 %all-gather.15.cloned.1.call-start = ((), (), s32[]{:S(2)}) async-start(), calls=%async_computation.5 | async-start | bytes 3317760 | tf_op jit(solution)/shard_map/all_gather | solution.py:238
  13.2 32.5 %collective-permute-start = (bf16[288,2304]{1,0:T(8,128)(2,1)}, bf16[288,2304]{1,0:T(8,128)(2,1)}, u32[]{:S(2)}, u32[]{:S(2)}) collective-permute-start(bf16[288,2304]{1,0:T(8,128)(2,1)} %fusion.41), channel_id=1, source_target_pairs={{0,4},{1,5},{2,6},{3,7},{4,0},{5,1},{6,2},{7,3},{8,12},{9,13},{10,... | collective-permute-start | bytes 3981320 | tf_op jit(solution)/shard_map/ppermute | solution.py:222
  16.3 29.4 %collective-permute-start.1 = (s32[1,8]{1,0:T(1,128)S(1)}, s32[1,8]{1,0:T(1,128)S(1)}, u32[]{:S(2)}, u32[]{:S(2)}) collective-permute-start(s32[1,8]{1,0:T(1,128)S(1)} %pad_add_fusion.1), channel_id=1, source_target_pairs={{0,4},{1,5},{2,6},{3,7},{4,0},{5,1},{6,2},{7,3},{8,12},{9,13},{10,... | collective-permute-start | bytes 104 | tf_op jit(solution)/shard_map/ppermute | solution.py:222
  16.4 259.4 %all-gather.17.cloned.1.call-start = ((), (), s32[]{:S(2)}) async-start(), calls=%async_computation.6 | async-start | bytes 4423680 | tf_op jit(solution)/shard_map/all_gather | solution.py:238
  45.7 42.9 %collective-permute-start.4 = (bf16[288,2304]{1,0:T(8,128)(2,1)}, bf16[288,2304]{1,0:T(8,128)(2,1)}, u32[]{:S(2)}, u32[]{:S(2)}) collective-permute-start(bf16[288,2304]{1,0:T(8,128)(2,1)} %collective-permute-done.refs_19_.refs_17_), channel_id=1, source_target_pairs={{0,2},{1,3},{2,0},{3,1},{4,6},{5,7},{6,4},{7,5},{8,10},{9,11},{10,... | collective-permute-start | bytes 3981320 | tf_op jit(solution)/shard_map/ppermute | solution.py:222
  47.4 41.1 %collective-permute-start.5 = (bf16[288,2304]{1,0:T(8,128)(2,1)}, bf16[288,2304]{1,0:T(8,128)(2,1)}, u32[]{:S(2)}, u32[]{:S(2)}) collective-permute-start(bf16[288,2304]{1,0:T(8,128)(2,1)} %collective-permute-done.refs_19_.refs_17_), channel_id=1, source_target_pairs={{0,1},{1,0},{2,3},{3,2},{4,5},{5,4},{6,7},{7,6},{8,9},{9,8},{10,11... | collective-permute-start | bytes 3981320 | tf_op jit(solution)/shard_map/ppermute | solution.py:222
  48.9 39.6 %collective-permute-start.3 = (bf16[288,1536]{1,0:T(8,128)(2,1)S(1)}, bf16[288,1536]{1,0:T(8,128)(2,1)}, u32[]{:S(2)}, u32[]{:S(2)}) collective-permute-start(bf16[288,1536]{1,0:T(8,128)(2,1)S(1)} %get-tuple-element.60), channel_id=1, source_target_pairs={{0,4},{1,5},{2,6},{3,7},{4,0},{5,1},{6,2},{7,3},{8,12},{9,13},{10,... | collective-permute-start | bytes 2654216 | tf_op jit(solution)/shard_map/ppermute | solution.py:222
  95.6 45.1 %collective-permute-start.7 = (bf16[3,288,1152]{2,1,0:T(8,128)(2,1)S(1)}, bf16[3,288,1152]{2,1,0:T(8,128)(2,1)}, u32[]{:S(2)}, u32[]{:S(2)}) collective-permute-start(bf16[3,288,1152]{2,1,0:T(8,128)(2,1)S(1)} %pad_maximum_fusion.7.refs_3_.refs_1_), channel_id=1, source_target_pairs={{0,2},{1,3},{2,0},{3,1},{4,6},{5,7},{6,4},{7,5},{8,10},{9,11},{10,... | collective-permute-start | bytes 5971976 | tf_op jit(solution)/shard_map/ppermute | solution.py:222
  97.1 55.9 %collective-permute-start.8 = (bf16[3,288,1152]{2,1,0:T(8,128)(2,1)S(1)}, bf16[3,288,1152]{2,1,0:T(8,128)(2,1)}, u32[]{:S(2)}, u32[]{:S(2)}) collective-permute-start(bf16[3,288,1152]{2,1,0:T(8,128)(2,1)S(1)} %pad_maximum_fusion.7.refs_3_.refs_1_), channel_id=1, source_target_pairs={{0,4},{1,5},{2,6},{3,7},{4,0},{5,1},{6,2},{7,3},{8,12},{9,13},{10,... | collective-permute-start | bytes 5971976 | tf_op jit(solution)/shard_map/ppermute | solution.py:222
  98.4 54.6 %collective-permute-start.9 = (bf16[3,288,1152]{2,1,0:T(8,128)(2,1)S(1)}, bf16[3,288,1152]{2,1,0:T(8,128)(2,1)}, u32[]{:S(2)}, u32[]{:S(2)}) collective-permute-start(bf16[3,288,1152]{2,1,0:T(8,128)(2,1)S(1)} %pad_maximum_fusion.7.refs_3_.refs_1_), channel_id=1, source_target_pairs={{0,1},{1,0},{2,3},{3,2},{4,5},{5,4},{6,7},{7,6},{8,9},{9,8},{10,11... | collective-permute-start | bytes 5971976 | tf_op jit(solution)/shard_map/ppermute | solution.py:222
  99.0 33.0 %collective-permute-start.10 = (bf16[288,2304]{1,0:T(8,128)(2,1)}, bf16[288,2304]{1,0:T(8,128)(2,1)}, u32[]{:S(2)}, u32[]{:S(2)}) collective-permute-start(bf16[288,2304]{1,0:T(8,128)(2,1)} %collective-permute-done.4.refs_21_.refs_19_), channel_id=1, source_target_pairs={{0,1},{1,0},{2,3},{3,2},{4,5},{5,4},{6,7},{7,6},{8,9},{9,8},{10,11... | collective-permute-start | bytes 3981320 | tf_op jit(solution)/shard_map/ppermute | solution.py:222
  112.7 75.0 %all-to-all-start = ((bf16[8,32,2304]{2,1,0:T(8,128)(2,1)}), bf16[8,32,2304]{2,1,0:T(8,128)(2,1)}, u32[]{:S(2)}, u32[]{:S(2)}) async-start(bf16[8,32,2304]{2,1,0:T(8,128)(2,1)} %bitcast.379), calls=%async_computation | async-start | bytes 2359296 | tf_op jit(solution)/shard_map/all_to_all | solution.py:635
  118.0 209.5 %all-gather.19.cloned.1.call-start = ((), (), s32[]{:S(2)}) async-start(), calls=%async_computation.7 | async-start | bytes 4423680 | tf_op jit(solution)/shard_map/all_gather | solution.py:238
  156.1 42.5 %collective-permute-start.11 = (bf16[3,288,1152]{2,1,0:T(8,128)(2,1)}, bf16[3,288,1152]{2,1,0:T(8,128)(2,1)}, u32[]{:S(2)}, u32[]{:S(2)}) collective-permute-start(bf16[3,288,1152]{2,1,0:T(8,128)(2,1)} %pad_maximum_fusion.8.refs_7_.refs_5_), channel_id=1, source_target_pairs={{0,2},{1,3},{2,0},{3,1},{4,6},{5,7},{6,4},{7,5},{8,10},{9,11},{10,... | collective-permute-start | bytes 5971976 | tf_op jit(solution)/shard_map/ppermute | solution.py:222
  157.3 42.8 %collective-permute-start.12 = (bf16[3,288,1152]{2,1,0:T(8,128)(2,1)}, bf16[3,288,1152]{2,1,0:T(8,128)(2,1)}, u32[]{:S(2)}, u32[]{:S(2)}) collective-permute-start(bf16[3,288,1152]{2,1,0:T(8,128)(2,1)} %pad_maximum_fusion.8.refs_7_.refs_5_), channel_id=1, source_target_pairs={{0,4},{1,5},{2,6},{3,7},{4,0},{5,1},{6,2},{7,3},{8,12},{9,13},{10,... | collective-permute-start | bytes 5971976 | tf_op jit(solution)/shard_map/ppermute | solution.py:222
  159.4 40.8 %collective-permute-start.13 = (bf16[3,288,1152]{2,1,0:T(8,128)(2,1)}, bf16[3,288,1152]{2,1,0:T(8,128)(2,1)}, u32[]{:S(2)}, u32[]{:S(2)}) collective-permute-start(bf16[3,288,1152]{2,1,0:T(8,128)(2,1)} %pad_maximum_fusion.8.refs_7_.refs_5_), channel_id=1, source_target_pairs={{0,1},{1,0},{2,3},{3,2},{4,5},{5,4},{6,7},{7,6},{8,9},{9,8},{10,11... | collective-permute-start | bytes 5971976 | tf_op jit(solution)/shard_map/ppermute | solution.py:222
  159.4 40.8 %collective-permute-start.14 = (bf16[3,288,1152]{2,1,0:T(8,128)(2,1)}, bf16[3,288,1152]{2,1,0:T(8,128)(2,1)}, u32[]{:S(2)}, u32[]{:S(2)}) collective-permute-start(bf16[3,288,1152]{2,1,0:T(8,128)(2,1)} %collective-permute-done.7.refs_5_.refs_3_), channel_id=1, source_target_pairs={{0,1},{1,0},{2,3},{3,2},{4,5},{5,4},{6,7},{7,6},{8,9},{9,8},{10,11... | collective-permute-start | bytes 5971976 | tf_op jit(solution)/shard_map/ppermute | solution.py:222
  159.9 40.3 %collective-permute-start.15 = (bf16[3,288,1152]{2,1,0:T(8,128)(2,1)}, bf16[3,288,1152]{2,1,0:T(8,128)(2,1)}, u32[]{:S(2)}, u32[]{:S(2)}) collective-permute-start(bf16[3,288,1152]{2,1,0:T(8,128)(2,1)} %collective-permute-done.8.refs_11_.refs_9_), channel_id=1, source_target_pairs={{0,1},{1,0},{2,3},{3,2},{4,5},{5,4},{6,7},{7,6},{8,9},{9,8},{10,11... | collective-permute-start | bytes 5971976 | tf_op jit(solution)/shard_map/ppermute | solution.py:222
  200.2 75.6 %collective-permute-start.17 = (bf16[3,288,1152]{2,1,0:T(8,128)(2,1)}, bf16[3,288,1152]{2,1,0:T(8,128)(2,1)}, u32[]{:S(2)}, u32[]{:S(2)}) collective-permute-start(bf16[3,288,1152]{2,1,0:T(8,128)(2,1)} %collective-permute-done.12.refs_15_.refs_13_), channel_id=1, source_target_pairs={{0,2},{1,3},{2,0},{3,1},{4,6},{5,7},{6,4},{7,5},{8,10},{9,11},{10,... | collective-permute-start | bytes 5971976 | tf_op jit(solution)/shard_map/ppermute | solution.py:222
  200.8 74.9 %collective-permute-start.19 = (bf16[3,288,1152]{2,1,0:T(8,128)(2,1)}, bf16[3,288,1152]{2,1,0:T(8,128)(2,1)}, u32[]{:S(2)}, u32[]{:S(2)}) collective-permute-start(bf16[3,288,1152]{2,1,0:T(8,128)(2,1)} %collective-permute-done.12.refs_15_.refs_13_), channel_id=1, source_target_pairs={{0,1},{1,0},{2,3},{3,2},{4,5},{5,4},{6,7},{7,6},{8,9},{9,8},{10,11... | collective-permute-start | bytes 5971976 | tf_op jit(solution)/shard_map/ppermute | solution.py:222
  200.8 74.9 %collective-permute-start.16 = (bf16[3,288,1152]{2,1,0:T(8,128)(2,1)}, bf16[3,288,1152]{2,1,0:T(8,128)(2,1)}, u32[]{:S(2)}, u32[]{:S(2)}) collective-permute-start(bf16[3,288,1152]{2,1,0:T(8,128)(2,1)} %collective-permute-done.7.refs_5_.refs_3_), channel_id=1, source_target_pairs={{0,4},{1,5},{2,6},{3,7},{4,0},{5,1},{6,2},{7,3},{8,12},{9,13},{10,... | collective-permute-start | bytes 5971976 | tf_op jit(solution)/shard_map/ppermute | solution.py:222
  202.3 73.4 %collective-permute-start.18 = (bf16[3,288,1152]{2,1,0:T(8,128)(2,1)}, bf16[3,288,1152]{2,1,0:T(8,128)(2,1)}, u32[]{:S(2)}, u32[]{:S(2)}) collective-permute-start(bf16[3,288,1152]{2,1,0:T(8,128)(2,1)} %collective-permute-done.11.refs_9_.refs_7_), channel_id=1, source_target_pairs={{0,1},{1,0},{2,3},{3,2},{4,5},{5,4},{6,7},{7,6},{8,9},{9,8},{10,11... | collective-permute-start | bytes 5971976 | tf_op jit(solution)/shard_map/ppermute | solution.py:222
  204.0 71.7 %collective-permute-start.20 = (bf16[192,2304]{1,0:T(8,128)(2,1)}, bf16[192,2304]{1,0:T(8,128)(2,1)}, u32[]{:S(2)}, u32[]{:S(2)}) collective-permute-start(bf16[192,2304]{1,0:T(8,128)(2,1)} %pad_bitcast_fusion), channel_id=1, source_target_pairs={{0,4},{1,5},{2,6},{3,7},{4,0},{5,1},{6,2},{7,3},{8,12},{9,13},{10,... | collective-permute-start | bytes 2654216 | tf_op jit(solution)/shard_map/ppermute | solution.py:222
  204.5 123.0 %all-to-all-start.1 = ((bf16[8,32,2304]{2,1,0:T(8,128)(2,1)}), bf16[8,32,2304]{2,1,0:T(8,128)(2,1)}, u32[]{:S(2)}, u32[]{:S(2)}) async-start(bf16[8,32,2304]{2,1,0:T(8,128)(2,1)} %bitcast.27), calls=%async_computation.1 | async-start | bytes 2359296 | tf_op jit(solution)/shard_map/all_to_all | solution.py:647
  210.4 192.9 %all-gather.21.cloned.1.call-start = ((), (), s32[]{:S(2)}) async-start(), calls=%async_computation.8 | async-start | bytes 4423680 | tf_op jit(solution)/shard_map/all_gather | solution.py:238
  280.0 123.3 %collective-permute-start.25 = (bf16[3,288,1536]{2,1,0:T(8,128)(2,1)}, bf16[3,288,1536]{2,1,0:T(8,128)(2,1)}, u32[]{:S(2)}, u32[]{:S(2)}) collective-permute-start(bf16[3,288,1536]{2,1,0:T(8,128)(2,1)} %pad_maximum_fusion.2), channel_id=1, source_target_pairs={{0,2},{1,3},{2,0},{3,1},{4,6},{5,7},{6,4},{7,5},{8,10},{9,11},{10,... | collective-permute-start | bytes 7962632 | tf_op jit(solution)/shard_map/ppermute | solution.py:222
  331.1 65.6 %collective-permute-start.29 = (bf16[3,288,1536]{2,1,0:T(8,128)(2,1)}, bf16[3,288,1536]{2,1,0:T(8,128)(2,1)}, u32[]{:S(2)}, u32[]{:S(2)}) collective-permute-start(bf16[3,288,1536]{2,1,0:T(8,128)(2,1)} %pad_maximum_fusion.4), channel_id=1, source_target_pairs={{0,2},{1,3},{2,0},{3,1},{4,6},{5,7},{6,4},{7,5},{8,10},{9,11},{10,... | collective-permute-start | bytes 7962632 | tf_op jit(solution)/shard_map/ppermute | solution.py:222
  342.7 30.3 %collective-permute-start.23 = (bf16[256,2432]{1,0:T(8,128)(2,1)}, bf16[256,2432]{1,0:T(8,128)(2,1)S(1)}, u32[]{:S(2)}, u32[]{:S(2)}) collective-permute-start(bf16[256,2432]{1,0:T(8,128)(2,1)} %pad_maximum_fusion.9), channel_id=1, source_target_pairs={{0,4},{1,5},{2,6},{3,7},{4,0},{5,1},{6,2},{7,3},{8,12},{9,13},{10,... | collective-permute-start | bytes 3735560 | tf_op jit(solution)/shard_map/ppermute | solution.py:222
  374.8 48.7 %collective-permute-start.24 = (bf16[512,2432]{1,0:T(8,128)(2,1)}, bf16[512,2432]{1,0:T(8,128)(2,1)}, u32[]{:S(2)}, u32[]{:S(2)}) collective-permute-start(bf16[512,2432]{1,0:T(8,128)(2,1)} %pad_maximum_fusion.5), channel_id=1, source_target_pairs={{0,1},{1,0},{2,3},{3,2},{4,5},{5,4},{6,7},{7,6},{8,9},{9,8},{10,11... | collective-permute-start | bytes 7471112 | tf_op jit(solution)/shard_map/ppermute | solution.py:222
  403.3 33.4 %collective-permute-start.27 = (bf16[256,2304]{1,0:T(8,128)(2,1)}, bf16[256,2304]{1,0:T(8,128)(2,1)S(1)}, u32[]{:S(2)}, u32[]{:S(2)}) collective-permute-start(bf16[256,2304]{1,0:T(8,128)(2,1)} %multiply_convert_fusion.4), channel_id=1, source_target_pairs={{0,4},{1,5},{2,6},{3,7},{4,0},{5,1},{6,2},{7,3},{8,12},{9,13},{10,... | collective-permute-start | bytes 3538952 | tf_op jit(solution)/shard_map/ppermute | solution.py:222
  411.1 58.6 %collective-permute-start.26 = (bf16[3,192,2304]{2,1,0:T(8,128)(2,1)}, bf16[3,192,2304]{2,1,0:T(8,128)(2,1)S(1)}, u32[]{:S(2)}, u32[]{:S(2)}) collective-permute-start(bf16[3,192,2304]{2,1,0:T(8,128)(2,1)} %pad_maximum_fusion.3), channel_id=1, source_target_pairs={{0,2},{1,3},{2,0},{3,1},{4,6},{5,7},{6,4},{7,5},{8,10},{9,11},{10,... | collective-permute-start | bytes 7962632 | tf_op jit(solution)/shard_map/ppermute | solution.py:222
  436.8 35.9 %collective-permute-start.28 = (bf16[512,2304]{1,0:T(8,128)(2,1)S(1)}, bf16[512,2304]{1,0:T(8,128)(2,1)S(1)}, u32[]{:S(2)}, u32[]{:S(2)}) collective-permute-start(bf16[512,2304]{1,0:T(8,128)(2,1)S(1)} %pad_maximum_fusion.6), channel_id=1, source_target_pairs={{0,1},{1,0},{2,3},{3,2},{4,5},{5,4},{6,7},{7,6},{8,9},{9,8},{10,11... | collective-permute-start | bytes 7077896 | tf_op jit(solution)/shard_map/ppermute | solution.py:222
  574.7 32.5 %collective-permute-start.31 = (bf16[256,2688]{1,0:T(8,128)(2,1)}, bf16[256,2688]{1,0:T(8,128)(2,1)}, u32[]{:S(2)}, u32[]{:S(2)}) collective-permute-start(bf16[256,2688]{1,0:T(8,128)(2,1)} %fusion.35), channel_id=1, source_target_pairs={{0,4},{1,5},{2,6},{3,7},{4,0},{5,1},{6,2},{7,3},{8,12},{9,13},{10,... | collective-permute-start | bytes 4128776 | tf_op jit(solution)/shard_map/ppermute | solution.py:222
  710.2 32.2 %collective-permute-start.35 = (bf16[4,2,664,128]{3,2,0,1:T(8,128)(2,1)}, bf16[4,2,664,128]{3,2,0,1:T(8,128)(2,1)}, u32[]{:S(2)}, u32[]{:S(2)}) collective-permute-start(bf16[4,2,664,128]{3,2,0,1:T(8,128)(2,1)} %dynamic-slice_bitcast_fusion.1), channel_id=1, source_target_pairs={{0,4},{1,5},{2,6},{3,7},{4,0},{5,1},{6,2},{7,3},{8,12},{9,13},{10,... | collective-permute-start | bytes 4079624 | tf_op jit(solution)/shard_map/ppermute | solution.py:222
  712.3 33.3 %collective-permute-start.37 = (bf16[4,2,672,128]{3,2,1,0:T(8,128)(2,1)}, bf16[4,2,672,128]{3,2,1,0:T(8,128)(2,1)S(1)}, u32[]{:S(2)}, u32[]{:S(2)}) collective-permute-start(bf16[4,2,672,128]{3,2,1,0:T(8,128)(2,1)} %dynamic-slice_bitcast_fusion), channel_id=1, source_target_pairs={{0,2},{1,3},{2,0},{3,1},{4,6},{5,7},{6,4},{7,5},{8,10},{9,11},{10,... | collective-permute-start | bytes 4128776 | tf_op jit(solution)/shard_map/ppermute | solution.py:222
  758.3 55.3 %collective-permute-start.33 = (bf16[2,256,2304]{2,1,0:T(8,128)(2,1)}, bf16[2,256,2304]{2,1,0:T(8,128)(2,1)}, u32[]{:S(2)}, u32[]{:S(2)}) collective-permute-start(bf16[2,256,2304]{2,1,0:T(8,128)(2,1)} %bitcast.79), channel_id=1, source_target_pairs={{0,1},{1,0},{2,3},{3,2},{4,5},{5,4},{6,7},{7,6},{8,9},{9,8},{10,11... | collective-permute-start | bytes 7077896 | tf_op jit(solution)/shard_map/ppermute | solution.py:222
  767.3 43.3 %collective-permute-start.40 = (bf16[1336,128]{1,0:T(8,128)(2,1)}, bf16[1336,128]{1,0:T(8,128)(2,1)}, u32[]{:S(2)}, u32[]{:S(2)}) collective-permute-start(bf16[1336,128]{1,0:T(8,128)(2,1)} %get-tuple-element.146), channel_id=1, source_target_pairs={{0,16},{1,17},{2,18},{3,19},{4,20},{5,21},{6,22},{7,23},{8,24},{9,... | collective-permute-start | bytes 1026056 | tf_op jit(solution)/shard_map/ppermute | solution.py:222
  767.3 43.3 %collective-permute-start.39 = (bf16[1336,128]{1,0:T(8,128)(2,1)}, bf16[1336,128]{1,0:T(8,128)(2,1)}, u32[]{:S(2)}, u32[]{:S(2)}) collective-permute-start(bf16[1336,128]{1,0:T(8,128)(2,1)} %get-tuple-element.145), channel_id=1, source_target_pairs={{0,8},{1,9},{2,10},{3,11},{4,12},{5,13},{6,14},{7,15},{8,16},{9,17... | collective-permute-start | bytes 1026056 | tf_op jit(solution)/shard_map/ppermute | solution.py:222
  771.9 52.1 %all-to-all-start.3 = ((bf16[8,32,2304]{2,1,0:T(8,128)(2,1)}), bf16[8,32,2304]{2,1,0:T(8,128)(2,1)S(1)}, u32[]{:S(2)}, u32[]{:S(2)}) async-start(bf16[8,32,2304]{2,1,0:T(8,128)(2,1)} %bitcast.85), calls=%async_computation.3 | async-start | bytes 2359296 | tf_op jit(solution)/shard_map/all_to_all | solution.py:834
  776.2 85.1 %all-gather.23.cloned.1.call-start = ((), (), s32[]{:S(2)}) async-start(), calls=%async_computation.9 | async-start | bytes 1710080 | tf_op jit(solution)/shard_map/all_gather | solution.py:238
  823.2 28.7 %collective-permute-start.34 = (bf16[256,2304]{1,0:T(8,128)(2,1)}, bf16[256,2304]{1,0:T(8,128)(2,1)}, u32[]{:S(2)}, u32[]{:S(2)}) collective-permute-start(bf16[256,2304]{1,0:T(8,128)(2,1)} %fusion.44), channel_id=1, source_target_pairs={{0,4},{1,5},{2,6},{3,7},{4,0},{5,1},{6,2},{7,3},{8,12},{9,13},{10,... | collective-permute-start | bytes 3538952 | tf_op jit(solution)/shard_map/ppermute | solution.py:222
  857.2 37.9 %all-to-all-start.2 = ((bf16[8,32,2304]{2,1,0:T(8,128)(2,1)}), bf16[8,32,2304]{2,1,0:T(8,128)(2,1)S(1)}, u32[]{:S(2)}, u32[]{:S(2)}) async-start(bf16[8,32,2304]{2,1,0:T(8,128)(2,1)} %bitcast.82), calls=%async_computation.2 | async-start | bytes 2359296 | tf_op jit(solution)/shard_map/all_to_all | solution.py:833
  863.3 28.8 %collective-permute-start.46 = (bf16[4,664,128]{2,1,0:T(8,128)(2,1)S(1)}, bf16[4,664,128]{2,1,0:T(8,128)(2,1)}, u32[]{:S(2)}, u32[]{:S(2)}) collective-permute-start(bf16[4,664,128]{2,1,0:T(8,128)(2,1)S(1)} %slice.313), channel_id=1, source_target_pairs={{0,4},{1,5},{2,6},{3,7},{4,0},{5,1},{6,2},{7,3},{8,12},{9,13},{10,... | collective-permute-start | bytes 2039816 | tf_op jit(solution)/shard_map/ppermute | solution.py:222
  868.7 38.0 %collective-permute-start.53 = (bf16[4,672,128]{2,1,0:T(8,128)(2,1)}, bf16[4,672,128]{2,1,0:T(8,128)(2,1)S(1)}, u32[]{:S(2)}, u32[]{:S(2)}) collective-permute-start(bf16[4,672,128]{2,1,0:T(8,128)(2,1)} %slice.314), channel_id=1, source_target_pairs={{0,4},{1,5},{2,6},{3,7},{4,0},{5,1},{6,2},{7,3},{8,12},{9,13},{10,... | collective-permute-start | bytes 2064392 | tf_op jit(solution)/shard_map/ppermute | solution.py:222
  880.4 39.9 %collective-permute-start.48 = (bf16[4,664,128]{2,1,0:T(8,128)(2,1)}, bf16[4,664,128]{2,1,0:T(8,128)(2,1)}, u32[]{:S(2)}, u32[]{:S(2)}) collective-permute-start(bf16[4,664,128]{2,1,0:T(8,128)(2,1)} %collective-permute-done.44), channel_id=1, source_target_pairs={{0,4},{1,5},{2,6},{3,7},{4,0},{5,1},{6,2},{7,3},{8,12},{9,13},{10,... | collective-permute-start | bytes 2039816 | tf_op jit(solution)/shard_map/ppermute | solution.py:222
  889.0 35.4 %collective-permute-start.51 = (bf16[4,672,128]{2,1,0:T(8,128)(2,1)}, bf16[4,672,128]{2,1,0:T(8,128)(2,1)}, u32[]{:S(2)}, u32[]{:S(2)}) collective-permute-start(bf16[4,672,128]{2,1,0:T(8,128)(2,1)} %slice.314), channel_id=1, source_target_pairs={{0,2},{1,3},{2,0},{3,1},{4,6},{5,7},{6,4},{7,5},{8,10},{9,11},{10,... | collective-permute-start | bytes 2064392 | tf_op jit(solution)/shard_map/ppermute | solution.py:222
  892.1 32.8 %collective-permute-start.47 = (bf16[4,664,128]{2,1,0:T(8,128)(2,1)}, bf16[4,664,128]{2,1,0:T(8,128)(2,1)}, u32[]{:S(2)}, u32[]{:S(2)}) collective-permute-start(bf16[4,664,128]{2,1,0:T(8,128)(2,1)} %collective-permute-done.46), channel_id=1, source_target_pairs={{0,1},{1,0},{2,3},{3,2},{4,5},{5,4},{6,7},{7,6},{8,9},{9,8},{10,11... | collective-permute-start | bytes 2039816 | tf_op jit(solution)/shard_map/ppermute | solution.py:222
  (146 other events, 2003.2 us)
Sparse Core Ops, SparseCore 0:
  13.2 58.0 all-gather.12
  73.5 58.5 all-gather.14
  134.2 76.1 all-gather.16
  211.8 84.5 all-gather.18
  297.8 69.0 all-gather.20
  820.5 30.7 all-gather.22

commit v3 on v2

--- a/solution.py
+++ b/solution.py
@@ -181,9 +181,9 @@
         out_specs=[spec(shape, axis) for shape, axis in outs],
         compiler_params=pltpu.CompilerParams(vmem_limit_bytes=48 << 20),
         cost_estimate=pl.CostEstimate(
-            flops=8 * count * count * MODEL_WIDTH,
-            bytes_accessed=24 * count * MODEL_WIDTH,
-            transcendentals=count * count * ATTENTION_HEADS,
+            flops=8 * count * count * MODEL_WIDTH // 16,
+            bytes_accessed=24 * count * MODEL_WIDTH // 16,
+            transcendentals=0,
         ),
     )(*[v for v, _ in operands])
 
@@ -249,13 +249,8 @@
         pair = jnp.concatenate([rows, self.by_y(rows)], axis=0)
         return jnp.concatenate([pair, self.by_c(pair)], axis=0)
 
-    def sum_group(self, partial):
-        rows = partial.shape[0] // GROUP
-        partial = partial.reshape(GROUP, rows, -1)
-        got = self.by_c(partial[2:].astype(jnp.bfloat16))
-        pair = partial[:2] + got.astype(jnp.float32)
-        got = self.by_y(pair[1].astype(jnp.bfloat16))
-        return pair[0] + got.astype(jnp.float32)
+    def half_sum(self, keep, send):
+        return (keep + self.by_c(send).astype(jnp.float32)).reshape(2, -1, keep.shape[1])
 
 
 def put(buffer, block, *where):
@@ -336,8 +331,8 @@
             ],
             compiler_params=pltpu.CompilerParams(vmem_limit_bytes=56 << 20),
             cost_estimate=pl.CostEstimate(
-                flops=2 * tokens * depth * width * count,
-                bytes_accessed=2 * depth * width * count + 4 * math.prod(shape),
+                flops=2 * tokens * depth * width * count // 16,
+                bytes_accessed=2 * depth * width * count // 16,
                 transcendentals=0,
             ),
         )(where, values, *pieces)
@@ -394,6 +389,280 @@
         return carry
 
     lax.fori_loop(0, 2 * count, step, 0)
+
+
+HIDDEN_TILE = 256
+
+
+def quarter_copies(line, z, x, pieces, target, sem):
+    planes, rest, mates = pieces
+    rows = rest.shape[0]
+
+    def copy(source, plane, side):
+        start = pl.multiple_of(rows * (2 * plane + side), 16)
+        pltpu.make_async_copy(source, target.at[pl.ds(start, rows)], sem).start()
+
+    for plane in range(line):
+        copy(planes.at[plane], plane, x)
+    copy(rest, z, 1 - x)
+    for k in range(1, line):
+        copy(mates.at[k - 1], lax.rem(z + k, line), 1 - x)
+
+
+def hidden_kernel(line, where, values, choices, down, up, planes, rest, mates, out, reduced, held, sems):
+    step = pl.program_id(0)
+    tiles = held.shape[0]
+
+    @pl.when(step == 0)
+    def _():
+        def start(tile, carry):
+            cols = pl.ds(pl.multiple_of(tile * HIDDEN_TILE, 128), HIDDEN_TILE)
+            pieces = (planes.at[:, :, cols], rest.at[:, cols], mates.at[:, :, cols])
+            quarter_copies(line, where[0], where[2], pieces, held.at[tile], sems.at[tile])
+            return carry
+
+        lax.fori_loop(0, tiles, start, 0)
+        reduced[...] = low(matrix_product(values[...], down[...]) * choices[...])
+
+    pltpu.make_async_copy(held.at[step], held.at[step], sems.at[step]).wait()
+    out[...] = matrix_product(values[...], held[step]) + adapter_scale * matrix_product(
+        reduced[...], up[...]
+    )
+
+
+def down_copies(line, where, left, right, target, sems):
+    planes, rest, mates = left
+    z, y, x = where[0], where[1], where[2]
+    rows, cut = rest.shape
+
+    def copy(source, plane, side, cols):
+        block = 2 * plane + side
+        start = pl.multiple_of(rows * block, 16)
+        pltpu.make_async_copy(source, target.at[pl.ds(start, rows), cols], sems.at[block]).start()
+
+    first, second = pl.ds(0, cut), pl.ds(cut, target.shape[1] - cut)
+    for plane in range(line):
+        copy(planes.at[plane], plane, x, first)
+        copy(right.at[plane, 0], plane, y, second)
+        copy(right.at[plane, 1], plane, 1 - y, second)
+    copy(rest, z, 1 - x, first)
+    for k in range(1, line):
+        copy(mates.at[k - 1], lax.rem(z + k, line), 1 - x, first)
+
+
+def wait_rows(target, rows, sems, block):
+    part = target.at[pl.ds(pl.multiple_of(rows * block, 16), rows)]
+    pltpu.make_async_copy(part, part, sems.at[block]).wait()
+
+
+def feed_forward_back_kernel(line, where, gt, up, sent, down_lower, upper_gate, upper_up, *refs):
+    left, right, gate_pieces, up_pieces = refs[:3], refs[3], refs[4:7], refs[7:10]
+    hidden, e_gate, e_up, keep, send, total, down, held, down_sems, sems = refs[10:]
+    step = pl.program_id(0)
+    tiles, rows = held.shape[1], left[1].shape[0]
+    blocks, width = 2 * line, down.shape[1]
+
+    @pl.when(step == 0)
+    def _():
+        down_copies(line, where, left, right, down, down_sems)
+
+        def start(tile, carry):
+            cols = pl.ds(pl.multiple_of(tile * HIDDEN_TILE, 128), HIDDEN_TILE)
+            for t, (planes, rest, mates) in enumerate((gate_pieces, up_pieces)):
+                pieces = (planes.at[:, :, cols], rest.at[:, cols], mates.at[:, :, cols])
+                quarter_copies(line, where[0], where[2], pieces, held.at[t, tile], sems.at[t, tile])
+            return carry
+
+        lax.fori_loop(0, tiles, start, 0)
+        keep[...] = jnp.zeros_like(keep)
+        total[...] = jnp.zeros_like(total)
+
+    seen = 0
+    for tile in range(tiles):
+        until = -(-(tile + 1) * HIDDEN_TILE // rows)
+
+        @pl.when(step == tile)
+        def _(seen=seen, until=until):
+            for block in range(seen, until):
+                wait_rows(down, rows, down_sems, block)
+
+        seen = until
+    for t in range(2):
+        pltpu.make_async_copy(held.at[t, step], held.at[t, step], sems.at[t, step]).wait()
+
+    tile_rows = down[pl.ds(pl.multiple_of(step * HIDDEN_TILE, HIDDEN_TILE), HIDDEN_TILE), :]
+    count = keep.shape[0]
+    for n, sums in enumerate((keep, total)):
+        own = slice(n * count, (n + 1) * count)
+        gate_value, up_value = gt[own, :], up[own, :]
+        dh = matrix_product_backward(sent[own, :width], tile_rows) + matrix_product_backward(
+            sent[own, width:], down_lower[...]
+        )
+        sg = jax.nn.sigmoid(gate_value)
+        act = gate_value * sg
+        h = low(act * up_value)
+        grad_gate = low(dh * up_value * (sg + gate_value * sg * (1.0 - sg)))
+        grad_up = low(dh * act)
+        hidden[own, :], e_gate[own, :], e_up[own, :] = h, grad_gate, grad_up
+        sums[:, :width] += matrix_product_backward(
+            grad_gate, held[0, step]
+        ) + matrix_product_backward(grad_up, held[1, step])
+        lanes = [width + k * ADAPTER_COLUMNS for k in range(4)]
+        sums[:, lanes[0] : lanes[1]] += matrix_product_backward(grad_gate, upper_gate[...])
+        sums[:, lanes[1] : lanes[2]] += matrix_product_backward(grad_up, upper_up[...])
+        sums[:, lanes[2] : lanes[3]] += matrix_product(h, down_lower[...])
+
+    @pl.when(step == tiles - 1)
+    def _():
+        send[...] = low(total[...])
+
+
+def feed_forward_out_kernel(line, where, hidden, *refs):
+    left, right = refs[:3], refs[3]
+    keep, send, down, down_sems = refs[4:]
+    rows = left[1].shape[0]
+    down_copies(line, where, left, right, down, down_sems)
+    for block in range(2 * line):
+        wait_rows(down, rows, down_sems, block)
+    count = keep.shape[0]
+    keep[...] = matrix_product(hidden[:count, :], down[...])
+    send[...] = low(matrix_product(hidden[count:, :], down[...]))
+
+
+def small_cost(flops):
+    return pl.CostEstimate(flops=flops // 16, bytes_accessed=flops // 8192, transcendentals=0)
+
+
+class FeedForward:
+    def __init__(self, place, left, right):
+        self.place, self.left, self.right = place, left, right
+        self.cut = left[1].shape[1]
+        self.padded = left[1].shape[0]
+        self.kernels = self.padded % 64 == 0
+        self.where = jnp.stack([place.z, place.y, place.x]).astype(jnp.int32)
+
+    def down(self):
+        right = jnp.where(self.place.y == 0, self.right, self.right[:, ::-1])
+        right = right.reshape(-1, right.shape[-1])
+        return jnp.concatenate([put_quarter(self.place, *self.left), right], axis=1)
+
+    def hidden(self, values, choices, lower, upper, pieces):
+        count, width = values.shape[0], upper.shape[1]
+        if not self.kernels:
+            reduced = low(matrix_product(values, lower) * choices)
+            full = put_quarter(self.place, *pieces)
+            return matrix_product(values, full) + adapter_scale * matrix_product(
+                reduced, upper
+            ), reduced
+        tiles = width // HIDDEN_TILE
+        once = lambda v: pl.BlockSpec(v.shape, lambda i: (0, 0), pipeline_mode=pl.Buffered(1))
+        columns = lambda n: pl.BlockSpec((n, HIDDEN_TILE), lambda i: (0, i))
+        return pl.pallas_call(
+            functools.partial(hidden_kernel, self.place.line),
+            grid=(tiles,),
+            out_shape=[
+                jax.ShapeDtypeStruct((count, width), jnp.float32),
+                jax.ShapeDtypeStruct((count, ADAPTER_COLUMNS), jnp.bfloat16),
+            ],
+            in_specs=[pl.BlockSpec(memory_space=pltpu.SMEM)]
+            + [once(v) for v in (values, choices, lower)]
+            + [columns(upper.shape[0])]
+            + [pl.BlockSpec(memory_space=pl.ANY)] * 3,
+            out_specs=[
+                columns(count),
+                pl.BlockSpec((count, ADAPTER_COLUMNS), lambda i: (0, 0)),
+            ],
+            scratch_shapes=[
+                pltpu.VMEM((tiles, values.shape[1], HIDDEN_TILE), jnp.bfloat16),
+                pltpu.SemaphoreType.DMA((tiles,)),
+            ],
+            compiler_params=pltpu.CompilerParams(vmem_limit_bytes=40 << 20),
+            cost_estimate=small_cost(2 * count * width * values.shape[1]),
+        )(self.where, values, choices, lower, upper, *pieces)
+
+    def back(self, gt, up, sent, lower, upper_gate, upper_up, gate_pieces, up_pieces):
+        count, width = gt.shape
+        half = count // 2
+        model = sent.shape[1] - ADAPTER_COLUMNS
+        sums = model + 3 * ADAPTER_COLUMNS
+        if not self.kernels:
+            down = self.down()
+            gate, up_part = put_quarter(self.place, *gate_pieces), put_quarter(self.place, *up_pieces)
+            sg = jax.nn.sigmoid(gt)
+            act = gt * sg
+            h = low(act * up)
+            dh = matrix_product_backward(sent[:, :model], down) + matrix_product_backward(
+                sent[:, model:], lower
+            )
+            e_gate = low(dh * up * (sg + gt * sg * (1.0 - sg)))
+            e_up = low(dh * act)
+            total = jnp.concatenate(
+                [
+                    matrix_product_backward(e_gate, gate) + matrix_product_backward(e_up, up_part),
+                    matrix_product_backward(e_gate, upper_gate),
+                    matrix_product_backward(e_up, upper_up),
+                    matrix_product(h, lower),
+                ],
+                axis=1,
+            )
+            return h, e_gate, e_up, total[:half], low(total[half:])
+        tiles = width // HIDDEN_TILE
+        once = lambda shape: pl.BlockSpec(shape, lambda i: (0, 0), pipeline_mode=pl.Buffered(1))
+        columns = lambda n: pl.BlockSpec((n, HIDDEN_TILE), lambda i: (0, i))
+        pieces = (*self.left, self.right, *gate_pieces, *up_pieces)
+        return pl.pallas_call(
+            functools.partial(feed_forward_back_kernel, self.place.line),
+            grid=(tiles,),
+            out_shape=[jax.ShapeDtypeStruct((count, width), jnp.bfloat16)] * 3
+            + [
+                jax.ShapeDtypeStruct((half, sums), jnp.float32),
+                jax.ShapeDtypeStruct((half, sums), jnp.bfloat16),
+            ],
+            in_specs=[
+                pl.BlockSpec(memory_space=pltpu.SMEM),
+                columns(count),
+                columns(count),
+                once(sent.shape),
+                pl.BlockSpec((HIDDEN_TILE, ADAPTER_COLUMNS), lambda i: (i, 0)),
+                columns(ADAPTER_COLUMNS),
+                columns(ADAPTER_COLUMNS),
+            ]
+            + [pl.BlockSpec(memory_space=pl.ANY)] * len(pieces),
+            out_specs=[columns(count)] * 3 + [once((half, sums))] * 2,
+            scratch_shapes=[
+                pltpu.VMEM((half, sums), jnp.float32),
+                pltpu.VMEM((width, model), jnp.bfloat16),
+                pltpu.VMEM((2, tiles, model, HIDDEN_TILE), jnp.bfloat16),
+                pltpu.SemaphoreType.DMA((2 * self.place.line,)),
+                pltpu.SemaphoreType.DMA((2, tiles)),
+            ],
+            compiler_params=pltpu.CompilerParams(vmem_limit_bytes=60 << 20),
+            cost_estimate=small_cost(6 * count * width * model),
+        )(self.where, gt, up, sent, lower, upper_gate, upper_up, *pieces)
+
+    def out(self, h, model):
+        count, width = h.shape
+        half = count // 2
+        if not self.kernels:
+            total = matrix_product(h, self.down())
+            return total[:half], low(total[half:])
+        held = pl.BlockSpec(memory_space=pltpu.VMEM)
+        return pl.pallas_call(
+            functools.partial(feed_forward_out_kernel, self.place.line),
+            out_shape=[
+                jax.ShapeDtypeStruct((half, model), jnp.float32),
+                jax.ShapeDtypeStruct((half, model), jnp.bfloat16),
+            ],
+            in_specs=[pl.BlockSpec(memory_space=pltpu.SMEM), held]
+            + [pl.BlockSpec(memory_space=pl.ANY)] * 4,
+            out_specs=[held] * 2,
+            scratch_shapes=[
+                pltpu.VMEM((width, model), jnp.bfloat16),
+                pltpu.SemaphoreType.DMA((2 * self.place.line,)),
+            ],
+            compiler_params=pltpu.CompilerParams(vmem_limit_bytes=40 << 20),
+            cost_estimate=small_cost(2 * count * width * model),
+        )(self.where, h, *self.left, self.right)
 
 
 def columns_kernel(own, padded, quarter, value, *outs):
@@ -525,25 +794,39 @@
     return both(keep, place.by_c(send))
 
 
-def reduce_to_owner(place, total, share):
-    half = total.shape[3]
-    cut = half // 16 * 8
-    one, two = total[:, :, :, :cut], total[:, :, :, cut:]
-    got_one = place.by_y(pick(one, 1 - place.y, 1))
-    got_two = place.by_x(pick(two, 1 - place.x, 2))
-    one, two = both(pick(one, place.y, 1), got_one), both(pick(two, place.x, 2), got_two)
-    got_one = place.by_x(pick(one, 1 - place.x, 1))
-    got_two = place.by_y(pick(two, 1 - place.y, 1))
-    one, two = both(pick(one, place.x, 1), got_one), both(pick(two, place.y, 1), got_two)
-    total = jnp.concatenate([one, two], axis=1)
-    result = pick(total, place.z, 0).astype(jnp.float32)
-    for k in range(1, place.line):
-        send = pick(total, (place.z + k) % place.line, 0)
-        result = result + place.ring_z(send, k).astype(jnp.float32)
-    return lax.dynamic_slice_in_dim(result, place.c * (half - share), share, 0)
-
-
-def gather_owners(place, own):
+class OwnerSum:
+    def __init__(self, place, total, share):
+        self.place, self.share, self.half = place, share, total.shape[3]
+        cut = self.half // 16 * 8
+        one, two = total[:, :, :, :cut], total[:, :, :, cut:]
+        self.kept = (pick(one, place.y, 1), pick(two, place.x, 2))
+        self.got = (
+            place.by_y(pick(one, 1 - place.y, 1)),
+            place.by_x(pick(two, 1 - place.x, 2)),
+        )
+
+    def over_chips(self):
+        place = self.place
+        one, two = both(self.kept[0], self.got[0]), both(self.kept[1], self.got[1])
+        got_one = place.by_x(pick(one, 1 - place.x, 1))
+        got_two = place.by_y(pick(two, 1 - place.y, 1))
+        one, two = both(pick(one, place.x, 1), got_one), both(pick(two, place.y, 1), got_two)
+        return jnp.concatenate([one, two], axis=1)
+
+    def over_planes(self, total):
+        place = self.place
+        got = [
+            place.ring_z(pick(total, (place.z + k) % place.line, 0), k)
+            for k in range(1, place.line)
+        ]
+        result = pick(total, place.z, 0).astype(jnp.float32)
+        for value in got:
+            result = result + value.astype(jnp.float32)
+        start = place.c * (self.half - self.share)
+        return lax.dynamic_slice_in_dim(result, start, self.share, 0)
+
+
+def gather_owners(place, own, event):
     share = own.shape[0]
     half = -(-share // 8) * 8
     start = 2 * share - half
@@ -551,6 +834,7 @@
     head, tail = jnp.where(place.c == 0, own, mate), jnp.where(place.c == 0, mate, own)
     pair = jnp.concatenate([head, tail], axis=0)
     planes = place.all_z(lax.dynamic_slice_in_dim(pair, place.c * start, half, 0))
+    planes, event = together(planes, event)
     cut = half // 16 * 8
     full = jnp.zeros(
         (place.line, 2, place.shard // 2, 2 * share, ADAPTER_COLUMNS), own.dtype
@@ -567,7 +851,7 @@
             for held, c in ((value, place.c), (place.by_c(value), 1 - place.c)):
                 where = (0, y, x, c * start + at, 0)
                 full = lax.dynamic_update_slice(full, held[:, None, None], where)
-    return full.reshape(-1)
+    return full.reshape(-1), event
 
 
 def shards(
@@ -599,6 +883,7 @@
 
     weights = (w_query, w_key, w_value, w_out)
     s, half = place.x * 2 + place.c, MODEL_WIDTH // 2
+    cut = MODEL_WIDTH - MODEL_WIDTH * 2 // 9
     stacked = jnp.stack(weights)
     mine = lax.dynamic_index_in_dim(stacked, s, 0, keepdims=False)
     first = place.all_z(mine[:, :half])
@@ -633,26 +918,31 @@
     x0, y0, lines_c = place.by_x(lines), place.by_y(lines), place.by_c(lines)
     near_x_c = place.by_c(near_x)
     arrived_x = lax.all_to_all(tokens, "dp", split_axis=0, concat_axis=0, tiled=True)
-    x0, y0, lines_c, near_x_c, second, cotangent = together(
-        x0, y0, lines_c, near_x_c, second, cotangent
-    )
+    x0, y0, lines_c, near_x_c, second = together(x0, y0, lines_c, near_x_c, second)
 
     lines2 = place.other_z(second)
     x1, y1, lines2_c = place.by_x(lines2), place.by_y(lines2), place.by_c(lines2)
     x0_c, y0_c = place.by_c(x0), place.by_c(y0)
-    x1, y1, lines2_c, x0_c, y0_c, x0, other_down, arrived_x, cotangent = together(
-        x1, y1, lines2_c, x0_c, y0_c, x0, other_down, arrived_x, cotangent
-    )
-
+    x1, y1, lines2_c, x0_c, y0_c, x0, arrived_x = together(
+        x1, y1, lines2_c, x0_c, y0_c, x0, arrived_x
+    )
+
+    A_model, A_hidden, B_model, B_hidden = restore_structure(adapters)
+    B_gate, _ = hidden_columns(place, B_hidden[0], dp, padded)
+    B_up, _ = hidden_columns(place, B_hidden[1], dp, padded)
+    A_down = hidden_rows(place, A_hidden, place.q, dp, padded)
+    choice, allowed, cosine_table, sine_table = block_tables(lengths[0], adapter_set[0])
+    choices = jnp.concatenate(
+        [block_tables(tables[k, :SEQ_DEV], tables[k, SEQ_DEV:])[0] for k in range(GROUP)], axis=0
+    )
+    xy0, xy1 = place.by_y(x0), place.by_x(y1)
+    x1_c, y1_c = place.by_c(x1), place.by_c(y1)
+    xy0, xy1, x1_c, y1_c, B_gate, B_up, A_down, choices, gate_planes, other_down, cotangent = together(
+        xy0, xy1, x1_c, y1_c, B_gate, B_up, A_down, choices, gate_planes, other_down, cotangent
+    )
+
+    got_down = place.by_y(other_down)
     arrived_cot = lax.all_to_all(cotangent, "dp", split_axis=0, concat_axis=0, tiled=True)
-    xy0, xy1, got_down = place.by_y(x0), place.by_x(y1), place.by_y(other_down)
-    x1_c, y1_c = place.by_c(x1), place.by_c(y1)
-    xy0, xy1, x1_c, y1_c, gate_planes, got_down = together(
-        xy0, xy1, x1_c, y1_c, gate_planes, got_down
-    )
-
-    down_planes = place.all_z(jnp.where(straight, own_down, got_down))
-    down_rest = jnp.where(straight, got_down, own_down)
     gate_mates = place.by_x(place.other_z(gate_planes))
     attention = AttentionWeights(
         place,
@@ -661,11 +951,6 @@
         ((y0, y0_c, xy0, place.by_c(xy0)), (y1, y1_c, xy1, place.by_c(xy1))),
         (near_y, near_y_c, near_x, near_x_c),
     )
-    A_model, A_hidden, B_model, B_hidden = restore_structure(adapters)
-    choice, allowed, cosine_table, sine_table = block_tables(lengths[0], adapter_set[0])
-    choices = jnp.concatenate(
-        [block_tables(tables[k, :SEQ_DEV], tables[k, SEQ_DEV:])[0] for k in range(GROUP)], axis=0
-    )
     gain_first = gain_one.astype(jnp.float32)
     gain_second = gain_two.astype(jnp.float32)
 
@@ -677,10 +962,14 @@
         jnp.einsum("nd,tdr->tnr", n1, A_model[:3], preferred_element_type=jnp.float32) * choice
     )
     bias = jnp.where(allowed, 0.0, -jnp.inf)
+    lin, got_down = together(attention.times(n1, 0, 3), got_down)
+    left_planes = place.all_z(jnp.where(straight, own_down, got_down)[:, :cut])
+    left_rest = jnp.where(straight, got_down, own_down)[:, :cut]
+    right_planes = place.all_z(jnp.stack([own_down[:, cut:], got_down[:, cut:]]))
     qkv, o = attention_call(
         attention_kernel,
         (
-            (attention.times(n1, 0, 3), 2),
+            (lin, 2),
             (z_qkv, None),
             (B_model[:3], 2),
             (cosine_table, None),
@@ -689,51 +978,46 @@
         ),
         (((3, count, MODEL_WIDTH), 2), ((count, MODEL_WIDTH), 1)),
     )
-    o, up_planes, arrived_cot = together(o, up_planes, arrived_cot)
+    o, up_planes, gate_mates = together(o, up_planes, gate_mates)
     up_mates = place.by_x(place.other_z(up_planes))
     z_out, delta_out = apply_adapter_delta(o, A_model[3], B_model[3], choice)
     m = x + residual_branch_scale * (attention.times(o, 3, 1)[0] + delta_out)
     scale_two = rms_scale(m)
     n2 = low(m * scale_two * gain_second)
 
+    n2_y = place.by_y(n2)
+    n2_y, arrived_cot, left_planes, up_mates = together(
+        n2_y, arrived_cot, left_planes, up_mates
+    )
+    left_mates = place.by_x(place.other_z(left_planes))
     g = arrived_cot[token_order].astype(jnp.float32)
     e_down = low(residual_branch_scale * g)
     dz_down = low(adapter_scale * matrix_product_backward(e_down, B_model[4]) * choice)
     sent = jnp.concatenate([e_down, dz_down], axis=1)
-    sent_pair = jnp.concatenate([sent, place.by_y(sent)], axis=0)
-    gate_mates, down_planes, n2 = together(gate_mates, down_planes, n2)
-    down_mates = place.by_x(place.other_z(down_planes))
-    n2_all = place.gather_group(n2)
-    sent = jnp.concatenate([sent_pair, place.by_c(sent_pair)], axis=0)
-    gate = put_quarter(place, gate_planes, gate_rest, gate_mates)
-    up_part = put_quarter(place, up_planes, up_rest, up_mates)
-    down = put_quarter(place, down_planes, down_rest, down_mates)
-    e_down_all, dz_down_all = sent[:, :MODEL_WIDTH], sent[:, MODEL_WIDTH:]
-    B_gate, _ = hidden_columns(place, B_hidden[0], dp, padded)
-    B_up, _ = hidden_columns(place, B_hidden[1], dp, padded)
-    A_down = hidden_rows(place, A_hidden, place.q, dp, padded)
-    z_gate = low(matrix_product(n2_all, A_model[4]) * choices)
-    z_up = low(matrix_product(n2_all, A_model[5]) * choices)
-    gt = matrix_product(n2_all, gate) + adapter_scale * matrix_product(z_gate, B_gate)
-    up = matrix_product(n2_all, up_part) + adapter_scale * matrix_product(z_up, B_up)
-    sg = jax.nn.sigmoid(gt)
-    act = gt * sg
-    h = low(act * up)
-    dh = matrix_product_backward(e_down_all, down) + matrix_product_backward(dz_down_all, A_down)
-    e_gate = low(dh * up * (sg + gt * sg * (1.0 - sg)))
-    e_up = low(dh * act)
-    back_sum = place.sum_group(
-        jnp.concatenate(
-            [
-                matrix_product_backward(e_gate, gate)
-                + matrix_product_backward(e_up, up_part),
-                matrix_product_backward(e_gate, B_gate),
-                matrix_product_backward(e_up, B_up),
-                matrix_product(h, A_down),
-            ],
-            axis=1,
-        )
-    )
+    sent_y = place.by_y(sent)
+    n2_all = jnp.concatenate([n2, n2_y], axis=0)
+    n2_all = jnp.concatenate([n2_all, place.by_c(n2_all)], axis=0)
+    gate_pieces = (gate_planes, gate_rest, gate_mates)
+    forward = FeedForward(place, (left_planes, left_rest, left_mates), right_planes)
+    gt, z_gate = forward.hidden(n2_all, choices, A_model[4], B_gate, gate_pieces)
+    up_pieces = (up_planes, up_rest, up_mates)
+    up, z_up = forward.hidden(n2_all, choices, A_model[5], B_up, up_pieces)
+    gt, up, left_mates, right_planes, sent_y = together(gt, up, left_mates, right_planes, sent_y)
+    sent = jnp.concatenate([sent, sent_y], axis=0)
+    sent = jnp.concatenate([sent, place.by_c(sent)], axis=0)
+    dz_down_all = sent[:, MODEL_WIDTH:]
+    feed = FeedForward(place, (left_planes, left_rest, left_mates), right_planes)
+    h, e_gate, e_up, keep, send = feed.back(
+        gt, up, sent, A_down, B_gate, B_up, gate_pieces, up_pieces
+    )
+    own_sum, other_sum = place.half_sum(keep, send)
+    other_sum, h = together(low(other_sum), h)
+    got = place.by_y(other_sum)
+    y_keep, y_send = feed.out(h, MODEL_WIDTH)
+    got, y_send = together(got, y_send)
+    back_sum = own_sum + got.astype(jnp.float32)
+    y_own, y_other = place.half_sum(y_keep, y_send)
+    y_got = place.by_y(low(y_other))
     cuts = [MODEL_WIDTH + k * ADAPTER_COLUMNS for k in range(3)]
     dz_gate, dz_up, z_down = jnp.split(back_sum, cuts, axis=1)[1:]
     dz_gate, dz_up = low(adapter_scale * dz_gate * choice), low(adapter_scale * dz_up * choice)
@@ -766,6 +1050,13 @@
         (((3, count, MODEL_WIDTH), 2),),
     )
     dA_out, dB_out = outer_product_sum(o, dz_out), adapter_scale * outer_product_sum(z_out, e_out)
+    e_qkv, y_got = together(e_qkv, y_got)
+    y = m + residual_branch_scale * (
+        y_own + y_got.astype(jnp.float32) + adapter_scale * matrix_product(z_down, B_model[4])
+    )
+    inverse = (
+        jnp.zeros_like(token_order).at[token_order].set(jnp.arange(count, dtype=jnp.int32))
+    )
     dz_qkv = low(
         adapter_scale
         * jnp.einsum("tnd,trd->tnr", e_qkv, B_model[:3], preferred_element_type=jnp.float32)
@@ -798,19 +1089,16 @@
             )
         ]
     )
-    flat, e_qkv, dz_qkv = together(flat, e_qkv, dz_qkv)
-    total = reduce_over_cores(place, flat)
+    share = flat.shape[0] // (dp * shard)
+    total, e_qkv, dz_qkv, y = together(reduce_over_cores(place, flat), e_qkv, dz_qkv, y)
+    owner = OwnerSum(place, total, share)
+    back_out = lax.all_to_all(low(y)[inverse], "dp", split_axis=0, concat_axis=0, tiled=True)
     dn1 = attention.times_transposed(e_qkv, 0, 3) + jnp.einsum(
         "tnr,tdr->nd", dz_qkv, A_model[:3], preferred_element_type=jnp.float32
     )
     dx = dm + norm_back(x, scale_one, gain_first, dn1)
-    total, h = together(total, h)
-    y = m + residual_branch_scale * (
-        place.sum_group(matrix_product(h, down))
-        + adapter_scale * matrix_product(z_down, B_model[4])
-    )
-    share = flat.shape[0] // (dp * shard)
-    gradient = reduce_to_owner(place, total, share)
+    owner.got, back_out = together(owner.got, back_out)
+    gradient = owner.over_planes(owner.over_chips())
     offset = lax.axis_index(AXES) * share
     own_params = lax.dynamic_slice_in_dim(
         adapters.reshape(-1, ADAPTER_COLUMNS), offset, share
@@ -825,13 +1113,9 @@
         unbiased_first / (jnp.sqrt(unbiased_second) + adaptive_epsilon)
         + weight_shrink_rate * own_params
     )
-    updated = gather_owners(place, low(own_params - learning_rate * update))
-
-    inverse = (
-        jnp.zeros_like(token_order).at[token_order].set(jnp.arange(count, dtype=jnp.int32))
-    )
-    back_out = lax.all_to_all(low(y)[inverse], "dp", split_axis=0, concat_axis=0, tiled=True)
+    updated, dx = gather_owners(place, low(own_params - learning_rate * update), dx)
     back_grad = lax.all_to_all(low(dx)[inverse], "dp", split_axis=0, concat_axis=0, tiled=True)
+
     return (
         back_out,
         back_grad,

time: 957 us -> 906 us (0.947)
  Pallas kernels: 107 us -> 194 us
  matrix products: 129 us -> 43.3 us
  waiting for transfers between devices: 364 us -> 326 us
  local copies, waits for them, and re-layouts: 191 us -> 169 us
    pallas_call x0 -> x4, Pallas kernels: none -> 86.4 us  [the longest x1 47.1 us: back(): pl.pallas_call(functools.partial(feed_forward_back_kernel, self.place.lin...]
    ppermute x57, waiting for transfers between devices: 350 us -> 294 us  [move(): return lax.ppermute(value, AXES, pairs)]
    dot_general x10 -> x4, matrix products: 61.1 us -> 8.41 us  [matrix_product_backward(): lax.dot_general(left_side, right_side, (((1,), (1,)), ((), ())), preferre...]
    dot_general x11 -> x3, matrix products: 43.5 us -> 4.87 us  [matrix_product(): return jnp.dot(left_side, right_side, preferred_element_type=jnp.float32)]
    dynamic_update_slice x12 -> x0, local copies, waits for them, and re-layouts: 19.6 us -> none  [the longest x9 15.1 us: put(): lax.dynamic_update_slice(buffer, block, tuple(where) + (0,) * (buffer.ndi...]
    all_gather x6 -> x7, waiting for transfers between devices: 13.8 us -> 28.8 us  [all_z(): return lax.all_gather(block, 'dp', axis=0, axis_index_groups=groups)]
    unnamed x260 -> x218, local copies, waits for them, and re-layouts: 37 us -> 38.3 us
  transfers between devices with their start and end apart: 67 -> 68, of which waited for: 25 -> 29; matrix products, arithmetic and copies ran while one was open for 23% -> 21% of each run, Pallas kernels for 8% -> 16%
where the time goes in v3:
time: 906 us; the launch traced here: 897 us
  waiting for transfers between devices  326 us (36%)
  Pallas kernels  194 us (21%)
  local copies, waits for them, and re-layouts  169 us (19%)
  other arithmetic  81.7 us (9%)
  starting transfers between devices  66.4 us (7%)
  matrix products  43.3 us (5%)
  between operations  16.1 us (2%)
    ppermute x57, waiting for transfers between devices, move(): return lax.ppermute(value, AXES, pairs)  294 us
    pallas_call x4, Pallas kernels, call(): pl.pallas_call(functools.partial(weights_kernel, place.line, first, count...  52.2 us
    pallas_call x1, Pallas kernels, back(): pl.pallas_call(functools.partial(feed_forward_back_kernel, self.place.lin...  47.1 us
    ppermute x57, starting transfers between devices, move(): return lax.ppermute(value, AXES, pairs)  46.8 us
    pallas_call x2, Pallas kernels, attention_call(): pl.pallas_call(kernel, grid=(ATTENTION_HEADS // 2,), out_shape=[jax.Shape...  45.1 us
    unnamed x218, local copies, waits for them, and re-layouts  38.3 us
    all_gather x7, waiting for transfers between devices, all_z(): return lax.all_gather(block, 'dp', axis=0, axis_index_groups=groups)  28.8 us
    pallas_call x2, Pallas kernels, hidden(): pl.pallas_call(functools.partial(hidden_kernel, self.place.line), grid=(t...  26.4 us
  transfers between devices with their start and end apart: 68, of which 29 were waited for; matrix products, arithmetic and copies ran while one was open for 21% of the time, Pallas kernels for 16%

profile of v3, /device:TPU:0, one launch (start us, length us, event | category | flops | bytes accessed | tf_op | source)
XLA Modules:
  0.0 897.0 jit_solution(10202356562783525023)
XLA Ops:
  20.2 24.2 %collective-permute-done.1 = s32[1,8]{1,0:T(1,128)S(1)} collective-permute-done((s32[1,8]{1,0:T(1,128)S(1)}, s32[1,8]{1,0:T(1,128)S(1)}, u32[]{:S(2)}, u32[]{:S(2)}) %collective-permute-start.1) | collective-permute-done | bytes 64 | tf_op jit(solution)/shard_map/ppermute | solution.py:222
  48.1 4.1 fusion.86
  53.4 15.4 %collective-permute-done.2 = bf16[288,1536]{1,0:T(8,128)(2,1)} collective-permute-done((bf16[288,1536]{1,0:T(8,128)(2,1)}, bf16[288,1536]{1,0:T(8,128)(2,1)}, u32[]{:S(2)}, u32[]{:S(2)}) %collective-permute-start.2) | collective-permute-done | bytes 884768 | tf_op jit(solution)/shard_map/ppermute | solution.py:222
  68.8 18.6 %collective-permute-done.3 = bf16[288,1536]{1,0:T(8,128)(2,1)} collective-permute-done((bf16[288,1536]{1,0:T(8,128)(2,1)S(1)}, bf16[288,1536]{1,0:T(8,128)(2,1)}, u32[]{:S(2)}, u32[]{:S(2)}) %collective-permute-start.3) | collective-permute-done | bytes 884768 | tf_op jit(solution)/shard_map/ppermute | solution.py:222
  96.2 4.5 fusion.87
  111.4 4.9 all-to-all-start
  116.4 14.8 %all-gather.17.cloned.1.call-done = bf16[1152,1152]{1,0:T(8,128)(2,1)} async-done(((bf16[288,1152]{1,0:T(8,128)(2,1)}), bf16[1152,1152]{1,0:T(8,128)(2,1)}) %all-gather.17.cloned.1.call-update) | async-done | bytes 2654224 | tf_op jit(solution)/shard_map/all_gather | solution.py:238
  131.2 5.2 collective-permute-done.7.refs_5_.refs_3_
  136.4 11.1 %collective-permute-done.8.refs_11_.refs_9_ = bf16[3,288,1152]{2,1,0:T(8,128)(2,1)} collective-permute-done((bf16[3,288,1152]{2,1,0:T(8,128)(2,1)}, bf16[3,288,1152]{2,1,0:T(8,128)(2,1)}, u32[]{:S(2)}, u32[]{:S(2)}) %collective-permute-start.8) | collective-permute-done | bytes 1990688 | tf_op jit(solution)/shard_map/ppermute | solution.py:222
  163.0 30.5 %collective-permute-done.11.refs_9_.refs_7_ = bf16[3,288,1152]{2,1,0:T(8,128)(2,1)} collective-permute-done((bf16[3,288,1152]{2,1,0:T(8,128)(2,1)}, bf16[3,288,1152]{2,1,0:T(8,128)(2,1)}, u32[]{:S(2)}, u32[]{:S(2)}) %collective-permute-start.11) | collective-permute-done | bytes 1990688 | tf_op jit(solution)/shard_map/ppermute | solution.py:222
  204.6 4.4 slice.203.up
  220.7 21.4 %collective-permute-done.16.refs_13_.refs_11_ = bf16[3,288,1152]{2,1,0:T(8,128)(2,1)} collective-permute-done((bf16[3,288,1152]{2,1,0:T(8,128)(2,1)}, bf16[3,288,1152]{2,1,0:T(8,128)(2,1)}, u32[]{:S(2)}, u32[]{:S(2)}) %collective-permute-start.16) | collective-permute-done | bytes 1990688 | tf_op jit(solution)/shard_map/ppermute | solution.py:222
  249.5 5.1 gather_fusion
  259.7 17.6 %shard_map.212.lin = f32[3,256,2304]{2,1,0:T(8,128)} custom-call(s32[3]{0:T(128)} %pad_add_fusion.1.where, bf16[256,2304]{1,0:T(8,128)(2,1)} %fusion.14.values, bf16[288,2304]{1,0:T(8,128)(2,1)} %refs_0_.7, bf16[288,2304]{1,0:T(8,128)(2,1)} %refs_1_.3, bf16[288,2304]{1,0:T(8,128)(2,1)} %refs_2_.3, bf16[3,288,1152]{2,1,0:T(8,128)(2,1)} %pad_maximum_fusion.7.refs_3_.refs_1_, ...), custom_call_target="tpu_custom_call" | custom-call | flops 509607936 | bytes 1990656 | tf_op jit(solution)/shard_map/pallas_call | solution.py:323
  282.4 5.5 all-to-all-start.1
  292.4 18.9 %shard_map.213 = (bf16[3,256,2304]{2,1,0:T(8,128)(2,1)}, bf16[256,2304]{1,0:T(8,128)(2,1)S(1)}) custom-call(f32[3,256,2304]{2,1,0:T(8,128)} %shard_map.212.lin, bf16[3,256,128]{2,1,0:T(8,128)(2,1)S(1)} %copy-done.35, bf16[3,128,2304]{2,1,0:T(8,128)(2,1)S(1)} %copy-done.11, f32[256,128]{1,0:T(8,128)S(1)} %copy-done.33, f32[256,128]{1,0:T(8,128)S(1)} %copy-done.31, ...), custom_call_target="tpu_custom_call" | custom-call | flops 75497472 | bytes 884736 | tf_op jit(solution)/shard_map/pallas_call | solution.py:176
  321.6 8.7 shard_map.214
  345.6 18.1 %collective-permute-done.24 = bf16[256,2304]{1,0:T(8,128)(2,1)} collective-permute-done((bf16[256,2304]{1,0:T(8,128)(2,1)}, bf16[256,2304]{1,0:T(8,128)(2,1)}, u32[]{:S(2)}, u32[]{:S(2)}) %collective-permute-start.24) | collective-permute-done | bytes 1179680 | tf_op jit(solution)/shard_map/ppermute | solution.py:222
  363.7 14.4 %collective-permute-done.25.mates.refs_9_ = bf16[3,288,1536]{2,1,0:T(8,128)(2,1)S(1)} collective-permute-done((bf16[3,288,1536]{2,1,0:T(8,128)(2,1)}, bf16[3,288,1536]{2,1,0:T(8,128)(2,1)S(1)}, u32[]{:S(2)}, u32[]{:S(2)}) %collective-permute-start.25) | collective-permute-done | bytes 2654240 | tf_op jit(solution)/shard_map/ppermute | solution.py:222
  378.0 4.2 pad_maximum_fusion.5
  399.3 13.0 %shard_map.215 = (f32[1024,1536]{1,0:T(8,128)}, bf16[1024,128]{1,0:T(8,128)(2,1)S(1)}) custom-call(s32[3]{0:T(128)S(1)} %pad_add_fusion.4.where, bf16[1024,2304]{1,0:T(8,128)(2,1)S(1)} %pad_maximum_fusion.1.values, f32[1024,128]{1,0:T(8,128)S(1)} %pad_maximum_fusion.10.choices, bf16[2304,128]{1,0:T(8,128)(2,1)S(1)} %copy-done.23, ...), custom_call_target="tpu_custom_call" | custom-call | flops 452984832 | bytes 884736 | tf_op jit(solution)/shard_map/pallas_call | solution.py:560
  412.4 13.3 %shard_map.216 = (f32[1024,1536]{1,0:T(8,128)}, bf16[1024,128]{1,0:T(8,128)(2,1)S(1)}) custom-call(s32[3]{0:T(128)S(1)} %pad_add_fusion.4.where, bf16[1024,2304]{1,0:T(8,128)(2,1)S(1)} %pad_maximum_fusion.1.values, f32[1024,128]{1,0:T(8,128)S(1)} %pad_maximum_fusion.10.choices, bf16[2304,128]{1,0:T(8,128)(2,1)S(1)} %copy-done.22, ...), custom_call_target="tpu_custom_call" | custom-call | flops 452984832 | bytes 884736 | tf_op jit(solution)/shard_map/pallas_call | solution.py:560
  425.8 5.7 collective-permute-done.27.refs_2_
  433.1 4.7 collective-permute-done.29
  437.8 5.4 pad_maximum_fusion.sent
  443.2 47.1 %shard_map.217 = (bf16[1024,1536]{1,0:T(8,128)(2,1)}, bf16[1024,1536]{1,0:T(8,128)(2,1)}, bf16[1024,1536]{1,0:T(8,128)(2,1)}, f32[512,2688]{1,0:T(8,128)}, bf16[512,2688]{1,0:T(8,128)(2,1)}) custom-call(s32[3]{0:T(128)} %copy-done.39, f32[1024,1536]{1,0:T(8,128)} %get-tuple-element.140.gt, f32[1024,1536]{1,0:T(8,128)} %get-tuple-element.141.up, ...), custom_call_target="tpu_custom_call" | custom-call | flops 1358954496 | bytes 2654208 | tf_op jit(solution)/shard_map/pallas_call | solution.py:613
  490.4 5.2 collective-permute-done.30
  515.9 4.3 reshape.427
  523.5 12.9 %shard_map.218 = (f32[512,2304]{1,0:T(8,128)}, bf16[512,2304]{1,0:T(8,128)(2,1)}) custom-call(s32[3]{0:T(128)S(1)} %copy-done.40, bf16[1024,1536]{1,0:T(8,128)(2,1)S(1)} %copy-done.21, bf16[4,192,1792]{2,1,0:T(8,128)(2,1)S(1)} %bitcast.251, bf16[192,1792]{1,0:T(8,128)(2,1)S(1)} %copy-done.14, bf16[3,192,1792]{2,1,0:T(8,128)(2,1)} %collective-permute-done.27.refs_2_, ...), custom_call_target="tpu_custom_call" | custom-call | flops 452984832 | bytes 884736 | tf_op jit(solution)/shard_map/pallas_call | solution.py:650
  563.2 8.9 shard_map.219.lin
  574.5 26.2 %shard_map.220.values = bf16[3,256,2304]{2,1,0:T(8,128)(2,1)} custom-call(bf16[3,256,2304]{2,1,0:T(8,128)(2,1)} %get-tuple-element.121.qkv, f32[256,2304]{1,0:T(8,128)S(1)} %copy-done.8, bf16[256,128]{1,0:T(8,128)(2,1)S(1)} %fusion.44.dz, bf16[2304,128]{1,0:T(8,128)(2,1)S(1)} %copy-done.24, f32[256,128]{1,0:T(8,128)S(1)} %copy-done.34, ...), custom_call_target="tpu_custom_call" | custom-call | flops 75497472 | bytes 884736 | tf_op jit(solution)/shard_map/pallas_call | solution.py:176
  600.8 4.1 fusion
  622.0 4.8 reshape.423
  634.9 5.4 constant_dynamic-slice_fusion
  645.1 4.5 collective-permute-done.34
  649.6 8.1 add_convert_fusion
  660.1 5.1 all-to-all-start.2
  676.9 34.5 %collective-permute-done.35 = bf16[4,2,664,128]{3,2,0,1:T(8,128)(2,1)} collective-permute-done((bf16[4,2,664,128]{3,2,0,1:T(8,128)(2,1)}, bf16[4,2,664,128]{3,2,0,1:T(8,128)(2,1)}, u32[]{:S(2)}, u32[]{:S(2)}) %collective-permute-start.35) | collective-permute-done | bytes 1359904 | tf_op jit(solution)/shard_map/ppermute | solution.py:222
  717.2 13.6 %collective-permute-done.37 = bf16[4,664,128]{2,1,0:T(8,128)(2,1)S(1)} collective-permute-done((bf16[4,664,128]{2,1,0:T(8,128)(2,1)}, bf16[4,664,128]{2,1,0:T(8,128)(2,1)S(1)}, u32[]{:S(2)}, u32[]{:S(2)}) %collective-permute-start.37) | collective-permute-done | bytes 679968 | tf_op jit(solution)/shard_map/ppermute | solution.py:222
  734.0 5.7 collective-permute-start.41
  740.6 7.6 collective-permute-done.41
  748.3 17.1 %collective-permute-done.40 = bf16[1336,128]{1,0:T(8,128)(2,1)} collective-permute-done((bf16[1336,128]{1,0:T(8,128)(2,1)S(1)}, bf16[1336,128]{1,0:T(8,128)(2,1)}, u32[]{:S(2)}, u32[]{:S(2)}) %collective-permute-start.40) | collective-permute-done | bytes 342048 | tf_op jit(solution)/shard_map/ppermute | solution.py:222
  774.4 17.1 %shard_map.223 = f32[256,2304]{1,0:T(8,128)} custom-call(s32[3]{0:T(128)} %pad_add_fusion.1.where, bf16[3,256,2304]{2,1,0:T(8,128)(2,1)} %shard_map.220.values, bf16[288,2304]{1,0:T(8,128)(2,1)} %refs_0_.7, bf16[288,2304]{1,0:T(8,128)(2,1)} %refs_1_.3, bf16[288,2304]{1,0:T(8,128)(2,1)} %refs_2_.3, bf16[3,288,1152]{2,1,0:T(8,128)(2,1)} %pad_maximum_fusion.7.refs_3_.refs_1_, ...), custom_call_target="tpu_custom_call" | custom-call | flops 509607936 | bytes 1990656 | tf_op jit(solution)/shard_map/pallas_call | solution.py:323
  795.5 13.9 %all-gather.27.cloned.1.call-done = bf16[5344,128]{1,0:T(8,128)(2,1)} async-done(((bf16[1336,128]{1,0:T(8,128)(2,1)}), bf16[5344,128]{1,0:T(8,128)(2,1)}) %all-gather.27.cloned.1.call-update) | async-done | bytes 1368080 | tf_op jit(solution)/shard_map/all_gather | solution.py:238
  823.8 4.2 collective-permute-done.44
  829.5 5.6 broadcast_in_dim.53
  840.6 17.9 %collective-permute-done.53 = bf16[4,672,128]{2,1,0:T(8,128)(2,1)S(1)} collective-permute-done((bf16[4,672,128]{2,1,0:T(8,128)(2,1)S(1)}, bf16[4,672,128]{2,1,0:T(8,128)(2,1)S(1)}, u32[]{:S(2)}, u32[]{:S(2)}) %collective-permute-start.53) | collective-permute-done | bytes 688160 | tf_op jit(solution)/shard_map/ppermute | solution.py:222
  859.0 13.6 %collective-permute-done.48 = bf16[4,664,128]{2,1,0:T(8,128)(2,1)S(1)} collective-permute-done((bf16[4,664,128]{2,1,0:T(8,128)(2,1)}, bf16[4,664,128]{2,1,0:T(8,128)(2,1)S(1)}, u32[]{:S(2)}, u32[]{:S(2)}) %collective-permute-start.48) | collective-permute-done | bytes 679968 | tf_op jit(solution)/shard_map/ppermute | solution.py:222
  (491 shorter events, 299.9 us)
Async XLA Ops:
  7.2 80.3 %all-gather.15.cloned.1.call-start = ((), (), s32[]{:S(2)}) async-start(), calls=%async_computation.4 | async-start | bytes 3317760 | tf_op jit(solution)/shard_map/all_gather | solution.py:238
  11.8 119.4 %all-gather.17.cloned.1.call-start = ((), (), s32[]{:S(2)}) async-start(), calls=%async_computation.5 | async-start | bytes 3317760 | tf_op jit(solution)/shard_map/all_gather | solution.py:238
  11.9 32.5 %collective-permute-start = (bf16[288,2304]{1,0:T(8,128)(2,1)}, bf16[288,2304]{1,0:T(8,128)(2,1)}, u32[]{:S(2)}, u32[]{:S(2)}) collective-permute-start(bf16[288,2304]{1,0:T(8,128)(2,1)} %copy-done.65), channel_id=1, source_target_pairs={{0,4},{1,5},{2,6},{3,7},{4,0},{5,1},{6,2},{7,3},{8,12},{9,13},{10,... | collective-permute-start | bytes 3981320 | tf_op jit(solution)/shard_map/ppermute | solution.py:222
  15.0 29.4 %collective-permute-start.1 = (s32[1,8]{1,0:T(1,128)S(1)}, s32[1,8]{1,0:T(1,128)S(1)}, u32[]{:S(2)}, u32[]{:S(2)}) collective-permute-start(s32[1,8]{1,0:T(1,128)S(1)} %pad_add_fusion.3), channel_id=1, source_target_pairs={{0,4},{1,5},{2,6},{3,7},{4,0},{5,1},{6,2},{7,3},{8,12},{9,13},{10,... | collective-permute-start | bytes 104 | tf_op jit(solution)/shard_map/ppermute | solution.py:222
  15.0 205.6 %all-gather.19.cloned.1.call-start = ((), (), s32[]{:S(2)}) async-start(), calls=%async_computation.6 | async-start | bytes 4423680 | tf_op jit(solution)/shard_map/all_gather | solution.py:238
  44.4 43.1 %collective-permute-start.4 = (bf16[288,2304]{1,0:T(8,128)(2,1)}, bf16[288,2304]{1,0:T(8,128)(2,1)S(1)}, u32[]{:S(2)}, u32[]{:S(2)}) collective-permute-start(bf16[288,2304]{1,0:T(8,128)(2,1)} %collective-permute-done.refs_19_.refs_17_), channel_id=1, source_target_pairs={{0,2},{1,3},{2,0},{3,1},{4,6},{5,7},{6,4},{7,5},{8,10},{9,11},{10,... | collective-permute-start | bytes 3981320 | tf_op jit(solution)/shard_map/ppermute | solution.py:222
  46.1 41.3 %collective-permute-start.5 = (bf16[288,2304]{1,0:T(8,128)(2,1)}, bf16[288,2304]{1,0:T(8,128)(2,1)}, u32[]{:S(2)}, u32[]{:S(2)}) collective-permute-start(bf16[288,2304]{1,0:T(8,128)(2,1)} %collective-permute-done.refs_19_.refs_17_), channel_id=1, source_target_pairs={{0,1},{1,0},{2,3},{3,2},{4,5},{5,4},{6,7},{7,6},{8,9},{9,8},{10,11... | collective-permute-start | bytes 3981320 | tf_op jit(solution)/shard_map/ppermute | solution.py:222
  46.1 22.8 %collective-permute-start.2 = (bf16[288,1536]{1,0:T(8,128)(2,1)}, bf16[288,1536]{1,0:T(8,128)(2,1)}, u32[]{:S(2)}, u32[]{:S(2)}) collective-permute-start(bf16[288,1536]{1,0:T(8,128)(2,1)} %get-tuple-element.90), channel_id=1, source_target_pairs={{0,4},{1,5},{2,6},{3,7},{4,0},{5,1},{6,2},{7,3},{8,12},{9,13},{10,... | collective-permute-start | bytes 2654216 | tf_op jit(solution)/shard_map/ppermute | solution.py:222
  47.6 39.8 %collective-permute-start.3 = (bf16[288,1536]{1,0:T(8,128)(2,1)S(1)}, bf16[288,1536]{1,0:T(8,128)(2,1)}, u32[]{:S(2)}, u32[]{:S(2)}) collective-permute-start(bf16[288,1536]{1,0:T(8,128)(2,1)S(1)} %get-tuple-element.91), channel_id=1, source_target_pairs={{0,4},{1,5},{2,6},{3,7},{4,0},{5,1},{6,2},{7,3},{8,12},{9,13},{10,... | collective-permute-start | bytes 2654216 | tf_op jit(solution)/shard_map/ppermute | solution.py:222
  91.1 45.3 %collective-permute-start.7 = (bf16[3,288,1152]{2,1,0:T(8,128)(2,1)}, bf16[3,288,1152]{2,1,0:T(8,128)(2,1)}, u32[]{:S(2)}, u32[]{:S(2)}) collective-permute-start(bf16[3,288,1152]{2,1,0:T(8,128)(2,1)} %pad_maximum_fusion.7.refs_3_.refs_1_), channel_id=1, source_target_pairs={{0,2},{1,3},{2,0},{3,1},{4,6},{5,7},{6,4},{7,5},{8,10},{9,11},{10,... | collective-permute-start | bytes 5971976 | tf_op jit(solution)/shard_map/ppermute | solution.py:222
  91.4 56.1 %collective-permute-start.8 = (bf16[3,288,1152]{2,1,0:T(8,128)(2,1)}, bf16[3,288,1152]{2,1,0:T(8,128)(2,1)}, u32[]{:S(2)}, u32[]{:S(2)}) collective-permute-start(bf16[3,288,1152]{2,1,0:T(8,128)(2,1)} %pad_maximum_fusion.7.refs_3_.refs_1_), channel_id=1, source_target_pairs={{0,4},{1,5},{2,6},{3,7},{4,0},{5,1},{6,2},{7,3},{8,12},{9,13},{10,... | collective-permute-start | bytes 5971976 | tf_op jit(solution)/shard_map/ppermute | solution.py:222
  93.2 54.3 %collective-permute-start.9 = (bf16[3,288,1152]{2,1,0:T(8,128)(2,1)}, bf16[3,288,1152]{2,1,0:T(8,128)(2,1)}, u32[]{:S(2)}, u32[]{:S(2)}) collective-permute-start(bf16[3,288,1152]{2,1,0:T(8,128)(2,1)} %pad_maximum_fusion.7.refs_3_.refs_1_), channel_id=1, source_target_pairs={{0,1},{1,0},{2,3},{3,2},{4,5},{5,4},{6,7},{7,6},{8,9},{9,8},{10,11... | collective-permute-start | bytes 5971976 | tf_op jit(solution)/shard_map/ppermute | solution.py:222
  93.2 38.0 %collective-permute-start.10 = (bf16[288,2304]{1,0:T(8,128)(2,1)S(1)}, bf16[288,2304]{1,0:T(8,128)(2,1)}, u32[]{:S(2)}, u32[]{:S(2)}) collective-permute-start(bf16[288,2304]{1,0:T(8,128)(2,1)S(1)} %collective-permute-done.4.refs_21_.refs_19_), channel_id=1, source_target_pairs={{0,1},{1,0},{2,3},{3,2},{4,5},{5,4},{6,7},{7,6},{8,9},{9,8},{10,11... | collective-permute-start | bytes 3981320 | tf_op jit(solution)/shard_map/ppermute | solution.py:222
  111.4 51.5 %all-to-all-start = ((bf16[8,32,2304]{2,1,0:T(8,128)(2,1)}), bf16[8,32,2304]{2,1,0:T(8,128)(2,1)S(1)}, u32[]{:S(2)}, u32[]{:S(2)}) async-start(bf16[8,32,2304]{2,1,0:T(8,128)(2,1)} %bitcast.277), calls=%async_computation | async-start | bytes 2359296 | tf_op jit(solution)/shard_map/all_to_all | solution.py:920
  116.3 196.0 %all-gather.21.cloned.1.call-start = ((), (), s32[]{:S(2)}) async-start(), calls=%async_computation.7 | async-start | bytes 4423680 | tf_op jit(solution)/shard_map/all_gather | solution.py:238
  150.8 42.7 %collective-permute-start.11 = (bf16[3,288,1152]{2,1,0:T(8,128)(2,1)}, bf16[3,288,1152]{2,1,0:T(8,128)(2,1)}, u32[]{:S(2)}, u32[]{:S(2)}) collective-permute-start(bf16[3,288,1152]{2,1,0:T(8,128)(2,1)} %pad_maximum_fusion.8.refs_7_.refs_5_), channel_id=1, source_target_pairs={{0,2},{1,3},{2,0},{3,1},{4,6},{5,7},{6,4},{7,5},{8,10},{9,11},{10,... | collective-permute-start | bytes 5971976 | tf_op jit(solution)/shard_map/ppermute | solution.py:222
  152.5 42.1 %collective-permute-start.12 = (bf16[3,288,1152]{2,1,0:T(8,128)(2,1)}, bf16[3,288,1152]{2,1,0:T(8,128)(2,1)}, u32[]{:S(2)}, u32[]{:S(2)}) collective-permute-start(bf16[3,288,1152]{2,1,0:T(8,128)(2,1)} %pad_maximum_fusion.8.refs_7_.refs_5_), channel_id=1, source_target_pairs={{0,4},{1,5},{2,6},{3,7},{4,0},{5,1},{6,2},{7,3},{8,12},{9,13},{10,... | collective-permute-start | bytes 5971976 | tf_op jit(solution)/shard_map/ppermute | solution.py:222
  152.5 42.1 %collective-permute-start.13 = (bf16[3,288,1152]{2,1,0:T(8,128)(2,1)}, bf16[3,288,1152]{2,1,0:T(8,128)(2,1)}, u32[]{:S(2)}, u32[]{:S(2)}) collective-permute-start(bf16[3,288,1152]{2,1,0:T(8,128)(2,1)} %pad_maximum_fusion.8.refs_7_.refs_5_), channel_id=1, source_target_pairs={{0,1},{1,0},{2,3},{3,2},{4,5},{5,4},{6,7},{7,6},{8,9},{9,8},{10,11... | collective-permute-start | bytes 5971976 | tf_op jit(solution)/shard_map/ppermute | solution.py:222
  152.5 42.1 %collective-permute-start.14 = (bf16[3,288,1152]{2,1,0:T(8,128)(2,1)}, bf16[3,288,1152]{2,1,0:T(8,128)(2,1)}, u32[]{:S(2)}, u32[]{:S(2)}) collective-permute-start(bf16[3,288,1152]{2,1,0:T(8,128)(2,1)} %collective-permute-done.7.refs_5_.refs_3_), channel_id=1, source_target_pairs={{0,1},{1,0},{2,3},{3,2},{4,5},{5,4},{6,7},{7,6},{8,9},{9,8},{10,11... | collective-permute-start | bytes 5971976 | tf_op jit(solution)/shard_map/ppermute | solution.py:222
  153.0 41.6 %collective-permute-start.15 = (bf16[3,288,1152]{2,1,0:T(8,128)(2,1)}, bf16[3,288,1152]{2,1,0:T(8,128)(2,1)}, u32[]{:S(2)}, u32[]{:S(2)}) collective-permute-start(bf16[3,288,1152]{2,1,0:T(8,128)(2,1)} %collective-permute-done.8.refs_11_.refs_9_), channel_id=1, source_target_pairs={{0,1},{1,0},{2,3},{3,2},{4,5},{5,4},{6,7},{7,6},{8,9},{9,8},{10,11... | collective-permute-start | bytes 5971976 | tf_op jit(solution)/shard_map/ppermute | solution.py:222
  160.6 217.5 %all-gather.23.cloned.1.call-start = ((), (), s32[]{:S(2)}) async-start(), calls=%async_computation.8 | async-start | bytes 3440640 | tf_op jit(solution)/shard_map/all_gather | solution.py:238
  194.7 47.4 %collective-permute-start.17 = (bf16[3,288,1152]{2,1,0:T(8,128)(2,1)}, bf16[3,288,1152]{2,1,0:T(8,128)(2,1)}, u32[]{:S(2)}, u32[]{:S(2)}) collective-permute-start(bf16[3,288,1152]{2,1,0:T(8,128)(2,1)} %collective-permute-done.12.refs_15_.refs_13_), channel_id=1, source_target_pairs={{0,2},{1,3},{2,0},{3,1},{4,6},{5,7},{6,4},{7,5},{8,10},{9,11},{10,... | collective-permute-start | bytes 5971976 | tf_op jit(solution)/shard_map/ppermute | solution.py:222
  196.0 46.1 %collective-permute-start.19 = (bf16[3,288,1152]{2,1,0:T(8,128)(2,1)}, bf16[3,288,1152]{2,1,0:T(8,128)(2,1)}, u32[]{:S(2)}, u32[]{:S(2)}) collective-permute-start(bf16[3,288,1152]{2,1,0:T(8,128)(2,1)} %collective-permute-done.12.refs_15_.refs_13_), channel_id=1, source_target_pairs={{0,1},{1,0},{2,3},{3,2},{4,5},{5,4},{6,7},{7,6},{8,9},{9,8},{10,11... | collective-permute-start | bytes 5971976 | tf_op jit(solution)/shard_map/ppermute | solution.py:222
  196.0 46.1 %collective-permute-start.16 = (bf16[3,288,1152]{2,1,0:T(8,128)(2,1)}, bf16[3,288,1152]{2,1,0:T(8,128)(2,1)}, u32[]{:S(2)}, u32[]{:S(2)}) collective-permute-start(bf16[3,288,1152]{2,1,0:T(8,128)(2,1)} %collective-permute-done.7.refs_5_.refs_3_), channel_id=1, source_target_pairs={{0,4},{1,5},{2,6},{3,7},{4,0},{5,1},{6,2},{7,3},{8,12},{9,13},{10,... | collective-permute-start | bytes 5971976 | tf_op jit(solution)/shard_map/ppermute | solution.py:222
  196.0 46.1 %collective-permute-start.18 = (bf16[3,288,1152]{2,1,0:T(8,128)(2,1)}, bf16[3,288,1152]{2,1,0:T(8,128)(2,1)}, u32[]{:S(2)}, u32[]{:S(2)}) collective-permute-start(bf16[3,288,1152]{2,1,0:T(8,128)(2,1)} %collective-permute-done.11.refs_9_.refs_7_), channel_id=1, source_target_pairs={{0,1},{1,0},{2,3},{3,2},{4,5},{5,4},{6,7},{7,6},{8,9},{9,8},{10,11... | collective-permute-start | bytes 5971976 | tf_op jit(solution)/shard_map/ppermute | solution.py:222
  246.4 65.9 %collective-permute-start.23 = (bf16[3,288,1536]{2,1,0:T(8,128)(2,1)}, bf16[3,288,1536]{2,1,0:T(8,128)(2,1)S(1)}, u32[]{:S(2)}, u32[]{:S(2)}) collective-permute-start(bf16[3,288,1536]{2,1,0:T(8,128)(2,1)} %pad_maximum_fusion.2), channel_id=1, source_target_pairs={{0,2},{1,3},{2,0},{3,1},{4,6},{5,7},{6,4},{7,5},{8,10},{9,11},{10,... | collective-permute-start | bytes 7962632 | tf_op jit(solution)/shard_map/ppermute | solution.py:222
  282.4 63.2 %all-to-all-start.1 = ((bf16[8,32,2304]{2,1,0:T(8,128)(2,1)}), bf16[8,32,2304]{2,1,0:T(8,128)(2,1)}, u32[]{:S(2)}, u32[]{:S(2)}) async-start(bf16[8,32,2304]{2,1,0:T(8,128)(2,1)} %bitcast.278), calls=%async_computation.1 | async-start | bytes 2359296 | tf_op jit(solution)/shard_map/all_to_all | solution.py:945
  288.0 137.8 %all-gather.25.cloned.1.call-start = ((), (), s32[]{:S(2)}) async-start(), calls=%async_computation.9 | async-start | bytes 1966080 | tf_op jit(solution)/shard_map/all_gather | solution.py:238
  317.0 61.1 %collective-permute-start.25 = (bf16[3,288,1536]{2,1,0:T(8,128)(2,1)}, bf16[3,288,1536]{2,1,0:T(8,128)(2,1)S(1)}, u32[]{:S(2)}, u32[]{:S(2)}) collective-permute-start(bf16[3,288,1536]{2,1,0:T(8,128)(2,1)} %pad_maximum_fusion.3), channel_id=1, source_target_pairs={{0,2},{1,3},{2,0},{3,1},{4,6},{5,7},{6,4},{7,5},{8,10},{9,11},{10,... | collective-permute-start | bytes 7962632 | tf_op jit(solution)/shard_map/ppermute | solution.py:222
  335.3 28.4 %collective-permute-start.24 = (bf16[256,2304]{1,0:T(8,128)(2,1)}, bf16[256,2304]{1,0:T(8,128)(2,1)}, u32[]{:S(2)}, u32[]{:S(2)}) collective-permute-start(bf16[256,2304]{1,0:T(8,128)(2,1)} %multiply_convert_fusion.1), channel_id=1, source_target_pairs={{0,4},{1,5},{2,6},{3,7},{4,0},{5,1},{6,2},{7,3},{8,12},{9,13},{10,... | collective-permute-start | bytes 3538952 | tf_op jit(solution)/shard_map/ppermute | solution.py:222
  383.9 47.6 %collective-permute-start.27 = (bf16[3,192,1792]{2,1,0:T(8,128)(2,1)}, bf16[3,192,1792]{2,1,0:T(8,128)(2,1)}, u32[]{:S(2)}, u32[]{:S(2)}) collective-permute-start(bf16[3,192,1792]{2,1,0:T(8,128)(2,1)} %pad_maximum_fusion.6), channel_id=1, source_target_pairs={{0,2},{1,3},{2,0},{3,1},{4,6},{5,7},{6,4},{7,5},{8,10},{9,11},{10,... | collective-permute-start | bytes 6193160 | tf_op jit(solution)/shard_map/ppermute | solution.py:222
  392.8 33.0 %collective-permute-start.28 = (bf16[256,2432]{1,0:T(8,128)(2,1)}, bf16[256,2432]{1,0:T(8,128)(2,1)}, u32[]{:S(2)}, u32[]{:S(2)}) collective-permute-start(bf16[256,2432]{1,0:T(8,128)(2,1)} %pad_maximum_fusion.9), channel_id=1, source_target_pairs={{0,4},{1,5},{2,6},{3,7},{4,0},{5,1},{6,2},{7,3},{8,12},{9,13},{10,... | collective-permute-start | bytes 3735560 | tf_op jit(solution)/shard_map/ppermute | solution.py:222
  502.5 33.9 %collective-permute-start.31 = (bf16[256,2688]{1,0:T(8,128)(2,1)}, bf16[256,2688]{1,0:T(8,128)(2,1)}, u32[]{:S(2)}, u32[]{:S(2)}) collective-permute-start(bf16[256,2688]{1,0:T(8,128)(2,1)} %unstack.34), channel_id=1, source_target_pairs={{0,4},{1,5},{2,6},{3,7},{4,0},{5,1},{6,2},{7,3},{8,12},{9,13},{10,... | collective-permute-start | bytes 4128776 | tf_op jit(solution)/shard_map/ppermute | solution.py:222
  551.2 49.5 %collective-permute-start.33 = (bf16[256,2304]{1,0:T(8,128)(2,1)}, bf16[256,2304]{1,0:T(8,128)(2,1)}, u32[]{:S(2)}, u32[]{:S(2)}) collective-permute-start(bf16[256,2304]{1,0:T(8,128)(2,1)} %unstack.35), channel_id=1, source_target_pairs={{0,4},{1,5},{2,6},{3,7},{4,0},{5,1},{6,2},{7,3},{8,12},{9,13},{10,... | collective-permute-start | bytes 3538952 | tf_op jit(solution)/shard_map/ppermute | solution.py:222
  660.1 51.3 %all-to-all-start.2 = ((bf16[8,32,2304]{2,1,0:T(8,128)(2,1)}), bf16[8,32,2304]{2,1,0:T(8,128)(2,1)}, u32[]{:S(2)}, u32[]{:S(2)}) async-start(bf16[8,32,2304]{2,1,0:T(8,128)(2,1)} %bitcast.270), calls=%async_computation.2 | async-start | bytes 2359296 | tf_op jit(solution)/shard_map/all_to_all | solution.py:1095
  665.2 144.1 %all-gather.27.cloned.1.call-start = ((), (), s32[]{:S(2)}) async-start(), calls=%async_computation.10 | async-start | bytes 1710080 | tf_op jit(solution)/shard_map/all_gather | solution.py:238
  672.0 39.4 %collective-permute-start.36 = (bf16[4,2,672,128]{3,2,1,0:T(8,128)(2,1)}, bf16[4,2,672,128]{3,2,1,0:T(8,128)(2,1)}, u32[]{:S(2)}, u32[]{:S(2)}) collective-permute-start(bf16[4,2,672,128]{3,2,1,0:T(8,128)(2,1)} %dynamic-slice_bitcast_fusion), channel_id=1, source_target_pairs={{0,2},{1,3},{2,0},{3,1},{4,6},{5,7},{6,4},{7,5},{8,10},{9,11},{10,... | collective-permute-start | bytes 4128776 | tf_op jit(solution)/shard_map/ppermute | solution.py:222
  674.9 36.5 %collective-permute-start.35 = (bf16[4,2,664,128]{3,2,0,1:T(8,128)(2,1)}, bf16[4,2,664,128]{3,2,0,1:T(8,128)(2,1)}, u32[]{:S(2)}, u32[]{:S(2)}) collective-permute-start(bf16[4,2,664,128]{3,2,0,1:T(8,128)(2,1)} %dynamic-slice_bitcast_fusion.1), channel_id=1, source_target_pairs={{0,4},{1,5},{2,6},{3,7},{4,0},{5,1},{6,2},{7,3},{8,12},{9,13},{10,... | collective-permute-start | bytes 4079624 | tf_op jit(solution)/shard_map/ppermute | solution.py:222
  739.7 25.6 %collective-permute-start.40 = (bf16[1336,128]{1,0:T(8,128)(2,1)S(1)}, bf16[1336,128]{1,0:T(8,128)(2,1)}, u32[]{:S(2)}, u32[]{:S(2)}) collective-permute-start(bf16[1336,128]{1,0:T(8,128)(2,1)S(1)} %get-tuple-element.215), channel_id=1, source_target_pairs={{0,16},{1,17},{2,18},{3,19},{4,20},{5,21},{6,22},{7,23},{8,24},{9,... | collective-permute-start | bytes 1026056 | tf_op jit(solution)/shard_map/ppermute | solution.py:222
  739.7 25.6 %collective-permute-start.39 = (bf16[1336,128]{1,0:T(8,128)(2,1)S(1)}, bf16[1336,128]{1,0:T(8,128)(2,1)}, u32[]{:S(2)}, u32[]{:S(2)}) collective-permute-start(bf16[1336,128]{1,0:T(8,128)(2,1)S(1)} %get-tuple-element.214), channel_id=1, source_target_pairs={{0,8},{1,9},{2,10},{3,11},{4,12},{5,13},{6,14},{7,15},{8,16},{9,17... | collective-permute-start | bytes 1026056 | tf_op jit(solution)/shard_map/ppermute | solution.py:222
  812.8 23.2 %collective-permute-start.43 = (bf16[4,664,128]{2,1,0:T(8,128)(2,1)}, bf16[4,664,128]{2,1,0:T(8,128)(2,1)S(1)}, u32[]{:S(2)}, u32[]{:S(2)}) collective-permute-start(bf16[4,664,128]{2,1,0:T(8,128)(2,1)} %slice.223), channel_id=1, source_target_pairs={{0,1},{1,0},{2,3},{3,2},{4,5},{5,4},{6,7},{7,6},{8,9},{9,8},{10,11... | collective-permute-start | bytes 2039816 | tf_op jit(solution)/shard_map/ppermute | solution.py:222
  812.8 24.7 %collective-permute-start.46 = (bf16[4,664,128]{2,1,0:T(8,128)(2,1)}, bf16[4,664,128]{2,1,0:T(8,128)(2,1)S(1)}, u32[]{:S(2)}, u32[]{:S(2)}) collective-permute-start(bf16[4,664,128]{2,1,0:T(8,128)(2,1)} %slice.223), channel_id=1, source_target_pairs={{0,4},{1,5},{2,6},{3,7},{4,0},{5,1},{6,2},{7,3},{8,12},{9,13},{10,... | collective-permute-start | bytes 2039816 | tf_op jit(solution)/shard_map/ppermute | solution.py:222
  817.9 67.4 %all-to-all-start.3 = ((bf16[8,32,2304]{2,1,0:T(8,128)(2,1)}), bf16[8,32,2304]{2,1,0:T(8,128)(2,1)S(1)}, u32[]{:S(2)}, u32[]{:S(2)}) async-start(bf16[8,32,2304]{2,1,0:T(8,128)(2,1)} %bitcast.76), calls=%async_computation.3 | async-start | bytes 2359296 | tf_op jit(solution)/shard_map/all_to_all | solution.py:1117
  821.8 36.7 %collective-permute-start.53 = (bf16[4,672,128]{2,1,0:T(8,128)(2,1)S(1)}, bf16[4,672,128]{2,1,0:T(8,128)(2,1)S(1)}, u32[]{:S(2)}, u32[]{:S(2)}) collective-permute-start(bf16[4,672,128]{2,1,0:T(8,128)(2,1)S(1)} %slice.224), channel_id=1, source_target_pairs={{0,4},{1,5},{2,6},{3,7},{4,0},{5,1},{6,2},{7,3},{8,12},{9,13},{10,... | collective-permute-start | bytes 2064392 | tf_op jit(solution)/shard_map/ppermute | solution.py:222
  828.0 30.5 %collective-permute-start.45 = (bf16[4,664,128]{2,1,0:T(8,128)(2,1)}, bf16[4,664,128]{2,1,0:T(8,128)(2,1)S(1)}, u32[]{:S(2)}, u32[]{:S(2)}) collective-permute-start(bf16[4,664,128]{2,1,0:T(8,128)(2,1)} %collective-permute-done.44), channel_id=1, source_target_pairs={{0,1},{1,0},{2,3},{3,2},{4,5},{5,4},{6,7},{7,6},{8,9},{9,8},{10,11... | collective-permute-start | bytes 2039816 | tf_op jit(solution)/shard_map/ppermute | solution.py:222
  828.0 44.7 %collective-permute-start.48 = (bf16[4,664,128]{2,1,0:T(8,128)(2,1)}, bf16[4,664,128]{2,1,0:T(8,128)(2,1)S(1)}, u32[]{:S(2)}, u32[]{:S(2)}) collective-permute-start(bf16[4,664,128]{2,1,0:T(8,128)(2,1)} %collective-permute-done.44), channel_id=1, source_target_pairs={{0,4},{1,5},{2,6},{3,7},{4,0},{5,1},{6,2},{7,3},{8,12},{9,13},{10,... | collective-permute-start | bytes 2039816 | tf_op jit(solution)/shard_map/ppermute | solution.py:222
  836.1 38.5 %collective-permute-start.51 = (bf16[4,672,128]{2,1,0:T(8,128)(2,1)S(1)}, bf16[4,672,128]{2,1,0:T(8,128)(2,1)S(1)}, u32[]{:S(2)}, u32[]{:S(2)}) collective-permute-start(bf16[4,672,128]{2,1,0:T(8,128)(2,1)S(1)} %slice.224), channel_id=1, source_target_pairs={{0,2},{1,3},{2,0},{3,1},{4,6},{5,7},{6,4},{7,5},{8,10},{9,11},{10,... | collective-permute-start | bytes 2064392 | tf_op jit(solution)/shard_map/ppermute | solution.py:222
  837.6 37.5 %collective-permute-start.47 = (bf16[4,664,128]{2,1,0:T(8,128)(2,1)S(1)}, bf16[4,664,128]{2,1,0:T(8,128)(2,1)S(1)}, u32[]{:S(2)}, u32[]{:S(2)}) collective-permute-start(bf16[4,664,128]{2,1,0:T(8,128)(2,1)S(1)} %collective-permute-done.46), channel_id=1, source_target_pairs={{0,1},{1,0},{2,3},{3,2},{4,5},{5,4},{6,7},{7,6},{8,9},{9,8},{10,11... | collective-permute-start | bytes 2039816 | tf_op jit(solution)/shard_map/ppermute | solution.py:222
  (125 other events, 1077.8 us)
Sparse Core Ops, SparseCore 0:
  11.9 58.0 all-gather.14
  72.2 58.9 all-gather.16
  133.4 76.3 all-gather.18
  211.2 68.5 all-gather.20
  281.2 80.8 all-gather.22
  363.6 37.2 all-gather.24
  774.5 34.8 all-gather.26

commit v4 on v3

--- a/solution.py
+++ b/solution.py
@@ -464,8 +464,6 @@
 
     @pl.when(step == 0)
     def _():
-        down_copies(line, where, left, right, down, down_sems)
-
         def start(tile, carry):
             cols = pl.ds(pl.multiple_of(tile * HIDDEN_TILE, 128), HIDDEN_TILE)
             for t, (planes, rest, mates) in enumerate((gate_pieces, up_pieces)):
@@ -473,7 +471,9 @@
                 quarter_copies(line, where[0], where[2], pieces, held.at[t, tile], sems.at[t, tile])
             return carry
 
-        lax.fori_loop(0, tiles, start, 0)
+        start(0, 0)
+        down_copies(line, where, left, right, down, down_sems)
+        lax.fori_loop(1, tiles, start, 0)
         keep[...] = jnp.zeros_like(keep)
         total[...] = jnp.zeros_like(total)
 
@@ -783,7 +783,57 @@
     return lax.dynamic_index_in_dim(values, index, axis, keepdims=False)
 
 
-def reduce_over_cores(place, flat):
+def gradients_kernel(lower_rows, upper_rows, *refs):
+    n1, dz_qkv, z_qkv, e_qkv, o, dz_out, z_out, e_out = refs[:8]
+    n2, dz_gate, dz_up, z_down, e_down, _, flat, turned, staged, sems = refs[8:]
+    lower = [(n1[...], dz_qkv[t]) for t in range(3)]
+    lower += [(o[...], dz_out[...]), (n2[...], dz_gate[...]), (n2[...], dz_up[...])]
+    upper = [(z_qkv[t], e_qkv[t]) for t in range(3)]
+    upper += [(z_out[...], e_out[...]), (z_down[...], e_down[...])]
+    rows = staged.shape[1]
+    ranks = ADAPTER_COLUMNS
+    parts = rows // ranks
+    starts = [lower_rows + rows * k for k in range(6)] + [upper_rows + rows * k for k in range(5)]
+    copies = []
+    for k, start in enumerate(starts):
+        slot = k % 2
+        if k > 1:
+            copies[k - 2].wait()
+        if k < 6:
+            staged[slot] = low(outer_product_sum(*lower[k]))
+        else:
+            full = adapter_scale * outer_product_sum(*upper[k - 6])
+            for j in range(parts):
+                turned[pl.ds(j, ranks, parts), :] = full[:, j * ranks : (j + 1) * ranks]
+            staged[slot] = low(turned[...])
+        copies.append(
+            pltpu.make_async_copy(staged.at[slot], flat.at[pl.ds(start, rows)], sems.at[slot])
+        )
+        copies[k].start()
+    copies[-2].wait()
+    copies[-1].wait()
+
+
+def model_gradients(operands, flat, lower_rows, upper_rows):
+    held = pl.BlockSpec(memory_space=pltpu.VMEM)
+    apart = pl.BlockSpec(memory_space=pl.ANY)
+    return pl.pallas_call(
+        functools.partial(gradients_kernel, lower_rows, upper_rows),
+        out_shape=jax.ShapeDtypeStruct(flat.shape, flat.dtype),
+        in_specs=[held] * len(operands) + [apart],
+        out_specs=apart,
+        scratch_shapes=[
+            pltpu.VMEM((MODEL_WIDTH, ADAPTER_COLUMNS), jnp.float32),
+            pltpu.VMEM((2, MODEL_WIDTH, ADAPTER_COLUMNS), jnp.bfloat16),
+            pltpu.SemaphoreType.DMA((2,)),
+        ],
+        input_output_aliases={len(operands): 0},
+        compiler_params=pltpu.CompilerParams(vmem_limit_bytes=40 << 20),
+        cost_estimate=pl.CostEstimate(flops=1 << 28, bytes_accessed=1 << 22, transcendentals=0),
+    )(*operands, flat)
+
+
+def reduce_over_cores(place, flat, later):
     pairs = place.line * 2 * (place.shard // 2)
     rows = flat.shape[0] // pairs
     half = -(-rows // 16) * 8
@@ -791,7 +841,8 @@
     start = rows - half
     keep = lax.dynamic_slice_in_dim(split, place.c * start, half, 3)
     send = lax.dynamic_slice_in_dim(split, (1 - place.c) * start, half, 3)
-    return both(keep, place.by_c(send))
+    got, later = together(place.by_c(send), later)
+    return both(keep, got), later
 
 
 class OwnerSum:
@@ -826,7 +877,7 @@
         return lax.dynamic_slice_in_dim(result, start, self.share, 0)
 
 
-def gather_owners(place, own, event):
+def gather_owners(place, own):
     share = own.shape[0]
     half = -(-share // 8) * 8
     start = 2 * share - half
@@ -834,7 +885,6 @@
     head, tail = jnp.where(place.c == 0, own, mate), jnp.where(place.c == 0, mate, own)
     pair = jnp.concatenate([head, tail], axis=0)
     planes = place.all_z(lax.dynamic_slice_in_dim(pair, place.c * start, half, 0))
-    planes, event = together(planes, event)
     cut = half // 16 * 8
     full = jnp.zeros(
         (place.line, 2, place.shard // 2, 2 * share, ADAPTER_COLUMNS), own.dtype
@@ -851,7 +901,7 @@
             for held, c in ((value, place.c), (place.by_c(value), 1 - place.c)):
                 where = (0, y, x, c * start + at, 0)
                 full = lax.dynamic_update_slice(full, held[:, None, None], where)
-    return full.reshape(-1), event
+    return full.reshape(-1)
 
 
 def shards(
@@ -1011,10 +1061,32 @@
         gt, up, sent, A_down, B_gate, B_up, gate_pieces, up_pieces
     )
     own_sum, other_sum = place.half_sum(keep, send)
-    other_sum, h = together(low(other_sum), h)
+    other_sum, h, e_gate, e_up = together(low(other_sum), h, e_gate, e_up)
     got = place.by_y(other_sum)
     y_keep, y_send = feed.out(h, MODEL_WIDTH)
-    got, y_send = together(got, y_send)
+    dA_down = low(outer_product_sum(h, dz_down_all))
+    own_hidden = FEEDFORWARD_UNITS // (dp * GROUP)
+    dA_hidden = lax.dynamic_update_slice(
+        jnp.zeros((dp, GROUP, own_hidden, ADAPTER_COLUMNS), jnp.bfloat16),
+        dA_down.reshape(dp, 1, padded, ADAPTER_COLUMNS)[:, :, :own_hidden],
+        (0, place.q, 0, 0),
+    )
+    lower_rows, upper_rows = 6 * MODEL_WIDTH, 5 * MODEL_WIDTH
+    hidden_rows_count = FEEDFORWARD_UNITS
+    flat = jnp.concatenate(
+        [
+            jnp.zeros((lower_rows, ADAPTER_COLUMNS), jnp.bfloat16),
+            dA_hidden.reshape(-1, ADAPTER_COLUMNS),
+            jnp.zeros((upper_rows, ADAPTER_COLUMNS), jnp.bfloat16),
+        ]
+        + [
+            spread_columns(
+                place, low(adapter_scale * outer_product_sum(z, e)), FEEDFORWARD_UNITS, dp, padded
+            ).reshape(-1, ADAPTER_COLUMNS)
+            for z, e in ((z_gate, e_gate), (z_up, e_up))
+        ]
+    )
+    got, y_send, flat = together(got, y_send, flat)
     back_sum = own_sum + got.astype(jnp.float32)
     y_own, y_other = place.half_sum(y_keep, y_send)
     y_got = place.by_y(low(y_other))
@@ -1027,12 +1099,6 @@
         + matrix_product_backward(dz_gate, A_model[4])
         + matrix_product_backward(dz_up, A_model[5])
     )
-    dA_gate, dA_up = outer_product_sum(n2, dz_gate), outer_product_sum(n2, dz_up)
-    dB_gate = adapter_scale * outer_product_sum(z_gate, e_gate)
-    dB_up = adapter_scale * outer_product_sum(z_up, e_up)
-    dA_down = outer_product_sum(h, dz_down_all)
-    dB_down = adapter_scale * outer_product_sum(z_down, e_down)
-
     dm = g + norm_back(m, scale_two, gain_second, dn2)
     e_out = low(residual_branch_scale * dm)
     dz_out = low(adapter_scale * matrix_product_backward(e_out, B_model[3]) * choice)
@@ -1049,7 +1115,6 @@
         ),
         (((3, count, MODEL_WIDTH), 2),),
     )
-    dA_out, dB_out = outer_product_sum(o, dz_out), adapter_scale * outer_product_sum(z_out, e_out)
     e_qkv, y_got = together(e_qkv, y_got)
     y = m + residual_branch_scale * (
         y_own + y_got.astype(jnp.float32) + adapter_scale * matrix_product(z_down, B_model[4])
@@ -1062,43 +1127,40 @@
         * jnp.einsum("tnd,trd->tnr", e_qkv, B_model[:3], preferred_element_type=jnp.float32)
         * choice
     )
-    dA_qkv = jnp.einsum("nd,tnr->tdr", n1, dz_qkv, preferred_element_type=jnp.float32)
-    dB_qkv = adapter_scale * jnp.einsum(
-        "tnr,tnd->trd", z_qkv, e_qkv, preferred_element_type=jnp.float32
-    )
-    own_hidden = FEEDFORWARD_UNITS // (dp * GROUP)
-    dA_hidden = lax.dynamic_update_slice(
-        jnp.zeros((dp, GROUP, own_hidden, ADAPTER_COLUMNS), jnp.bfloat16),
-        low(dA_down).reshape(dp, 1, padded, ADAPTER_COLUMNS)[:, :, :own_hidden],
-        (0, place.q, 0, 0),
-    )
-    flat = jnp.concatenate(
-        [
-            low(piece).reshape(-1, ADAPTER_COLUMNS)
-            for piece in (
-                dA_qkv,
-                dA_out,
-                dA_gate,
-                dA_up,
-                dA_hidden,
-                dB_qkv,
-                dB_out,
-                dB_down,
-                spread_columns(place, low(dB_gate), FEEDFORWARD_UNITS, dp, padded),
-                spread_columns(place, low(dB_up), FEEDFORWARD_UNITS, dp, padded),
-            )
-        ]
+    flat = model_gradients(
+        (
+            n1,
+            dz_qkv,
+            z_qkv,
+            e_qkv,
+            o,
+            dz_out,
+            z_out,
+            e_out,
+            n2,
+            dz_gate,
+            dz_up,
+            z_down,
+            e_down,
+        ),
+        flat,
+        0,
+        lower_rows + hidden_rows_count,
     )
     share = flat.shape[0] // (dp * shard)
-    total, e_qkv, dz_qkv, y = together(reduce_over_cores(place, flat), e_qkv, dz_qkv, y)
+    total, (e_qkv, dz_qkv, y) = reduce_over_cores(place, flat, (e_qkv, dz_qkv, y))
     owner = OwnerSum(place, total, share)
     back_out = lax.all_to_all(low(y)[inverse], "dp", split_axis=0, concat_axis=0, tiled=True)
     dn1 = attention.times_transposed(e_qkv, 0, 3) + jnp.einsum(
         "tnr,tdr->nd", dz_qkv, A_model[:3], preferred_element_type=jnp.float32
     )
     dx = dm + norm_back(x, scale_one, gain_first, dn1)
-    owner.got, back_out = together(owner.got, back_out)
-    gradient = owner.over_planes(owner.over_chips())
+    owner.got, back_out, dx = together(owner.got, back_out, low(dx))
+    total = owner.over_chips()
+    total, back_grad = together(
+        total, lax.all_to_all(dx[inverse], "dp", split_axis=0, concat_axis=0, tiled=True)
+    )
+    gradient = owner.over_planes(total)
     offset = lax.axis_index(AXES) * share
     own_params = lax.dynamic_slice_in_dim(
         adapters.reshape(-1, ADAPTER_COLUMNS), offset, share
@@ -1113,8 +1175,7 @@
         unbiased_first / (jnp.sqrt(unbiased_second) + adaptive_epsilon)
         + weight_shrink_rate * own_params
     )
-    updated, dx = gather_owners(place, low(own_params - learning_rate * update), dx)
-    back_grad = lax.all_to_all(low(dx)[inverse], "dp", split_axis=0, concat_axis=0, tiled=True)
+    updated = gather_owners(place, low(own_params - learning_rate * update))
 
     return (
         back_out,

time: 906 us -> 871 us (0.961)
  local copies, waits for them, and re-layouts: 169 us -> 130 us
  matrix products: 43.3 us -> 25.8 us
  waiting for transfers between devices: 326 us -> 342 us
    all_gather x7, waiting for transfers between devices: 28.8 us -> 55.6 us  [all_z(): return lax.all_gather(block, 'dp', axis=0, axis_index_groups=groups)]
    dot_general x8 -> x3, matrix products: 17 us -> 5.31 us  [outer_product_sum(): lax.dot_general(left_side, right_side, (((0,), (0,)), ((), ())), preferre...]
    reshape x6 -> x3, local copies, waits for them, and re-layouts: 18.2 us -> 7.31 us  [the longest x2 6.02 us: shards(): flat = jnp.concatenate([jnp.zeros((lower_rows, ADAPTER_COLUMNS), jnp.bflo...]
    ppermute x57, waiting for transfers between devices: 294 us -> 283 us  [move(): return lax.ppermute(value, AXES, pairs)]
    dynamic_update_slice x16, local copies, waits for them, and re-layouts: 16.5 us -> 7 us  [gather_owners(): full = lax.dynamic_update_slice(full, held[:, None, None], where)]
    convert_element_type x8 -> x13, other arithmetic: 17.2 us -> 26 us  [low(): return values.astype(jnp.bfloat16)]
    unnamed x218 -> x228, local copies, waits for them, and re-layouts: 38.3 us -> 33.9 us
  transfers between devices with their start and end apart: 68 -> 68, of which waited for: 29 -> 33; matrix products, arithmetic and copies ran while one was open for 21% -> 20% of each run, Pallas kernels for 16% -> 16%
where the time goes in v4:
time: 871 us; the launch traced here: 862 us
  waiting for transfers between devices  342 us (39%)
  Pallas kernels  200 us (23%)
  local copies, waits for them, and re-layouts  130 us (15%)
  other arithmetic  77.4 us (9%)
  starting transfers between devices  70.5 us (8%)
  matrix products  25.8 us (3%)
  between operations  16.3 us (2%)
    ppermute x57, waiting for transfers between devices, move(): return lax.ppermute(value, AXES, pairs)  283 us
    all_gather x7, waiting for transfers between devices, all_z(): return lax.all_gather(block, 'dp', axis=0, axis_index_groups=groups)  55.6 us
    pallas_call x4, Pallas kernels, call(): pl.pallas_call(functools.partial(weights_kernel, place.line, first, count...  52.1 us
    pallas_call x1, Pallas kernels, back(): pl.pallas_call(functools.partial(feed_forward_back_kernel, self.place.lin...  46.9 us
    ppermute x57, starting transfers between devices, move(): return lax.ppermute(value, AXES, pairs)  46.1 us
    pallas_call x2, Pallas kernels, attention_call(): pl.pallas_call(kernel, grid=(ATTENTION_HEADS // 2,), out_shape=[jax.Shape...  45.2 us
    unnamed x228, local copies, waits for them, and re-layouts  33.9 us
    pallas_call x2, Pallas kernels, hidden(): pl.pallas_call(functools.partial(hidden_kernel, self.place.line), grid=(t...  26.2 us
  transfers between devices with their start and end apart: 68, of which 33 were waited for; matrix products, arithmetic and copies ran while one was open for 20% of the time, Pallas kernels for 16%

profile of v4, /device:TPU:0, one launch (start us, length us, event | category | flops | bytes accessed | tf_op | source)
XLA Modules:
  0.0 862.4 jit_solution(632920054623860499)
XLA Ops:
  20.2 24.2 %collective-permute-done.1 = s32[1,8]{1,0:T(1,128)S(1)} collective-permute-done((s32[1,8]{1,0:T(1,128)S(1)}, s32[1,8]{1,0:T(1,128)S(1)}, u32[]{:S(2)}, u32[]{:S(2)}) %collective-permute-start.1) | collective-permute-done | bytes 64 | tf_op jit(solution)/shard_map/ppermute | solution.py:222
  48.1 4.1 fusion.61
  53.4 15.4 %collective-permute-done.2 = bf16[288,1536]{1,0:T(8,128)(2,1)} collective-permute-done((bf16[288,1536]{1,0:T(8,128)(2,1)}, bf16[288,1536]{1,0:T(8,128)(2,1)}, u32[]{:S(2)}, u32[]{:S(2)}) %collective-permute-start.2) | collective-permute-done | bytes 884768 | tf_op jit(solution)/shard_map/ppermute | solution.py:222
  68.8 18.6 %collective-permute-done.3 = bf16[288,1536]{1,0:T(8,128)(2,1)} collective-permute-done((bf16[288,1536]{1,0:T(8,128)(2,1)S(1)}, bf16[288,1536]{1,0:T(8,128)(2,1)}, u32[]{:S(2)}, u32[]{:S(2)}) %collective-permute-start.3) | collective-permute-done | bytes 884768 | tf_op jit(solution)/shard_map/ppermute | solution.py:222
  95.9 4.5 fusion.62
  101.8 3.5 reshape.404
  108.7 4.8 all-to-all-start
  113.6 20.6 %all-gather.17.cloned.1.call-done = bf16[1152,1152]{1,0:T(8,128)(2,1)} async-done(((bf16[288,1152]{1,0:T(8,128)(2,1)}), bf16[1152,1152]{1,0:T(8,128)(2,1)}) %all-gather.17.cloned.1.call-update) | async-done | bytes 2654224 | tf_op jit(solution)/shard_map/all_gather | solution.py:238
  136.4 11.1 %collective-permute-done.8.refs_11_.refs_9_ = bf16[3,288,1152]{2,1,0:T(8,128)(2,1)} collective-permute-done((bf16[3,288,1152]{2,1,0:T(8,128)(2,1)}, bf16[3,288,1152]{2,1,0:T(8,128)(2,1)}, u32[]{:S(2)}, u32[]{:S(2)}) %collective-permute-start.8) | collective-permute-done | bytes 1990688 | tf_op jit(solution)/shard_map/ppermute | solution.py:222
  162.1 31.4 %collective-permute-done.11.refs_9_.refs_7_ = bf16[3,288,1152]{2,1,0:T(8,128)(2,1)} collective-permute-done((bf16[3,288,1152]{2,1,0:T(8,128)(2,1)}, bf16[3,288,1152]{2,1,0:T(8,128)(2,1)}, u32[]{:S(2)}, u32[]{:S(2)}) %collective-permute-start.11) | collective-permute-done | bytes 1990688 | tf_op jit(solution)/shard_map/ppermute | solution.py:222
  197.3 4.0 slice.190.value
  204.6 4.4 slice.203.up
  220.8 21.4 %collective-permute-done.16.refs_13_.refs_11_ = bf16[3,288,1152]{2,1,0:T(8,128)(2,1)} collective-permute-done((bf16[3,288,1152]{2,1,0:T(8,128)(2,1)}, bf16[3,288,1152]{2,1,0:T(8,128)(2,1)}, u32[]{:S(2)}, u32[]{:S(2)}) %collective-permute-start.16) | collective-permute-done | bytes 1990688 | tf_op jit(solution)/shard_map/ppermute | solution.py:222
  255.8 17.6 %shard_map.212.lin = f32[3,256,2304]{2,1,0:T(8,128)} custom-call(s32[3]{0:T(128)} %pad_add_fusion.2.where, bf16[256,2304]{1,0:T(8,128)(2,1)} %fusion.7.values.refs_0_, bf16[288,2304]{1,0:T(8,128)(2,1)} %refs_0_.7, bf16[288,2304]{1,0:T(8,128)(2,1)} %refs_1_.3, bf16[288,2304]{1,0:T(8,128)(2,1)} %refs_2_.3, ...), custom_call_target="tpu_custom_call" | custom-call | flops 509607936 | bytes 1990656 | tf_op jit(solution)/shard_map/pallas_call | solution.py:323
  277.5 6.4 all-to-all-start.1
  284.3 18.8 %shard_map.213 = (bf16[3,256,2304]{2,1,0:T(8,128)(2,1)}, bf16[256,2304]{1,0:T(8,128)(2,1)S(1)}) custom-call(f32[3,256,2304]{2,1,0:T(8,128)} %shard_map.212.lin, bf16[3,256,128]{2,1,0:T(8,128)(2,1)S(1)} %fusion.30.z.refs_2_, bf16[3,128,2304]{2,1,0:T(8,128)(2,1)S(1)} %copy-done.15, f32[256,128]{1,0:T(8,128)S(1)} %pad_maximum_fusion.13.cosine, ...), custom_call_target="tpu_custom_call" | custom-call | flops 75497472 | bytes 884736 | tf_op jit(solution)/shard_map/pallas_call | solution.py:176
  312.7 8.8 %shard_map.214 = f32[1,256,2304]{2,1,0:T(8,128)} custom-call(s32[3]{0:T(128)} %pad_add_fusion.2.where, bf16[256,2304]{1,0:T(8,128)(2,1)} %copy-done.20, bf16[288,2304]{1,0:T(8,128)(2,1)} %refs_0_.6, bf16[3,288,1152]{2,1,0:T(8,128)(2,1)} %pad_maximum_fusion.7.refs_3_.refs_1_, bf16[3,288,1152]{2,1,0:T(8,128)(2,1)} %collective-permute-done.9.refs_4_.refs_2_, ...), custom_call_target="tpu_custom_call" | custom-call | flops 169869312 | bytes 663552 | tf_op jit(solution)/shard_map/pallas_call | solution.py:323
  337.0 18.1 %collective-permute-done.24 = bf16[256,2304]{1,0:T(8,128)(2,1)S(1)} collective-permute-done((bf16[256,2304]{1,0:T(8,128)(2,1)S(1)}, bf16[256,2304]{1,0:T(8,128)(2,1)S(1)}, u32[]{:S(2)}, u32[]{:S(2)}) %collective-permute-start.24) | collective-permute-done | bytes 1179680 | tf_op jit(solution)/shard_map/ppermute | solution.py:222
  355.1 14.1 %collective-permute-done.25.mates.refs_9_ = bf16[3,288,1536]{2,1,0:T(8,128)(2,1)} collective-permute-done((bf16[3,288,1536]{2,1,0:T(8,128)(2,1)}, bf16[3,288,1536]{2,1,0:T(8,128)(2,1)}, u32[]{:S(2)}, u32[]{:S(2)}) %collective-permute-start.25) | collective-permute-done | bytes 2654240 | tf_op jit(solution)/shard_map/ppermute | solution.py:222
  375.3 5.0 gather_fusion.1
  390.3 12.9 %shard_map.215 = (f32[1024,1536]{1,0:T(8,128)}, bf16[1024,128]{1,0:T(8,128)(2,1)S(1)}) custom-call(s32[3]{0:T(128)S(1)} %pad_add_fusion.4.where, bf16[1024,2304]{1,0:T(8,128)(2,1)S(1)} %pad_maximum_fusion.1.values, f32[1024,128]{1,0:T(8,128)S(1)} %copy-done.23, bf16[2304,128]{1,0:T(8,128)(2,1)S(1)} %copy-done.28, bf16[128,1536]{1,0:T(8,128)(2,1)S(1)} %copy-done.31, ...), custom_call_target="tpu_custom_call" | custom-call | flops 452984832 | bytes 884736 | tf_op jit(solution)/shard_map/pallas_call | solution.py:560
  404.0 13.2 %shard_map.216 = (f32[1024,1536]{1,0:T(8,128)}, bf16[1024,128]{1,0:T(8,128)(2,1)S(1)}) custom-call(s32[3]{0:T(128)S(1)} %pad_add_fusion.4.where, bf16[1024,2304]{1,0:T(8,128)(2,1)S(1)} %pad_maximum_fusion.1.values, f32[1024,128]{1,0:T(8,128)S(1)} %copy-done.23, bf16[2304,128]{1,0:T(8,128)(2,1)S(1)} %copy-done.27, bf16[128,1536]{1,0:T(8,128)(2,1)S(1)} %copy-done.33, ...), custom_call_target="tpu_custom_call" | custom-call | flops 452984832 | bytes 884736 | tf_op jit(solution)/shard_map/pallas_call | solution.py:560
  422.0 4.7 collective-permute-done.29
  426.7 5.4 pad_maximum_fusion.sent
  432.1 46.9 %shard_map.217 = (bf16[1024,1536]{1,0:T(8,128)(2,1)}, bf16[1024,1536]{1,0:T(8,128)(2,1)}, bf16[1024,1536]{1,0:T(8,128)(2,1)}, f32[512,2688]{1,0:T(8,128)}, bf16[512,2688]{1,0:T(8,128)(2,1)}) custom-call(s32[3]{0:T(128)} %copy-done.54, f32[1024,1536]{1,0:T(8,128)} %get-tuple-element.144.gt, f32[1024,1536]{1,0:T(8,128)} %get-tuple-element.145.up, ...), custom_call_target="tpu_custom_call" | custom-call | flops 1358954496 | bytes 2654208 | tf_op jit(solution)/shard_map/pallas_call | solution.py:613
  491.7 10.4 %shard_map.218 = (f32[512,2304]{1,0:T(8,128)}, bf16[512,2304]{1,0:T(8,128)(2,1)S(1)}) custom-call(s32[3]{0:T(128)S(1)} %copy-done.55, bf16[1024,1536]{1,0:T(8,128)(2,1)S(1)} %copy-done.26, bf16[4,192,1792]{2,1,0:T(8,128)(2,1)S(1)} %bitcast.246, bf16[192,1792]{1,0:T(8,128)(2,1)S(1)} %copy-done.18, bf16[3,192,1792]{2,1,0:T(8,128)(2,1)} %collective-permute-done.27.refs_2_, ...), custom_call_target="tpu_custom_call" | custom-call | flops 452984832 | bytes 884736 | tf_op jit(solution)/shard_map/pallas_call | solution.py:650
  528.1 8.9 %collective-permute-done.31 = bf16[256,2688]{1,0:T(8,128)(2,1)} collective-permute-done((bf16[256,2688]{1,0:T(8,128)(2,1)}, bf16[256,2688]{1,0:T(8,128)(2,1)}, u32[]{:S(2)}, u32[]{:S(2)}) %collective-permute-start.31) | collective-permute-done | bytes 1376288 | tf_op jit(solution)/shard_map/ppermute | solution.py:222
  550.2 4.2 multiply_convert_fusion
  554.5 8.9 %shard_map.221.lin = f32[256,2304]{1,0:T(8,128)} custom-call(s32[3]{0:T(128)} %pad_add_fusion.2.where, bf16[1,256,2304]{2,1,0:T(8,128)(2,1)} %bitcast.247, bf16[288,2304]{1,0:T(8,128)(2,1)} %refs_0_.6, bf16[3,288,1152]{2,1,0:T(8,128)(2,1)} %pad_maximum_fusion.7.refs_3_.refs_1_, bf16[3,288,1152]{2,1,0:T(8,128)(2,1)} %collective-permute-done.9.refs_4_.refs_2_, ...), custom_call_target="tpu_custom_call" | custom-call | flops 169869312 | bytes 663552 | tf_op jit(solution)/shard_map/pallas_call | solution.py:323
  565.6 26.3 %shard_map.222.refs_3_.values = bf16[3,256,2304]{2,1,0:T(8,128)(2,1)} custom-call(bf16[3,256,2304]{2,1,0:T(8,128)(2,1)} %get-tuple-element.125.qkv, f32[256,2304]{1,0:T(8,128)S(1)} %copy-done.12, bf16[256,128]{1,0:T(8,128)(2,1)S(1)} %fusion.37.dz.refs_5_, bf16[2304,128]{1,0:T(8,128)(2,1)S(1)} %copy-done.29, f32[256,128]{1,0:T(8,128)S(1)} %copy-done.37, ...), custom_call_target="tpu_custom_call" | custom-call | flops 75497472 | bytes 884736 | tf_op jit(solution)/shard_map/pallas_call | solution.py:176
  597.7 9.0 %shard_map.223 = bf16[42624,128]{1,0:T(8,128)(2,1)} custom-call(bf16[256,2304]{1,0:T(8,128)(2,1)S(1)} %copy-done.11, bf16[3,256,128]{2,1,0:T(8,128)(2,1)S(1)} %fusion.26.refs_1_, bf16[3,256,128]{2,1,0:T(8,128)(2,1)S(1)} %copy-done.41, bf16[3,256,2304]{2,1,0:T(8,128)(2,1)S(1)} %copy-done, ...), custom_call_target="tpu_custom_call", output_to_operand_aliasing={{}: (13, {})} | custom-call | flops 268435456 | bytes 4194304 | tf_op jit(solution)/shard_map/pallas_call | solution.py:820
  606.8 5.5 constant_dynamic-slice_fusion.2
  617.5 4.3 collective-permute-done.34
  624.3 5.9 all-to-all-start.2
  630.1 5.6 add_convert_fusion
  642.6 16.9 %shard_map.224 = f32[256,2304]{1,0:T(8,128)} custom-call(s32[3]{0:T(128)} %pad_add_fusion.2.where, bf16[3,256,2304]{2,1,0:T(8,128)(2,1)} %shard_map.222.refs_3_.values, bf16[288,2304]{1,0:T(8,128)(2,1)} %refs_0_.7, bf16[288,2304]{1,0:T(8,128)(2,1)} %refs_1_.3, bf16[288,2304]{1,0:T(8,128)(2,1)} %refs_2_.3, ...), custom_call_target="tpu_custom_call" | custom-call | flops 509607936 | bytes 1990656 | tf_op jit(solution)/shard_map/pallas_call | solution.py:323
  663.6 12.2 %collective-permute-done.35 = bf16[4,2,664,128]{3,2,0,1:T(8,128)(2,1)} collective-permute-done((bf16[4,2,664,128]{3,2,0,1:T(8,128)(2,1)}, bf16[4,2,664,128]{3,2,0,1:T(8,128)(2,1)}, u32[]{:S(2)}, u32[]{:S(2)}) %collective-permute-start.35) | collective-permute-done | bytes 1359904 | tf_op jit(solution)/shard_map/ppermute | solution.py:222
  678.2 6.5 all-to-all-start.3
  692.9 10.8 %collective-permute-done.37 = bf16[4,664,128]{2,1,0:T(8,128)(2,1)} collective-permute-done((bf16[4,664,128]{2,1,0:T(8,128)(2,1)S(1)}, bf16[4,664,128]{2,1,0:T(8,128)(2,1)}, u32[]{:S(2)}, u32[]{:S(2)}) %collective-permute-start.37) | collective-permute-done | bytes 679968 | tf_op jit(solution)/shard_map/ppermute | solution.py:222
  705.2 9.9 %collective-permute-done.38 = bf16[4,672,128]{2,1,0:T(8,128)(2,1)S(1)} collective-permute-done((bf16[4,672,128]{2,1,0:T(8,128)(2,1)}, bf16[4,672,128]{2,1,0:T(8,128)(2,1)S(1)}, u32[]{:S(2)}, u32[]{:S(2)}) %collective-permute-start.38) | collective-permute-done | bytes 688160 | tf_op jit(solution)/shard_map/ppermute | solution.py:222
  716.4 4.6 collective-permute-start.41
  721.8 8.0 collective-permute-done.41
  729.9 17.4 %collective-permute-done.40 = bf16[1336,128]{1,0:T(8,128)(2,1)S(1)} collective-permute-done((bf16[1336,128]{1,0:T(8,128)(2,1)}, bf16[1336,128]{1,0:T(8,128)(2,1)S(1)}, u32[]{:S(2)}, u32[]{:S(2)}) %collective-permute-start.40) | collective-permute-done | bytes 342048 | tf_op jit(solution)/shard_map/ppermute | solution.py:222
  755.4 35.0 %all-gather.27.cloned.1.call-done = bf16[5344,128]{1,0:T(8,128)(2,1)} async-done(((bf16[1336,128]{1,0:T(8,128)(2,1)}), bf16[5344,128]{1,0:T(8,128)(2,1)}) %all-gather.27.cloned.1.call-update) | async-done | bytes 1368080 | tf_op jit(solution)/shard_map/all_gather | solution.py:238
  798.2 12.3 %collective-permute-done.44 = bf16[4,664,128]{2,1,0:T(8,128)(2,1)} collective-permute-done((bf16[4,664,128]{2,1,0:T(8,128)(2,1)}, bf16[4,664,128]{2,1,0:T(8,128)(2,1)}, u32[]{:S(2)}, u32[]{:S(2)}) %collective-permute-start.44) | collective-permute-done | bytes 679968 | tf_op jit(solution)/shard_map/ppermute | solution.py:222
  817.5 9.6 %collective-permute-done.53 = bf16[4,672,128]{2,1,0:T(8,128)(2,1)S(1)} collective-permute-done((bf16[4,672,128]{2,1,0:T(8,128)(2,1)}, bf16[4,672,128]{2,1,0:T(8,128)(2,1)S(1)}, u32[]{:S(2)}, u32[]{:S(2)}) %collective-permute-start.53) | collective-permute-done | bytes 688160 | tf_op jit(solution)/shard_map/ppermute | solution.py:222
  827.6 13.4 %collective-permute-done.48 = bf16[4,664,128]{2,1,0:T(8,128)(2,1)} collective-permute-done((bf16[4,664,128]{2,1,0:T(8,128)(2,1)}, bf16[4,664,128]{2,1,0:T(8,128)(2,1)}, u32[]{:S(2)}, u32[]{:S(2)}) %collective-permute-start.48) | collective-permute-done | bytes 679968 | tf_op jit(solution)/shard_map/ppermute | solution.py:222
  848.4 3.9 copy.133
  (490 shorter events, 256.6 us)
Async XLA Ops:
  7.2 80.3 %all-gather.15.cloned.1.call-start = ((), (), s32[]{:S(2)}) async-start(), calls=%async_computation.4 | async-start | bytes 3317760 | tf_op jit(solution)/shard_map/all_gather | solution.py:238
  11.8 122.4 %all-gather.17.cloned.1.call-start = ((), (), s32[]{:S(2)}) async-start(), calls=%async_computation.5 | async-start | bytes 3317760 | tf_op jit(solution)/shard_map/all_gather | solution.py:238
  11.9 32.5 %collective-permute-start = (bf16[288,2304]{1,0:T(8,128)(2,1)}, bf16[288,2304]{1,0:T(8,128)(2,1)}, u32[]{:S(2)}, u32[]{:S(2)}) collective-permute-start(bf16[288,2304]{1,0:T(8,128)(2,1)} %copy-done.75), channel_id=1, source_target_pairs={{0,4},{1,5},{2,6},{3,7},{4,0},{5,1},{6,2},{7,3},{8,12},{9,13},{10,... | collective-permute-start | bytes 3981320 | tf_op jit(solution)/shard_map/ppermute | solution.py:222
  15.0 29.4 %collective-permute-start.1 = (s32[1,8]{1,0:T(1,128)S(1)}, s32[1,8]{1,0:T(1,128)S(1)}, u32[]{:S(2)}, u32[]{:S(2)}) collective-permute-start(s32[1,8]{1,0:T(1,128)S(1)} %pad_add_fusion.1), channel_id=1, source_target_pairs={{0,4},{1,5},{2,6},{3,7},{4,0},{5,1},{6,2},{7,3},{8,12},{9,13},{10,... | collective-permute-start | bytes 104 | tf_op jit(solution)/shard_map/ppermute | solution.py:222
  15.0 205.7 %all-gather.19.cloned.1.call-start = ((), (), s32[]{:S(2)}) async-start(), calls=%async_computation.6 | async-start | bytes 4423680 | tf_op jit(solution)/shard_map/all_gather | solution.py:238
  44.4 43.1 %collective-permute-start.4 = (bf16[288,2304]{1,0:T(8,128)(2,1)}, bf16[288,2304]{1,0:T(8,128)(2,1)}, u32[]{:S(2)}, u32[]{:S(2)}) collective-permute-start(bf16[288,2304]{1,0:T(8,128)(2,1)} %collective-permute-done.refs_19_.refs_17_), channel_id=1, source_target_pairs={{0,2},{1,3},{2,0},{3,1},{4,6},{5,7},{6,4},{7,5},{8,10},{9,11},{10,... | collective-permute-start | bytes 3981320 | tf_op jit(solution)/shard_map/ppermute | solution.py:222
  46.1 41.3 %collective-permute-start.5 = (bf16[288,2304]{1,0:T(8,128)(2,1)}, bf16[288,2304]{1,0:T(8,128)(2,1)S(1)}, u32[]{:S(2)}, u32[]{:S(2)}) collective-permute-start(bf16[288,2304]{1,0:T(8,128)(2,1)} %collective-permute-done.refs_19_.refs_17_), channel_id=1, source_target_pairs={{0,1},{1,0},{2,3},{3,2},{4,5},{5,4},{6,7},{7,6},{8,9},{9,8},{10,11... | collective-permute-start | bytes 3981320 | tf_op jit(solution)/shard_map/ppermute | solution.py:222
  46.1 22.8 %collective-permute-start.2 = (bf16[288,1536]{1,0:T(8,128)(2,1)}, bf16[288,1536]{1,0:T(8,128)(2,1)}, u32[]{:S(2)}, u32[]{:S(2)}) collective-permute-start(bf16[288,1536]{1,0:T(8,128)(2,1)} %get-tuple-element.94), channel_id=1, source_target_pairs={{0,4},{1,5},{2,6},{3,7},{4,0},{5,1},{6,2},{7,3},{8,12},{9,13},{10,... | collective-permute-start | bytes 2654216 | tf_op jit(solution)/shard_map/ppermute | solution.py:222
  47.6 39.8 %collective-permute-start.3 = (bf16[288,1536]{1,0:T(8,128)(2,1)S(1)}, bf16[288,1536]{1,0:T(8,128)(2,1)}, u32[]{:S(2)}, u32[]{:S(2)}) collective-permute-start(bf16[288,1536]{1,0:T(8,128)(2,1)S(1)} %get-tuple-element.95), channel_id=1, source_target_pairs={{0,4},{1,5},{2,6},{3,7},{4,0},{5,1},{6,2},{7,3},{8,12},{9,13},{10,... | collective-permute-start | bytes 2654216 | tf_op jit(solution)/shard_map/ppermute | solution.py:222
  91.1 45.3 %collective-permute-start.7 = (bf16[3,288,1152]{2,1,0:T(8,128)(2,1)}, bf16[3,288,1152]{2,1,0:T(8,128)(2,1)}, u32[]{:S(2)}, u32[]{:S(2)}) collective-permute-start(bf16[3,288,1152]{2,1,0:T(8,128)(2,1)} %pad_maximum_fusion.7.refs_3_.refs_1_), channel_id=1, source_target_pairs={{0,2},{1,3},{2,0},{3,1},{4,6},{5,7},{6,4},{7,5},{8,10},{9,11},{10,... | collective-permute-start | bytes 5971976 | tf_op jit(solution)/shard_map/ppermute | solution.py:222
  91.4 56.1 %collective-permute-start.8 = (bf16[3,288,1152]{2,1,0:T(8,128)(2,1)}, bf16[3,288,1152]{2,1,0:T(8,128)(2,1)}, u32[]{:S(2)}, u32[]{:S(2)}) collective-permute-start(bf16[3,288,1152]{2,1,0:T(8,128)(2,1)} %pad_maximum_fusion.7.refs_3_.refs_1_), channel_id=1, source_target_pairs={{0,4},{1,5},{2,6},{3,7},{4,0},{5,1},{6,2},{7,3},{8,12},{9,13},{10,... | collective-permute-start | bytes 5971976 | tf_op jit(solution)/shard_map/ppermute | solution.py:222
  93.2 54.3 %collective-permute-start.9 = (bf16[3,288,1152]{2,1,0:T(8,128)(2,1)}, bf16[3,288,1152]{2,1,0:T(8,128)(2,1)}, u32[]{:S(2)}, u32[]{:S(2)}) collective-permute-start(bf16[3,288,1152]{2,1,0:T(8,128)(2,1)} %pad_maximum_fusion.7.refs_3_.refs_1_), channel_id=1, source_target_pairs={{0,1},{1,0},{2,3},{3,2},{4,5},{5,4},{6,7},{7,6},{8,9},{9,8},{10,11... | collective-permute-start | bytes 5971976 | tf_op jit(solution)/shard_map/ppermute | solution.py:222
  93.2 41.0 %collective-permute-start.10 = (bf16[288,2304]{1,0:T(8,128)(2,1)}, bf16[288,2304]{1,0:T(8,128)(2,1)}, u32[]{:S(2)}, u32[]{:S(2)}) collective-permute-start(bf16[288,2304]{1,0:T(8,128)(2,1)} %collective-permute-done.4.refs_21_.refs_19_), channel_id=1, source_target_pairs={{0,1},{1,0},{2,3},{3,2},{4,5},{5,4},{6,7},{7,6},{8,9},{9,8},{10,11... | collective-permute-start | bytes 3981320 | tf_op jit(solution)/shard_map/ppermute | solution.py:222
  108.7 53.4 %all-to-all-start = ((bf16[8,32,2304]{2,1,0:T(8,128)(2,1)}), bf16[8,32,2304]{2,1,0:T(8,128)(2,1)S(1)}, u32[]{:S(2)}, u32[]{:S(2)}) async-start(bf16[8,32,2304]{2,1,0:T(8,128)(2,1)} %bitcast.272), calls=%async_computation | async-start | bytes 2359296 | tf_op jit(solution)/shard_map/all_to_all | solution.py:970
  113.6 190.6 %all-gather.21.cloned.1.call-start = ((), (), s32[]{:S(2)}) async-start(), calls=%async_computation.7 | async-start | bytes 4423680 | tf_op jit(solution)/shard_map/all_gather | solution.py:238
  150.9 42.7 %collective-permute-start.11 = (bf16[3,288,1152]{2,1,0:T(8,128)(2,1)}, bf16[3,288,1152]{2,1,0:T(8,128)(2,1)}, u32[]{:S(2)}, u32[]{:S(2)}) collective-permute-start(bf16[3,288,1152]{2,1,0:T(8,128)(2,1)} %pad_maximum_fusion.8.refs_7_.refs_5_), channel_id=1, source_target_pairs={{0,2},{1,3},{2,0},{3,1},{4,6},{5,7},{6,4},{7,5},{8,10},{9,11},{10,... | collective-permute-start | bytes 5971976 | tf_op jit(solution)/shard_map/ppermute | solution.py:222
  152.6 42.1 %collective-permute-start.12 = (bf16[3,288,1152]{2,1,0:T(8,128)(2,1)}, bf16[3,288,1152]{2,1,0:T(8,128)(2,1)}, u32[]{:S(2)}, u32[]{:S(2)}) collective-permute-start(bf16[3,288,1152]{2,1,0:T(8,128)(2,1)} %pad_maximum_fusion.8.refs_7_.refs_5_), channel_id=1, source_target_pairs={{0,4},{1,5},{2,6},{3,7},{4,0},{5,1},{6,2},{7,3},{8,12},{9,13},{10,... | collective-permute-start | bytes 5971976 | tf_op jit(solution)/shard_map/ppermute | solution.py:222
  152.6 42.1 %collective-permute-start.13 = (bf16[3,288,1152]{2,1,0:T(8,128)(2,1)}, bf16[3,288,1152]{2,1,0:T(8,128)(2,1)}, u32[]{:S(2)}, u32[]{:S(2)}) collective-permute-start(bf16[3,288,1152]{2,1,0:T(8,128)(2,1)} %pad_maximum_fusion.8.refs_7_.refs_5_), channel_id=1, source_target_pairs={{0,1},{1,0},{2,3},{3,2},{4,5},{5,4},{6,7},{7,6},{8,9},{9,8},{10,11... | collective-permute-start | bytes 5971976 | tf_op jit(solution)/shard_map/ppermute | solution.py:222
  152.6 42.1 %collective-permute-start.14 = (bf16[3,288,1152]{2,1,0:T(8,128)(2,1)}, bf16[3,288,1152]{2,1,0:T(8,128)(2,1)}, u32[]{:S(2)}, u32[]{:S(2)}) collective-permute-start(bf16[3,288,1152]{2,1,0:T(8,128)(2,1)} %collective-permute-done.7.refs_5_.refs_3_), channel_id=1, source_target_pairs={{0,1},{1,0},{2,3},{3,2},{4,5},{5,4},{6,7},{7,6},{8,9},{9,8},{10,11... | collective-permute-start | bytes 5971976 | tf_op jit(solution)/shard_map/ppermute | solution.py:222
  153.1 41.6 %collective-permute-start.15 = (bf16[3,288,1152]{2,1,0:T(8,128)(2,1)}, bf16[3,288,1152]{2,1,0:T(8,128)(2,1)}, u32[]{:S(2)}, u32[]{:S(2)}) collective-permute-start(bf16[3,288,1152]{2,1,0:T(8,128)(2,1)} %collective-permute-done.8.refs_11_.refs_9_), channel_id=1, source_target_pairs={{0,1},{1,0},{2,3},{3,2},{4,5},{5,4},{6,7},{7,6},{8,9},{9,8},{10,11... | collective-permute-start | bytes 5971976 | tf_op jit(solution)/shard_map/ppermute | solution.py:222
  160.1 209.2 %all-gather.23.cloned.1.call-start = ((), (), s32[]{:S(2)}) async-start(), calls=%async_computation.8 | async-start | bytes 3440640 | tf_op jit(solution)/shard_map/all_gather | solution.py:238
  194.7 47.5 %collective-permute-start.17 = (bf16[3,288,1152]{2,1,0:T(8,128)(2,1)}, bf16[3,288,1152]{2,1,0:T(8,128)(2,1)}, u32[]{:S(2)}, u32[]{:S(2)}) collective-permute-start(bf16[3,288,1152]{2,1,0:T(8,128)(2,1)} %collective-permute-done.12.refs_15_.refs_13_), channel_id=1, source_target_pairs={{0,2},{1,3},{2,0},{3,1},{4,6},{5,7},{6,4},{7,5},{8,10},{9,11},{10,... | collective-permute-start | bytes 5971976 | tf_op jit(solution)/shard_map/ppermute | solution.py:222
  196.1 46.1 %collective-permute-start.19 = (bf16[3,288,1152]{2,1,0:T(8,128)(2,1)}, bf16[3,288,1152]{2,1,0:T(8,128)(2,1)}, u32[]{:S(2)}, u32[]{:S(2)}) collective-permute-start(bf16[3,288,1152]{2,1,0:T(8,128)(2,1)} %collective-permute-done.12.refs_15_.refs_13_), channel_id=1, source_target_pairs={{0,1},{1,0},{2,3},{3,2},{4,5},{5,4},{6,7},{7,6},{8,9},{9,8},{10,11... | collective-permute-start | bytes 5971976 | tf_op jit(solution)/shard_map/ppermute | solution.py:222
  196.1 46.1 %collective-permute-start.16 = (bf16[3,288,1152]{2,1,0:T(8,128)(2,1)}, bf16[3,288,1152]{2,1,0:T(8,128)(2,1)}, u32[]{:S(2)}, u32[]{:S(2)}) collective-permute-start(bf16[3,288,1152]{2,1,0:T(8,128)(2,1)} %collective-permute-done.7.refs_5_.refs_3_), channel_id=1, source_target_pairs={{0,4},{1,5},{2,6},{3,7},{4,0},{5,1},{6,2},{7,3},{8,12},{9,13},{10,... | collective-permute-start | bytes 5971976 | tf_op jit(solution)/shard_map/ppermute | solution.py:222
  196.1 46.1 %collective-permute-start.18 = (bf16[3,288,1152]{2,1,0:T(8,128)(2,1)}, bf16[3,288,1152]{2,1,0:T(8,128)(2,1)}, u32[]{:S(2)}, u32[]{:S(2)}) collective-permute-start(bf16[3,288,1152]{2,1,0:T(8,128)(2,1)} %collective-permute-done.11.refs_9_.refs_7_), channel_id=1, source_target_pairs={{0,1},{1,0},{2,3},{3,2},{4,5},{5,4},{6,7},{7,6},{8,9},{9,8},{10,11... | collective-permute-start | bytes 5971976 | tf_op jit(solution)/shard_map/ppermute | solution.py:222
  246.5 59.9 %collective-permute-start.23 = (bf16[3,288,1536]{2,1,0:T(8,128)(2,1)}, bf16[3,288,1536]{2,1,0:T(8,128)(2,1)}, u32[]{:S(2)}, u32[]{:S(2)}) collective-permute-start(bf16[3,288,1536]{2,1,0:T(8,128)(2,1)} %pad_maximum_fusion.2), channel_id=1, source_target_pairs={{0,2},{1,3},{2,0},{3,1},{4,6},{5,7},{6,4},{7,5},{8,10},{9,11},{10,... | collective-permute-start | bytes 7962632 | tf_op jit(solution)/shard_map/ppermute | solution.py:222
  252.1 21.6 %collective-permute-start.22 = (bf16[192,2304]{1,0:T(8,128)(2,1)}, bf16[192,2304]{1,0:T(8,128)(2,1)S(1)}, u32[]{:S(2)}, u32[]{:S(2)}) collective-permute-start(bf16[192,2304]{1,0:T(8,128)(2,1)} %pad_bitcast_fusion.1), channel_id=1, source_target_pairs={{0,4},{1,5},{2,6},{3,7},{4,0},{5,1},{6,2},{7,3},{8,12},{9,13},{10,... | collective-permute-start | bytes 2654216 | tf_op jit(solution)/shard_map/ppermute | solution.py:222
  277.5 59.5 %all-to-all-start.1 = ((bf16[8,32,2304]{2,1,0:T(8,128)(2,1)}), bf16[8,32,2304]{2,1,0:T(8,128)(2,1)}, u32[]{:S(2)}, u32[]{:S(2)}) async-start(bf16[8,32,2304]{2,1,0:T(8,128)(2,1)} %bitcast.273), calls=%async_computation.1 | async-start | bytes 2359296 | tf_op jit(solution)/shard_map/all_to_all | solution.py:995
  283.8 133.4 %all-gather.25.cloned.1.call-start = ((), (), s32[]{:S(2)}) async-start(), calls=%async_computation.9 | async-start | bytes 1966080 | tf_op jit(solution)/shard_map/all_gather | solution.py:238
  310.0 59.2 %collective-permute-start.25 = (bf16[3,288,1536]{2,1,0:T(8,128)(2,1)}, bf16[3,288,1536]{2,1,0:T(8,128)(2,1)}, u32[]{:S(2)}, u32[]{:S(2)}) collective-permute-start(bf16[3,288,1536]{2,1,0:T(8,128)(2,1)} %pad_maximum_fusion.3), channel_id=1, source_target_pairs={{0,2},{1,3},{2,0},{3,1},{4,6},{5,7},{6,4},{7,5},{8,10},{9,11},{10,... | collective-permute-start | bytes 7962632 | tf_op jit(solution)/shard_map/ppermute | solution.py:222
  326.9 28.2 %collective-permute-start.24 = (bf16[256,2304]{1,0:T(8,128)(2,1)S(1)}, bf16[256,2304]{1,0:T(8,128)(2,1)S(1)}, u32[]{:S(2)}, u32[]{:S(2)}) collective-permute-start(bf16[256,2304]{1,0:T(8,128)(2,1)S(1)} %multiply_convert_fusion.1.refs_8_), channel_id=1, source_target_pairs={{0,4},{1,5},{2,6},{3,7},{4,0},{5,1},{6,2},{7,3},{8,12},{9,13},{10,... | collective-permute-start | bytes 3538952 | tf_op jit(solution)/shard_map/ppermute | solution.py:222
  373.5 46.9 %collective-permute-start.27 = (bf16[3,192,1792]{2,1,0:T(8,128)(2,1)}, bf16[3,192,1792]{2,1,0:T(8,128)(2,1)}, u32[]{:S(2)}, u32[]{:S(2)}) collective-permute-start(bf16[3,192,1792]{2,1,0:T(8,128)(2,1)} %pad_maximum_fusion.6), channel_id=1, source_target_pairs={{0,2},{1,3},{2,0},{3,1},{4,6},{5,7},{6,4},{7,5},{8,10},{9,11},{10,... | collective-permute-start | bytes 6193160 | tf_op jit(solution)/shard_map/ppermute | solution.py:222
  385.3 32.0 %collective-permute-start.28 = (bf16[256,2432]{1,0:T(8,128)(2,1)}, bf16[256,2432]{1,0:T(8,128)(2,1)}, u32[]{:S(2)}, u32[]{:S(2)}) collective-permute-start(bf16[256,2432]{1,0:T(8,128)(2,1)} %pad_maximum_fusion.10), channel_id=1, source_target_pairs={{0,4},{1,5},{2,6},{3,7},{4,0},{5,1},{6,2},{7,3},{8,12},{9,13},{10,... | collective-permute-start | bytes 3735560 | tf_op jit(solution)/shard_map/ppermute | solution.py:222
  504.4 32.6 %collective-permute-start.31 = (bf16[256,2688]{1,0:T(8,128)(2,1)}, bf16[256,2688]{1,0:T(8,128)(2,1)}, u32[]{:S(2)}, u32[]{:S(2)}) collective-permute-start(bf16[256,2688]{1,0:T(8,128)(2,1)} %unstack.34), channel_id=1, source_target_pairs={{0,4},{1,5},{2,6},{3,7},{4,0},{5,1},{6,2},{7,3},{8,12},{9,13},{10,... | collective-permute-start | bytes 4128776 | tf_op jit(solution)/shard_map/ppermute | solution.py:222
  548.2 44.7 %collective-permute-start.33 = (bf16[256,2304]{1,0:T(8,128)(2,1)S(1)}, bf16[256,2304]{1,0:T(8,128)(2,1)S(1)}, u32[]{:S(2)}, u32[]{:S(2)}) collective-permute-start(bf16[256,2304]{1,0:T(8,128)(2,1)S(1)} %unstack.35), channel_id=1, source_target_pairs={{0,4},{1,5},{2,6},{3,7},{4,0},{5,1},{6,2},{7,3},{8,12},{9,13},{10,... | collective-permute-start | bytes 3538952 | tf_op jit(solution)/shard_map/ppermute | solution.py:222
  624.3 51.5 %all-to-all-start.2 = ((bf16[8,32,2304]{2,1,0:T(8,128)(2,1)}), bf16[8,32,2304]{2,1,0:T(8,128)(2,1)}, u32[]{:S(2)}, u32[]{:S(2)}) async-start(bf16[8,32,2304]{2,1,0:T(8,128)(2,1)} %bitcast.57), calls=%async_computation.2 | async-start | bytes 2359296 | tf_op jit(solution)/shard_map/all_to_all | solution.py:1153
  637.7 38.0 %collective-permute-start.35 = (bf16[4,2,664,128]{3,2,0,1:T(8,128)(2,1)}, bf16[4,2,664,128]{3,2,0,1:T(8,128)(2,1)}, u32[]{:S(2)}, u32[]{:S(2)}) collective-permute-start(bf16[4,2,664,128]{3,2,0,1:T(8,128)(2,1)} %bitcast.237), channel_id=1, source_target_pairs={{0,4},{1,5},{2,6},{3,7},{4,0},{5,1},{6,2},{7,3},{8,12},{9,13},{10,... | collective-permute-start | bytes 4079624 | tf_op jit(solution)/shard_map/ppermute | solution.py:222
  641.0 34.7 %collective-permute-start.36 = (bf16[4,2,672,128]{3,2,1,0:T(8,128)(2,1)}, bf16[4,2,672,128]{3,2,1,0:T(8,128)(2,1)}, u32[]{:S(2)}, u32[]{:S(2)}) collective-permute-start(bf16[4,2,672,128]{3,2,1,0:T(8,128)(2,1)} %dynamic-slice_bitcast_fusion), channel_id=1, source_target_pairs={{0,2},{1,3},{2,0},{3,1},{4,6},{5,7},{6,4},{7,5},{8,10},{9,11},{10,... | collective-permute-start | bytes 4128776 | tf_op jit(solution)/shard_map/ppermute | solution.py:222
  678.2 37.2 %all-to-all-start.3 = ((bf16[8,32,2304]{2,1,0:T(8,128)(2,1)}), bf16[8,32,2304]{2,1,0:T(8,128)(2,1)}, u32[]{:S(2)}, u32[]{:S(2)}) async-start(bf16[8,32,2304]{2,1,0:T(8,128)(2,1)} %bitcast.265), calls=%async_computation.3 | async-start | bytes 2359296 | tf_op jit(solution)/shard_map/all_to_all | solution.py:1161
  684.6 105.8 %all-gather.27.cloned.1.call-start = ((), (), s32[]{:S(2)}) async-start(), calls=%async_computation.10 | async-start | bytes 1710080 | tf_op jit(solution)/shard_map/all_gather | solution.py:238
  690.9 24.2 %collective-permute-start.38 = (bf16[4,672,128]{2,1,0:T(8,128)(2,1)}, bf16[4,672,128]{2,1,0:T(8,128)(2,1)S(1)}, u32[]{:S(2)}, u32[]{:S(2)}) collective-permute-start(bf16[4,672,128]{2,1,0:T(8,128)(2,1)} %dynamic-slice_bitcast_fusion.3), channel_id=1, source_target_pairs={{0,4},{1,5},{2,6},{3,7},{4,0},{5,1},{6,2},{7,3},{8,12},{9,13},{10,... | collective-permute-start | bytes 2064392 | tf_op jit(solution)/shard_map/ppermute | solution.py:222
  721.0 26.2 %collective-permute-start.40 = (bf16[1336,128]{1,0:T(8,128)(2,1)}, bf16[1336,128]{1,0:T(8,128)(2,1)S(1)}, u32[]{:S(2)}, u32[]{:S(2)}) collective-permute-start(bf16[1336,128]{1,0:T(8,128)(2,1)} %get-tuple-element.225), channel_id=1, source_target_pairs={{0,16},{1,17},{2,18},{3,19},{4,20},{5,21},{6,22},{7,23},{8,24},{9,... | collective-permute-start | bytes 1026056 | tf_op jit(solution)/shard_map/ppermute | solution.py:222
  721.0 26.2 %collective-permute-start.39 = (bf16[1336,128]{1,0:T(8,128)(2,1)}, bf16[1336,128]{1,0:T(8,128)(2,1)S(1)}, u32[]{:S(2)}, u32[]{:S(2)}) collective-permute-start(bf16[1336,128]{1,0:T(8,128)(2,1)} %get-tuple-element.226), channel_id=1, source_target_pairs={{0,8},{1,9},{2,10},{3,11},{4,12},{5,13},{6,14},{7,15},{8,16},{9,17... | collective-permute-start | bytes 1026056 | tf_op jit(solution)/shard_map/ppermute | solution.py:222
  794.0 21.1 %collective-permute-start.46 = (bf16[4,664,128]{2,1,0:T(8,128)(2,1)}, bf16[4,664,128]{2,1,0:T(8,128)(2,1)}, u32[]{:S(2)}, u32[]{:S(2)}) collective-permute-start(bf16[4,664,128]{2,1,0:T(8,128)(2,1)} %slice.245), channel_id=1, source_target_pairs={{0,4},{1,5},{2,6},{3,7},{4,0},{5,1},{6,2},{7,3},{8,12},{9,13},{10,... | collective-permute-start | bytes 2039816 | tf_op jit(solution)/shard_map/ppermute | solution.py:222
  797.7 29.4 %collective-permute-start.53 = (bf16[4,672,128]{2,1,0:T(8,128)(2,1)}, bf16[4,672,128]{2,1,0:T(8,128)(2,1)S(1)}, u32[]{:S(2)}, u32[]{:S(2)}) collective-permute-start(bf16[4,672,128]{2,1,0:T(8,128)(2,1)} %slice.246), channel_id=1, source_target_pairs={{0,4},{1,5},{2,6},{3,7},{4,0},{5,1},{6,2},{7,3},{8,12},{9,13},{10,... | collective-permute-start | bytes 2064392 | tf_op jit(solution)/shard_map/ppermute | solution.py:222
  810.5 30.5 %collective-permute-start.48 = (bf16[4,664,128]{2,1,0:T(8,128)(2,1)}, bf16[4,664,128]{2,1,0:T(8,128)(2,1)}, u32[]{:S(2)}, u32[]{:S(2)}) collective-permute-start(bf16[4,664,128]{2,1,0:T(8,128)(2,1)} %collective-permute-done.44), channel_id=1, source_target_pairs={{0,4},{1,5},{2,6},{3,7},{4,0},{5,1},{6,2},{7,3},{8,12},{9,13},{10,... | collective-permute-start | bytes 2039816 | tf_op jit(solution)/shard_map/ppermute | solution.py:222
  813.5 29.9 %collective-permute-start.51 = (bf16[4,672,128]{2,1,0:T(8,128)(2,1)}, bf16[4,672,128]{2,1,0:T(8,128)(2,1)S(1)}, u32[]{:S(2)}, u32[]{:S(2)}) collective-permute-start(bf16[4,672,128]{2,1,0:T(8,128)(2,1)} %slice.246), channel_id=1, source_target_pairs={{0,2},{1,3},{2,0},{3,1},{4,6},{5,7},{6,4},{7,5},{8,10},{9,11},{10,... | collective-permute-start | bytes 2064392 | tf_op jit(solution)/shard_map/ppermute | solution.py:222
  815.1 28.9 %collective-permute-start.47 = (bf16[4,664,128]{2,1,0:T(8,128)(2,1)}, bf16[4,664,128]{2,1,0:T(8,128)(2,1)S(1)}, u32[]{:S(2)}, u32[]{:S(2)}) collective-permute-start(bf16[4,664,128]{2,1,0:T(8,128)(2,1)} %collective-permute-done.46), channel_id=1, source_target_pairs={{0,1},{1,0},{2,3},{3,2},{4,5},{5,4},{6,7},{7,6},{8,9},{9,8},{10,11... | collective-permute-start | bytes 2039816 | tf_op jit(solution)/shard_map/ppermute | solution.py:222
  (130 other events, 1762.8 us)
Sparse Core Ops, SparseCore 0:
  11.9 58.0 all-gather.14
  72.2 61.9 all-gather.16
  136.3 74.7 all-gather.18
  212.6 68.5 all-gather.20
  282.6 75.4 all-gather.22
  359.5 37.3 all-gather.24
  755.5 34.8 all-gather.26

commit v5 on v4

--- a/solution.py
+++ b/solution.py
@@ -455,7 +455,9 @@
     pltpu.make_async_copy(part, part, sems.at[block]).wait()
 
 
-def feed_forward_back_kernel(line, where, gt, up, sent, down_lower, upper_gate, upper_up, *refs):
+def feed_forward_back_kernel(
+    line, where, gt, up, near, far, down_lower, upper_gate, upper_up, *refs
+):
     left, right, gate_pieces, up_pieces = refs[:3], refs[3], refs[4:7], refs[7:10]
     hidden, e_gate, e_up, keep, send, total, down, held, down_sems, sems = refs[10:]
     step = pl.program_id(0)
@@ -492,11 +494,11 @@
 
     tile_rows = down[pl.ds(pl.multiple_of(step * HIDDEN_TILE, HIDDEN_TILE), HIDDEN_TILE), :]
     count = keep.shape[0]
-    for n, sums in enumerate((keep, total)):
+    for n, (sums, sent) in enumerate(((keep, near), (total, far))):
         own = slice(n * count, (n + 1) * count)
         gate_value, up_value = gt[own, :], up[own, :]
-        dh = matrix_product_backward(sent[own, :width], tile_rows) + matrix_product_backward(
-            sent[own, width:], down_lower[...]
+        dh = matrix_product_backward(sent[:, :width], tile_rows) + matrix_product_backward(
+            sent[:, width:], down_lower[...]
         )
         sg = jax.nn.sigmoid(gate_value)
         act = gate_value * sg
@@ -583,9 +585,11 @@
     def back(self, gt, up, sent, lower, upper_gate, upper_up, gate_pieces, up_pieces):
         count, width = gt.shape
         half = count // 2
-        model = sent.shape[1] - ADAPTER_COLUMNS
+        near, far = sent
+        model = near.shape[1] - ADAPTER_COLUMNS
         sums = model + 3 * ADAPTER_COLUMNS
         if not self.kernels:
+            sent = jnp.concatenate([near, far], axis=0)
             down = self.down()
             gate, up_part = put_quarter(self.place, *gate_pieces), put_quarter(self.place, *up_pieces)
             sg = jax.nn.sigmoid(gt)
@@ -622,7 +626,8 @@
                 pl.BlockSpec(memory_space=pltpu.SMEM),
                 columns(count),
                 columns(count),
-                once(sent.shape),
+                once(near.shape),
+                once(far.shape),
                 pl.BlockSpec((HIDDEN_TILE, ADAPTER_COLUMNS), lambda i: (i, 0)),
                 columns(ADAPTER_COLUMNS),
                 columns(ADAPTER_COLUMNS),
@@ -638,7 +643,7 @@
             ],
             compiler_params=pltpu.CompilerParams(vmem_limit_bytes=60 << 20),
             cost_estimate=small_cost(6 * count * width * model),
-        )(self.where, gt, up, sent, lower, upper_gate, upper_up, *pieces)
+        )(self.where, gt, up, near, far, lower, upper_gate, upper_up, *pieces)
 
     def out(self, h, model):
         count, width = h.shape
@@ -661,7 +666,7 @@
                 pltpu.SemaphoreType.DMA((2 * self.place.line,)),
             ],
             compiler_params=pltpu.CompilerParams(vmem_limit_bytes=40 << 20),
-            cost_estimate=small_cost(2 * count * width * model),
+            cost_estimate=small_cost(64 * count * width * model),
         )(self.where, h, *self.left, self.right)
 
 
@@ -783,9 +788,10 @@
     return lax.dynamic_index_in_dim(values, index, axis, keepdims=False)
 
 
-def gradients_kernel(lower_rows, upper_rows, *refs):
+def gradients_kernel(*refs):
     n1, dz_qkv, z_qkv, e_qkv, o, dz_out, z_out, e_out = refs[:8]
-    n2, dz_gate, dz_up, z_down, e_down, _, flat, turned, staged, sems = refs[8:]
+    n2, dz_gate, dz_up, z_down, e_down = refs[8:13]
+    parts_given, (flat, turned, staged, sems, part_sems) = refs[13:16], refs[16:]
     lower = [(n1[...], dz_qkv[t]) for t in range(3)]
     lower += [(o[...], dz_out[...]), (n2[...], dz_gate[...]), (n2[...], dz_up[...])]
     upper = [(z_qkv[t], e_qkv[t]) for t in range(3)]
@@ -793,7 +799,16 @@
     rows = staged.shape[1]
     ranks = ADAPTER_COLUMNS
     parts = rows // ranks
-    starts = [lower_rows + rows * k for k in range(6)] + [upper_rows + rows * k for k in range(5)]
+    given = parts_given[0].shape[0]
+    second = 6 * rows + given
+    starts = [rows * k for k in range(6)] + [second + rows * k for k in range(5)]
+    places = (6 * rows, second + 5 * rows, second + 5 * rows + given)
+    moves = [
+        pltpu.make_async_copy(part, flat.at[pl.ds(start, given)], part_sems.at[n])
+        for n, (part, start) in enumerate(zip(parts_given, places))
+    ]
+    for move in moves:
+        move.start()
     copies = []
     for k, start in enumerate(starts):
         slot = k % 2
@@ -812,25 +827,28 @@
         copies[k].start()
     copies[-2].wait()
     copies[-1].wait()
-
-
-def model_gradients(operands, flat, lower_rows, upper_rows):
+    for move in moves:
+        move.wait()
+
+
+def model_gradients(operands, hidden_parts):
     held = pl.BlockSpec(memory_space=pltpu.VMEM)
     apart = pl.BlockSpec(memory_space=pl.ANY)
+    rows = 11 * MODEL_WIDTH + sum(part.shape[0] for part in hidden_parts)
     return pl.pallas_call(
-        functools.partial(gradients_kernel, lower_rows, upper_rows),
-        out_shape=jax.ShapeDtypeStruct(flat.shape, flat.dtype),
-        in_specs=[held] * len(operands) + [apart],
+        gradients_kernel,
+        out_shape=jax.ShapeDtypeStruct((rows, ADAPTER_COLUMNS), jnp.bfloat16),
+        in_specs=[held] * len(operands) + [apart] * len(hidden_parts),
         out_specs=apart,
         scratch_shapes=[
             pltpu.VMEM((MODEL_WIDTH, ADAPTER_COLUMNS), jnp.float32),
             pltpu.VMEM((2, MODEL_WIDTH, ADAPTER_COLUMNS), jnp.bfloat16),
             pltpu.SemaphoreType.DMA((2,)),
+            pltpu.SemaphoreType.DMA((len(hidden_parts),)),
         ],
-        input_output_aliases={len(operands): 0},
         compiler_params=pltpu.CompilerParams(vmem_limit_bytes=40 << 20),
         cost_estimate=pl.CostEstimate(flops=1 << 28, bytes_accessed=1 << 22, transcendentals=0),
-    )(*operands, flat)
+    )(*operands, *hidden_parts)
 
 
 def reduce_over_cores(place, flat, later):
@@ -933,7 +951,7 @@
 
     weights = (w_query, w_key, w_value, w_out)
     s, half = place.x * 2 + place.c, MODEL_WIDTH // 2
-    cut = MODEL_WIDTH - MODEL_WIDTH * 2 // 9
+    cut = MODEL_WIDTH - MODEL_WIDTH // 3
     stacked = jnp.stack(weights)
     mine = lax.dynamic_index_in_dim(stacked, s, 0, keepdims=False)
     first = place.all_z(mine[:, :half])
@@ -1053,12 +1071,14 @@
     up_pieces = (up_planes, up_rest, up_mates)
     up, z_up = forward.hidden(n2_all, choices, A_model[5], B_up, up_pieces)
     gt, up, left_mates, right_planes, sent_y = together(gt, up, left_mates, right_planes, sent_y)
-    sent = jnp.concatenate([sent, sent_y], axis=0)
-    sent = jnp.concatenate([sent, place.by_c(sent)], axis=0)
-    dz_down_all = sent[:, MODEL_WIDTH:]
+    sent_pair = jnp.concatenate([sent, sent_y], axis=0)
+    sent_mate = place.by_c(sent_pair)
+    dz_down_all = jnp.concatenate(
+        [sent_pair[:, MODEL_WIDTH:], sent_mate[:, MODEL_WIDTH:]], axis=0
+    )
     feed = FeedForward(place, (left_planes, left_rest, left_mates), right_planes)
     h, e_gate, e_up, keep, send = feed.back(
-        gt, up, sent, A_down, B_gate, B_up, gate_pieces, up_pieces
+        gt, up, (sent_pair, sent_mate), A_down, B_gate, B_up, gate_pieces, up_pieces
     )
     own_sum, other_sum = place.half_sum(keep, send)
     other_sum, h, e_gate, e_up = together(low(other_sum), h, e_gate, e_up)
@@ -1071,22 +1091,13 @@
         dA_down.reshape(dp, 1, padded, ADAPTER_COLUMNS)[:, :, :own_hidden],
         (0, place.q, 0, 0),
     )
-    lower_rows, upper_rows = 6 * MODEL_WIDTH, 5 * MODEL_WIDTH
-    hidden_rows_count = FEEDFORWARD_UNITS
-    flat = jnp.concatenate(
-        [
-            jnp.zeros((lower_rows, ADAPTER_COLUMNS), jnp.bfloat16),
-            dA_hidden.reshape(-1, ADAPTER_COLUMNS),
-            jnp.zeros((upper_rows, ADAPTER_COLUMNS), jnp.bfloat16),
-        ]
-        + [
-            spread_columns(
-                place, low(adapter_scale * outer_product_sum(z, e)), FEEDFORWARD_UNITS, dp, padded
-            ).reshape(-1, ADAPTER_COLUMNS)
-            for z, e in ((z_gate, e_gate), (z_up, e_up))
-        ]
-    )
-    got, y_send, flat = together(got, y_send, flat)
+    hidden_parts = [dA_hidden.reshape(-1, ADAPTER_COLUMNS)] + [
+        spread_columns(
+            place, low(adapter_scale * outer_product_sum(z, e)), FEEDFORWARD_UNITS, dp, padded
+        ).reshape(-1, ADAPTER_COLUMNS)
+        for z, e in ((z_gate, e_gate), (z_up, e_up))
+    ]
+    got, y_send, *hidden_parts = together(got, y_send, *hidden_parts)
     back_sum = own_sum + got.astype(jnp.float32)
     y_own, y_other = place.half_sum(y_keep, y_send)
     y_got = place.by_y(low(y_other))
@@ -1143,9 +1154,7 @@
             z_down,
             e_down,
         ),
-        flat,
-        0,
-        lower_rows + hidden_rows_count,
+        hidden_parts,
     )
     share = flat.shape[0] // (dp * shard)
     total, (e_qkv, dz_qkv, y) = reduce_over_cores(place, flat, (e_qkv, dz_qkv, y))

time: 871 us -> 851 us (0.977)
  waiting for transfers between devices: 342 us -> 326 us
    ppermute x57, waiting for transfers between devices: 283 us -> 235 us  [move(): return lax.ppermute(value, AXES, pairs)]
    all_gather x7, waiting for transfers between devices: 55.6 us -> 91.6 us  [all_z(): return lax.all_gather(block, 'dp', axis=0, axis_index_groups=groups)]
    unnamed x228 -> x252, local copies, waits for them, and re-layouts: 33.9 us -> 35.6 us
  transfers between devices with their start and end apart: 68 -> 68, of which waited for: 33 -> 29; matrix products, arithmetic and copies ran while one was open for 20% -> 19% of each run, Pallas kernels for 16% -> 17%
where the time goes in v5:
time: 851 us; the launch traced here: 844 us
  waiting for transfers between devices  326 us (38%)
  Pallas kernels  201 us (24%)
  local copies, waits for them, and re-layouts  135 us (16%)
  other arithmetic  74.6 us (9%)
  starting transfers between devices  69.1 us (8%)
  matrix products  21.1 us (2%)
  between operations  16.2 us (2%)
    ppermute x57, waiting for transfers between devices, move(): return lax.ppermute(value, AXES, pairs)  235 us
    all_gather x7, waiting for transfers between devices, all_z(): return lax.all_gather(block, 'dp', axis=0, axis_index_groups=groups)  91.6 us
    pallas_call x4, Pallas kernels, call(): pl.pallas_call(functools.partial(weights_kernel, place.line, first, count...  52.2 us
    ppermute x57, starting transfers between devices, move(): return lax.ppermute(value, AXES, pairs)  48.2 us
    pallas_call x1, Pallas kernels, back(): pl.pallas_call(functools.partial(feed_forward_back_kernel, self.place.lin...  46.6 us
    pallas_call x2, Pallas kernels, attention_call(): pl.pallas_call(kernel, grid=(ATTENTION_HEADS // 2,), out_shape=[jax.Shape...  45.2 us
    unnamed x252, local copies, waits for them, and re-layouts  35.6 us
    pallas_call x2, Pallas kernels, hidden(): pl.pallas_call(functools.partial(hidden_kernel, self.place.line), grid=(t...  25.9 us
  transfers between devices with their start and end apart: 68, of which 29 were waited for; matrix products, arithmetic and copies ran while one was open for 19% of the time, Pallas kernels for 17%

profile of v5, /device:TPU:0, one launch (start us, length us, event | category | flops | bytes accessed | tf_op | source)
XLA Modules:
  0.0 843.5 jit_solution(18063006781810277410)
XLA Ops:
  20.2 24.2 %collective-permute-done.1 = s32[1,8]{1,0:T(1,128)S(1)} collective-permute-done((s32[1,8]{1,0:T(1,128)S(1)}, s32[1,8]{1,0:T(1,128)S(1)}, u32[]{:S(2)}, u32[]{:S(2)}) %collective-permute-start.1) | collective-permute-done | bytes 64 | tf_op jit(solution)/shard_map/ppermute | solution.py:222
  48.1 4.0 fusion.64
  53.4 15.4 %collective-permute-done.2 = bf16[288,1536]{1,0:T(8,128)(2,1)S(1)} collective-permute-done((bf16[288,1536]{1,0:T(8,128)(2,1)}, bf16[288,1536]{1,0:T(8,128)(2,1)S(1)}, u32[]{:S(2)}, u32[]{:S(2)}) %collective-permute-start.2) | collective-permute-done | bytes 884768 | tf_op jit(solution)/shard_map/ppermute | solution.py:222
  68.7 18.6 %collective-permute-done.3 = bf16[288,1536]{1,0:T(8,128)(2,1)S(1)} collective-permute-done((bf16[288,1536]{1,0:T(8,128)(2,1)S(1)}, bf16[288,1536]{1,0:T(8,128)(2,1)S(1)}, u32[]{:S(2)}, u32[]{:S(2)}) %collective-permute-start.3) | collective-permute-done | bytes 884768 | tf_op jit(solution)/shard_map/ppermute | solution.py:222
  94.8 4.5 fusion.65
  99.3 4.9 all-to-all-start
  104.2 43.7 %all-gather.17.cloned.1.call-done = bf16[1152,1152]{1,0:T(8,128)(2,1)} async-done(((bf16[288,1152]{1,0:T(8,128)(2,1)}), bf16[1152,1152]{1,0:T(8,128)(2,1)}) %all-gather.17.cloned.1.call-update) | async-done | bytes 2654224 | tf_op jit(solution)/shard_map/all_gather | solution.py:238
  158.7 4.3 slice.193.value
  163.1 4.1 slice.195.value
  207.3 11.4 %all-gather.19.cloned.1.call-done = bf16[1152,1536]{1,0:T(8,128)(2,1)} async-done(((bf16[288,1536]{1,0:T(8,128)(2,1)}), bf16[1152,1536]{1,0:T(8,128)(2,1)}) %all-gather.19.cloned.1.call-update) | async-done | bytes 3538960 | tf_op jit(solution)/shard_map/all_gather | solution.py:238
  218.6 25.9 %collective-permute-done.16.refs_13_.refs_11_ = bf16[3,288,1152]{2,1,0:T(8,128)(2,1)} collective-permute-done((bf16[3,288,1152]{2,1,0:T(8,128)(2,1)}, bf16[3,288,1152]{2,1,0:T(8,128)(2,1)}, u32[]{:S(2)}, u32[]{:S(2)}) %collective-permute-start.16) | collective-permute-done | bytes 1990688 | tf_op jit(solution)/shard_map/ppermute | solution.py:222
  253.2 4.1 gather_fusion
  262.9 4.3 all-to-all-start.1
  267.7 17.5 %shard_map.212.lin = f32[3,256,2304]{2,1,0:T(8,128)} custom-call(s32[3]{0:T(128)} %pad_add_fusion.2.where, bf16[256,2304]{1,0:T(8,128)(2,1)} %copy-done.10, bf16[288,2304]{1,0:T(8,128)(2,1)} %refs_0_.7, bf16[288,2304]{1,0:T(8,128)(2,1)} %refs_1_.3, bf16[288,2304]{1,0:T(8,128)(2,1)} %refs_2_.3, bf16[3,288,1152]{2,1,0:T(8,128)(2,1)} %pad_maximum_fusion.5.refs_3_.refs_1_, ...), custom_call_target="tpu_custom_call" | custom-call | flops 509607936 | bytes 1990656 | tf_op jit(solution)/shard_map/pallas_call | solution.py:323
  289.8 18.7 %shard_map.213 = (bf16[3,256,2304]{2,1,0:T(8,128)(2,1)}, bf16[256,2304]{1,0:T(8,128)(2,1)S(1)}) custom-call(f32[3,256,2304]{2,1,0:T(8,128)} %shard_map.212.lin, bf16[3,256,128]{2,1,0:T(8,128)(2,1)S(1)} %copy-done.49, bf16[3,128,2304]{2,1,0:T(8,128)(2,1)S(1)} %slice.206.up, f32[256,128]{1,0:T(8,128)S(1)} %copy-done.45, f32[256,128]{1,0:T(8,128)S(1)} %copy-done.43, ...), custom_call_target="tpu_custom_call" | custom-call | flops 75497472 | bytes 884736 | tf_op jit(solution)/shard_map/pallas_call | solution.py:176
  318.3 8.9 %shard_map.214 = f32[1,256,2304]{2,1,0:T(8,128)} custom-call(s32[3]{0:T(128)} %pad_add_fusion.2.where, bf16[256,2304]{1,0:T(8,128)(2,1)} %copy-done.25, bf16[288,2304]{1,0:T(8,128)(2,1)} %refs_0_.6, bf16[3,288,1152]{2,1,0:T(8,128)(2,1)} %pad_maximum_fusion.5.refs_3_.refs_1_, bf16[3,288,1152]{2,1,0:T(8,128)(2,1)} %collective-permute-done.9.refs_4_.refs_2_, ...), custom_call_target="tpu_custom_call" | custom-call | flops 169869312 | bytes 663552 | tf_op jit(solution)/shard_map/pallas_call | solution.py:323
  327.2 3.6 multiply_reduce_fusion.1
  338.6 21.9 %collective-permute-done.24 = bf16[256,2304]{1,0:T(8,128)(2,1)S(1)} collective-permute-done((bf16[256,2304]{1,0:T(8,128)(2,1)S(1)}, bf16[256,2304]{1,0:T(8,128)(2,1)S(1)}, u32[]{:S(2)}, u32[]{:S(2)}) %collective-permute-start.24) | collective-permute-done | bytes 1179680 | tf_op jit(solution)/shard_map/ppermute | solution.py:222
  360.5 12.7 %collective-permute-done.25.mates.refs_9_ = bf16[3,288,1536]{2,1,0:T(8,128)(2,1)} collective-permute-done((bf16[3,288,1536]{2,1,0:T(8,128)(2,1)}, bf16[3,288,1536]{2,1,0:T(8,128)(2,1)}, u32[]{:S(2)}, u32[]{:S(2)}) %collective-permute-start.25) | collective-permute-done | bytes 2654240 | tf_op jit(solution)/shard_map/ppermute | solution.py:222
  379.0 4.1 gather_fusion.1
  390.9 12.8 %shard_map.215 = (f32[1024,1536]{1,0:T(8,128)}, bf16[1024,128]{1,0:T(8,128)(2,1)S(1)}) custom-call(s32[3]{0:T(128)S(1)} %pad_add_fusion.4.where, bf16[1024,2304]{1,0:T(8,128)(2,1)S(1)} %pad_maximum_fusion.values, f32[1024,128]{1,0:T(8,128)S(1)} %copy-done.27, bf16[2304,128]{1,0:T(8,128)(2,1)S(1)} %copy-done.31, bf16[128,1536]{1,0:T(8,128)(2,1)S(1)} %copy-done.40, ...), custom_call_target="tpu_custom_call" | custom-call | flops 452984832 | bytes 884736 | tf_op jit(solution)/shard_map/pallas_call | solution.py:562
  404.5 13.1 %shard_map.216 = (f32[1024,1536]{1,0:T(8,128)}, bf16[1024,128]{1,0:T(8,128)(2,1)S(1)}) custom-call(s32[3]{0:T(128)S(1)} %pad_add_fusion.4.where, bf16[1024,2304]{1,0:T(8,128)(2,1)S(1)} %pad_maximum_fusion.values, f32[1024,128]{1,0:T(8,128)S(1)} %copy-done.27, bf16[2304,128]{1,0:T(8,128)(2,1)S(1)} %copy-done.30, bf16[128,1536]{1,0:T(8,128)(2,1)S(1)} %copy-done.42, ...), custom_call_target="tpu_custom_call" | custom-call | flops 452984832 | bytes 884736 | tf_op jit(solution)/shard_map/pallas_call | solution.py:562
  426.6 46.6 %shard_map.217 = (bf16[1024,1536]{1,0:T(8,128)(2,1)}, bf16[1024,1536]{1,0:T(8,128)(2,1)}, bf16[1024,1536]{1,0:T(8,128)(2,1)}, f32[512,2688]{1,0:T(8,128)}, bf16[512,2688]{1,0:T(8,128)(2,1)}) custom-call(s32[3]{0:T(128)} %copy-done.57, f32[1024,1536]{1,0:T(8,128)} %get-tuple-element.146.gt, f32[1024,1536]{1,0:T(8,128)} %get-tuple-element.147.up, ...), custom_call_target="tpu_custom_call" | custom-call | flops 1358954496 | bytes 2654208 | tf_op jit(solution)/shard_map/pallas_call | solution.py:617
  474.3 4.3 collective-permute-done.30
  490.6 3.7 reshape.409.refs_13_
  499.8 4.3 reshape.411.refs_15_
  509.1 11.4 %shard_map.218 = (f32[512,2304]{1,0:T(8,128)}, bf16[512,2304]{1,0:T(8,128)(2,1)}) custom-call(s32[3]{0:T(128)S(1)} %copy-done.58, bf16[1024,1536]{1,0:T(8,128)(2,1)S(1)} %copy-done.60, bf16[4,192,1536]{2,1,0:T(8,128)(2,1)S(1)} %bitcast.247, bf16[192,1536]{1,0:T(8,128)(2,1)S(1)} %copy-done.36, bf16[3,192,1536]{2,1,0:T(8,128)(2,1)S(1)} %copy-done.38, ...), custom_call_target="tpu_custom_call" | custom-call | flops 14495514624 | bytes 28311552 | tf_op jit(solution)/shard_map/pallas_call | solution.py:655
  532.5 4.5 multiply_convert_fusion
  537.0 8.9 %shard_map.221.lin = f32[256,2304]{1,0:T(8,128)} custom-call(s32[3]{0:T(128)} %pad_add_fusion.2.where, bf16[1,256,2304]{2,1,0:T(8,128)(2,1)} %bitcast.244, bf16[288,2304]{1,0:T(8,128)(2,1)} %refs_0_.6, bf16[3,288,1152]{2,1,0:T(8,128)(2,1)} %pad_maximum_fusion.5.refs_3_.refs_1_, bf16[3,288,1152]{2,1,0:T(8,128)(2,1)} %collective-permute-done.9.refs_4_.refs_2_, ...), custom_call_target="tpu_custom_call" | custom-call | flops 169869312 | bytes 663552 | tf_op jit(solution)/shard_map/pallas_call | solution.py:323
  548.1 26.5 %shard_map.222.refs_3_.values = bf16[3,256,2304]{2,1,0:T(8,128)(2,1)} custom-call(bf16[3,256,2304]{2,1,0:T(8,128)(2,1)} %get-tuple-element.127.qkv, f32[256,2304]{1,0:T(8,128)S(1)} %copy-done.12, bf16[256,128]{1,0:T(8,128)(2,1)S(1)} %fusion.37.dz.refs_5_, bf16[2304,128]{1,0:T(8,128)(2,1)S(1)} %copy-done.32, f32[256,128]{1,0:T(8,128)S(1)} %copy-done.46, ...), custom_call_target="tpu_custom_call" | custom-call | flops 75497472 | bytes 884736 | tf_op jit(solution)/shard_map/pallas_call | solution.py:176
  579.9 9.7 %shard_map.223 = bf16[42624,128]{1,0:T(8,128)(2,1)} custom-call(bf16[256,2304]{1,0:T(8,128)(2,1)S(1)} %copy-done.11, bf16[3,256,128]{2,1,0:T(8,128)(2,1)S(1)} %fusion.26.refs_1_, bf16[3,256,128]{2,1,0:T(8,128)(2,1)S(1)} %copy-done.50, bf16[3,256,2304]{2,1,0:T(8,128)(2,1)S(1)} %copy-done, bf16[256,2304]{1,0:T(8,128)(2,1)S(1)} %copy-done.26, ...), custom_call_target="tpu_custom_call" | custom-call | flops 268435456 | bytes 4194304 | tf_op jit(solution)/shard_map/pallas_call | solution.py:838
  589.6 5.4 constant_dynamic-slice_fusion.2
  600.3 4.1 collective-permute-done.34
  606.8 4.5 all-to-all-start.2
  611.3 5.6 add_convert_fusion
  623.9 17.0 %shard_map.224 = f32[256,2304]{1,0:T(8,128)} custom-call(s32[3]{0:T(128)} %pad_add_fusion.2.where, bf16[3,256,2304]{2,1,0:T(8,128)(2,1)} %shard_map.222.refs_3_.values, bf16[288,2304]{1,0:T(8,128)(2,1)} %refs_0_.7, bf16[288,2304]{1,0:T(8,128)(2,1)} %refs_1_.3, bf16[288,2304]{1,0:T(8,128)(2,1)} %refs_2_.3, ...), custom_call_target="tpu_custom_call" | custom-call | flops 509607936 | bytes 1990656 | tf_op jit(solution)/shard_map/pallas_call | solution.py:323
  644.9 12.2 %collective-permute-done.35 = bf16[4,2,664,128]{3,2,0,1:T(8,128)(2,1)} collective-permute-done((bf16[4,2,664,128]{3,2,0,1:T(8,128)(2,1)}, bf16[4,2,664,128]{3,2,0,1:T(8,128)(2,1)}, u32[]{:S(2)}, u32[]{:S(2)}) %collective-permute-start.35) | collective-permute-done | bytes 1359904 | tf_op jit(solution)/shard_map/ppermute | solution.py:222
  659.6 6.6 all-to-all-start.3
  674.2 10.9 %collective-permute-done.37 = bf16[4,664,128]{2,1,0:T(8,128)(2,1)} collective-permute-done((bf16[4,664,128]{2,1,0:T(8,128)(2,1)S(1)}, bf16[4,664,128]{2,1,0:T(8,128)(2,1)}, u32[]{:S(2)}, u32[]{:S(2)}) %collective-permute-start.37) | collective-permute-done | bytes 679968 | tf_op jit(solution)/shard_map/ppermute | solution.py:222
  686.6 9.9 %collective-permute-done.38 = bf16[4,672,128]{2,1,0:T(8,128)(2,1)S(1)} collective-permute-done((bf16[4,672,128]{2,1,0:T(8,128)(2,1)}, bf16[4,672,128]{2,1,0:T(8,128)(2,1)S(1)}, u32[]{:S(2)}, u32[]{:S(2)}) %collective-permute-start.38) | collective-permute-done | bytes 688160 | tf_op jit(solution)/shard_map/ppermute | solution.py:222
  697.9 4.6 collective-permute-start.41
  703.2 8.0 collective-permute-done.41
  711.3 17.6 %collective-permute-done.40 = bf16[1336,128]{1,0:T(8,128)(2,1)S(1)} collective-permute-done((bf16[1336,128]{1,0:T(8,128)(2,1)}, bf16[1336,128]{1,0:T(8,128)(2,1)S(1)}, u32[]{:S(2)}, u32[]{:S(2)}) %collective-permute-start.40) | collective-permute-done | bytes 342048 | tf_op jit(solution)/shard_map/ppermute | solution.py:222
  737.0 34.7 %all-gather.27.cloned.1.call-done = bf16[5344,128]{1,0:T(8,128)(2,1)} async-done(((bf16[1336,128]{1,0:T(8,128)(2,1)}), bf16[5344,128]{1,0:T(8,128)(2,1)}) %all-gather.27.cloned.1.call-update) | async-done | bytes 1368080 | tf_op jit(solution)/shard_map/all_gather | solution.py:238
  779.5 12.3 %collective-permute-done.44 = bf16[4,664,128]{2,1,0:T(8,128)(2,1)} collective-permute-done((bf16[4,664,128]{2,1,0:T(8,128)(2,1)}, bf16[4,664,128]{2,1,0:T(8,128)(2,1)}, u32[]{:S(2)}, u32[]{:S(2)}) %collective-permute-start.44) | collective-permute-done | bytes 679968 | tf_op jit(solution)/shard_map/ppermute | solution.py:222
  798.7 9.6 %collective-permute-done.53 = bf16[4,672,128]{2,1,0:T(8,128)(2,1)S(1)} collective-permute-done((bf16[4,672,128]{2,1,0:T(8,128)(2,1)}, bf16[4,672,128]{2,1,0:T(8,128)(2,1)S(1)}, u32[]{:S(2)}, u32[]{:S(2)}) %collective-permute-start.53) | collective-permute-done | bytes 688160 | tf_op jit(solution)/shard_map/ppermute | solution.py:222
  808.9 13.4 %collective-permute-done.48 = bf16[4,664,128]{2,1,0:T(8,128)(2,1)} collective-permute-done((bf16[4,664,128]{2,1,0:T(8,128)(2,1)}, bf16[4,664,128]{2,1,0:T(8,128)(2,1)}, u32[]{:S(2)}, u32[]{:S(2)}) %collective-permute-start.48) | collective-permute-done | bytes 679968 | tf_op jit(solution)/shard_map/ppermute | solution.py:222
  829.6 3.9 copy.127
  (515 shorter events, 244.8 us)
Async XLA Ops:
  7.2 80.2 %all-gather.15.cloned.1.call-start = ((), (), s32[]{:S(2)}) async-start(), calls=%async_computation.4 | async-start | bytes 3317760 | tf_op jit(solution)/shard_map/all_gather | solution.py:238
  11.8 136.1 %all-gather.17.cloned.1.call-start = ((), (), s32[]{:S(2)}) async-start(), calls=%async_computation.5 | async-start | bytes 3317760 | tf_op jit(solution)/shard_map/all_gather | solution.py:238
  11.9 32.5 %collective-permute-start = (bf16[288,2304]{1,0:T(8,128)(2,1)}, bf16[288,2304]{1,0:T(8,128)(2,1)}, u32[]{:S(2)}, u32[]{:S(2)}) collective-permute-start(bf16[288,2304]{1,0:T(8,128)(2,1)} %copy-done.80), channel_id=1, source_target_pairs={{0,4},{1,5},{2,6},{3,7},{4,0},{5,1},{6,2},{7,3},{8,12},{9,13},{10,... | collective-permute-start | bytes 3981320 | tf_op jit(solution)/shard_map/ppermute | solution.py:222
  15.0 29.4 %collective-permute-start.1 = (s32[1,8]{1,0:T(1,128)S(1)}, s32[1,8]{1,0:T(1,128)S(1)}, u32[]{:S(2)}, u32[]{:S(2)}) collective-permute-start(s32[1,8]{1,0:T(1,128)S(1)} %pad_add_fusion.1), channel_id=1, source_target_pairs={{0,4},{1,5},{2,6},{3,7},{4,0},{5,1},{6,2},{7,3},{8,12},{9,13},{10,... | collective-permute-start | bytes 104 | tf_op jit(solution)/shard_map/ppermute | solution.py:222
  15.0 203.6 %all-gather.19.cloned.1.call-start = ((), (), s32[]{:S(2)}) async-start(), calls=%async_computation.6 | async-start | bytes 4423680 | tf_op jit(solution)/shard_map/all_gather | solution.py:238
  44.4 43.0 %collective-permute-start.4 = (bf16[288,2304]{1,0:T(8,128)(2,1)}, bf16[288,2304]{1,0:T(8,128)(2,1)}, u32[]{:S(2)}, u32[]{:S(2)}) collective-permute-start(bf16[288,2304]{1,0:T(8,128)(2,1)} %collective-permute-done.refs_19_.refs_17_), channel_id=1, source_target_pairs={{0,2},{1,3},{2,0},{3,1},{4,6},{5,7},{6,4},{7,5},{8,10},{9,11},{10,... | collective-permute-start | bytes 3981320 | tf_op jit(solution)/shard_map/ppermute | solution.py:222
  46.1 41.2 %collective-permute-start.5 = (bf16[288,2304]{1,0:T(8,128)(2,1)}, bf16[288,2304]{1,0:T(8,128)(2,1)}, u32[]{:S(2)}, u32[]{:S(2)}) collective-permute-start(bf16[288,2304]{1,0:T(8,128)(2,1)} %collective-permute-done.refs_19_.refs_17_), channel_id=1, source_target_pairs={{0,1},{1,0},{2,3},{3,2},{4,5},{5,4},{6,7},{7,6},{8,9},{9,8},{10,11... | collective-permute-start | bytes 3981320 | tf_op jit(solution)/shard_map/ppermute | solution.py:222
  47.6 39.7 %collective-permute-start.3 = (bf16[288,1536]{1,0:T(8,128)(2,1)S(1)}, bf16[288,1536]{1,0:T(8,128)(2,1)S(1)}, u32[]{:S(2)}, u32[]{:S(2)}) collective-permute-start(bf16[288,1536]{1,0:T(8,128)(2,1)S(1)} %get-tuple-element.97), channel_id=1, source_target_pairs={{0,4},{1,5},{2,6},{3,7},{4,0},{5,1},{6,2},{7,3},{8,12},{9,13},{10,... | collective-permute-start | bytes 2654216 | tf_op jit(solution)/shard_map/ppermute | solution.py:222
  90.9 57.1 %collective-permute-start.7 = (bf16[3,288,1152]{2,1,0:T(8,128)(2,1)}, bf16[3,288,1152]{2,1,0:T(8,128)(2,1)}, u32[]{:S(2)}, u32[]{:S(2)}) collective-permute-start(bf16[3,288,1152]{2,1,0:T(8,128)(2,1)} %pad_maximum_fusion.5.refs_3_.refs_1_), channel_id=1, source_target_pairs={{0,2},{1,3},{2,0},{3,1},{4,6},{5,7},{6,4},{7,5},{8,10},{9,11},{10,... | collective-permute-start | bytes 5971976 | tf_op jit(solution)/shard_map/ppermute | solution.py:222
  91.2 56.8 %collective-permute-start.8 = (bf16[3,288,1152]{2,1,0:T(8,128)(2,1)}, bf16[3,288,1152]{2,1,0:T(8,128)(2,1)}, u32[]{:S(2)}, u32[]{:S(2)}) collective-permute-start(bf16[3,288,1152]{2,1,0:T(8,128)(2,1)} %pad_maximum_fusion.5.refs_3_.refs_1_), channel_id=1, source_target_pairs={{0,4},{1,5},{2,6},{3,7},{4,0},{5,1},{6,2},{7,3},{8,12},{9,13},{10,... | collective-permute-start | bytes 5971976 | tf_op jit(solution)/shard_map/ppermute | solution.py:222
  92.9 55.0 %collective-permute-start.9 = (bf16[3,288,1152]{2,1,0:T(8,128)(2,1)}, bf16[3,288,1152]{2,1,0:T(8,128)(2,1)}, u32[]{:S(2)}, u32[]{:S(2)}) collective-permute-start(bf16[3,288,1152]{2,1,0:T(8,128)(2,1)} %pad_maximum_fusion.5.refs_3_.refs_1_), channel_id=1, source_target_pairs={{0,1},{1,0},{2,3},{3,2},{4,5},{5,4},{6,7},{7,6},{8,9},{9,8},{10,11... | collective-permute-start | bytes 5971976 | tf_op jit(solution)/shard_map/ppermute | solution.py:222
  92.9 55.0 %collective-permute-start.10 = (bf16[288,2304]{1,0:T(8,128)(2,1)}, bf16[288,2304]{1,0:T(8,128)(2,1)S(1)}, u32[]{:S(2)}, u32[]{:S(2)}) collective-permute-start(bf16[288,2304]{1,0:T(8,128)(2,1)} %collective-permute-done.4.refs_21_.refs_19_), channel_id=1, source_target_pairs={{0,1},{1,0},{2,3},{3,2},{4,5},{5,4},{6,7},{7,6},{8,9},{9,8},{10,11... | collective-permute-start | bytes 3981320 | tf_op jit(solution)/shard_map/ppermute | solution.py:222
  99.3 94.3 %all-to-all-start = ((bf16[8,32,2304]{2,1,0:T(8,128)(2,1)}), bf16[8,32,2304]{2,1,0:T(8,128)(2,1)}, u32[]{:S(2)}, u32[]{:S(2)}) async-start(bf16[8,32,2304]{2,1,0:T(8,128)(2,1)} %bitcast.271), calls=%async_computation | async-start | bytes 2359296 | tf_op jit(solution)/shard_map/all_to_all | solution.py:988
  104.2 206.2 %all-gather.21.cloned.1.call-start = ((), (), s32[]{:S(2)}) async-start(), calls=%async_computation.7 | async-start | bytes 4423680 | tf_op jit(solution)/shard_map/all_gather | solution.py:238
  151.7 45.0 %collective-permute-start.11 = (bf16[3,288,1152]{2,1,0:T(8,128)(2,1)}, bf16[3,288,1152]{2,1,0:T(8,128)(2,1)}, u32[]{:S(2)}, u32[]{:S(2)}) collective-permute-start(bf16[3,288,1152]{2,1,0:T(8,128)(2,1)} %pad_maximum_fusion.6.refs_7_.refs_5_), channel_id=1, source_target_pairs={{0,2},{1,3},{2,0},{3,1},{4,6},{5,7},{6,4},{7,5},{8,10},{9,11},{10,... | collective-permute-start | bytes 5971976 | tf_op jit(solution)/shard_map/ppermute | solution.py:222
  153.1 44.7 %collective-permute-start.12 = (bf16[3,288,1152]{2,1,0:T(8,128)(2,1)}, bf16[3,288,1152]{2,1,0:T(8,128)(2,1)}, u32[]{:S(2)}, u32[]{:S(2)}) collective-permute-start(bf16[3,288,1152]{2,1,0:T(8,128)(2,1)} %pad_maximum_fusion.6.refs_7_.refs_5_), channel_id=1, source_target_pairs={{0,4},{1,5},{2,6},{3,7},{4,0},{5,1},{6,2},{7,3},{8,12},{9,13},{10,... | collective-permute-start | bytes 5971976 | tf_op jit(solution)/shard_map/ppermute | solution.py:222
  154.7 43.1 %collective-permute-start.13 = (bf16[3,288,1152]{2,1,0:T(8,128)(2,1)}, bf16[3,288,1152]{2,1,0:T(8,128)(2,1)}, u32[]{:S(2)}, u32[]{:S(2)}) collective-permute-start(bf16[3,288,1152]{2,1,0:T(8,128)(2,1)} %pad_maximum_fusion.6.refs_7_.refs_5_), channel_id=1, source_target_pairs={{0,1},{1,0},{2,3},{3,2},{4,5},{5,4},{6,7},{7,6},{8,9},{9,8},{10,11... | collective-permute-start | bytes 5971976 | tf_op jit(solution)/shard_map/ppermute | solution.py:222
  154.7 43.1 %collective-permute-start.14 = (bf16[3,288,1152]{2,1,0:T(8,128)(2,1)}, bf16[3,288,1152]{2,1,0:T(8,128)(2,1)}, u32[]{:S(2)}, u32[]{:S(2)}) collective-permute-start(bf16[3,288,1152]{2,1,0:T(8,128)(2,1)} %collective-permute-done.7.refs_5_.refs_3_), channel_id=1, source_target_pairs={{0,1},{1,0},{2,3},{3,2},{4,5},{5,4},{6,7},{7,6},{8,9},{9,8},{10,11... | collective-permute-start | bytes 5971976 | tf_op jit(solution)/shard_map/ppermute | solution.py:222
  155.2 42.6 %collective-permute-start.15 = (bf16[3,288,1152]{2,1,0:T(8,128)(2,1)}, bf16[3,288,1152]{2,1,0:T(8,128)(2,1)}, u32[]{:S(2)}, u32[]{:S(2)}) collective-permute-start(bf16[3,288,1152]{2,1,0:T(8,128)(2,1)} %collective-permute-done.8.refs_11_.refs_9_), channel_id=1, source_target_pairs={{0,1},{1,0},{2,3},{3,2},{4,5},{5,4},{6,7},{7,6},{8,9},{9,8},{10,11... | collective-permute-start | bytes 5971976 | tf_op jit(solution)/shard_map/ppermute | solution.py:222
  197.8 46.7 %collective-permute-start.17 = (bf16[3,288,1152]{2,1,0:T(8,128)(2,1)}, bf16[3,288,1152]{2,1,0:T(8,128)(2,1)}, u32[]{:S(2)}, u32[]{:S(2)}) collective-permute-start(bf16[3,288,1152]{2,1,0:T(8,128)(2,1)} %collective-permute-done.12.refs_15_.refs_13_), channel_id=1, source_target_pairs={{0,2},{1,3},{2,0},{3,1},{4,6},{5,7},{6,4},{7,5},{8,10},{9,11},{10,... | collective-permute-start | bytes 5971976 | tf_op jit(solution)/shard_map/ppermute | solution.py:222
  198.4 46.1 %collective-permute-start.19 = (bf16[3,288,1152]{2,1,0:T(8,128)(2,1)}, bf16[3,288,1152]{2,1,0:T(8,128)(2,1)}, u32[]{:S(2)}, u32[]{:S(2)}) collective-permute-start(bf16[3,288,1152]{2,1,0:T(8,128)(2,1)} %collective-permute-done.12.refs_15_.refs_13_), channel_id=1, source_target_pairs={{0,1},{1,0},{2,3},{3,2},{4,5},{5,4},{6,7},{7,6},{8,9},{9,8},{10,11... | collective-permute-start | bytes 5971976 | tf_op jit(solution)/shard_map/ppermute | solution.py:222
  198.4 46.1 %collective-permute-start.16 = (bf16[3,288,1152]{2,1,0:T(8,128)(2,1)}, bf16[3,288,1152]{2,1,0:T(8,128)(2,1)}, u32[]{:S(2)}, u32[]{:S(2)}) collective-permute-start(bf16[3,288,1152]{2,1,0:T(8,128)(2,1)} %collective-permute-done.7.refs_5_.refs_3_), channel_id=1, source_target_pairs={{0,4},{1,5},{2,6},{3,7},{4,0},{5,1},{6,2},{7,3},{8,12},{9,13},{10,... | collective-permute-start | bytes 5971976 | tf_op jit(solution)/shard_map/ppermute | solution.py:222
  200.0 44.5 %collective-permute-start.18 = (bf16[3,288,1152]{2,1,0:T(8,128)(2,1)}, bf16[3,288,1152]{2,1,0:T(8,128)(2,1)}, u32[]{:S(2)}, u32[]{:S(2)}) collective-permute-start(bf16[3,288,1152]{2,1,0:T(8,128)(2,1)} %collective-permute-done.11.refs_9_.refs_7_), channel_id=1, source_target_pairs={{0,1},{1,0},{2,3},{3,2},{4,5},{5,4},{6,7},{7,6},{8,9},{9,8},{10,11... | collective-permute-start | bytes 5971976 | tf_op jit(solution)/shard_map/ppermute | solution.py:222
  244.5 23.2 %collective-permute-start.20 = (bf16[3,288,1152]{2,1,0:T(8,128)(2,1)}, bf16[3,288,1152]{2,1,0:T(8,128)(2,1)}, u32[]{:S(2)}, u32[]{:S(2)}) collective-permute-start(bf16[3,288,1152]{2,1,0:T(8,128)(2,1)} %collective-permute-done.16.refs_13_.refs_11_), channel_id=1, source_target_pairs={{0,1},{1,0},{2,3},{3,2},{4,5},{5,4},{6,7},{7,6},{8,9},{9,8},{10,11... | collective-permute-start | bytes 5971976 | tf_op jit(solution)/shard_map/ppermute | solution.py:222
  244.6 23.1 %collective-permute-start.21 = (bf16[3,288,1152]{2,1,0:T(8,128)(2,1)}, bf16[3,288,1152]{2,1,0:T(8,128)(2,1)}, u32[]{:S(2)}, u32[]{:S(2)}) collective-permute-start(bf16[3,288,1152]{2,1,0:T(8,128)(2,1)} %collective-permute-done.17.refs_17_.refs_15_), channel_id=1, source_target_pairs={{0,1},{1,0},{2,3},{3,2},{4,5},{5,4},{6,7},{7,6},{8,9},{9,8},{10,11... | collective-permute-start | bytes 5971976 | tf_op jit(solution)/shard_map/ppermute | solution.py:222
  248.8 61.6 %collective-permute-start.23 = (bf16[3,288,1536]{2,1,0:T(8,128)(2,1)}, bf16[3,288,1536]{2,1,0:T(8,128)(2,1)}, u32[]{:S(2)}, u32[]{:S(2)}) collective-permute-start(bf16[3,288,1536]{2,1,0:T(8,128)(2,1)} %pad_maximum_fusion.1), channel_id=1, source_target_pairs={{0,2},{1,3},{2,0},{3,1},{4,6},{5,7},{6,4},{7,5},{8,10},{9,11},{10,... | collective-permute-start | bytes 7962632 | tf_op jit(solution)/shard_map/ppermute | solution.py:222
  258.2 28.3 %collective-permute-start.22 = (bf16[192,2304]{1,0:T(8,128)(2,1)}, bf16[192,2304]{1,0:T(8,128)(2,1)}, u32[]{:S(2)}, u32[]{:S(2)}) collective-permute-start(bf16[192,2304]{1,0:T(8,128)(2,1)} %pad_bitcast_fusion.1), channel_id=1, source_target_pairs={{0,4},{1,5},{2,6},{3,7},{4,0},{5,1},{6,2},{7,3},{8,12},{9,13},{10,... | collective-permute-start | bytes 2654216 | tf_op jit(solution)/shard_map/ppermute | solution.py:222
  262.9 75.7 %all-to-all-start.1 = ((bf16[8,32,2304]{2,1,0:T(8,128)(2,1)}), bf16[8,32,2304]{2,1,0:T(8,128)(2,1)}, u32[]{:S(2)}, u32[]{:S(2)}) async-start(bf16[8,32,2304]{2,1,0:T(8,128)(2,1)} %bitcast.272), calls=%async_computation.1 | async-start | bytes 2359296 | tf_op jit(solution)/shard_map/all_to_all | solution.py:1013
  267.2 106.0 %all-gather.23.cloned.1.call-start = ((), (), s32[]{:S(2)}) async-start(), calls=%async_computation.8 | async-start | bytes 2949120 | tf_op jit(solution)/shard_map/all_gather | solution.py:238
  288.8 129.5 %all-gather.25.cloned.1.call-start = ((), (), s32[]{:S(2)}) async-start(), calls=%async_computation.9 | async-start | bytes 2949120 | tf_op jit(solution)/shard_map/all_gather | solution.py:238
  314.0 59.2 %collective-permute-start.25 = (bf16[3,288,1536]{2,1,0:T(8,128)(2,1)}, bf16[3,288,1536]{2,1,0:T(8,128)(2,1)}, u32[]{:S(2)}, u32[]{:S(2)}) collective-permute-start(bf16[3,288,1536]{2,1,0:T(8,128)(2,1)} %pad_maximum_fusion.2), channel_id=1, source_target_pairs={{0,2},{1,3},{2,0},{3,1},{4,6},{5,7},{6,4},{7,5},{8,10},{9,11},{10,... | collective-permute-start | bytes 7962632 | tf_op jit(solution)/shard_map/ppermute | solution.py:222
  333.3 27.2 %collective-permute-start.24 = (bf16[256,2304]{1,0:T(8,128)(2,1)S(1)}, bf16[256,2304]{1,0:T(8,128)(2,1)S(1)}, u32[]{:S(2)}, u32[]{:S(2)}) collective-permute-start(bf16[256,2304]{1,0:T(8,128)(2,1)S(1)} %multiply_convert_fusion.1.refs_8_), channel_id=1, source_target_pairs={{0,4},{1,5},{2,6},{3,7},{4,0},{5,1},{6,2},{7,3},{8,12},{9,13},{10,... | collective-permute-start | bytes 3538952 | tf_op jit(solution)/shard_map/ppermute | solution.py:222
  377.3 41.0 %collective-permute-start.27 = (bf16[3,192,1536]{2,1,0:T(8,128)(2,1)}, bf16[3,192,1536]{2,1,0:T(8,128)(2,1)S(1)}, u32[]{:S(2)}, u32[]{:S(2)}) collective-permute-start(bf16[3,192,1536]{2,1,0:T(8,128)(2,1)} %pad_maximum_fusion.7), channel_id=1, source_target_pairs={{0,2},{1,3},{2,0},{3,1},{4,6},{5,7},{6,4},{7,5},{8,10},{9,11},{10,... | collective-permute-start | bytes 5308424 | tf_op jit(solution)/shard_map/ppermute | solution.py:222
  385.8 32.4 %collective-permute-start.28 = (bf16[256,2432]{1,0:T(8,128)(2,1)}, bf16[256,2432]{1,0:T(8,128)(2,1)}, u32[]{:S(2)}, u32[]{:S(2)}) collective-permute-start(bf16[256,2432]{1,0:T(8,128)(2,1)} %pad_maximum_fusion.9), channel_id=1, source_target_pairs={{0,4},{1,5},{2,6},{3,7},{4,0},{5,1},{6,2},{7,3},{8,12},{9,13},{10,... | collective-permute-start | bytes 3735560 | tf_op jit(solution)/shard_map/ppermute | solution.py:222
  483.2 37.3 %collective-permute-start.31 = (bf16[256,2688]{1,0:T(8,128)(2,1)}, bf16[256,2688]{1,0:T(8,128)(2,1)}, u32[]{:S(2)}, u32[]{:S(2)}) collective-permute-start(bf16[256,2688]{1,0:T(8,128)(2,1)} %unstack.34), channel_id=1, source_target_pairs={{0,4},{1,5},{2,6},{3,7},{4,0},{5,1},{6,2},{7,3},{8,12},{9,13},{10,... | collective-permute-start | bytes 4128776 | tf_op jit(solution)/shard_map/ppermute | solution.py:222
  531.6 43.2 %collective-permute-start.33 = (bf16[256,2304]{1,0:T(8,128)(2,1)}, bf16[256,2304]{1,0:T(8,128)(2,1)}, u32[]{:S(2)}, u32[]{:S(2)}) collective-permute-start(bf16[256,2304]{1,0:T(8,128)(2,1)} %unstack.35), channel_id=1, source_target_pairs={{0,4},{1,5},{2,6},{3,7},{4,0},{5,1},{6,2},{7,3},{8,12},{9,13},{10,... | collective-permute-start | bytes 3538952 | tf_op jit(solution)/shard_map/ppermute | solution.py:222
  606.8 50.3 %all-to-all-start.2 = ((bf16[8,32,2304]{2,1,0:T(8,128)(2,1)}), bf16[8,32,2304]{2,1,0:T(8,128)(2,1)}, u32[]{:S(2)}, u32[]{:S(2)}) async-start(bf16[8,32,2304]{2,1,0:T(8,128)(2,1)} %bitcast.57), calls=%async_computation.2 | async-start | bytes 2359296 | tf_op jit(solution)/shard_map/all_to_all | solution.py:1162
  618.9 38.2 %collective-permute-start.35 = (bf16[4,2,664,128]{3,2,0,1:T(8,128)(2,1)}, bf16[4,2,664,128]{3,2,0,1:T(8,128)(2,1)}, u32[]{:S(2)}, u32[]{:S(2)}) collective-permute-start(bf16[4,2,664,128]{3,2,0,1:T(8,128)(2,1)} %bitcast.237), channel_id=1, source_target_pairs={{0,4},{1,5},{2,6},{3,7},{4,0},{5,1},{6,2},{7,3},{8,12},{9,13},{10,... | collective-permute-start | bytes 4079624 | tf_op jit(solution)/shard_map/ppermute | solution.py:222
  622.2 34.9 %collective-permute-start.36 = (bf16[4,2,672,128]{3,2,1,0:T(8,128)(2,1)}, bf16[4,2,672,128]{3,2,1,0:T(8,128)(2,1)}, u32[]{:S(2)}, u32[]{:S(2)}) collective-permute-start(bf16[4,2,672,128]{3,2,1,0:T(8,128)(2,1)} %dynamic-slice_bitcast_fusion), channel_id=1, source_target_pairs={{0,2},{1,3},{2,0},{3,1},{4,6},{5,7},{6,4},{7,5},{8,10},{9,11},{10,... | collective-permute-start | bytes 4128776 | tf_op jit(solution)/shard_map/ppermute | solution.py:222
  659.6 37.3 %all-to-all-start.3 = ((bf16[8,32,2304]{2,1,0:T(8,128)(2,1)}), bf16[8,32,2304]{2,1,0:T(8,128)(2,1)}, u32[]{:S(2)}, u32[]{:S(2)}) async-start(bf16[8,32,2304]{2,1,0:T(8,128)(2,1)} %bitcast.264), calls=%async_computation.3 | async-start | bytes 2359296 | tf_op jit(solution)/shard_map/all_to_all | solution.py:1170
  666.1 105.6 %all-gather.27.cloned.1.call-start = ((), (), s32[]{:S(2)}) async-start(), calls=%async_computation.10 | async-start | bytes 1710080 | tf_op jit(solution)/shard_map/all_gather | solution.py:238
  672.3 24.3 %collective-permute-start.38 = (bf16[4,672,128]{2,1,0:T(8,128)(2,1)}, bf16[4,672,128]{2,1,0:T(8,128)(2,1)S(1)}, u32[]{:S(2)}, u32[]{:S(2)}) collective-permute-start(bf16[4,672,128]{2,1,0:T(8,128)(2,1)} %dynamic-slice_bitcast_fusion.3), channel_id=1, source_target_pairs={{0,4},{1,5},{2,6},{3,7},{4,0},{5,1},{6,2},{7,3},{8,12},{9,13},{10,... | collective-permute-start | bytes 2064392 | tf_op jit(solution)/shard_map/ppermute | solution.py:222
  702.4 26.4 %collective-permute-start.40 = (bf16[1336,128]{1,0:T(8,128)(2,1)}, bf16[1336,128]{1,0:T(8,128)(2,1)S(1)}, u32[]{:S(2)}, u32[]{:S(2)}) collective-permute-start(bf16[1336,128]{1,0:T(8,128)(2,1)} %get-tuple-element.229), channel_id=1, source_target_pairs={{0,16},{1,17},{2,18},{3,19},{4,20},{5,21},{6,22},{7,23},{8,24},{9,... | collective-permute-start | bytes 1026056 | tf_op jit(solution)/shard_map/ppermute | solution.py:222
  702.5 26.4 %collective-permute-start.39 = (bf16[1336,128]{1,0:T(8,128)(2,1)}, bf16[1336,128]{1,0:T(8,128)(2,1)S(1)}, u32[]{:S(2)}, u32[]{:S(2)}) collective-permute-start(bf16[1336,128]{1,0:T(8,128)(2,1)} %get-tuple-element.230), channel_id=1, source_target_pairs={{0,8},{1,9},{2,10},{3,11},{4,12},{5,13},{6,14},{7,15},{8,16},{9,17... | collective-permute-start | bytes 1026056 | tf_op jit(solution)/shard_map/ppermute | solution.py:222
  778.9 29.4 %collective-permute-start.53 = (bf16[4,672,128]{2,1,0:T(8,128)(2,1)}, bf16[4,672,128]{2,1,0:T(8,128)(2,1)S(1)}, u32[]{:S(2)}, u32[]{:S(2)}) collective-permute-start(bf16[4,672,128]{2,1,0:T(8,128)(2,1)} %slice.251), channel_id=1, source_target_pairs={{0,4},{1,5},{2,6},{3,7},{4,0},{5,1},{6,2},{7,3},{8,12},{9,13},{10,... | collective-permute-start | bytes 2064392 | tf_op jit(solution)/shard_map/ppermute | solution.py:222
  791.8 30.5 %collective-permute-start.48 = (bf16[4,664,128]{2,1,0:T(8,128)(2,1)}, bf16[4,664,128]{2,1,0:T(8,128)(2,1)}, u32[]{:S(2)}, u32[]{:S(2)}) collective-permute-start(bf16[4,664,128]{2,1,0:T(8,128)(2,1)} %collective-permute-done.44), channel_id=1, source_target_pairs={{0,4},{1,5},{2,6},{3,7},{4,0},{5,1},{6,2},{7,3},{8,12},{9,13},{10,... | collective-permute-start | bytes 2039816 | tf_op jit(solution)/shard_map/ppermute | solution.py:222
  794.8 29.9 %collective-permute-start.51 = (bf16[4,672,128]{2,1,0:T(8,128)(2,1)}, bf16[4,672,128]{2,1,0:T(8,128)(2,1)S(1)}, u32[]{:S(2)}, u32[]{:S(2)}) collective-permute-start(bf16[4,672,128]{2,1,0:T(8,128)(2,1)} %slice.251), channel_id=1, source_target_pairs={{0,2},{1,3},{2,0},{3,1},{4,6},{5,7},{6,4},{7,5},{8,10},{9,11},{10,... | collective-permute-start | bytes 2064392 | tf_op jit(solution)/shard_map/ppermute | solution.py:222
  796.3 28.9 %collective-permute-start.47 = (bf16[4,664,128]{2,1,0:T(8,128)(2,1)}, bf16[4,664,128]{2,1,0:T(8,128)(2,1)S(1)}, u32[]{:S(2)}, u32[]{:S(2)}) collective-permute-start(bf16[4,664,128]{2,1,0:T(8,128)(2,1)} %collective-permute-done.46), channel_id=1, source_target_pairs={{0,1},{1,0},{2,3},{3,2},{4,5},{5,4},{6,7},{7,6},{8,9},{9,8},{10,11... | collective-permute-start | bytes 2039816 | tf_op jit(solution)/shard_map/ppermute | solution.py:222
  (145 other events, 1433.7 us)
Sparse Core Ops, SparseCore 0:
  11.9 58.0 all-gather.14
  72.2 75.7 all-gather.16
  150.1 68.4 all-gather.18
  220.1 90.2 all-gather.20
  311.8 49.2 all-gather.22
  362.4 49.2 all-gather.24
  737.1 34.5 all-gather.26

commit v6 on v5

--- a/solution.py
+++ b/solution.py
@@ -72,8 +72,8 @@
     return (
         adapter_choice_index,
         allowed,
-        jnp.concatenate([cosine] * 4, axis=1),
-        jnp.concatenate([-sine, sine] * 2, axis=1),
+        jnp.concatenate([cosine] * (2 * HEADS_AT_ONCE), axis=1),
+        jnp.concatenate([-sine, sine] * HEADS_AT_ONCE, axis=1),
     )
 
 
@@ -109,6 +109,21 @@
     return (reduced_total, adapter_scale * matrix_product(reduced_total, adapter_up_pair))
 
 
+HEADS_AT_ONCE = 4
+
+
+def head_masks(shape):
+    lane = lax.broadcasted_iota(jnp.int32, shape, 1)
+    return [lane // HEAD_SIZE == n for n in range(HEADS_AT_ONCE)]
+
+
+def join_heads(masks, results):
+    joined = results[0]
+    for mask, result in zip(masks[1:], results[1:]):
+        joined = jnp.where(mask, result, joined)
+    return joined
+
+
 def swap_halves(values):
     lane = lax.broadcasted_iota(jnp.int32, values.shape, 1)
     half, width = HEAD_SIZE // 2, values.shape[1]
@@ -130,21 +145,21 @@
     )
     value = low(full[2])
     qkv[0], qkv[1], qkv[2] = query, key, value
-    first = lax.broadcasted_iota(jnp.int32, query.shape, 1) < HEAD_SIZE
+    masks = head_masks(query.shape)
     results = []
-    for mine in (first, ~first):
+    for mine in masks:
         probs = head_scores(jnp.where(mine, query, jnp.zeros_like(query)), key, bias[...])
         results.append(matrix_product(low(probs), value))
-    attended[...] = low(jnp.where(first, results[0], results[1]))
+    attended[...] = low(join_heads(masks, results))
 
 
 def attention_back_kernel(qkv, lin, dz, down, cosine, sine, bias, grads):
     query, key, value = qkv[0], qkv[1], qkv[2]
     grad = low(lin[...] + matrix_product_backward(dz[...], down[...]))
-    first = lax.broadcasted_iota(jnp.int32, query.shape, 1) < HEAD_SIZE
+    masks = head_masks(query.shape)
     nothing = jnp.zeros_like(query)
     results = []
-    for mine in (first, ~first):
+    for mine in masks:
         probs = head_scores(jnp.where(mine, query, nothing), key, bias[...])
         grad_probs = matrix_product_backward(jnp.where(mine, grad, nothing), value)
         row_delta = jnp.sum(probs * grad_probs, axis=-1, keepdims=True)
@@ -158,7 +173,7 @@
         )
     scale = HEAD_SIZE ** (-0.5)
     grad_query, grad_key, grad_value = (
-        jnp.where(first, one, two) for one, two in zip(*results)
+        join_heads(masks, parts) for parts in zip(*results)
     )
     for t, v in enumerate((grad_query * scale, grad_key * scale)):
         grads[t] = low(v * cosine[...] - swap_halves(v) * sine[...])
@@ -166,7 +181,7 @@
 
 
 def attention_call(kernel, operands, outs):
-    pairs = 2 * HEAD_SIZE
+    pairs = HEADS_AT_ONCE * HEAD_SIZE
 
     def spec(shape, axis):
         block = tuple(pairs if k == axis else n for k, n in enumerate(shape))
@@ -175,7 +190,7 @@
     count = operands[-1][0].shape[0]
     return pl.pallas_call(
         kernel,
-        grid=(ATTENTION_HEADS // 2,),
+        grid=(ATTENTION_HEADS // HEADS_AT_ONCE,),
         out_shape=[jax.ShapeDtypeStruct(shape, jnp.bfloat16) for shape, _ in outs],
         in_specs=[spec(v.shape, axis) for v, axis in operands],
         out_specs=[spec(shape, axis) for shape, axis in outs],

time: 851 us -> 850 us (level)
  waiting for transfers between devices: 326 us -> 335 us
    unnamed x252 -> x258, local copies, waits for them, and re-layouts: 35.6 us -> 37.1 us
where the time goes in v6:
time: 850 us; the launch traced here: 843 us
  waiting for transfers between devices  335 us (39%)
  Pallas kernels  195 us (23%)
  local copies, waits for them, and re-layouts  137 us (16%)
  other arithmetic  69.8 us (8%)
  starting transfers between devices  68.3 us (8%)
  matrix products  21 us (2%)
  between operations  16.2 us (2%)
    ppermute x57, waiting for transfers between devices, move(): return lax.ppermute(value, AXES, pairs)  239 us
    all_gather x7, waiting for transfers between devices, all_z(): return lax.all_gather(block, 'dp', axis=0, axis_index_groups=groups)  95.7 us
    pallas_call x4, Pallas kernels, call(): pl.pallas_call(functools.partial(weights_kernel, place.line, first, count...  52.2 us
    ppermute x57, starting transfers between devices, move(): return lax.ppermute(value, AXES, pairs)  47.4 us
    pallas_call x1, Pallas kernels, back(): pl.pallas_call(functools.partial(feed_forward_back_kernel, self.place.lin...  46.6 us
    pallas_call x2, Pallas kernels, attention_call(): pl.pallas_call(kernel, grid=(ATTENTION_HEADS // HEADS_AT_ONCE,), out_shap...  39 us
    unnamed x258, local copies, waits for them, and re-layouts  37.1 us
    pallas_call x2, Pallas kernels, hidden(): pl.pallas_call(functools.partial(hidden_kernel, self.place.line), grid=(t...  25.9 us
  transfers between devices with their start and end apart: 68, of which 29 were waited for; matrix products, arithmetic and copies ran while one was open for 19% of the time, Pallas kernels for 17%

profile of v6, /device:TPU:0, one launch (start us, length us, event | category | flops | bytes accessed | tf_op | source)
XLA Modules:
  0.0 842.7 jit_solution(6518882652132743810)
XLA Ops:
  20.2 24.2 %collective-permute-done.1 = s32[1,8]{1,0:T(1,128)S(1)} collective-permute-done((s32[1,8]{1,0:T(1,128)S(1)}, s32[1,8]{1,0:T(1,128)S(1)}, u32[]{:S(2)}, u32[]{:S(2)}) %collective-permute-start.1) | collective-permute-done | bytes 64 | tf_op jit(solution)/shard_map/ppermute | solution.py:237
  48.1 4.1 fusion.64
  53.4 15.4 %collective-permute-done.2 = bf16[288,1536]{1,0:T(8,128)(2,1)S(1)} collective-permute-done((bf16[288,1536]{1,0:T(8,128)(2,1)}, bf16[288,1536]{1,0:T(8,128)(2,1)S(1)}, u32[]{:S(2)}, u32[]{:S(2)}) %collective-permute-start.2) | collective-permute-done | bytes 884768 | tf_op jit(solution)/shard_map/ppermute | solution.py:237
  68.7 18.6 %collective-permute-done.3 = bf16[288,1536]{1,0:T(8,128)(2,1)S(1)} collective-permute-done((bf16[288,1536]{1,0:T(8,128)(2,1)S(1)}, bf16[288,1536]{1,0:T(8,128)(2,1)S(1)}, u32[]{:S(2)}, u32[]{:S(2)}) %collective-permute-start.3) | collective-permute-done | bytes 884768 | tf_op jit(solution)/shard_map/ppermute | solution.py:237
  94.8 4.5 fusion.65
  99.3 4.9 all-to-all-start
  104.2 43.8 %all-gather.17.cloned.1.call-done = bf16[1152,1152]{1,0:T(8,128)(2,1)} async-done(((bf16[288,1152]{1,0:T(8,128)(2,1)}), bf16[1152,1152]{1,0:T(8,128)(2,1)}) %all-gather.17.cloned.1.call-update) | async-done | bytes 2654224 | tf_op jit(solution)/shard_map/all_gather | solution.py:253
  158.8 4.3 slice.193.value
  163.1 4.1 slice.195.value
  191.0 5.6 collective-permute-done.11.refs_9_.refs_7_
  206.7 12.0 %all-gather.19.cloned.1.call-done = bf16[1152,1536]{1,0:T(8,128)(2,1)} async-done(((bf16[288,1536]{1,0:T(8,128)(2,1)}), bf16[1152,1536]{1,0:T(8,128)(2,1)}) %all-gather.19.cloned.1.call-update) | async-done | bytes 3538960 | tf_op jit(solution)/shard_map/all_gather | solution.py:253
  218.6 25.9 %collective-permute-done.16.refs_13_.refs_11_ = bf16[3,288,1152]{2,1,0:T(8,128)(2,1)} collective-permute-done((bf16[3,288,1152]{2,1,0:T(8,128)(2,1)}, bf16[3,288,1152]{2,1,0:T(8,128)(2,1)}, u32[]{:S(2)}, u32[]{:S(2)}) %collective-permute-start.16) | collective-permute-done | bytes 1990688 | tf_op jit(solution)/shard_map/ppermute | solution.py:237
  253.5 4.0 gather_fusion
  263.1 4.3 all-to-all-start.1
  267.5 17.5 %shard_map.212.lin = f32[3,256,2304]{2,1,0:T(8,128)} custom-call(s32[3]{0:T(128)} %pad_add_fusion.2.where, bf16[256,2304]{1,0:T(8,128)(2,1)} %copy-done.10, bf16[288,2304]{1,0:T(8,128)(2,1)} %refs_0_.7, bf16[288,2304]{1,0:T(8,128)(2,1)} %refs_1_.3, bf16[288,2304]{1,0:T(8,128)(2,1)} %refs_2_.3, bf16[3,288,1152]{2,1,0:T(8,128)(2,1)} %pad_maximum_fusion.5.refs_3_.refs_1_, ...), custom_call_target="tpu_custom_call" | custom-call | flops 509607936 | bytes 1990656 | tf_op jit(solution)/shard_map/pallas_call | solution.py:338
  291.3 13.3 %shard_map.213 = (bf16[3,256,2304]{2,1,0:T(8,128)(2,1)}, bf16[256,2304]{1,0:T(8,128)(2,1)S(1)}) custom-call(f32[3,256,2304]{2,1,0:T(8,128)} %shard_map.212.lin, bf16[3,256,128]{2,1,0:T(8,128)(2,1)S(1)} %copy-done.49, bf16[3,128,2304]{2,1,0:T(8,128)(2,1)S(1)} %slice.206.up, f32[256,256]{1,0:T(8,128)S(1)} %copy-done.32, f32[256,256]{1,0:T(8,128)S(1)} %copy-done.34, ...), custom_call_target="tpu_custom_call" | custom-call | flops 75497472 | bytes 884736 | tf_op jit(solution)/shard_map/pallas_call | solution.py:191
  304.6 5.7 all-gather.21.cloned.1.call-done
  318.3 8.8 %shard_map.214 = f32[1,256,2304]{2,1,0:T(8,128)} custom-call(s32[3]{0:T(128)} %pad_add_fusion.2.where, bf16[256,2304]{1,0:T(8,128)(2,1)} %copy-done.25, bf16[288,2304]{1,0:T(8,128)(2,1)} %refs_0_.6, bf16[3,288,1152]{2,1,0:T(8,128)(2,1)} %pad_maximum_fusion.5.refs_3_.refs_1_, bf16[3,288,1152]{2,1,0:T(8,128)(2,1)} %collective-permute-done.9.refs_4_.refs_2_, ...), custom_call_target="tpu_custom_call" | custom-call | flops 169869312 | bytes 663552 | tf_op jit(solution)/shard_map/pallas_call | solution.py:338
  338.6 21.9 %collective-permute-done.24 = bf16[256,2304]{1,0:T(8,128)(2,1)S(1)} collective-permute-done((bf16[256,2304]{1,0:T(8,128)(2,1)S(1)}, bf16[256,2304]{1,0:T(8,128)(2,1)S(1)}, u32[]{:S(2)}, u32[]{:S(2)}) %collective-permute-start.24) | collective-permute-done | bytes 1179680 | tf_op jit(solution)/shard_map/ppermute | solution.py:237
  360.5 12.8 %collective-permute-done.25.mates.refs_9_ = bf16[3,288,1536]{2,1,0:T(8,128)(2,1)} collective-permute-done((bf16[3,288,1536]{2,1,0:T(8,128)(2,1)}, bf16[3,288,1536]{2,1,0:T(8,128)(2,1)}, u32[]{:S(2)}, u32[]{:S(2)}) %collective-permute-start.25) | collective-permute-done | bytes 2654240 | tf_op jit(solution)/shard_map/ppermute | solution.py:237
  378.9 4.1 gather_fusion.1
  390.8 12.8 %shard_map.215 = (f32[1024,1536]{1,0:T(8,128)}, bf16[1024,128]{1,0:T(8,128)(2,1)S(1)}) custom-call(s32[3]{0:T(128)S(1)} %pad_add_fusion.4.where, bf16[1024,2304]{1,0:T(8,128)(2,1)S(1)} %pad_maximum_fusion.values, f32[1024,128]{1,0:T(8,128)S(1)} %copy-done.27, bf16[2304,128]{1,0:T(8,128)(2,1)S(1)} %copy-done.31, bf16[128,1536]{1,0:T(8,128)(2,1)S(1)} %copy-done.44, ...), custom_call_target="tpu_custom_call" | custom-call | flops 452984832 | bytes 884736 | tf_op jit(solution)/shard_map/pallas_call | solution.py:577
  404.4 13.1 %shard_map.216 = (f32[1024,1536]{1,0:T(8,128)}, bf16[1024,128]{1,0:T(8,128)(2,1)S(1)}) custom-call(s32[3]{0:T(128)S(1)} %pad_add_fusion.4.where, bf16[1024,2304]{1,0:T(8,128)(2,1)S(1)} %pad_maximum_fusion.values, f32[1024,128]{1,0:T(8,128)S(1)} %copy-done.27, bf16[2304,128]{1,0:T(8,128)(2,1)S(1)} %copy-done.30, bf16[128,1536]{1,0:T(8,128)(2,1)S(1)} %copy-done.46, ...), custom_call_target="tpu_custom_call" | custom-call | flops 452984832 | bytes 884736 | tf_op jit(solution)/shard_map/pallas_call | solution.py:577
  426.5 46.6 %shard_map.217 = (bf16[1024,1536]{1,0:T(8,128)(2,1)}, bf16[1024,1536]{1,0:T(8,128)(2,1)}, bf16[1024,1536]{1,0:T(8,128)(2,1)}, f32[512,2688]{1,0:T(8,128)}, bf16[512,2688]{1,0:T(8,128)(2,1)}) custom-call(s32[3]{0:T(128)} %copy-done.57, f32[1024,1536]{1,0:T(8,128)} %get-tuple-element.146.gt, f32[1024,1536]{1,0:T(8,128)} %get-tuple-element.147.up, ...), custom_call_target="tpu_custom_call" | custom-call | flops 1358954496 | bytes 2654208 | tf_op jit(solution)/shard_map/pallas_call | solution.py:632
  474.3 4.3 collective-permute-done.30
  499.7 4.3 reshape.411.refs_15_
  509.1 11.4 %shard_map.218 = (f32[512,2304]{1,0:T(8,128)}, bf16[512,2304]{1,0:T(8,128)(2,1)}) custom-call(s32[3]{0:T(128)S(1)} %copy-done.58, bf16[1024,1536]{1,0:T(8,128)(2,1)S(1)} %copy-done.60, bf16[4,192,1536]{2,1,0:T(8,128)(2,1)S(1)} %bitcast.247, bf16[192,1536]{1,0:T(8,128)(2,1)S(1)} %copy-done.40, bf16[3,192,1536]{2,1,0:T(8,128)(2,1)S(1)} %copy-done.42, ...), custom_call_target="tpu_custom_call" | custom-call | flops 14495514624 | bytes 28311552 | tf_op jit(solution)/shard_map/pallas_call | solution.py:670
  532.5 4.5 multiply_convert_fusion
  537.0 8.9 %shard_map.221.lin = f32[256,2304]{1,0:T(8,128)} custom-call(s32[3]{0:T(128)} %pad_add_fusion.2.where, bf16[1,256,2304]{2,1,0:T(8,128)(2,1)} %bitcast.244, bf16[288,2304]{1,0:T(8,128)(2,1)} %refs_0_.6, bf16[3,288,1152]{2,1,0:T(8,128)(2,1)} %pad_maximum_fusion.5.refs_3_.refs_1_, bf16[3,288,1152]{2,1,0:T(8,128)(2,1)} %collective-permute-done.9.refs_4_.refs_2_, ...), custom_call_target="tpu_custom_call" | custom-call | flops 169869312 | bytes 663552 | tf_op jit(solution)/shard_map/pallas_call | solution.py:338
  548.1 25.7 %shard_map.222.refs_3_.values = bf16[3,256,2304]{2,1,0:T(8,128)(2,1)} custom-call(bf16[3,256,2304]{2,1,0:T(8,128)(2,1)} %get-tuple-element.127.qkv, f32[256,2304]{1,0:T(8,128)S(1)} %copy-done.12, bf16[256,128]{1,0:T(8,128)(2,1)S(1)} %fusion.37.dz.refs_5_, bf16[2304,128]{1,0:T(8,128)(2,1)S(1)} %copy-done.38, f32[256,256]{1,0:T(8,128)S(1)} %copy-done.33, ...), custom_call_target="tpu_custom_call" | custom-call | flops 75497472 | bytes 884736 | tf_op jit(solution)/shard_map/pallas_call | solution.py:191
  579.1 9.7 %shard_map.223 = bf16[42624,128]{1,0:T(8,128)(2,1)} custom-call(bf16[256,2304]{1,0:T(8,128)(2,1)S(1)} %copy-done.11, bf16[3,256,128]{2,1,0:T(8,128)(2,1)S(1)} %fusion.26.refs_1_, bf16[3,256,128]{2,1,0:T(8,128)(2,1)S(1)} %copy-done.50, bf16[3,256,2304]{2,1,0:T(8,128)(2,1)S(1)} %copy-done, bf16[256,2304]{1,0:T(8,128)(2,1)S(1)} %copy-done.26, ...), custom_call_target="tpu_custom_call" | custom-call | flops 268435456 | bytes 4194304 | tf_op jit(solution)/shard_map/pallas_call | solution.py:853
  588.8 5.4 constant_dynamic-slice_fusion.2
  599.5 4.0 collective-permute-done.34
  606.0 4.5 all-to-all-start.2
  610.5 5.6 add_convert_fusion
  622.7 17.0 %shard_map.224 = f32[256,2304]{1,0:T(8,128)} custom-call(s32[3]{0:T(128)} %pad_add_fusion.2.where, bf16[3,256,2304]{2,1,0:T(8,128)(2,1)} %shard_map.222.refs_3_.values, bf16[288,2304]{1,0:T(8,128)(2,1)} %refs_0_.7, bf16[288,2304]{1,0:T(8,128)(2,1)} %refs_1_.3, bf16[288,2304]{1,0:T(8,128)(2,1)} %refs_2_.3, ...), custom_call_target="tpu_custom_call" | custom-call | flops 509607936 | bytes 1990656 | tf_op jit(solution)/shard_map/pallas_call | solution.py:338
  643.6 12.7 %collective-permute-done.35 = bf16[4,2,664,128]{3,2,0,1:T(8,128)(2,1)} collective-permute-done((bf16[4,2,664,128]{3,2,0,1:T(8,128)(2,1)}, bf16[4,2,664,128]{3,2,0,1:T(8,128)(2,1)}, u32[]{:S(2)}, u32[]{:S(2)}) %collective-permute-start.35) | collective-permute-done | bytes 1359904 | tf_op jit(solution)/shard_map/ppermute | solution.py:237
  658.8 6.6 all-to-all-start.3
  673.1 11.4 %collective-permute-done.37 = bf16[4,664,128]{2,1,0:T(8,128)(2,1)} collective-permute-done((bf16[4,664,128]{2,1,0:T(8,128)(2,1)S(1)}, bf16[4,664,128]{2,1,0:T(8,128)(2,1)}, u32[]{:S(2)}, u32[]{:S(2)}) %collective-permute-start.37) | collective-permute-done | bytes 679968 | tf_op jit(solution)/shard_map/ppermute | solution.py:237
  685.9 9.8 %collective-permute-done.38 = bf16[4,672,128]{2,1,0:T(8,128)(2,1)S(1)} collective-permute-done((bf16[4,672,128]{2,1,0:T(8,128)(2,1)}, bf16[4,672,128]{2,1,0:T(8,128)(2,1)S(1)}, u32[]{:S(2)}, u32[]{:S(2)}) %collective-permute-start.38) | collective-permute-done | bytes 688160 | tf_op jit(solution)/shard_map/ppermute | solution.py:237
  697.0 4.5 collective-permute-start.41
  702.3 8.0 collective-permute-done.41
  710.4 18.2 %collective-permute-done.40 = bf16[1336,128]{1,0:T(8,128)(2,1)S(1)} collective-permute-done((bf16[1336,128]{1,0:T(8,128)(2,1)}, bf16[1336,128]{1,0:T(8,128)(2,1)S(1)}, u32[]{:S(2)}, u32[]{:S(2)}) %collective-permute-start.40) | collective-permute-done | bytes 342048 | tf_op jit(solution)/shard_map/ppermute | solution.py:237
  736.7 34.1 %all-gather.27.cloned.1.call-done = bf16[5344,128]{1,0:T(8,128)(2,1)} async-done(((bf16[1336,128]{1,0:T(8,128)(2,1)}), bf16[5344,128]{1,0:T(8,128)(2,1)}) %all-gather.27.cloned.1.call-update) | async-done | bytes 1368080 | tf_op jit(solution)/shard_map/all_gather | solution.py:253
  778.7 12.3 %collective-permute-done.44 = bf16[4,664,128]{2,1,0:T(8,128)(2,1)} collective-permute-done((bf16[4,664,128]{2,1,0:T(8,128)(2,1)}, bf16[4,664,128]{2,1,0:T(8,128)(2,1)}, u32[]{:S(2)}, u32[]{:S(2)}) %collective-permute-start.44) | collective-permute-done | bytes 679968 | tf_op jit(solution)/shard_map/ppermute | solution.py:237
  797.9 9.6 %collective-permute-done.53 = bf16[4,672,128]{2,1,0:T(8,128)(2,1)S(1)} collective-permute-done((bf16[4,672,128]{2,1,0:T(8,128)(2,1)}, bf16[4,672,128]{2,1,0:T(8,128)(2,1)S(1)}, u32[]{:S(2)}, u32[]{:S(2)}) %collective-permute-start.53) | collective-permute-done | bytes 688160 | tf_op jit(solution)/shard_map/ppermute | solution.py:237
  808.1 13.4 %collective-permute-done.48 = bf16[4,664,128]{2,1,0:T(8,128)(2,1)} collective-permute-done((bf16[4,664,128]{2,1,0:T(8,128)(2,1)}, bf16[4,664,128]{2,1,0:T(8,128)(2,1)}, u32[]{:S(2)}, u32[]{:S(2)}) %collective-permute-start.48) | collective-permute-done | bytes 679968 | tf_op jit(solution)/shard_map/ppermute | solution.py:237
  828.8 3.9 copy.127
  (521 shorter events, 244.7 us)
Async XLA Ops:
  7.2 80.2 %all-gather.15.cloned.1.call-start = ((), (), s32[]{:S(2)}) async-start(), calls=%async_computation.4 | async-start | bytes 3317760 | tf_op jit(solution)/shard_map/all_gather | solution.py:253
  11.8 136.1 %all-gather.17.cloned.1.call-start = ((), (), s32[]{:S(2)}) async-start(), calls=%async_computation.5 | async-start | bytes 3317760 | tf_op jit(solution)/shard_map/all_gather | solution.py:253
  11.9 32.5 %collective-permute-start = (bf16[288,2304]{1,0:T(8,128)(2,1)}, bf16[288,2304]{1,0:T(8,128)(2,1)}, u32[]{:S(2)}, u32[]{:S(2)}) collective-permute-start(bf16[288,2304]{1,0:T(8,128)(2,1)} %copy-done.80), channel_id=1, source_target_pairs={{0,4},{1,5},{2,6},{3,7},{4,0},{5,1},{6,2},{7,3},{8,12},{9,13},{10,... | collective-permute-start | bytes 3981320 | tf_op jit(solution)/shard_map/ppermute | solution.py:237
  15.0 29.4 %collective-permute-start.1 = (s32[1,8]{1,0:T(1,128)S(1)}, s32[1,8]{1,0:T(1,128)S(1)}, u32[]{:S(2)}, u32[]{:S(2)}) collective-permute-start(s32[1,8]{1,0:T(1,128)S(1)} %pad_add_fusion.1), channel_id=1, source_target_pairs={{0,4},{1,5},{2,6},{3,7},{4,0},{5,1},{6,2},{7,3},{8,12},{9,13},{10,... | collective-permute-start | bytes 104 | tf_op jit(solution)/shard_map/ppermute | solution.py:237
  15.0 203.6 %all-gather.19.cloned.1.call-start = ((), (), s32[]{:S(2)}) async-start(), calls=%async_computation.6 | async-start | bytes 4423680 | tf_op jit(solution)/shard_map/all_gather | solution.py:253
  44.4 43.0 %collective-permute-start.4 = (bf16[288,2304]{1,0:T(8,128)(2,1)}, bf16[288,2304]{1,0:T(8,128)(2,1)}, u32[]{:S(2)}, u32[]{:S(2)}) collective-permute-start(bf16[288,2304]{1,0:T(8,128)(2,1)} %collective-permute-done.refs_19_.refs_17_), channel_id=1, source_target_pairs={{0,2},{1,3},{2,0},{3,1},{4,6},{5,7},{6,4},{7,5},{8,10},{9,11},{10,... | collective-permute-start | bytes 3981320 | tf_op jit(solution)/shard_map/ppermute | solution.py:237
  46.1 41.2 %collective-permute-start.5 = (bf16[288,2304]{1,0:T(8,128)(2,1)}, bf16[288,2304]{1,0:T(8,128)(2,1)}, u32[]{:S(2)}, u32[]{:S(2)}) collective-permute-start(bf16[288,2304]{1,0:T(8,128)(2,1)} %collective-permute-done.refs_19_.refs_17_), channel_id=1, source_target_pairs={{0,1},{1,0},{2,3},{3,2},{4,5},{5,4},{6,7},{7,6},{8,9},{9,8},{10,11... | collective-permute-start | bytes 3981320 | tf_op jit(solution)/shard_map/ppermute | solution.py:237
  47.6 39.7 %collective-permute-start.3 = (bf16[288,1536]{1,0:T(8,128)(2,1)S(1)}, bf16[288,1536]{1,0:T(8,128)(2,1)S(1)}, u32[]{:S(2)}, u32[]{:S(2)}) collective-permute-start(bf16[288,1536]{1,0:T(8,128)(2,1)S(1)} %get-tuple-element.97), channel_id=1, source_target_pairs={{0,4},{1,5},{2,6},{3,7},{4,0},{5,1},{6,2},{7,3},{8,12},{9,13},{10,... | collective-permute-start | bytes 2654216 | tf_op jit(solution)/shard_map/ppermute | solution.py:237
  90.9 57.1 %collective-permute-start.7 = (bf16[3,288,1152]{2,1,0:T(8,128)(2,1)}, bf16[3,288,1152]{2,1,0:T(8,128)(2,1)}, u32[]{:S(2)}, u32[]{:S(2)}) collective-permute-start(bf16[3,288,1152]{2,1,0:T(8,128)(2,1)} %pad_maximum_fusion.5.refs_3_.refs_1_), channel_id=1, source_target_pairs={{0,2},{1,3},{2,0},{3,1},{4,6},{5,7},{6,4},{7,5},{8,10},{9,11},{10,... | collective-permute-start | bytes 5971976 | tf_op jit(solution)/shard_map/ppermute | solution.py:237
  91.2 56.8 %collective-permute-start.8 = (bf16[3,288,1152]{2,1,0:T(8,128)(2,1)}, bf16[3,288,1152]{2,1,0:T(8,128)(2,1)}, u32[]{:S(2)}, u32[]{:S(2)}) collective-permute-start(bf16[3,288,1152]{2,1,0:T(8,128)(2,1)} %pad_maximum_fusion.5.refs_3_.refs_1_), channel_id=1, source_target_pairs={{0,4},{1,5},{2,6},{3,7},{4,0},{5,1},{6,2},{7,3},{8,12},{9,13},{10,... | collective-permute-start | bytes 5971976 | tf_op jit(solution)/shard_map/ppermute | solution.py:237
  92.9 55.1 %collective-permute-start.9 = (bf16[3,288,1152]{2,1,0:T(8,128)(2,1)}, bf16[3,288,1152]{2,1,0:T(8,128)(2,1)}, u32[]{:S(2)}, u32[]{:S(2)}) collective-permute-start(bf16[3,288,1152]{2,1,0:T(8,128)(2,1)} %pad_maximum_fusion.5.refs_3_.refs_1_), channel_id=1, source_target_pairs={{0,1},{1,0},{2,3},{3,2},{4,5},{5,4},{6,7},{7,6},{8,9},{9,8},{10,11... | collective-permute-start | bytes 5971976 | tf_op jit(solution)/shard_map/ppermute | solution.py:237
  92.9 55.0 %collective-permute-start.10 = (bf16[288,2304]{1,0:T(8,128)(2,1)}, bf16[288,2304]{1,0:T(8,128)(2,1)S(1)}, u32[]{:S(2)}, u32[]{:S(2)}) collective-permute-start(bf16[288,2304]{1,0:T(8,128)(2,1)} %collective-permute-done.4.refs_21_.refs_19_), channel_id=1, source_target_pairs={{0,1},{1,0},{2,3},{3,2},{4,5},{5,4},{6,7},{7,6},{8,9},{9,8},{10,11... | collective-permute-start | bytes 3981320 | tf_op jit(solution)/shard_map/ppermute | solution.py:237
  99.3 91.7 %all-to-all-start = ((bf16[8,32,2304]{2,1,0:T(8,128)(2,1)}), bf16[8,32,2304]{2,1,0:T(8,128)(2,1)}, u32[]{:S(2)}, u32[]{:S(2)}) async-start(bf16[8,32,2304]{2,1,0:T(8,128)(2,1)} %bitcast.271), calls=%async_computation | async-start | bytes 2359296 | tf_op jit(solution)/shard_map/all_to_all | solution.py:1003
  104.2 206.2 %all-gather.21.cloned.1.call-start = ((), (), s32[]{:S(2)}) async-start(), calls=%async_computation.7 | async-start | bytes 4423680 | tf_op jit(solution)/shard_map/all_gather | solution.py:253
  151.7 45.0 %collective-permute-start.11 = (bf16[3,288,1152]{2,1,0:T(8,128)(2,1)}, bf16[3,288,1152]{2,1,0:T(8,128)(2,1)}, u32[]{:S(2)}, u32[]{:S(2)}) collective-permute-start(bf16[3,288,1152]{2,1,0:T(8,128)(2,1)} %pad_maximum_fusion.6.refs_7_.refs_5_), channel_id=1, source_target_pairs={{0,2},{1,3},{2,0},{3,1},{4,6},{5,7},{6,4},{7,5},{8,10},{9,11},{10,... | collective-permute-start | bytes 5971976 | tf_op jit(solution)/shard_map/ppermute | solution.py:237
  153.1 44.7 %collective-permute-start.12 = (bf16[3,288,1152]{2,1,0:T(8,128)(2,1)}, bf16[3,288,1152]{2,1,0:T(8,128)(2,1)}, u32[]{:S(2)}, u32[]{:S(2)}) collective-permute-start(bf16[3,288,1152]{2,1,0:T(8,128)(2,1)} %pad_maximum_fusion.6.refs_7_.refs_5_), channel_id=1, source_target_pairs={{0,4},{1,5},{2,6},{3,7},{4,0},{5,1},{6,2},{7,3},{8,12},{9,13},{10,... | collective-permute-start | bytes 5971976 | tf_op jit(solution)/shard_map/ppermute | solution.py:237
  154.7 43.1 %collective-permute-start.13 = (bf16[3,288,1152]{2,1,0:T(8,128)(2,1)}, bf16[3,288,1152]{2,1,0:T(8,128)(2,1)}, u32[]{:S(2)}, u32[]{:S(2)}) collective-permute-start(bf16[3,288,1152]{2,1,0:T(8,128)(2,1)} %pad_maximum_fusion.6.refs_7_.refs_5_), channel_id=1, source_target_pairs={{0,1},{1,0},{2,3},{3,2},{4,5},{5,4},{6,7},{7,6},{8,9},{9,8},{10,11... | collective-permute-start | bytes 5971976 | tf_op jit(solution)/shard_map/ppermute | solution.py:237
  154.7 43.1 %collective-permute-start.14 = (bf16[3,288,1152]{2,1,0:T(8,128)(2,1)}, bf16[3,288,1152]{2,1,0:T(8,128)(2,1)}, u32[]{:S(2)}, u32[]{:S(2)}) collective-permute-start(bf16[3,288,1152]{2,1,0:T(8,128)(2,1)} %collective-permute-done.7.refs_5_.refs_3_), channel_id=1, source_target_pairs={{0,1},{1,0},{2,3},{3,2},{4,5},{5,4},{6,7},{7,6},{8,9},{9,8},{10,11... | collective-permute-start | bytes 5971976 | tf_op jit(solution)/shard_map/ppermute | solution.py:237
  155.2 42.6 %collective-permute-start.15 = (bf16[3,288,1152]{2,1,0:T(8,128)(2,1)}, bf16[3,288,1152]{2,1,0:T(8,128)(2,1)}, u32[]{:S(2)}, u32[]{:S(2)}) collective-permute-start(bf16[3,288,1152]{2,1,0:T(8,128)(2,1)} %collective-permute-done.8.refs_11_.refs_9_), channel_id=1, source_target_pairs={{0,1},{1,0},{2,3},{3,2},{4,5},{5,4},{6,7},{7,6},{8,9},{9,8},{10,11... | collective-permute-start | bytes 5971976 | tf_op jit(solution)/shard_map/ppermute | solution.py:237
  197.8 46.7 %collective-permute-start.17 = (bf16[3,288,1152]{2,1,0:T(8,128)(2,1)}, bf16[3,288,1152]{2,1,0:T(8,128)(2,1)}, u32[]{:S(2)}, u32[]{:S(2)}) collective-permute-start(bf16[3,288,1152]{2,1,0:T(8,128)(2,1)} %collective-permute-done.12.refs_15_.refs_13_), channel_id=1, source_target_pairs={{0,2},{1,3},{2,0},{3,1},{4,6},{5,7},{6,4},{7,5},{8,10},{9,11},{10,... | collective-permute-start | bytes 5971976 | tf_op jit(solution)/shard_map/ppermute | solution.py:237
  198.4 46.1 %collective-permute-start.19 = (bf16[3,288,1152]{2,1,0:T(8,128)(2,1)}, bf16[3,288,1152]{2,1,0:T(8,128)(2,1)}, u32[]{:S(2)}, u32[]{:S(2)}) collective-permute-start(bf16[3,288,1152]{2,1,0:T(8,128)(2,1)} %collective-permute-done.12.refs_15_.refs_13_), channel_id=1, source_target_pairs={{0,1},{1,0},{2,3},{3,2},{4,5},{5,4},{6,7},{7,6},{8,9},{9,8},{10,11... | collective-permute-start | bytes 5971976 | tf_op jit(solution)/shard_map/ppermute | solution.py:237
  198.5 46.1 %collective-permute-start.16 = (bf16[3,288,1152]{2,1,0:T(8,128)(2,1)}, bf16[3,288,1152]{2,1,0:T(8,128)(2,1)}, u32[]{:S(2)}, u32[]{:S(2)}) collective-permute-start(bf16[3,288,1152]{2,1,0:T(8,128)(2,1)} %collective-permute-done.7.refs_5_.refs_3_), channel_id=1, source_target_pairs={{0,4},{1,5},{2,6},{3,7},{4,0},{5,1},{6,2},{7,3},{8,12},{9,13},{10,... | collective-permute-start | bytes 5971976 | tf_op jit(solution)/shard_map/ppermute | solution.py:237
  200.0 44.5 %collective-permute-start.18 = (bf16[3,288,1152]{2,1,0:T(8,128)(2,1)}, bf16[3,288,1152]{2,1,0:T(8,128)(2,1)}, u32[]{:S(2)}, u32[]{:S(2)}) collective-permute-start(bf16[3,288,1152]{2,1,0:T(8,128)(2,1)} %collective-permute-done.11.refs_9_.refs_7_), channel_id=1, source_target_pairs={{0,1},{1,0},{2,3},{3,2},{4,5},{5,4},{6,7},{7,6},{8,9},{9,8},{10,11... | collective-permute-start | bytes 5971976 | tf_op jit(solution)/shard_map/ppermute | solution.py:237
  244.5 22.9 %collective-permute-start.20 = (bf16[3,288,1152]{2,1,0:T(8,128)(2,1)}, bf16[3,288,1152]{2,1,0:T(8,128)(2,1)}, u32[]{:S(2)}, u32[]{:S(2)}) collective-permute-start(bf16[3,288,1152]{2,1,0:T(8,128)(2,1)} %collective-permute-done.16.refs_13_.refs_11_), channel_id=1, source_target_pairs={{0,1},{1,0},{2,3},{3,2},{4,5},{5,4},{6,7},{7,6},{8,9},{9,8},{10,11... | collective-permute-start | bytes 5971976 | tf_op jit(solution)/shard_map/ppermute | solution.py:237
  244.6 22.9 %collective-permute-start.21 = (bf16[3,288,1152]{2,1,0:T(8,128)(2,1)}, bf16[3,288,1152]{2,1,0:T(8,128)(2,1)}, u32[]{:S(2)}, u32[]{:S(2)}) collective-permute-start(bf16[3,288,1152]{2,1,0:T(8,128)(2,1)} %collective-permute-done.17.refs_17_.refs_15_), channel_id=1, source_target_pairs={{0,1},{1,0},{2,3},{3,2},{4,5},{5,4},{6,7},{7,6},{8,9},{9,8},{10,11... | collective-permute-start | bytes 5971976 | tf_op jit(solution)/shard_map/ppermute | solution.py:237
  248.8 61.6 %collective-permute-start.23 = (bf16[3,288,1536]{2,1,0:T(8,128)(2,1)}, bf16[3,288,1536]{2,1,0:T(8,128)(2,1)}, u32[]{:S(2)}, u32[]{:S(2)}) collective-permute-start(bf16[3,288,1536]{2,1,0:T(8,128)(2,1)} %pad_maximum_fusion.1), channel_id=1, source_target_pairs={{0,2},{1,3},{2,0},{3,1},{4,6},{5,7},{6,4},{7,5},{8,10},{9,11},{10,... | collective-permute-start | bytes 7962632 | tf_op jit(solution)/shard_map/ppermute | solution.py:237
  258.4 28.3 %collective-permute-start.22 = (bf16[192,2304]{1,0:T(8,128)(2,1)}, bf16[192,2304]{1,0:T(8,128)(2,1)}, u32[]{:S(2)}, u32[]{:S(2)}) collective-permute-start(bf16[192,2304]{1,0:T(8,128)(2,1)} %pad_bitcast_fusion.1), channel_id=1, source_target_pairs={{0,4},{1,5},{2,6},{3,7},{4,0},{5,1},{6,2},{7,3},{8,12},{9,13},{10,... | collective-permute-start | bytes 2654216 | tf_op jit(solution)/shard_map/ppermute | solution.py:237
  263.1 75.5 %all-to-all-start.1 = ((bf16[8,32,2304]{2,1,0:T(8,128)(2,1)}), bf16[8,32,2304]{2,1,0:T(8,128)(2,1)}, u32[]{:S(2)}, u32[]{:S(2)}) async-start(bf16[8,32,2304]{2,1,0:T(8,128)(2,1)} %bitcast.272), calls=%async_computation.1 | async-start | bytes 2359296 | tf_op jit(solution)/shard_map/all_to_all | solution.py:1028
  267.4 105.8 %all-gather.23.cloned.1.call-start = ((), (), s32[]{:S(2)}) async-start(), calls=%async_computation.8 | async-start | bytes 2949120 | tf_op jit(solution)/shard_map/all_gather | solution.py:253
  288.9 129.2 %all-gather.25.cloned.1.call-start = ((), (), s32[]{:S(2)}) async-start(), calls=%async_computation.9 | async-start | bytes 2949120 | tf_op jit(solution)/shard_map/all_gather | solution.py:253
  314.1 59.2 %collective-permute-start.25 = (bf16[3,288,1536]{2,1,0:T(8,128)(2,1)}, bf16[3,288,1536]{2,1,0:T(8,128)(2,1)}, u32[]{:S(2)}, u32[]{:S(2)}) collective-permute-start(bf16[3,288,1536]{2,1,0:T(8,128)(2,1)} %pad_maximum_fusion.2), channel_id=1, source_target_pairs={{0,2},{1,3},{2,0},{3,1},{4,6},{5,7},{6,4},{7,5},{8,10},{9,11},{10,... | collective-permute-start | bytes 7962632 | tf_op jit(solution)/shard_map/ppermute | solution.py:237
  333.3 27.2 %collective-permute-start.24 = (bf16[256,2304]{1,0:T(8,128)(2,1)S(1)}, bf16[256,2304]{1,0:T(8,128)(2,1)S(1)}, u32[]{:S(2)}, u32[]{:S(2)}) collective-permute-start(bf16[256,2304]{1,0:T(8,128)(2,1)S(1)} %multiply_convert_fusion.1.refs_8_), channel_id=1, source_target_pairs={{0,4},{1,5},{2,6},{3,7},{4,0},{5,1},{6,2},{7,3},{8,12},{9,13},{10,... | collective-permute-start | bytes 3538952 | tf_op jit(solution)/shard_map/ppermute | solution.py:237
  377.3 40.9 %collective-permute-start.27 = (bf16[3,192,1536]{2,1,0:T(8,128)(2,1)}, bf16[3,192,1536]{2,1,0:T(8,128)(2,1)S(1)}, u32[]{:S(2)}, u32[]{:S(2)}) collective-permute-start(bf16[3,192,1536]{2,1,0:T(8,128)(2,1)} %pad_maximum_fusion.7), channel_id=1, source_target_pairs={{0,2},{1,3},{2,0},{3,1},{4,6},{5,7},{6,4},{7,5},{8,10},{9,11},{10,... | collective-permute-start | bytes 5308424 | tf_op jit(solution)/shard_map/ppermute | solution.py:237
  385.7 32.4 %collective-permute-start.28 = (bf16[256,2432]{1,0:T(8,128)(2,1)}, bf16[256,2432]{1,0:T(8,128)(2,1)}, u32[]{:S(2)}, u32[]{:S(2)}) collective-permute-start(bf16[256,2432]{1,0:T(8,128)(2,1)} %pad_maximum_fusion.9), channel_id=1, source_target_pairs={{0,4},{1,5},{2,6},{3,7},{4,0},{5,1},{6,2},{7,3},{8,12},{9,13},{10,... | collective-permute-start | bytes 3735560 | tf_op jit(solution)/shard_map/ppermute | solution.py:237
  483.1 37.4 %collective-permute-start.31 = (bf16[256,2688]{1,0:T(8,128)(2,1)}, bf16[256,2688]{1,0:T(8,128)(2,1)}, u32[]{:S(2)}, u32[]{:S(2)}) collective-permute-start(bf16[256,2688]{1,0:T(8,128)(2,1)} %unstack.34), channel_id=1, source_target_pairs={{0,4},{1,5},{2,6},{3,7},{4,0},{5,1},{6,2},{7,3},{8,12},{9,13},{10,... | collective-permute-start | bytes 4128776 | tf_op jit(solution)/shard_map/ppermute | solution.py:237
  531.5 42.4 %collective-permute-start.33 = (bf16[256,2304]{1,0:T(8,128)(2,1)}, bf16[256,2304]{1,0:T(8,128)(2,1)}, u32[]{:S(2)}, u32[]{:S(2)}) collective-permute-start(bf16[256,2304]{1,0:T(8,128)(2,1)} %unstack.35), channel_id=1, source_target_pairs={{0,4},{1,5},{2,6},{3,7},{4,0},{5,1},{6,2},{7,3},{8,12},{9,13},{10,... | collective-permute-start | bytes 3538952 | tf_op jit(solution)/shard_map/ppermute | solution.py:237
  606.0 50.3 %all-to-all-start.2 = ((bf16[8,32,2304]{2,1,0:T(8,128)(2,1)}), bf16[8,32,2304]{2,1,0:T(8,128)(2,1)}, u32[]{:S(2)}, u32[]{:S(2)}) async-start(bf16[8,32,2304]{2,1,0:T(8,128)(2,1)} %bitcast.57), calls=%async_computation.2 | async-start | bytes 2359296 | tf_op jit(solution)/shard_map/all_to_all | solution.py:1177
  618.1 38.2 %collective-permute-start.35 = (bf16[4,2,664,128]{3,2,0,1:T(8,128)(2,1)}, bf16[4,2,664,128]{3,2,0,1:T(8,128)(2,1)}, u32[]{:S(2)}, u32[]{:S(2)}) collective-permute-start(bf16[4,2,664,128]{3,2,0,1:T(8,128)(2,1)} %bitcast.237), channel_id=1, source_target_pairs={{0,4},{1,5},{2,6},{3,7},{4,0},{5,1},{6,2},{7,3},{8,12},{9,13},{10,... | collective-permute-start | bytes 4079624 | tf_op jit(solution)/shard_map/ppermute | solution.py:237
  621.3 35.0 %collective-permute-start.36 = (bf16[4,2,672,128]{3,2,1,0:T(8,128)(2,1)}, bf16[4,2,672,128]{3,2,1,0:T(8,128)(2,1)}, u32[]{:S(2)}, u32[]{:S(2)}) collective-permute-start(bf16[4,2,672,128]{3,2,1,0:T(8,128)(2,1)} %dynamic-slice_bitcast_fusion), channel_id=1, source_target_pairs={{0,2},{1,3},{2,0},{3,1},{4,6},{5,7},{6,4},{7,5},{8,10},{9,11},{10,... | collective-permute-start | bytes 4128776 | tf_op jit(solution)/shard_map/ppermute | solution.py:237
  658.8 37.3 %all-to-all-start.3 = ((bf16[8,32,2304]{2,1,0:T(8,128)(2,1)}), bf16[8,32,2304]{2,1,0:T(8,128)(2,1)}, u32[]{:S(2)}, u32[]{:S(2)}) async-start(bf16[8,32,2304]{2,1,0:T(8,128)(2,1)} %bitcast.264), calls=%async_computation.3 | async-start | bytes 2359296 | tf_op jit(solution)/shard_map/all_to_all | solution.py:1185
  665.4 105.5 %all-gather.27.cloned.1.call-start = ((), (), s32[]{:S(2)}) async-start(), calls=%async_computation.10 | async-start | bytes 1710080 | tf_op jit(solution)/shard_map/all_gather | solution.py:253
  671.1 24.6 %collective-permute-start.38 = (bf16[4,672,128]{2,1,0:T(8,128)(2,1)}, bf16[4,672,128]{2,1,0:T(8,128)(2,1)S(1)}, u32[]{:S(2)}, u32[]{:S(2)}) collective-permute-start(bf16[4,672,128]{2,1,0:T(8,128)(2,1)} %dynamic-slice_bitcast_fusion.3), channel_id=1, source_target_pairs={{0,4},{1,5},{2,6},{3,7},{4,0},{5,1},{6,2},{7,3},{8,12},{9,13},{10,... | collective-permute-start | bytes 2064392 | tf_op jit(solution)/shard_map/ppermute | solution.py:237
  701.5 27.1 %collective-permute-start.40 = (bf16[1336,128]{1,0:T(8,128)(2,1)}, bf16[1336,128]{1,0:T(8,128)(2,1)S(1)}, u32[]{:S(2)}, u32[]{:S(2)}) collective-permute-start(bf16[1336,128]{1,0:T(8,128)(2,1)} %get-tuple-element.229), channel_id=1, source_target_pairs={{0,16},{1,17},{2,18},{3,19},{4,20},{5,21},{6,22},{7,23},{8,24},{9,... | collective-permute-start | bytes 1026056 | tf_op jit(solution)/shard_map/ppermute | solution.py:237
  701.5 27.1 %collective-permute-start.39 = (bf16[1336,128]{1,0:T(8,128)(2,1)}, bf16[1336,128]{1,0:T(8,128)(2,1)S(1)}, u32[]{:S(2)}, u32[]{:S(2)}) collective-permute-start(bf16[1336,128]{1,0:T(8,128)(2,1)} %get-tuple-element.230), channel_id=1, source_target_pairs={{0,8},{1,9},{2,10},{3,11},{4,12},{5,13},{6,14},{7,15},{8,16},{9,17... | collective-permute-start | bytes 1026056 | tf_op jit(solution)/shard_map/ppermute | solution.py:237
  778.1 29.4 %collective-permute-start.53 = (bf16[4,672,128]{2,1,0:T(8,128)(2,1)}, bf16[4,672,128]{2,1,0:T(8,128)(2,1)S(1)}, u32[]{:S(2)}, u32[]{:S(2)}) collective-permute-start(bf16[4,672,128]{2,1,0:T(8,128)(2,1)} %slice.251), channel_id=1, source_target_pairs={{0,4},{1,5},{2,6},{3,7},{4,0},{5,1},{6,2},{7,3},{8,12},{9,13},{10,... | collective-permute-start | bytes 2064392 | tf_op jit(solution)/shard_map/ppermute | solution.py:237
  791.0 30.5 %collective-permute-start.48 = (bf16[4,664,128]{2,1,0:T(8,128)(2,1)}, bf16[4,664,128]{2,1,0:T(8,128)(2,1)}, u32[]{:S(2)}, u32[]{:S(2)}) collective-permute-start(bf16[4,664,128]{2,1,0:T(8,128)(2,1)} %collective-permute-done.44), channel_id=1, source_target_pairs={{0,4},{1,5},{2,6},{3,7},{4,0},{5,1},{6,2},{7,3},{8,12},{9,13},{10,... | collective-permute-start | bytes 2039816 | tf_op jit(solution)/shard_map/ppermute | solution.py:237
  794.0 29.9 %collective-permute-start.51 = (bf16[4,672,128]{2,1,0:T(8,128)(2,1)}, bf16[4,672,128]{2,1,0:T(8,128)(2,1)S(1)}, u32[]{:S(2)}, u32[]{:S(2)}) collective-permute-start(bf16[4,672,128]{2,1,0:T(8,128)(2,1)} %slice.251), channel_id=1, source_target_pairs={{0,2},{1,3},{2,0},{3,1},{4,6},{5,7},{6,4},{7,5},{8,10},{9,11},{10,... | collective-permute-start | bytes 2064392 | tf_op jit(solution)/shard_map/ppermute | solution.py:237
  795.5 28.9 %collective-permute-start.47 = (bf16[4,664,128]{2,1,0:T(8,128)(2,1)}, bf16[4,664,128]{2,1,0:T(8,128)(2,1)S(1)}, u32[]{:S(2)}, u32[]{:S(2)}) collective-permute-start(bf16[4,664,128]{2,1,0:T(8,128)(2,1)} %collective-permute-done.46), channel_id=1, source_target_pairs={{0,1},{1,0},{2,3},{3,2},{4,5},{5,4},{6,7},{7,6},{8,9},{9,8},{10,11... | collective-permute-start | bytes 2039816 | tf_op jit(solution)/shard_map/ppermute | solution.py:237
  (148 other events, 1514.0 us)
Sparse Core Ops, SparseCore 0:
  11.9 58.0 all-gather.14
  72.2 75.7 all-gather.16
  150.1 68.4 all-gather.18
  220.1 90.2 all-gather.20
  311.8 49.2 all-gather.22
  362.5 49.2 all-gather.24
  736.8 33.9 all-gather.26

commit v7 on v6

--- a/solution.py
+++ b/solution.py
@@ -1061,10 +1061,11 @@
         ),
         (((3, count, MODEL_WIDTH), 2), ((count, MODEL_WIDTH), 1)),
     )
-    o, up_planes, gate_mates = together(o, up_planes, gate_mates)
+    o, up_planes = together(o, up_planes)
     up_mates = place.by_x(place.other_z(up_planes))
     z_out, delta_out = apply_adapter_delta(o, A_model[3], B_model[3], choice)
-    m = x + residual_branch_scale * (attention.times(o, 3, 1)[0] + delta_out)
+    out_rows, gate_mates = together(attention.times(o, 3, 1), gate_mates)
+    m = x + residual_branch_scale * (out_rows[0] + delta_out)
     scale_two = rms_scale(m)
     n2 = low(m * scale_two * gain_second)
 

time: 850 us -> 844 us (level)
  waiting for transfers between devices: 335 us -> 317 us
  starting transfers between devices: 68.3 us -> 82.1 us
    all_gather x7, waiting for transfers between devices: 95.7 us -> 52.9 us  [all_z(): return lax.all_gather(block, 'dp', axis=0, axis_index_groups=groups)]
    ppermute x57, waiting for transfers between devices: 239 us -> 264 us  [move(): return lax.ppermute(value, AXES, pairs)]
    all_gather x7, starting transfers between devices: 0.68 us -> 12 us  [all_z(): return lax.all_gather(block, 'dp', axis=0, axis_index_groups=groups)]
  transfers between devices with their start and end apart: 68 -> 68, of which waited for: 29 -> 30; matrix products, arithmetic and copies ran while one was open for 19% -> 19% of each run, Pallas kernels for 17% -> 17%
where the time goes in v7:
time: 844 us; the launch traced here: 839 us
  waiting for transfers between devices  317 us (38%)
  Pallas kernels  196 us (23%)
  local copies, waits for them, and re-layouts  133 us (16%)
  starting transfers between devices  82.1 us (10%)
  other arithmetic  73.5 us (9%)
  matrix products  21.1 us (2%)
  between operations  16.1 us (2%)
    ppermute x57, waiting for transfers between devices, move(): return lax.ppermute(value, AXES, pairs)  264 us
    all_gather x7, waiting for transfers between devices, all_z(): return lax.all_gather(block, 'dp', axis=0, axis_index_groups=groups)  52.9 us
    pallas_call x4, Pallas kernels, call(): pl.pallas_call(functools.partial(weights_kernel, place.line, first, count...  52.4 us
    ppermute x57, starting transfers between devices, move(): return lax.ppermute(value, AXES, pairs)  47 us
    pallas_call x1, Pallas kernels, back(): pl.pallas_call(functools.partial(feed_forward_back_kernel, self.place.lin...  46.9 us
    pallas_call x2, Pallas kernels, attention_call(): pl.pallas_call(kernel, grid=(ATTENTION_HEADS // HEADS_AT_ONCE,), out_shap...  39.1 us
    unnamed x258, local copies, waits for them, and re-layouts  34.7 us
    pallas_call x2, Pallas kernels, hidden(): pl.pallas_call(functools.partial(hidden_kernel, self.place.line), grid=(t...  25.7 us
  transfers between devices with their start and end apart: 68, of which 30 were waited for; matrix products, arithmetic and copies ran while one was open for 19% of the time, Pallas kernels for 17%

profile of v7, /device:TPU:0, one launch (start us, length us, event | category | flops | bytes accessed | tf_op | source)
XLA Modules:
  0.0 838.9 jit_solution(12534022461564141313)
XLA Ops:
  20.2 24.2 %collective-permute-done.1 = s32[1,8]{1,0:T(1,128)S(1)} collective-permute-done((s32[1,8]{1,0:T(1,128)S(1)}, s32[1,8]{1,0:T(1,128)S(1)}, u32[]{:S(2)}, u32[]{:S(2)}) %collective-permute-start.1) | collective-permute-done | bytes 64 | tf_op jit(solution)/shard_map/ppermute | solution.py:237
  48.1 4.1 fusion.64
  53.4 15.4 %collective-permute-done.2 = bf16[288,1536]{1,0:T(8,128)(2,1)} collective-permute-done((bf16[288,1536]{1,0:T(8,128)(2,1)}, bf16[288,1536]{1,0:T(8,128)(2,1)}, u32[]{:S(2)}, u32[]{:S(2)}) %collective-permute-start.2) | collective-permute-done | bytes 884768 | tf_op jit(solution)/shard_map/ppermute | solution.py:237
  68.8 18.6 %collective-permute-done.3 = bf16[288,1536]{1,0:T(8,128)(2,1)} collective-permute-done((bf16[288,1536]{1,0:T(8,128)(2,1)S(1)}, bf16[288,1536]{1,0:T(8,128)(2,1)}, u32[]{:S(2)}, u32[]{:S(2)}) %collective-permute-start.3) | collective-permute-done | bytes 884768 | tf_op jit(solution)/shard_map/ppermute | solution.py:237
  95.7 4.3 fusion.65
  112.1 4.9 all-to-all-start
  117.4 12.9 %all-gather.17.cloned.1.call-done = bf16[1152,1152]{1,0:T(8,128)(2,1)} async-done(((bf16[288,1152]{1,0:T(8,128)(2,1)}), bf16[1152,1152]{1,0:T(8,128)(2,1)}) %all-gather.17.cloned.1.call-update) | async-done | bytes 2654224 | tf_op jit(solution)/shard_map/all_gather | solution.py:253
  130.3 6.1 collective-permute-done.7.refs_5_.refs_3_
  136.4 11.1 %collective-permute-done.8.refs_11_.refs_9_ = bf16[3,288,1152]{2,1,0:T(8,128)(2,1)} collective-permute-done((bf16[3,288,1152]{2,1,0:T(8,128)(2,1)}, bf16[3,288,1152]{2,1,0:T(8,128)(2,1)}, u32[]{:S(2)}, u32[]{:S(2)}) %collective-permute-start.8) | collective-permute-done | bytes 1990688 | tf_op jit(solution)/shard_map/ppermute | solution.py:237
  157.5 4.0 slice.193.value
  184.4 9.2 %collective-permute-done.11.refs_9_.refs_7_ = bf16[3,288,1152]{2,1,0:T(8,128)(2,1)} collective-permute-done((bf16[3,288,1152]{2,1,0:T(8,128)(2,1)}, bf16[3,288,1152]{2,1,0:T(8,128)(2,1)}, u32[]{:S(2)}, u32[]{:S(2)}) %collective-permute-start.11) | collective-permute-done | bytes 1990688 | tf_op jit(solution)/shard_map/ppermute | solution.py:237
  204.6 4.4 all-gather.19.cloned.1.call-done
  209.0 33.0 %collective-permute-done.16.refs_13_.refs_11_ = bf16[3,288,1152]{2,1,0:T(8,128)(2,1)} collective-permute-done((bf16[3,288,1152]{2,1,0:T(8,128)(2,1)}, bf16[3,288,1152]{2,1,0:T(8,128)(2,1)}, u32[]{:S(2)}, u32[]{:S(2)}) %collective-permute-start.16) | collective-permute-done | bytes 1990688 | tf_op jit(solution)/shard_map/ppermute | solution.py:237
  251.8 6.1 all-to-all-start.1
  257.9 11.4 %all-gather.23.cloned.1.call-start = ((), (), s32[]{:S(2)}) async-start(), calls=%async_computation.8 | async-start | bytes 2949120 | tf_op jit(solution)/shard_map/all_gather | solution.py:253
  269.3 17.5 %shard_map.212.lin = f32[3,256,2304]{2,1,0:T(8,128)} custom-call(s32[3]{0:T(128)} %pad_add_fusion.2.where, bf16[256,2304]{1,0:T(8,128)(2,1)} %copy-done.10, bf16[288,2304]{1,0:T(8,128)(2,1)} %refs_0_.7, bf16[288,2304]{1,0:T(8,128)(2,1)} %refs_1_.3, bf16[288,2304]{1,0:T(8,128)(2,1)} %refs_2_.3, bf16[3,288,1152]{2,1,0:T(8,128)(2,1)} %pad_maximum_fusion.5.refs_3_.refs_1_, ...), custom_call_target="tpu_custom_call" | custom-call | flops 509607936 | bytes 1990656 | tf_op jit(solution)/shard_map/pallas_call | solution.py:338
  286.9 13.3 %shard_map.213 = (bf16[3,256,2304]{2,1,0:T(8,128)(2,1)}, bf16[256,2304]{1,0:T(8,128)(2,1)S(1)}) custom-call(f32[3,256,2304]{2,1,0:T(8,128)} %shard_map.212.lin, bf16[3,256,128]{2,1,0:T(8,128)(2,1)S(1)} %copy-done.49, bf16[3,128,2304]{2,1,0:T(8,128)(2,1)S(1)} %slice.206.up, f32[256,256]{1,0:T(8,128)S(1)} %copy-done.32, f32[256,256]{1,0:T(8,128)S(1)} %copy-done.34, ...), custom_call_target="tpu_custom_call" | custom-call | flops 75497472 | bytes 884736 | tf_op jit(solution)/shard_map/pallas_call | solution.py:191
  311.6 9.0 %shard_map.214 = f32[1,256,2304]{2,1,0:T(8,128)} custom-call(s32[3]{0:T(128)} %pad_add_fusion.2.where, bf16[256,2304]{1,0:T(8,128)(2,1)} %copy-done.25, bf16[288,2304]{1,0:T(8,128)(2,1)} %refs_0_.6, bf16[3,288,1152]{2,1,0:T(8,128)(2,1)} %pad_maximum_fusion.5.refs_3_.refs_1_, bf16[3,288,1152]{2,1,0:T(8,128)(2,1)} %collective-permute-done.9.refs_4_.refs_2_, ...), custom_call_target="tpu_custom_call" | custom-call | flops 169869312 | bytes 663552 | tf_op jit(solution)/shard_map/pallas_call | solution.py:338
  332.7 22.6 %collective-permute-done.24 = bf16[256,2304]{1,0:T(8,128)(2,1)S(1)} collective-permute-done((bf16[256,2304]{1,0:T(8,128)(2,1)S(1)}, bf16[256,2304]{1,0:T(8,128)(2,1)S(1)}, u32[]{:S(2)}, u32[]{:S(2)}) %collective-permute-start.24) | collective-permute-done | bytes 1179680 | tf_op jit(solution)/shard_map/ppermute | solution.py:237
  355.3 12.3 %collective-permute-done.25.mates.refs_9_ = bf16[3,288,1536]{2,1,0:T(8,128)(2,1)} collective-permute-done((bf16[3,288,1536]{2,1,0:T(8,128)(2,1)}, bf16[3,288,1536]{2,1,0:T(8,128)(2,1)}, u32[]{:S(2)}, u32[]{:S(2)}) %collective-permute-start.25) | collective-permute-done | bytes 2654240 | tf_op jit(solution)/shard_map/ppermute | solution.py:237
  373.7 4.1 gather_fusion.1
  385.9 12.8 %shard_map.215 = (f32[1024,1536]{1,0:T(8,128)}, bf16[1024,128]{1,0:T(8,128)(2,1)S(1)}) custom-call(s32[3]{0:T(128)S(1)} %pad_add_fusion.4.where, bf16[1024,2304]{1,0:T(8,128)(2,1)S(1)} %pad_maximum_fusion.values, f32[1024,128]{1,0:T(8,128)S(1)} %copy-done.27, bf16[2304,128]{1,0:T(8,128)(2,1)S(1)} %copy-done.31, bf16[128,1536]{1,0:T(8,128)(2,1)S(1)} %copy-done.44, ...), custom_call_target="tpu_custom_call" | custom-call | flops 452984832 | bytes 884736 | tf_op jit(solution)/shard_map/pallas_call | solution.py:577
  399.5 12.9 %shard_map.216 = (f32[1024,1536]{1,0:T(8,128)}, bf16[1024,128]{1,0:T(8,128)(2,1)S(1)}) custom-call(s32[3]{0:T(128)S(1)} %pad_add_fusion.4.where, bf16[1024,2304]{1,0:T(8,128)(2,1)S(1)} %pad_maximum_fusion.values, f32[1024,128]{1,0:T(8,128)S(1)} %copy-done.27, bf16[2304,128]{1,0:T(8,128)(2,1)S(1)} %copy-done.30, bf16[128,1536]{1,0:T(8,128)(2,1)S(1)} %copy-done.46, ...), custom_call_target="tpu_custom_call" | custom-call | flops 452984832 | bytes 884736 | tf_op jit(solution)/shard_map/pallas_call | solution.py:577
  421.4 46.9 %shard_map.217 = (bf16[1024,1536]{1,0:T(8,128)(2,1)}, bf16[1024,1536]{1,0:T(8,128)(2,1)}, bf16[1024,1536]{1,0:T(8,128)(2,1)}, f32[512,2688]{1,0:T(8,128)}, bf16[512,2688]{1,0:T(8,128)(2,1)}) custom-call(s32[3]{0:T(128)} %copy-done.57, f32[1024,1536]{1,0:T(8,128)} %get-tuple-element.148.gt, f32[1024,1536]{1,0:T(8,128)} %get-tuple-element.149.up, ...), custom_call_target="tpu_custom_call" | custom-call | flops 1358954496 | bytes 2654208 | tf_op jit(solution)/shard_map/pallas_call | solution.py:632
  469.5 4.3 collective-permute-done.30
  494.8 4.3 reshape.411.refs_15_
  504.2 11.4 %shard_map.218 = (f32[512,2304]{1,0:T(8,128)}, bf16[512,2304]{1,0:T(8,128)(2,1)}) custom-call(s32[3]{0:T(128)S(1)} %copy-done.58, bf16[1024,1536]{1,0:T(8,128)(2,1)S(1)} %copy-done.60, bf16[4,192,1536]{2,1,0:T(8,128)(2,1)S(1)} %bitcast.247, bf16[192,1536]{1,0:T(8,128)(2,1)S(1)} %copy-done.40, bf16[3,192,1536]{2,1,0:T(8,128)(2,1)S(1)} %copy-done.42, ...), custom_call_target="tpu_custom_call" | custom-call | flops 14495514624 | bytes 28311552 | tf_op jit(solution)/shard_map/pallas_call | solution.py:670
  527.9 4.3 multiply_convert_fusion
  532.2 8.9 %shard_map.221.lin = f32[256,2304]{1,0:T(8,128)} custom-call(s32[3]{0:T(128)} %pad_add_fusion.2.where, bf16[1,256,2304]{2,1,0:T(8,128)(2,1)} %bitcast.244, bf16[288,2304]{1,0:T(8,128)(2,1)} %refs_0_.6, bf16[3,288,1152]{2,1,0:T(8,128)(2,1)} %pad_maximum_fusion.5.refs_3_.refs_1_, bf16[3,288,1152]{2,1,0:T(8,128)(2,1)} %collective-permute-done.9.refs_4_.refs_2_, ...), custom_call_target="tpu_custom_call" | custom-call | flops 169869312 | bytes 663552 | tf_op jit(solution)/shard_map/pallas_call | solution.py:338
  543.3 25.7 %shard_map.222.refs_3_.values = bf16[3,256,2304]{2,1,0:T(8,128)(2,1)} custom-call(bf16[3,256,2304]{2,1,0:T(8,128)(2,1)} %get-tuple-element.128.qkv, f32[256,2304]{1,0:T(8,128)S(1)} %copy-done.12, bf16[256,128]{1,0:T(8,128)(2,1)S(1)} %fusion.37.dz.refs_5_, bf16[2304,128]{1,0:T(8,128)(2,1)S(1)} %copy-done.38, f32[256,256]{1,0:T(8,128)S(1)} %copy-done.33, ...), custom_call_target="tpu_custom_call" | custom-call | flops 75497472 | bytes 884736 | tf_op jit(solution)/shard_map/pallas_call | solution.py:191
  574.3 9.7 %shard_map.223 = bf16[42624,128]{1,0:T(8,128)(2,1)} custom-call(bf16[256,2304]{1,0:T(8,128)(2,1)S(1)} %copy-done.11, bf16[3,256,128]{2,1,0:T(8,128)(2,1)S(1)} %fusion.26.refs_1_, bf16[3,256,128]{2,1,0:T(8,128)(2,1)S(1)} %copy-done.50, bf16[3,256,2304]{2,1,0:T(8,128)(2,1)S(1)} %copy-done, bf16[256,2304]{1,0:T(8,128)(2,1)S(1)} %copy-done.26, ...), custom_call_target="tpu_custom_call" | custom-call | flops 268435456 | bytes 4194304 | tf_op jit(solution)/shard_map/pallas_call | solution.py:853
  584.0 5.4 constant_dynamic-slice_fusion.2
  594.7 4.1 collective-permute-done.34
  601.2 5.6 all-to-all-start.2
  606.8 5.6 add_convert_fusion
  619.3 16.9 %shard_map.224 = f32[256,2304]{1,0:T(8,128)} custom-call(s32[3]{0:T(128)} %pad_add_fusion.2.where, bf16[3,256,2304]{2,1,0:T(8,128)(2,1)} %shard_map.222.refs_3_.values, bf16[288,2304]{1,0:T(8,128)(2,1)} %refs_0_.7, bf16[288,2304]{1,0:T(8,128)(2,1)} %refs_1_.3, bf16[288,2304]{1,0:T(8,128)(2,1)} %refs_2_.3, ...), custom_call_target="tpu_custom_call" | custom-call | flops 509607936 | bytes 1990656 | tf_op jit(solution)/shard_map/pallas_call | solution.py:338
  640.2 12.2 %collective-permute-done.35 = bf16[4,2,664,128]{3,2,0,1:T(8,128)(2,1)} collective-permute-done((bf16[4,2,664,128]{3,2,0,1:T(8,128)(2,1)}, bf16[4,2,664,128]{3,2,0,1:T(8,128)(2,1)}, u32[]{:S(2)}, u32[]{:S(2)}) %collective-permute-start.35) | collective-permute-done | bytes 1359904 | tf_op jit(solution)/shard_map/ppermute | solution.py:237
  654.9 6.5 all-to-all-start.3
  669.6 10.8 %collective-permute-done.37 = bf16[4,664,128]{2,1,0:T(8,128)(2,1)} collective-permute-done((bf16[4,664,128]{2,1,0:T(8,128)(2,1)S(1)}, bf16[4,664,128]{2,1,0:T(8,128)(2,1)}, u32[]{:S(2)}, u32[]{:S(2)}) %collective-permute-start.37) | collective-permute-done | bytes 679968 | tf_op jit(solution)/shard_map/ppermute | solution.py:237
  681.9 10.0 %collective-permute-done.38 = bf16[4,672,128]{2,1,0:T(8,128)(2,1)S(1)} collective-permute-done((bf16[4,672,128]{2,1,0:T(8,128)(2,1)}, bf16[4,672,128]{2,1,0:T(8,128)(2,1)S(1)}, u32[]{:S(2)}, u32[]{:S(2)}) %collective-permute-start.38) | collective-permute-done | bytes 688160 | tf_op jit(solution)/shard_map/ppermute | solution.py:237
  693.1 4.6 collective-permute-start.41
  698.4 8.1 collective-permute-done.41
  706.6 17.4 %collective-permute-done.40 = bf16[1336,128]{1,0:T(8,128)(2,1)S(1)} collective-permute-done((bf16[1336,128]{1,0:T(8,128)(2,1)}, bf16[1336,128]{1,0:T(8,128)(2,1)S(1)}, u32[]{:S(2)}, u32[]{:S(2)}) %collective-permute-start.40) | collective-permute-done | bytes 342048 | tf_op jit(solution)/shard_map/ppermute | solution.py:237
  732.1 35.0 %all-gather.27.cloned.1.call-done = bf16[5344,128]{1,0:T(8,128)(2,1)} async-done(((bf16[1336,128]{1,0:T(8,128)(2,1)}), bf16[5344,128]{1,0:T(8,128)(2,1)}) %all-gather.27.cloned.1.call-update) | async-done | bytes 1368080 | tf_op jit(solution)/shard_map/all_gather | solution.py:253
  774.9 12.3 %collective-permute-done.44 = bf16[4,664,128]{2,1,0:T(8,128)(2,1)} collective-permute-done((bf16[4,664,128]{2,1,0:T(8,128)(2,1)}, bf16[4,664,128]{2,1,0:T(8,128)(2,1)}, u32[]{:S(2)}, u32[]{:S(2)}) %collective-permute-start.44) | collective-permute-done | bytes 679968 | tf_op jit(solution)/shard_map/ppermute | solution.py:237
  794.1 9.6 %collective-permute-done.53 = bf16[4,672,128]{2,1,0:T(8,128)(2,1)S(1)} collective-permute-done((bf16[4,672,128]{2,1,0:T(8,128)(2,1)}, bf16[4,672,128]{2,1,0:T(8,128)(2,1)S(1)}, u32[]{:S(2)}, u32[]{:S(2)}) %collective-permute-start.53) | collective-permute-done | bytes 688160 | tf_op jit(solution)/shard_map/ppermute | solution.py:237
  804.3 13.4 %collective-permute-done.48 = bf16[4,664,128]{2,1,0:T(8,128)(2,1)} collective-permute-done((bf16[4,664,128]{2,1,0:T(8,128)(2,1)}, bf16[4,664,128]{2,1,0:T(8,128)(2,1)}, u32[]{:S(2)}, u32[]{:S(2)}) %collective-permute-start.48) | collective-permute-done | bytes 679968 | tf_op jit(solution)/shard_map/ppermute | solution.py:237
  825.1 3.9 copy.127
  (521 shorter events, 251.7 us)
Async XLA Ops:
  7.2 80.3 %all-gather.15.cloned.1.call-start = ((), (), s32[]{:S(2)}) async-start(), calls=%async_computation.4 | async-start | bytes 3317760 | tf_op jit(solution)/shard_map/all_gather | solution.py:253
  11.8 118.5 %all-gather.17.cloned.1.call-start = ((), (), s32[]{:S(2)}) async-start(), calls=%async_computation.5 | async-start | bytes 3317760 | tf_op jit(solution)/shard_map/all_gather | solution.py:253
  11.9 32.5 %collective-permute-start = (bf16[288,2304]{1,0:T(8,128)(2,1)}, bf16[288,2304]{1,0:T(8,128)(2,1)}, u32[]{:S(2)}, u32[]{:S(2)}) collective-permute-start(bf16[288,2304]{1,0:T(8,128)(2,1)} %copy-done.81), channel_id=1, source_target_pairs={{0,4},{1,5},{2,6},{3,7},{4,0},{5,1},{6,2},{7,3},{8,12},{9,13},{10,... | collective-permute-start | bytes 3981320 | tf_op jit(solution)/shard_map/ppermute | solution.py:237
  15.0 29.4 %collective-permute-start.1 = (s32[1,8]{1,0:T(1,128)S(1)}, s32[1,8]{1,0:T(1,128)S(1)}, u32[]{:S(2)}, u32[]{:S(2)}) collective-permute-start(s32[1,8]{1,0:T(1,128)S(1)} %pad_add_fusion.1), channel_id=1, source_target_pairs={{0,4},{1,5},{2,6},{3,7},{4,0},{5,1},{6,2},{7,3},{8,12},{9,13},{10,... | collective-permute-start | bytes 104 | tf_op jit(solution)/shard_map/ppermute | solution.py:237
  15.0 194.0 %all-gather.19.cloned.1.call-start = ((), (), s32[]{:S(2)}) async-start(), calls=%async_computation.6 | async-start | bytes 4423680 | tf_op jit(solution)/shard_map/all_gather | solution.py:253
  44.4 43.1 %collective-permute-start.4 = (bf16[288,2304]{1,0:T(8,128)(2,1)}, bf16[288,2304]{1,0:T(8,128)(2,1)}, u32[]{:S(2)}, u32[]{:S(2)}) collective-permute-start(bf16[288,2304]{1,0:T(8,128)(2,1)} %collective-permute-done.refs_19_.refs_17_), channel_id=1, source_target_pairs={{0,2},{1,3},{2,0},{3,1},{4,6},{5,7},{6,4},{7,5},{8,10},{9,11},{10,... | collective-permute-start | bytes 3981320 | tf_op jit(solution)/shard_map/ppermute | solution.py:237
  46.1 41.3 %collective-permute-start.5 = (bf16[288,2304]{1,0:T(8,128)(2,1)}, bf16[288,2304]{1,0:T(8,128)(2,1)S(1)}, u32[]{:S(2)}, u32[]{:S(2)}) collective-permute-start(bf16[288,2304]{1,0:T(8,128)(2,1)} %collective-permute-done.refs_19_.refs_17_), channel_id=1, source_target_pairs={{0,1},{1,0},{2,3},{3,2},{4,5},{5,4},{6,7},{7,6},{8,9},{9,8},{10,11... | collective-permute-start | bytes 3981320 | tf_op jit(solution)/shard_map/ppermute | solution.py:237
  47.6 39.8 %collective-permute-start.3 = (bf16[288,1536]{1,0:T(8,128)(2,1)S(1)}, bf16[288,1536]{1,0:T(8,128)(2,1)}, u32[]{:S(2)}, u32[]{:S(2)}) collective-permute-start(bf16[288,1536]{1,0:T(8,128)(2,1)S(1)} %get-tuple-element.98), channel_id=1, source_target_pairs={{0,4},{1,5},{2,6},{3,7},{4,0},{5,1},{6,2},{7,3},{8,12},{9,13},{10,... | collective-permute-start | bytes 2654216 | tf_op jit(solution)/shard_map/ppermute | solution.py:237
  91.2 45.3 %collective-permute-start.7 = (bf16[3,288,1152]{2,1,0:T(8,128)(2,1)}, bf16[3,288,1152]{2,1,0:T(8,128)(2,1)}, u32[]{:S(2)}, u32[]{:S(2)}) collective-permute-start(bf16[3,288,1152]{2,1,0:T(8,128)(2,1)} %pad_maximum_fusion.5.refs_3_.refs_1_), channel_id=1, source_target_pairs={{0,2},{1,3},{2,0},{3,1},{4,6},{5,7},{6,4},{7,5},{8,10},{9,11},{10,... | collective-permute-start | bytes 5971976 | tf_op jit(solution)/shard_map/ppermute | solution.py:237
  91.5 56.1 %collective-permute-start.8 = (bf16[3,288,1152]{2,1,0:T(8,128)(2,1)}, bf16[3,288,1152]{2,1,0:T(8,128)(2,1)}, u32[]{:S(2)}, u32[]{:S(2)}) collective-permute-start(bf16[3,288,1152]{2,1,0:T(8,128)(2,1)} %pad_maximum_fusion.5.refs_3_.refs_1_), channel_id=1, source_target_pairs={{0,4},{1,5},{2,6},{3,7},{4,0},{5,1},{6,2},{7,3},{8,12},{9,13},{10,... | collective-permute-start | bytes 5971976 | tf_op jit(solution)/shard_map/ppermute | solution.py:237
  93.2 54.3 %collective-permute-start.9 = (bf16[3,288,1152]{2,1,0:T(8,128)(2,1)}, bf16[3,288,1152]{2,1,0:T(8,128)(2,1)}, u32[]{:S(2)}, u32[]{:S(2)}) collective-permute-start(bf16[3,288,1152]{2,1,0:T(8,128)(2,1)} %pad_maximum_fusion.5.refs_3_.refs_1_), channel_id=1, source_target_pairs={{0,1},{1,0},{2,3},{3,2},{4,5},{5,4},{6,7},{7,6},{8,9},{9,8},{10,11... | collective-permute-start | bytes 5971976 | tf_op jit(solution)/shard_map/ppermute | solution.py:237
  100.0 30.4 %collective-permute-start.10 = (bf16[288,2304]{1,0:T(8,128)(2,1)}, bf16[288,2304]{1,0:T(8,128)(2,1)}, u32[]{:S(2)}, u32[]{:S(2)}) collective-permute-start(bf16[288,2304]{1,0:T(8,128)(2,1)} %collective-permute-done.4.refs_21_.refs_19_), channel_id=1, source_target_pairs={{0,1},{1,0},{2,3},{3,2},{4,5},{5,4},{6,7},{7,6},{8,9},{9,8},{10,11... | collective-permute-start | bytes 3981320 | tf_op jit(solution)/shard_map/ppermute | solution.py:237
  112.1 72.3 %all-to-all-start = ((bf16[8,32,2304]{2,1,0:T(8,128)(2,1)}), bf16[8,32,2304]{2,1,0:T(8,128)(2,1)S(1)}, u32[]{:S(2)}, u32[]{:S(2)}) async-start(bf16[8,32,2304]{2,1,0:T(8,128)(2,1)} %bitcast.272), calls=%async_computation | async-start | bytes 2359296 | tf_op jit(solution)/shard_map/all_to_all | solution.py:1003
  117.0 183.7 %all-gather.21.cloned.1.call-start = ((), (), s32[]{:S(2)}) async-start(), calls=%async_computation.7 | async-start | bytes 4423680 | tf_op jit(solution)/shard_map/all_gather | solution.py:253
  150.7 42.8 %collective-permute-start.11 = (bf16[3,288,1152]{2,1,0:T(8,128)(2,1)}, bf16[3,288,1152]{2,1,0:T(8,128)(2,1)}, u32[]{:S(2)}, u32[]{:S(2)}) collective-permute-start(bf16[3,288,1152]{2,1,0:T(8,128)(2,1)} %pad_maximum_fusion.6.refs_7_.refs_5_), channel_id=1, source_target_pairs={{0,2},{1,3},{2,0},{3,1},{4,6},{5,7},{6,4},{7,5},{8,10},{9,11},{10,... | collective-permute-start | bytes 5971976 | tf_op jit(solution)/shard_map/ppermute | solution.py:237
  152.5 42.4 %collective-permute-start.12 = (bf16[3,288,1152]{2,1,0:T(8,128)(2,1)}, bf16[3,288,1152]{2,1,0:T(8,128)(2,1)}, u32[]{:S(2)}, u32[]{:S(2)}) collective-permute-start(bf16[3,288,1152]{2,1,0:T(8,128)(2,1)} %pad_maximum_fusion.6.refs_7_.refs_5_), channel_id=1, source_target_pairs={{0,4},{1,5},{2,6},{3,7},{4,0},{5,1},{6,2},{7,3},{8,12},{9,13},{10,... | collective-permute-start | bytes 5971976 | tf_op jit(solution)/shard_map/ppermute | solution.py:237
  152.5 42.4 %collective-permute-start.13 = (bf16[3,288,1152]{2,1,0:T(8,128)(2,1)}, bf16[3,288,1152]{2,1,0:T(8,128)(2,1)}, u32[]{:S(2)}, u32[]{:S(2)}) collective-permute-start(bf16[3,288,1152]{2,1,0:T(8,128)(2,1)} %pad_maximum_fusion.6.refs_7_.refs_5_), channel_id=1, source_target_pairs={{0,1},{1,0},{2,3},{3,2},{4,5},{5,4},{6,7},{7,6},{8,9},{9,8},{10,11... | collective-permute-start | bytes 5971976 | tf_op jit(solution)/shard_map/ppermute | solution.py:237
  152.5 42.4 %collective-permute-start.14 = (bf16[3,288,1152]{2,1,0:T(8,128)(2,1)}, bf16[3,288,1152]{2,1,0:T(8,128)(2,1)}, u32[]{:S(2)}, u32[]{:S(2)}) collective-permute-start(bf16[3,288,1152]{2,1,0:T(8,128)(2,1)} %collective-permute-done.7.refs_5_.refs_3_), channel_id=1, source_target_pairs={{0,1},{1,0},{2,3},{3,2},{4,5},{5,4},{6,7},{7,6},{8,9},{9,8},{10,11... | collective-permute-start | bytes 5971976 | tf_op jit(solution)/shard_map/ppermute | solution.py:237
  153.0 41.9 %collective-permute-start.15 = (bf16[3,288,1152]{2,1,0:T(8,128)(2,1)}, bf16[3,288,1152]{2,1,0:T(8,128)(2,1)}, u32[]{:S(2)}, u32[]{:S(2)}) collective-permute-start(bf16[3,288,1152]{2,1,0:T(8,128)(2,1)} %collective-permute-done.8.refs_11_.refs_9_), channel_id=1, source_target_pairs={{0,1},{1,0},{2,3},{3,2},{4,5},{5,4},{6,7},{7,6},{8,9},{9,8},{10,11... | collective-permute-start | bytes 5971976 | tf_op jit(solution)/shard_map/ppermute | solution.py:237
  194.9 47.2 %collective-permute-start.17 = (bf16[3,288,1152]{2,1,0:T(8,128)(2,1)}, bf16[3,288,1152]{2,1,0:T(8,128)(2,1)}, u32[]{:S(2)}, u32[]{:S(2)}) collective-permute-start(bf16[3,288,1152]{2,1,0:T(8,128)(2,1)} %collective-permute-done.12.refs_15_.refs_13_), channel_id=1, source_target_pairs={{0,2},{1,3},{2,0},{3,1},{4,6},{5,7},{6,4},{7,5},{8,10},{9,11},{10,... | collective-permute-start | bytes 5971976 | tf_op jit(solution)/shard_map/ppermute | solution.py:237
  196.0 46.1 %collective-permute-start.19 = (bf16[3,288,1152]{2,1,0:T(8,128)(2,1)}, bf16[3,288,1152]{2,1,0:T(8,128)(2,1)}, u32[]{:S(2)}, u32[]{:S(2)}) collective-permute-start(bf16[3,288,1152]{2,1,0:T(8,128)(2,1)} %collective-permute-done.12.refs_15_.refs_13_), channel_id=1, source_target_pairs={{0,1},{1,0},{2,3},{3,2},{4,5},{5,4},{6,7},{7,6},{8,9},{9,8},{10,11... | collective-permute-start | bytes 5971976 | tf_op jit(solution)/shard_map/ppermute | solution.py:237
  196.0 46.1 %collective-permute-start.16 = (bf16[3,288,1152]{2,1,0:T(8,128)(2,1)}, bf16[3,288,1152]{2,1,0:T(8,128)(2,1)}, u32[]{:S(2)}, u32[]{:S(2)}) collective-permute-start(bf16[3,288,1152]{2,1,0:T(8,128)(2,1)} %collective-permute-done.7.refs_5_.refs_3_), channel_id=1, source_target_pairs={{0,4},{1,5},{2,6},{3,7},{4,0},{5,1},{6,2},{7,3},{8,12},{9,13},{10,... | collective-permute-start | bytes 5971976 | tf_op jit(solution)/shard_map/ppermute | solution.py:237
  196.0 46.1 %collective-permute-start.18 = (bf16[3,288,1152]{2,1,0:T(8,128)(2,1)}, bf16[3,288,1152]{2,1,0:T(8,128)(2,1)}, u32[]{:S(2)}, u32[]{:S(2)}) collective-permute-start(bf16[3,288,1152]{2,1,0:T(8,128)(2,1)} %collective-permute-done.11.refs_9_.refs_7_), channel_id=1, source_target_pairs={{0,1},{1,0},{2,3},{3,2},{4,5},{5,4},{6,7},{7,6},{8,9},{9,8},{10,11... | collective-permute-start | bytes 5971976 | tf_op jit(solution)/shard_map/ppermute | solution.py:237
  242.1 27.2 %collective-permute-start.20 = (bf16[3,288,1152]{2,1,0:T(8,128)(2,1)}, bf16[3,288,1152]{2,1,0:T(8,128)(2,1)}, u32[]{:S(2)}, u32[]{:S(2)}) collective-permute-start(bf16[3,288,1152]{2,1,0:T(8,128)(2,1)} %collective-permute-done.16.refs_13_.refs_11_), channel_id=1, source_target_pairs={{0,1},{1,0},{2,3},{3,2},{4,5},{5,4},{6,7},{7,6},{8,9},{9,8},{10,11... | collective-permute-start | bytes 5971976 | tf_op jit(solution)/shard_map/ppermute | solution.py:237
  242.2 27.1 %collective-permute-start.21 = (bf16[3,288,1152]{2,1,0:T(8,128)(2,1)}, bf16[3,288,1152]{2,1,0:T(8,128)(2,1)}, u32[]{:S(2)}, u32[]{:S(2)}) collective-permute-start(bf16[3,288,1152]{2,1,0:T(8,128)(2,1)} %collective-permute-done.17.refs_17_.refs_15_), channel_id=1, source_target_pairs={{0,1},{1,0},{2,3},{3,2},{4,5},{5,4},{6,7},{7,6},{8,9},{9,8},{10,11... | collective-permute-start | bytes 5971976 | tf_op jit(solution)/shard_map/ppermute | solution.py:237
  244.9 42.0 %collective-permute-start.22 = (bf16[192,2304]{1,0:T(8,128)(2,1)}, bf16[192,2304]{1,0:T(8,128)(2,1)}, u32[]{:S(2)}, u32[]{:S(2)}) collective-permute-start(bf16[192,2304]{1,0:T(8,128)(2,1)} %pad_bitcast_fusion.1), channel_id=1, source_target_pairs={{0,4},{1,5},{2,6},{3,7},{4,0},{5,1},{6,2},{7,3},{8,12},{9,13},{10,... | collective-permute-start | bytes 2654216 | tf_op jit(solution)/shard_map/ppermute | solution.py:237
  248.8 71.9 %collective-permute-start.23 = (bf16[3,288,1536]{2,1,0:T(8,128)(2,1)}, bf16[3,288,1536]{2,1,0:T(8,128)(2,1)}, u32[]{:S(2)}, u32[]{:S(2)}) collective-permute-start(bf16[3,288,1536]{2,1,0:T(8,128)(2,1)} %pad_maximum_fusion.1), channel_id=1, source_target_pairs={{0,2},{1,3},{2,0},{3,1},{4,6},{5,7},{6,4},{7,5},{8,10},{9,11},{10,... | collective-permute-start | bytes 7962632 | tf_op jit(solution)/shard_map/ppermute | solution.py:237
  251.8 80.9 %all-to-all-start.1 = ((bf16[8,32,2304]{2,1,0:T(8,128)(2,1)}), bf16[8,32,2304]{2,1,0:T(8,128)(2,1)}, u32[]{:S(2)}, u32[]{:S(2)}) async-start(bf16[8,32,2304]{2,1,0:T(8,128)(2,1)} %bitcast.273), calls=%async_computation.1 | async-start | bytes 2359296 | tf_op jit(solution)/shard_map/all_to_all | solution.py:1028
  257.9 109.8 %all-gather.23.cloned.1.call-start = ((), (), s32[]{:S(2)}) async-start(), calls=%async_computation.8 | async-start | bytes 2949120 | tf_op jit(solution)/shard_map/all_gather | solution.py:253
  303.1 110.0 %all-gather.25.cloned.1.call-start = ((), (), s32[]{:S(2)}) async-start(), calls=%async_computation.9 | async-start | bytes 2949120 | tf_op jit(solution)/shard_map/all_gather | solution.py:253
  306.8 60.8 %collective-permute-start.25 = (bf16[3,288,1536]{2,1,0:T(8,128)(2,1)}, bf16[3,288,1536]{2,1,0:T(8,128)(2,1)}, u32[]{:S(2)}, u32[]{:S(2)}) collective-permute-start(bf16[3,288,1536]{2,1,0:T(8,128)(2,1)} %pad_maximum_fusion.2), channel_id=1, source_target_pairs={{0,2},{1,3},{2,0},{3,1},{4,6},{5,7},{6,4},{7,5},{8,10},{9,11},{10,... | collective-permute-start | bytes 7962632 | tf_op jit(solution)/shard_map/ppermute | solution.py:237
  326.9 28.5 %collective-permute-start.24 = (bf16[256,2304]{1,0:T(8,128)(2,1)S(1)}, bf16[256,2304]{1,0:T(8,128)(2,1)S(1)}, u32[]{:S(2)}, u32[]{:S(2)}) collective-permute-start(bf16[256,2304]{1,0:T(8,128)(2,1)S(1)} %multiply_convert_fusion.1.refs_8_), channel_id=1, source_target_pairs={{0,4},{1,5},{2,6},{3,7},{4,0},{5,1},{6,2},{7,3},{8,12},{9,13},{10,... | collective-permute-start | bytes 3538952 | tf_op jit(solution)/shard_map/ppermute | solution.py:237
  371.7 41.4 %collective-permute-start.27 = (bf16[3,192,1536]{2,1,0:T(8,128)(2,1)}, bf16[3,192,1536]{2,1,0:T(8,128)(2,1)S(1)}, u32[]{:S(2)}, u32[]{:S(2)}) collective-permute-start(bf16[3,192,1536]{2,1,0:T(8,128)(2,1)} %pad_maximum_fusion.7), channel_id=1, source_target_pairs={{0,2},{1,3},{2,0},{3,1},{4,6},{5,7},{6,4},{7,5},{8,10},{9,11},{10,... | collective-permute-start | bytes 5308424 | tf_op jit(solution)/shard_map/ppermute | solution.py:237
  380.6 32.5 %collective-permute-start.28 = (bf16[256,2432]{1,0:T(8,128)(2,1)}, bf16[256,2432]{1,0:T(8,128)(2,1)}, u32[]{:S(2)}, u32[]{:S(2)}) collective-permute-start(bf16[256,2432]{1,0:T(8,128)(2,1)} %pad_maximum_fusion.9), channel_id=1, source_target_pairs={{0,4},{1,5},{2,6},{3,7},{4,0},{5,1},{6,2},{7,3},{8,12},{9,13},{10,... | collective-permute-start | bytes 3735560 | tf_op jit(solution)/shard_map/ppermute | solution.py:237
  478.4 37.2 %collective-permute-start.31 = (bf16[256,2688]{1,0:T(8,128)(2,1)}, bf16[256,2688]{1,0:T(8,128)(2,1)}, u32[]{:S(2)}, u32[]{:S(2)}) collective-permute-start(bf16[256,2688]{1,0:T(8,128)(2,1)} %unstack.34), channel_id=1, source_target_pairs={{0,4},{1,5},{2,6},{3,7},{4,0},{5,1},{6,2},{7,3},{8,12},{9,13},{10,... | collective-permute-start | bytes 4128776 | tf_op jit(solution)/shard_map/ppermute | solution.py:237
  526.6 42.6 %collective-permute-start.33 = (bf16[256,2304]{1,0:T(8,128)(2,1)}, bf16[256,2304]{1,0:T(8,128)(2,1)}, u32[]{:S(2)}, u32[]{:S(2)}) collective-permute-start(bf16[256,2304]{1,0:T(8,128)(2,1)} %unstack.35), channel_id=1, source_target_pairs={{0,4},{1,5},{2,6},{3,7},{4,0},{5,1},{6,2},{7,3},{8,12},{9,13},{10,... | collective-permute-start | bytes 3538952 | tf_op jit(solution)/shard_map/ppermute | solution.py:237
  601.2 51.2 %all-to-all-start.2 = ((bf16[8,32,2304]{2,1,0:T(8,128)(2,1)}), bf16[8,32,2304]{2,1,0:T(8,128)(2,1)}, u32[]{:S(2)}, u32[]{:S(2)}) async-start(bf16[8,32,2304]{2,1,0:T(8,128)(2,1)} %bitcast.57), calls=%async_computation.2 | async-start | bytes 2359296 | tf_op jit(solution)/shard_map/all_to_all | solution.py:1178
  614.5 38.0 %collective-permute-start.35 = (bf16[4,2,664,128]{3,2,0,1:T(8,128)(2,1)}, bf16[4,2,664,128]{3,2,0,1:T(8,128)(2,1)}, u32[]{:S(2)}, u32[]{:S(2)}) collective-permute-start(bf16[4,2,664,128]{3,2,0,1:T(8,128)(2,1)} %bitcast.237), channel_id=1, source_target_pairs={{0,4},{1,5},{2,6},{3,7},{4,0},{5,1},{6,2},{7,3},{8,12},{9,13},{10,... | collective-permute-start | bytes 4079624 | tf_op jit(solution)/shard_map/ppermute | solution.py:237
  617.7 34.7 %collective-permute-start.36 = (bf16[4,2,672,128]{3,2,1,0:T(8,128)(2,1)}, bf16[4,2,672,128]{3,2,1,0:T(8,128)(2,1)}, u32[]{:S(2)}, u32[]{:S(2)}) collective-permute-start(bf16[4,2,672,128]{3,2,1,0:T(8,128)(2,1)} %dynamic-slice_bitcast_fusion), channel_id=1, source_target_pairs={{0,2},{1,3},{2,0},{3,1},{4,6},{5,7},{6,4},{7,5},{8,10},{9,11},{10,... | collective-permute-start | bytes 4128776 | tf_op jit(solution)/shard_map/ppermute | solution.py:237
  654.9 37.2 %all-to-all-start.3 = ((bf16[8,32,2304]{2,1,0:T(8,128)(2,1)}), bf16[8,32,2304]{2,1,0:T(8,128)(2,1)}, u32[]{:S(2)}, u32[]{:S(2)}) async-start(bf16[8,32,2304]{2,1,0:T(8,128)(2,1)} %bitcast.265), calls=%async_computation.3 | async-start | bytes 2359296 | tf_op jit(solution)/shard_map/all_to_all | solution.py:1186
  661.3 105.8 %all-gather.27.cloned.1.call-start = ((), (), s32[]{:S(2)}) async-start(), calls=%async_computation.10 | async-start | bytes 1710080 | tf_op jit(solution)/shard_map/all_gather | solution.py:253
  667.6 24.2 %collective-permute-start.38 = (bf16[4,672,128]{2,1,0:T(8,128)(2,1)}, bf16[4,672,128]{2,1,0:T(8,128)(2,1)S(1)}, u32[]{:S(2)}, u32[]{:S(2)}) collective-permute-start(bf16[4,672,128]{2,1,0:T(8,128)(2,1)} %dynamic-slice_bitcast_fusion.3), channel_id=1, source_target_pairs={{0,4},{1,5},{2,6},{3,7},{4,0},{5,1},{6,2},{7,3},{8,12},{9,13},{10,... | collective-permute-start | bytes 2064392 | tf_op jit(solution)/shard_map/ppermute | solution.py:237
  697.7 26.2 %collective-permute-start.40 = (bf16[1336,128]{1,0:T(8,128)(2,1)}, bf16[1336,128]{1,0:T(8,128)(2,1)S(1)}, u32[]{:S(2)}, u32[]{:S(2)}) collective-permute-start(bf16[1336,128]{1,0:T(8,128)(2,1)} %get-tuple-element.231), channel_id=1, source_target_pairs={{0,16},{1,17},{2,18},{3,19},{4,20},{5,21},{6,22},{7,23},{8,24},{9,... | collective-permute-start | bytes 1026056 | tf_op jit(solution)/shard_map/ppermute | solution.py:237
  697.7 26.2 %collective-permute-start.39 = (bf16[1336,128]{1,0:T(8,128)(2,1)}, bf16[1336,128]{1,0:T(8,128)(2,1)S(1)}, u32[]{:S(2)}, u32[]{:S(2)}) collective-permute-start(bf16[1336,128]{1,0:T(8,128)(2,1)} %get-tuple-element.232), channel_id=1, source_target_pairs={{0,8},{1,9},{2,10},{3,11},{4,12},{5,13},{6,14},{7,15},{8,16},{9,17... | collective-permute-start | bytes 1026056 | tf_op jit(solution)/shard_map/ppermute | solution.py:237
  774.3 29.4 %collective-permute-start.53 = (bf16[4,672,128]{2,1,0:T(8,128)(2,1)}, bf16[4,672,128]{2,1,0:T(8,128)(2,1)S(1)}, u32[]{:S(2)}, u32[]{:S(2)}) collective-permute-start(bf16[4,672,128]{2,1,0:T(8,128)(2,1)} %slice.251), channel_id=1, source_target_pairs={{0,4},{1,5},{2,6},{3,7},{4,0},{5,1},{6,2},{7,3},{8,12},{9,13},{10,... | collective-permute-start | bytes 2064392 | tf_op jit(solution)/shard_map/ppermute | solution.py:237
  787.2 30.5 %collective-permute-start.48 = (bf16[4,664,128]{2,1,0:T(8,128)(2,1)}, bf16[4,664,128]{2,1,0:T(8,128)(2,1)}, u32[]{:S(2)}, u32[]{:S(2)}) collective-permute-start(bf16[4,664,128]{2,1,0:T(8,128)(2,1)} %collective-permute-done.44), channel_id=1, source_target_pairs={{0,4},{1,5},{2,6},{3,7},{4,0},{5,1},{6,2},{7,3},{8,12},{9,13},{10,... | collective-permute-start | bytes 2039816 | tf_op jit(solution)/shard_map/ppermute | solution.py:237
  790.2 29.9 %collective-permute-start.51 = (bf16[4,672,128]{2,1,0:T(8,128)(2,1)}, bf16[4,672,128]{2,1,0:T(8,128)(2,1)S(1)}, u32[]{:S(2)}, u32[]{:S(2)}) collective-permute-start(bf16[4,672,128]{2,1,0:T(8,128)(2,1)} %slice.251), channel_id=1, source_target_pairs={{0,2},{1,3},{2,0},{3,1},{4,6},{5,7},{6,4},{7,5},{8,10},{9,11},{10,... | collective-permute-start | bytes 2064392 | tf_op jit(solution)/shard_map/ppermute | solution.py:237
  791.8 28.9 %collective-permute-start.47 = (bf16[4,664,128]{2,1,0:T(8,128)(2,1)}, bf16[4,664,128]{2,1,0:T(8,128)(2,1)S(1)}, u32[]{:S(2)}, u32[]{:S(2)}) collective-permute-start(bf16[4,664,128]{2,1,0:T(8,128)(2,1)} %collective-permute-done.46), channel_id=1, source_target_pairs={{0,1},{1,0},{2,3},{3,2},{4,5},{5,4},{6,7},{7,6},{8,9},{9,8},{10,11... | collective-permute-start | bytes 2039816 | tf_op jit(solution)/shard_map/ppermute | solution.py:237
  (148 other events, 1569.4 us)
Sparse Core Ops, SparseCore 0:
  11.9 58.0 all-gather.14
  72.2 58.1 all-gather.16
  132.5 76.5 all-gather.18
  210.5 90.2 all-gather.20
  303.2 52.7 all-gather.22
  357.4 49.2 all-gather.24
  732.2 34.8 all-gather.26
